TPU v7x, 32 devices: a whole 2x2x4 slice. The times are simulated.
32 devices in a mesh: shard: 2 (over y), expert: 16 (over z, x, core).
Axes of the slice: x: 2, y: 2, z: 4, core: 2. Of those that a mesh axis runs over, the one named last changes fastest.
Arguments:
- tokens: bfloat16 [4096, 2048], P(('shard', 'expert')), may hold values from -6 to 6
- document_lengths: int32 [2, 4], replicated, may hold values from 1 to 1280, 2048 in all within a row
- routes: int32 [4096, 6], P(('shard', 'expert')), may hold values from 0 to 15, all different within a row; in each aligned block of 128 rows (0 to 127, 128 to 255, ...) at most 64 rows name the same one
- first_gain: float32 [2048], replicated, may hold values from 0.5 to 1.5
- query_weight: bfloat16 [2048, 3072], P('shard'), may hold values from -0.125 to 0.125
- latent_down: bfloat16 [2048, 576], P('shard'), may hold values from -0.125 to 0.125
- latent_gain: float32 [512], replicated, may hold values from 0.5 to 1.5
- latent_up: bfloat16 [512, 4096], P('shard'), may hold values from -0.25 to 0.25
- output_weight: bfloat16 [2048, 2048], P('shard'), may hold values from -1.5 to 1.5
- second_gain: float32 [2048], replicated, may hold values from 0.5 to 1.5
- router_weight: bfloat16 [2048, 16], replicated, may hold values from -0.0625 to 0.0625
- shared_gate: bfloat16 [2048, 2816], P('shard'), may hold values from -0.125 to 0.125
- shared_up: bfloat16 [2048, 2816], P('shard'), may hold values from -0.125 to 0.125
- shared_down: bfloat16 [2816, 2048], P('shard'), may hold values from -0.15625 to 0.15625
- expert_gate: bfloat16 [16, 2048, 1408], P('expert', 'shard'), may hold values from -0.125 to 0.125
- expert_up: bfloat16 [16, 2048, 1408], P('expert', 'shard'), may hold values from -0.125 to 0.125
- expert_down: bfloat16 [16, 1408, 2048], P('expert', 'shard'), may hold values from -0.4375 to 0.4375
- cotangent: bfloat16 [4096, 2048], P(('shard', 'expert')), may hold values from -6 to 6
Outputs:
- activations: bfloat16 [4096, 2048], P(('shard', 'expert'))
- input_grad: float32 [4096, 2048], P(('shard', 'expert'))
- first_gain_grad: float32 [2048], P(('shard', 'expert'))
- query_weight_grad: float32 [2048, 3072], P(('shard', 'expert'))
- latent_down_grad: float32 [2048, 576], P(('shard', 'expert'))
- latent_gain_grad: float32 [512], P(('shard', 'expert'))
- latent_up_grad: float32 [512, 4096], P(('shard', 'expert'))
- output_weight_grad: float32 [2048, 2048], P(('shard', 'expert'))
- second_gain_grad: float32 [2048], P(('shard', 'expert'))
- router_weight_grad: float32 [2048, 16], P(('shard', 'expert'))
- shared_gate_grad: float32 [2048, 2816], P(('shard', 'expert'))
- shared_up_grad: float32 [2048, 2816], P(('shard', 'expert'))
- shared_down_grad: float32 [2816, 2048], P(('shard', 'expert'))
- expert_gate_grad: float32 [16, 2048, 1408], P('expert', 'shard')
- expert_up_grad: float32 [16, 2048, 1408], P('expert', 'shard')
- expert_down_grad: float32 [16, 1408, 2048], P('expert', 'shard')
Inputs may be any that keep to these rules, and one draw needn't show every extreme that they name: `routes`: each row names 6 different experts; among the rows of one device no expert is named more than 64 times, and in every draw some device names some expert exactly 64 times. `document_lengths`: each row lists the documents of one packed sequence in order and sums to 2048; its last entry is padding; the largest entry of every row is 1280.
All inputs are finite; a program needn't handle non-finite values.
Results may differ from a plain program's by a relative error of at most 0.02.
Values may be sent and summed in bfloat16 or wider, within the bound.
A program may use at most 512 MiB of HBM per device.

v0:
```python
import math

import jax
import jax.numpy as jnp
from jax import lax
from jax.sharding import PartitionSpec as P

HEADS = 16
QK_NOPE = 128
QK_ROPE = 64
V_HEAD = 128
KV_RANK = 512
TOP = 6
SEQ = 2048
WINDOW = 1024


EPS = 1e-06
THETA = 10000.0
NEG = -1e30
HIGH = lax.Precision.HIGHEST


def passed_along(value, axis, steps):
    count = lax.axis_size(axis)
    initial, last = (max(0, -steps), min(count, count - steps))
    return lax.ppermute(value, axis, [(source, source + steps) for source in range(initial, last)])


def matmul(left, right):
    return jnp.dot(left, right, preferred_element_type=jnp.float32)


def matmul_tn(left, right):
    return lax.dot_general(
        left, right, (((0,), (0,)), ((), ())), preferred_element_type=jnp.float32
    )


def matmul_nt(left, right):
    return lax.dot_general(
        left, right, (((1,), (1,)), ((), ())), preferred_element_type=jnp.float32
    )


def norm_scale(values, gain):
    return values * lax.rsqrt(jnp.mean(values * values, axis=-1, keepdims=True) + EPS) * gain


def rotary_tables(positions, width):
    half = width // 2
    freqs = THETA ** (-jnp.arange(half, dtype=jnp.float32) / half)
    angles = positions.astype(jnp.float32)[:, None] * freqs[None, :]
    return (jnp.cos(angles), jnp.sin(angles))


def rotate(values, cosine_part, sine_part):
    half = values.shape[-1] // 2
    first = values[..., :half]
    second = values[..., half:]
    return jnp.concatenate(
        [first * cosine_part - second * sine_part, second * cosine_part + first * sine_part],
        axis=-1,
    )


def unrotate(values, cosine_part, sine_part):
    half = values.shape[-1] // 2
    first = values[..., :half]
    second = values[..., half:]
    return jnp.concatenate(
        [first * cosine_part + second * sine_part, second * cosine_part - first * sine_part],
        axis=-1,
    )


def swish_parts(values):
    sigmoid_part = jax.nn.sigmoid(values)
    return (values * sigmoid_part, sigmoid_part * (1.0 + values * (1.0 - sigmoid_part)))


def document_ids(positions, lengths):
    sequence_count = lengths.shape[0]
    entry_count = lengths.shape[1]
    ends = jnp.cumsum(lengths, axis=1)
    sequence = jnp.maximum(positions, 0) // SEQ
    local_pos = positions - sequence * SEQ
    picked = sequence[:, None, None] == jnp.arange(sequence_count, dtype=jnp.int32)[None, :, None]
    row_ends = jnp.sum(jnp.where(picked, ends[None], 0), axis=1)
    inside = jnp.sum((local_pos[:, None] >= row_ends).astype(jnp.int32), axis=1)
    return (sequence * entry_count + inside, inside < entry_count - 1)


def on_device(
    tokens,
    document_lengths,
    routes,
    first_gain,
    query_weight,
    latent_down,
    latent_gain,
    latent_up,
    output_weight,
    second_gain,
    router_weight,
    shared_gate,
    shared_up,
    shared_down,
    expert_gate,
    expert_up,
    expert_down,
    cotangent,
):
    local_rows = tokens.shape[0]
    model_width = tokens.shape[1]
    expert_count = router_weight.shape[1]
    capacity = local_rows * TOP * 4 // (3 * expert_count)
    hop_count = WINDOW // local_rows
    key_count = (hop_count + 1) * local_rows
    head_dim = QK_NOPE + QK_ROPE
    packed_width = KV_RANK + QK_ROPE
    score_scale = 1.0 / math.sqrt(head_dim)
    device = lax.axis_index(("shard", "expert"))
    query_pos = device * local_rows + jnp.arange(local_rows, dtype=jnp.int32)
    key_pos = (device - hop_count) * local_rows + jnp.arange(key_count, dtype=jnp.int32)
    cosine_part, sine_part = rotary_tables(query_pos % SEQ, QK_ROPE)
    query_docs, query_real = document_ids(query_pos, document_lengths)
    key_docs = document_ids(key_pos, document_lengths)[0]
    allowed = (
        (query_docs[:, None] == key_docs[None, :])
        & (key_pos[None, :] <= query_pos[:, None])
        & (key_pos[None, :] > query_pos[:, None] - WINDOW)
        & (key_pos[None, :] >= 0)
    )
    query_mask = query_real.astype(jnp.float32)
    full_query, full_down, full_up, full_out = (
        lax.all_gather(query_weight, "shard", axis=0, tiled=True),
        lax.all_gather(latent_down, "shard", axis=0, tiled=True),
        lax.all_gather(latent_up, "shard", axis=0, tiled=True),
        lax.all_gather(output_weight, "shard", axis=0, tiled=True),
    )
    gate_shared, up_shared, down_shared, gate_expert, up_expert, down_expert = (
        lax.all_gather(shared_gate, "shard", axis=0, tiled=True),
        lax.all_gather(shared_up, "shard", axis=0, tiled=True),
        lax.all_gather(shared_down, "shard", axis=0, tiled=True),
        lax.all_gather(expert_gate, "shard", axis=1, tiled=True),
        lax.all_gather(expert_up, "shard", axis=1, tiled=True),
        lax.all_gather(expert_down, "shard", axis=1, tiled=True),
    )
    gate_single = gate_expert[0]
    up_single = up_expert[0]
    down_single = down_expert[0]
    up_heads = full_up.reshape(KV_RANK, HEADS, QK_NOPE + V_HEAD)
    key_up = up_heads[:, :, :QK_NOPE]
    value_up = up_heads[:, :, QK_NOPE:]
    hidden_input_rows = tokens.astype(jnp.float32)
    normed_one = norm_scale(hidden_input_rows, first_gain).astype(jnp.bfloat16)
    query_full = matmul(normed_one, full_query).reshape(local_rows, HEADS, head_dim)
    query_nope = query_full[..., :QK_NOPE].astype(jnp.bfloat16)
    query_rope = rotate(
        query_full[..., QK_NOPE:], cosine_part[:, None, :], sine_part[:, None, :]
    ).astype(jnp.bfloat16)
    compressed = matmul(normed_one, full_down)
    latent_own = norm_scale(compressed[:, :KV_RANK], latent_gain).astype(jnp.bfloat16)
    rope_own = rotate(compressed[:, KV_RANK:], cosine_part, sine_part).astype(jnp.bfloat16)
    packed_own = jnp.concatenate([latent_own, rope_own], axis=1)

    def fetch(block, discarded_value):
        moved = passed_along(block, ("shard", "expert"), 1)
        return (moved, moved)

    last_block, fetched = lax.scan(fetch, packed_own, None, length=hop_count)
    key_rows = jnp.concatenate(
        [fetched[::-1].reshape(hop_count * local_rows, packed_width), packed_own], axis=0
    )
    key_latent = key_rows[:, :KV_RANK]
    key_rope = key_rows[:, KV_RANK:]
    query_latent = jnp.einsum(
        "thn,chn->thc", query_nope, key_up, preferred_element_type=jnp.float32
    ).astype(jnp.bfloat16)

    def scores_of():
        raw = jnp.einsum(
            "thc,kc->htk", query_latent, key_latent, preferred_element_type=jnp.float32
        )
        raw = raw + jnp.einsum(
            "thr,kr->htk", query_rope, key_rope, preferred_element_type=jnp.float32
        )
        return jnp.where(allowed[None], raw * score_scale, NEG)

    scores = scores_of()
    top_score = jnp.max(scores, axis=2, keepdims=True)
    expo = jnp.exp(scores - top_score)
    expo_total = jnp.sum(expo, axis=2, keepdims=True)
    log_total = top_score + jnp.log(expo_total)
    attention_probs = expo / expo_total
    latent_out = jnp.einsum(
        "htk,kc->thc",
        attention_probs.astype(jnp.bfloat16),
        key_latent,
        preferred_element_type=jnp.float32,
    ).astype(jnp.bfloat16)
    heads_full = (
        jnp.einsum("thc,chv->thv", latent_out, value_up, preferred_element_type=jnp.float32)
        * query_mask[:, None, None]
    )
    heads_out = heads_full.astype(jnp.bfloat16).reshape(local_rows, HEADS * V_HEAD)
    middle = hidden_input_rows + matmul(heads_out, full_out)
    second_normed_rows = norm_scale(middle, second_gain).astype(jnp.bfloat16)
    logits = matmul(second_normed_rows, router_weight)
    choose = routes[:, :, None] == jnp.arange(expert_count, dtype=jnp.int32)[None, None, :]
    chosen = jnp.sum(jnp.where(choose, logits[:, None, :], 0.0), axis=2)
    chosen_top = jnp.max(chosen, axis=1, keepdims=True)
    chosen_exp = jnp.exp(chosen - chosen_top)
    gate_values = chosen_exp / jnp.sum(chosen_exp, axis=1, keepdims=True)
    shared_gate_pre = matmul(second_normed_rows, gate_shared)
    shared_up_pre = matmul(second_normed_rows, up_shared)
    shared_swished, shared_slope = swish_parts(shared_gate_pre)
    shared_hidden = (shared_swished * shared_up_pre).astype(jnp.bfloat16)
    shared_out = matmul(shared_hidden, down_shared)
    flat_routes = routes.reshape(-1)
    route_marks = (
        flat_routes[:, None] == jnp.arange(expert_count, dtype=jnp.int32)[None, :]
    ).astype(jnp.int32)
    slot_ranks = jnp.sum(route_marks * (jnp.cumsum(route_marks, axis=0) - 1), axis=1)
    slot_index = flat_routes * capacity + slot_ranks
    slot_total = expert_count * capacity
    source_indices = (
        jnp.zeros((slot_total,), jnp.int32)
        .at[slot_index]
        .set(jnp.arange(local_rows * TOP, dtype=jnp.int32))
    )
    occupied = jnp.zeros((slot_total,), jnp.int32).at[slot_index].set(1) > 0
    source_rows = source_indices // TOP
    outgoing = jnp.where(
        occupied[:, None], second_normed_rows[source_rows], jnp.zeros((), jnp.bfloat16)
    ).reshape(expert_count, capacity, model_width)
    arrived = lax.all_to_all(outgoing, "expert", split_axis=0, concat_axis=0, tiled=True)
    sender_count = arrived.shape[0]
    slot_count = arrived.shape[1]
    flat_rows = arrived.reshape(sender_count * slot_count, model_width)
    gate_hidden = matmul(flat_rows, gate_single)
    up_hidden = matmul(flat_rows, up_single)
    swished, unused_slope = swish_parts(gate_hidden)
    mixed_rows = (swished * up_hidden).astype(jnp.bfloat16)
    result = (
        matmul(mixed_rows, down_single)
        .astype(jnp.bfloat16)
        .reshape(sender_count, slot_count, model_width)
    )
    coming_home = lax.all_to_all(result, "expert", split_axis=0, concat_axis=0, tiled=True)
    hidden_width = gate_hidden.shape[1]
    kept_gate = gate_hidden.reshape(sender_count, slot_count, hidden_width)
    kept_up = up_hidden.reshape(sender_count, slot_count, hidden_width)
    expert_rows = coming_home.reshape(slot_total, model_width)[slot_index].reshape(
        local_rows, TOP, model_width
    )
    routed_output = jnp.sum(gate_values[:, :, None] * expert_rows.astype(jnp.float32), axis=1)
    activations = (middle + shared_out + routed_output).astype(jnp.bfloat16)
    grad_out = cotangent.astype(jnp.float32)
    gate_grad = jnp.sum(grad_out[:, None, :] * expert_rows.astype(jnp.float32), axis=2)
    chosen_grad = gate_values * (
        gate_grad - jnp.sum(gate_values * gate_grad, axis=1, keepdims=True)
    )
    logit_grad = jnp.sum(jnp.where(choose, chosen_grad[:, :, None], 0.0), axis=1)
    router_term = lax.dot_general(
        second_normed_rows.astype(jnp.float32),
        logit_grad,
        (((0,), (0,)), ((), ())),
        precision=HIGH,
        preferred_element_type=jnp.float32,
    )
    normed_grad = lax.dot_general(
        logit_grad,
        router_weight.astype(jnp.float32),
        (((1,), (1,)), ((), ())),
        precision=HIGH,
        preferred_element_type=jnp.float32,
    )
    slot_grads = (
        (gate_values[:, :, None] * grad_out[:, None, :])
        .astype(jnp.bfloat16)
        .reshape(local_rows * TOP, model_width)
    )
    outgoing_grad = jnp.where(
        occupied[:, None], slot_grads[source_indices], jnp.zeros((), jnp.bfloat16)
    ).reshape(expert_count, capacity, model_width)
    arrived_grad = lax.all_to_all(outgoing_grad, "expert", split_axis=0, concat_axis=0, tiled=True)
    grad_rows = arrived_grad.reshape(-1, model_width)
    input_rows = arrived.reshape(-1, model_width)
    gate_hidden = kept_gate.reshape(grad_rows.shape[0], -1)
    up_hidden = kept_up.reshape(grad_rows.shape[0], -1)
    swished, slope = swish_parts(gate_hidden)
    mixed_rows = (swished * up_hidden).astype(jnp.bfloat16)
    mixed_grad = matmul_nt(grad_rows, down_single)
    down_term = matmul_tn(mixed_rows, grad_rows)
    gate_hgrad = (mixed_grad * up_hidden * slope).astype(jnp.bfloat16)
    up_hgrad = (mixed_grad * swished).astype(jnp.bfloat16)
    gate_term = matmul_tn(input_rows, gate_hgrad)
    up_term_expert = matmul_tn(input_rows, up_hgrad)
    back_rows = (
        (matmul_nt(gate_hgrad, gate_single) + matmul_nt(up_hgrad, up_single))
        .astype(jnp.bfloat16)
        .reshape(arrived_grad.shape)
    )
    back_home = lax.all_to_all(back_rows, "expert", split_axis=0, concat_axis=0, tiled=True)
    expert_gate_grad, expert_up_grad, expert_down_grad = (
        lax.psum_scatter(
            gate_term[None].astype(jnp.bfloat16), "shard", scatter_dimension=1, tiled=True
        ).astype(jnp.float32),
        lax.psum_scatter(
            up_term_expert[None].astype(jnp.bfloat16), "shard", scatter_dimension=1, tiled=True
        ).astype(jnp.float32),
        lax.psum_scatter(
            down_term[None].astype(jnp.bfloat16), "shard", scatter_dimension=1, tiled=True
        ).astype(jnp.float32),
    )
    slot_back = back_home.reshape(slot_total, model_width)[slot_index].reshape(
        local_rows, TOP, model_width
    )
    normed_grad = normed_grad + jnp.sum(slot_back, axis=1, dtype=jnp.float32)
    grad_low = grad_out.astype(jnp.bfloat16)
    sdown_term = matmul_tn(shared_hidden, grad_low)
    shared_mgrad = matmul_nt(grad_low, down_shared)
    shared_ggrad = (shared_mgrad * shared_up_pre * shared_slope).astype(jnp.bfloat16)
    shared_ugrad = (shared_mgrad * shared_swished).astype(jnp.bfloat16)
    sgate_term = matmul_tn(second_normed_rows, shared_ggrad)
    sup_term = matmul_tn(second_normed_rows, shared_ugrad)
    normed_grad = (
        normed_grad + matmul_nt(shared_ggrad, gate_shared) + matmul_nt(shared_ugrad, up_shared)
    )
    unused_two, second_back = jax.vjp(norm_scale, middle, second_gain)
    middle_norm_grad, second_term = second_back(normed_grad)
    middle_grad = grad_out + middle_norm_grad
    shared_gate_grad, shared_up_grad, shared_down_grad, router_weight_grad, second_gain_grad = (
        lax.psum_scatter(sgate_term, ("shard", "expert"), scatter_dimension=0, tiled=True),
        lax.psum_scatter(sup_term, ("shard", "expert"), scatter_dimension=0, tiled=True),
        lax.psum_scatter(sdown_term, ("shard", "expert"), scatter_dimension=0, tiled=True),
        lax.psum_scatter(router_term, ("shard", "expert"), scatter_dimension=0, tiled=True),
        lax.psum_scatter(second_term, ("shard", "expert"), scatter_dimension=0, tiled=True),
    )
    middle_low = middle_grad.astype(jnp.bfloat16)
    out_term = matmul_tn(heads_out, middle_low)
    heads_grad = (
        (matmul_nt(middle_low, full_out) * query_mask[:, None])
        .astype(jnp.bfloat16)
        .reshape(local_rows, HEADS, V_HEAD)
    )
    value_term = jnp.einsum(
        "thc,thv->chv", latent_out, heads_grad, preferred_element_type=jnp.float32
    )
    latent_out_grad = jnp.einsum(
        "thv,chv->thc", heads_grad, value_up, preferred_element_type=jnp.float32
    ).astype(jnp.bfloat16)
    again_probs = jnp.exp(scores_of() - log_total)
    prob_grad = jnp.einsum(
        "thc,kc->htk", latent_out_grad, key_latent, preferred_element_type=jnp.float32
    )
    key_latent_grad = jnp.einsum(
        "htk,thc->kc",
        again_probs.astype(jnp.bfloat16),
        latent_out_grad,
        preferred_element_type=jnp.float32,
    )
    score_grad = again_probs * (prob_grad - jnp.sum(again_probs * prob_grad, axis=2, keepdims=True))
    raw_grad = (score_grad * score_scale).astype(jnp.bfloat16)
    query_latent_grad = jnp.einsum(
        "htk,kc->thc", raw_grad, key_latent, preferred_element_type=jnp.float32
    ).astype(jnp.bfloat16)
    query_rope_grad = jnp.einsum(
        "htk,kr->thr", raw_grad, key_rope, preferred_element_type=jnp.float32
    )
    key_rope_grad = jnp.einsum(
        "htk,thr->kr", raw_grad, query_rope, preferred_element_type=jnp.float32
    )
    key_latent_grad = key_latent_grad + jnp.einsum(
        "htk,thc->kc", raw_grad, query_latent, preferred_element_type=jnp.float32
    )
    key_term = jnp.einsum(
        "thn,thc->chn", query_nope, query_latent_grad, preferred_element_type=jnp.float32
    )
    query_nope_grad = jnp.einsum(
        "thc,chn->thn", query_latent_grad, key_up, preferred_element_type=jnp.float32
    )
    query_grad = (
        jnp.concatenate(
            [
                query_nope_grad,
                unrotate(query_rope_grad, cosine_part[:, None, :], sine_part[:, None, :]),
            ],
            axis=2,
        )
        .astype(jnp.bfloat16)
        .reshape(local_rows, HEADS * head_dim)
    )
    latent_up_term = jnp.concatenate([key_term, value_term], axis=2).reshape(
        KV_RANK, HEADS * (QK_NOPE + V_HEAD)
    )
    key_grad_blocks = jnp.concatenate([key_latent_grad, key_rope_grad], axis=1).reshape(
        hop_count + 1, local_rows, packed_width
    )

    def return_step(step, carried):
        carried = carried + lax.dynamic_index_in_dim(key_grad_blocks, step, 0, keepdims=False)
        return passed_along(carried.astype(jnp.bfloat16), ("shard", "expert"), -1).astype(
            carried.dtype
        )

    travelled = lax.fori_loop(
        0, hop_count, return_step, jnp.zeros((local_rows, packed_width), jnp.float32)
    )
    own_key_grad = travelled + key_grad_blocks[hop_count]
    unused_latent, latent_back = jax.vjp(norm_scale, compressed[:, :KV_RANK], latent_gain)
    latent_in_grad, latent_gain_term = latent_back(own_key_grad[:, :KV_RANK])
    rope_in_grad = unrotate(own_key_grad[:, KV_RANK:], cosine_part, sine_part)
    compressed_grad = jnp.concatenate([latent_in_grad, rope_in_grad], axis=1).astype(jnp.bfloat16)
    query_term = matmul_tn(normed_one, query_grad)
    down_term_attention = matmul_tn(normed_one, compressed_grad)
    normed_one_grad = matmul_nt(query_grad, full_query) + matmul_nt(compressed_grad, full_down)
    unused_one, first_back = jax.vjp(norm_scale, hidden_input_rows, first_gain)
    input_norm_grad, first_term = first_back(normed_one_grad)
    input_grad = middle_grad + input_norm_grad
    (
        query_weight_grad,
        latent_down_grad,
        latent_up_grad,
        output_weight_grad,
        first_gain_grad,
        latent_gain_grad,
    ) = (
        lax.psum_scatter(query_term, ("shard", "expert"), scatter_dimension=0, tiled=True),
        lax.psum_scatter(down_term_attention, ("shard", "expert"), scatter_dimension=0, tiled=True),
        lax.psum_scatter(latent_up_term, ("shard", "expert"), scatter_dimension=0, tiled=True),
        lax.psum_scatter(out_term, ("shard", "expert"), scatter_dimension=0, tiled=True),
        lax.psum_scatter(first_term, ("shard", "expert"), scatter_dimension=0, tiled=True),
        lax.psum_scatter(latent_gain_term, ("shard", "expert"), scatter_dimension=0, tiled=True),
    )
    return (
        activations,
        input_grad,
        first_gain_grad,
        query_weight_grad,
        latent_down_grad,
        latent_gain_grad,
        latent_up_grad,
        output_weight_grad,
        second_gain_grad,
        router_weight_grad,
        shared_gate_grad,
        shared_up_grad,
        shared_down_grad,
        expert_gate_grad,
        expert_up_grad,
        expert_down_grad,
    )


def solution(mesh):
    return jax.shard_map(
        on_device,
        mesh=mesh,
        in_specs=(
            P(("shard", "expert"), None),
            P(),
            P(("shard", "expert"), None),
            P(),
            P("shard", None),
            P("shard", None),
            P(),
            P("shard", None),
            P("shard", None),
            P(),
            P(),
            P("shard", None),
            P("shard", None),
            P("shard", None),
            P("expert", "shard", None),
            P("expert", "shard", None),
            P("expert", "shard", None),
            P(("shard", "expert"), None),
        ),
        out_specs=(
            P(("shard", "expert"), None),
            P(("shard", "expert"), None),
            P(("shard", "expert")),
            P(("shard", "expert"), None),
            P(("shard", "expert"), None),
            P(("shard", "expert")),
            P(("shard", "expert"), None),
            P(("shard", "expert"), None),
            P(("shard", "expert")),
            P(("shard", "expert"), None),
            P(("shard", "expert"), None),
            P(("shard", "expert"), None),
            P(("shard", "expert"), None),
            P("expert", "shard", None),
            P("expert", "shard", None),
            P("expert", "shard", None),
        ),
        check_vma=False,
    )
```

profile of v0, /device:TPU:9, one launch (start us, length us, event | category | flops | bytes accessed | tf_op | source)
XLA Modules:
  0.0 2885.0 jit_solution(17049063554854987767)
XLA Ops:
  20.5 8.4 mul.511
  39.5 7.3 all-gather.11.cloned.1.call-done
  50.5 61.8 %while.26 = (s32[]{:T(128)}, bf16[128,576]{1,0:T(8,128)(2,1)S(1)}, bf16[8,128,576]{2,1,0:T(8,128)(2,1)}, s32[]{:T(128)}) while((s32[]{:T(128)}, bf16[128,576]{1,0:T(8,128)(2,1)S(1)}, bf16[8,128,576]{2,1,0:T(8,128)(2,1)}, s32[]{:T(128)}) %tuple.80), condition=%wide.region_3.4_spmd, body=%wide.region_2.3_spmd.sunk | while | flops 2 | bytes 1196137 | solution.py:172
  98.2 5.2 collective-permute-done
  106.0 5.6 collective-permute-done
  114.9 86.0 %all-gather.13.cloned.1.call-done = bf16[2048,3072]{1,0:T(8,128)(2,1)} async-done(((bf16[1024,3072]{1,0:T(8,128)(2,1)}), bf16[2048,3072]{1,0:T(8,128)(2,1)}) %all-gather.13.cloned.1.call-update) | async-done | bytes 12582928 | tf_op jit(solution)/shard_map/all_gather | solution.py:137
  201.0 8.0 fusion.141
  209.1 59.1 %all-gather.15.cloned.1.call-done = bf16[512,4096]{0,1:T(8,128)(2,1)} async-done(((bf16[256,4096]{0,1:T(8,128)(2,1)}), bf16[512,4096]{0,1:T(8,128)(2,1)}) %all-gather.15.cloned.1.call-update) | async-done | bytes 4194320 | tf_op jit(solution)/shard_map/all_gather | solution.py:139
  285.6 88.0 %all-gather.17.cloned.1.call-done = bf16[2048,2048]{1,0:T(8,128)(2,1)} async-done(((bf16[1024,2048]{1,0:T(8,128)(2,1)}), bf16[2048,2048]{1,0:T(8,128)(2,1)}) %all-gather.17.cloned.1.call-update) | async-done | bytes 8388624 | tf_op jit(solution)/shard_map/all_gather | solution.py:140
  380.2 6.0 gather_fusion
  386.1 5.4 multiply_convert_fusion
  391.5 11.1 gather_fusion.2
  402.6 5.9 broadcast_select_fusion
  408.5 6.4 all-to-all-start.2
  415.6 89.6 %all-to-all-done.2 = bf16[16,64,2048]{2,1,0:T(8,128)(2,1)} async-done(((bf16[16,64,2048]{2,1,0:T(8,128)(2,1)}), bf16[16,64,2048]{2,1,0:T(8,128)(2,1)}, u32[]{:S(2)}, u32[]{:S(2)}) %all-to-all-start.2) | async-done | bytes 4194336 | tf_op jit(solution)/shard_map/all_to_all | solution.py:288
  505.2 7.1 all-to-all-start
  512.9 12.3 fusion.11
  525.5 77.1 %all-to-all-done = bf16[16,64,2048]{2,1,0:T(8,128)(2,1)} async-done(((bf16[16,64,2048]{2,1,0:T(8,128)(2,1)}), bf16[16,64,2048]{2,1,0:T(8,128)(2,1)}, u32[]{:S(2)}, u32[]{:S(2)}) %all-to-all-start) | async-done | bytes 4194336 | tf_op jit(solution)/shard_map/all_to_all | solution.py:238
  602.6 12.0 fusion.17
  614.6 18.2 multiply_convert_fusion.2
  632.8 12.0 fusion.29
  644.8 6.7 all-to-all-start.1
  651.7 90.1 %all-to-all-done.1 = bf16[16,64,2048]{2,1,0:T(8,128)(2,1)} async-done(((bf16[16,64,2048]{2,1,0:T(8,128)(2,1)}), bf16[16,64,2048]{2,1,0:T(8,128)(2,1)}, u32[]{:S(2)}, u32[]{:S(2)}) %all-to-all-start.1) | async-done | bytes 4194336 | tf_op jit(solution)/shard_map/all_to_all | solution.py:251
  741.9 10.0 gather_fusion.1
  751.9 7.0 reshape.657
  758.9 7.8 multiply_reduce_fusion
  768.6 11.2 fusion.8
  779.8 11.2 fusion.9
  791.0 9.8 fusion.15
  800.8 11.0 add_convert_fusion
  811.8 6.7 all-to-all-start.3
  818.6 9.4 fusion.148
  828.7 11.1 fusion.10
  839.8 46.9 %all-gather.21.cloned.1.call-done = bf16[2048,2816]{1,0:T(8,128)(2,1)} async-done(((bf16[1024,2816]{1,0:T(8,128)(2,1)}), bf16[2048,2816]{1,0:T(8,128)(2,1)}) %all-gather.21.cloned.1.call-update) | async-done | bytes 11534352 | tf_op jit(solution)/shard_map/all_gather | solution.py:144
  886.7 7.1 fusion.146
  893.8 135.4 %all-gather.19.cloned.1.call-done = bf16[2048,2816]{1,0:T(8,128)(2,1)} async-done(((bf16[1024,2816]{1,0:T(8,128)(2,1)}), bf16[2048,2816]{1,0:T(8,128)(2,1)}) %all-gather.19.cloned.1.call-update) | async-done | bytes 11534352 | tf_op jit(solution)/shard_map/all_gather | solution.py:143
  1029.2 8.3 multiply_convert_fusion.5
  1037.5 8.6 fusion.149
  1051.0 10.0 gather_fusion.3
  1061.0 6.6 reshape.658
  1067.6 7.1 reduce_sum.261
  1078.4 7.1 fusion.42
  1095.8 16.9 convolution_bitcast_fusion.1
  1112.8 8.8 fusion.33
  1121.6 18.9 fusion.32
  1147.4 78.8 %while.27 = (s32[]{:T(128)}, f32[128,576]{1,0:T(8,128)S(1)}, f32[9,128,576]{2,1,0:T(8,128)}, s32[]{:T(128)}, s32[]{:T(128)}) while((s32[]{:T(128)}, f32[128,576]{1,0:T(8,128)S(1)}, f32[9,128,576]{2,1,0:T(8,128)}, s32[]{:T(128)}, s32[]{:T(128)}) %tuple.128), condition=%wide.region_28.29_spmd.clone, body=%wide.region_27.28_spmd.clone.sunk | while | flops 294915 | bytes 1769587 | solution.py:409
  1240.4 18.4 convolution_convert_fusion.3
  1266.9 9.1 copy.223
  1276.1 10.9 fusion.153
  1287.0 10.6 fusion.154
  1298.6 10.6 fusion.155
  1310.3 8.2 fusion.85
  1319.4 16.8 fusion.72
  1341.2 10.6 fusion.139
  1351.8 9.7 fusion.151
  1363.3 66.7 %all-reduce.3 = (f32[2048]{0:T(1024)S(1)}, f32[512]{0:T(512)S(1)}, f32[2048]{0:T(1024)S(1)}) all-reduce(f32[2048]{0:T(1024)S(1)} %get-tuple-element.136, f32[512]{0:T(512)S(1)} %copy-done.49, f32[2048]{0:T(1024)S(1)} %copy-done.44), channel_id=2, replica_groups=mesh['shard'=2,'expert'=16] {'shard','expert'}, use_global_device_ids=true, to_apply=%region_32.33.clone | all-reduce | flops 4608 | bytes 36864
  1434.3 7.3 fusion.41
  1457.7 67.2 %reduce-scatter.16.cloned.1.call-done = f32[64,576]{1,0:T(8,128)} async-done(((f32[2048,576]{1,0:T(8,128)}), f32[64,576]{1,0:T(8,128)}) %reduce-scatter.16.cloned.1.call-update) | async-done | bytes 147472 | tf_op jit(solution)/shard_map/reduce_scatter | solution.py:432
  1524.9 148.8 %reduce-scatter.18.cloned.1.call-done = f32[16,4096]{1,0:T(8,128)} async-done(((f32[512,4096]{1,0:T(8,128)}), f32[16,4096]{1,0:T(8,128)}) %reduce-scatter.18.cloned.1.call-update) | async-done | bytes 262160 | tf_op jit(solution)/shard_map/reduce_scatter | solution.py:433
  1673.6 262.1 %reduce-scatter.22.cloned.1.call-done = f32[64,2816]{1,0:T(8,128)} async-done(((f32[2048,2816]{1,0:T(8,128)}), f32[64,2816]{1,0:T(8,128)}) %reduce-scatter.22.cloned.1.call-update) | async-done | bytes 720912 | tf_op jit(solution)/shard_map/reduce_scatter | solution.py:336
  1935.8 251.4 %reduce-scatter.24.cloned.1.call-done = f32[64,2816]{1,0:T(8,128)} async-done(((f32[2048,2816]{1,0:T(8,128)}), f32[64,2816]{1,0:T(8,128)}) %reduce-scatter.24.cloned.1.call-update) | async-done | bytes 720912 | tf_op jit(solution)/shard_map/reduce_scatter | solution.py:337
  2187.1 251.5 %reduce-scatter.26.cloned.1.call-done = f32[88,2048]{1,0:T(8,128)} async-done(((f32[2816,2048]{1,0:T(8,128)}), f32[88,2048]{1,0:T(8,128)}) %reduce-scatter.26.cloned.1.call-update) | async-done | bytes 720912 | tf_op jit(solution)/shard_map/reduce_scatter | solution.py:338
  2438.7 187.9 %reduce-scatter.20.cloned.1.call-done = f32[64,2048]{1,0:T(8,128)} async-done(((f32[2048,2048]{1,0:T(8,128)}), f32[64,2048]{1,0:T(8,128)}) %reduce-scatter.20.cloned.1.call-update) | async-done | bytes 524304 | tf_op jit(solution)/shard_map/reduce_scatter | solution.py:434
  2626.6 251.3 %reduce-scatter.14.cloned.1.call-done = f32[64,3072]{1,0:T(8,128)} async-done(((f32[2048,3072]{1,0:T(8,128)}), f32[64,3072]{1,0:T(8,128)}) %reduce-scatter.14.cloned.1.call-update) | async-done | bytes 786448 | tf_op jit(solution)/shard_map/reduce_scatter | solution.py:431
  (367 shorter events, 265.4 us)
Async XLA Ops:
  7.2 372.4 %copy-start = (bf16[2048,16]{0,1:T(8,128)(2,1)S(1)}, bf16[2048,16]{0,1:T(8,128)(2,1)}, u32[]{:S(2)}) copy-start(bf16[2048,16]{0,1:T(8,128)(2,1)} %param.32) | copy-start | bytes 196612
  7.2 39.6 %all-gather.11.cloned.1.call-start = ((), (), s32[]{:S(2)}) async-start(), calls=%async_computation.15 | async-start | bytes 3538944 | tf_op jit(solution)/shard_map/all_gather | solution.py:138
  7.9 193.0 %all-gather.13.cloned.1.call-start = ((), (), s32[]{:S(2)}) async-start(), calls=%async_computation.16 | async-start | bytes 18874368 | tf_op jit(solution)/shard_map/all_gather | solution.py:137
  8.7 259.5 %all-gather.15.cloned.1.call-start = ((), (), s32[]{:S(2)}) async-start(), calls=%async_computation.17 | async-start | bytes 6291456 | tf_op jit(solution)/shard_map/all_gather | solution.py:139
  11.3 362.4 %all-gather.17.cloned.1.call-start = ((), (), s32[]{:S(2)}) async-start(), calls=%async_computation.18 | async-start | bytes 12582912 | tf_op jit(solution)/shard_map/all_gather | solution.py:140
  11.9 501.0 %all-gather.29.cloned.1.call-start = ((), (), s32[]{:S(2)}) async-start(), calls=%async_computation.24 | async-start | bytes 8650752 | tf_op jit(solution)/shard_map/all_gather | solution.py:148
  12.4 513.0 %all-gather.27.cloned.1.call-start = ((), (), s32[]{:S(2)}) async-start(), calls=%async_computation.23 | async-start | bytes 8650752 | tf_op jit(solution)/shard_map/all_gather | solution.py:147
  13.1 601.5 %all-gather.25.cloned.1.call-start = ((), (), s32[]{:S(2)}) async-start(), calls=%async_computation.22 | async-start | bytes 8650752 | tf_op jit(solution)/shard_map/all_gather | solution.py:146
  13.8 804.8 %all-gather.23.cloned.1.call-start = ((), (), s32[]{:S(2)}) async-start(), calls=%async_computation.21 | async-start | bytes 17301504 | tf_op jit(solution)/shard_map/all_gather | solution.py:145
  14.6 35.1 %copy-start.55 = (f32[32]{0:T(128)}, f32[32]{0:T(128)S(1)}, u32[]{:S(2)}) copy-start(f32[32]{0:T(128)S(1)} %multiply_power_fusion) | copy-start | bytes 388
  14.6 35.0 %copy-start.56 = (f32[128]{0:T(128)}, f32[128]{0:T(128)S(1)}, u32[]{:S(2)}) copy-start(f32[128]{0:T(128)S(1)} %fusion.121) | copy-start | bytes 1540
  15.1 268.6 %copy-start.63 = (f32[128]{0:T(128)}, f32[128]{0:T(128)S(1)}, u32[]{:S(2)}) copy-start(f32[128]{0:T(128)S(1)} %compare_convert_fusion) | copy-start | bytes 1540
  15.7 185.3 %copy-start.45 = (f32[128]{0:T(128)}, f32[128]{0:T(128)S(1)}, u32[]{:S(2)}) copy-start(f32[128]{0:T(128)S(1)} %fusion.127) | copy-start | bytes 1540
  20.5 26.3 copy-start.29
  20.5 28.9 %copy-start.47 = (f32[512]{0:T(512)S(1)}, f32[512]{0:T(512)}, u32[]{:S(2)}) copy-start(f32[512]{0:T(512)} %param.28) | copy-start | bytes 6148
  50.3 158.7 %copy-start.33 = (f32[128,32]{0,1:T(8,128)}, f32[128,32]{0,1:T(8,128)S(1)}, u32[]{:S(2)}) copy-start(f32[128,32]{0,1:T(8,128)S(1)} %get-tuple-element.173) | copy-start | bytes 49156
  50.3 158.7 %copy-start.35 = (f32[128,32]{0,1:T(8,128)}, f32[128,32]{0,1:T(8,128)S(1)}, u32[]{:S(2)}) copy-start(f32[128,32]{0,1:T(8,128)S(1)} %get-tuple-element.174) | copy-start | bytes 49156
  50.5 5.9 collective-permute-start
  57.1 6.6 collective-permute-start
  64.5 6.6 collective-permute-start
  71.8 6.9 collective-permute-start
  79.4 7.5 collective-permute-start
  87.6 7.5 collective-permute-start
  95.8 7.5 collective-permute-start
  104.1 7.5 collective-permute-start
  113.8 159.5 %copy-start.27 = (bf16[1152,64,1]{1,0,2:T(8,128)(2,1)}, bf16[1152,64,1]{1,0,2:T(8,128)(2,1)S(1)}, u32[]{:S(2)}) copy-start(bf16[1152,64,1]{1,0,2:T(8,128)(2,1)S(1)} %fusion.83) | copy-start | bytes 442372
  209.0 64.3 %copy-start.10 = (f32[128,3072]{0,1:T(8,128)}, f32[128,3072]{0,1:T(8,128)S(1)}, u32[]{:S(2)}) copy-start(f32[128,3072]{0,1:T(8,128)S(1)} %fusion.141) | copy-start | bytes 4718596
  209.1 64.2 %copy-start.31 = (bf16[128,16,32]{0,2,1:T(8,128)(2,1)}, bf16[128,16,32]{0,2,1:T(8,128)(2,1)S(1)}, u32[]{:S(2)}) copy-start(bf16[128,16,32]{0,2,1:T(8,128)(2,1)S(1)} %get-tuple-element.161) | copy-start | bytes 393220
  209.1 64.2 %copy-start.32 = (bf16[128,16,32]{0,2,1:T(8,128)(2,1)}, bf16[128,16,32]{0,2,1:T(8,128)(2,1)S(1)}, u32[]{:S(2)}) copy-start(bf16[128,16,32]{0,2,1:T(8,128)(2,1)S(1)} %get-tuple-element.162) | copy-start | bytes 393220
  285.6 92.8 %copy-start.15 = (bf16[16,128,128]{1,2,0:T(8,128)(2,1)}, bf16[16,128,128]{1,2,0:T(8,128)(2,1)S(1)}, u32[]{:S(2)}) copy-start(bf16[16,128,128]{1,2,0:T(8,128)(2,1)S(1)} %fusion.61) | copy-start | bytes 1572868
  408.5 96.7 %all-to-all-start.2 = ((bf16[16,64,2048]{2,1,0:T(8,128)(2,1)}), bf16[16,64,2048]{2,1,0:T(8,128)(2,1)}, u32[]{:S(2)}, u32[]{:S(2)}) async-start(bf16[16,64,2048]{2,1,0:T(8,128)(2,1)} %get-tuple-element.171), calls=%async_computation.2 | async-start | bytes 8388608 | tf_op jit(solution)/shard_map/all_to_all | solution.py:288
  414.9 471.9 %all-gather.21.cloned.1.call-start = ((), (), s32[]{:S(2)}) async-start(), calls=%async_computation.20 | async-start | bytes 17301504 | tf_op jit(solution)/shard_map/all_gather | solution.py:144
  505.2 97.4 %all-to-all-start = ((bf16[16,64,2048]{2,1,0:T(8,128)(2,1)}), bf16[16,64,2048]{2,1,0:T(8,128)(2,1)}, u32[]{:S(2)}, u32[]{:S(2)}) async-start(bf16[16,64,2048]{2,1,0:T(8,128)(2,1)} %get-tuple-element.172), calls=%async_computation | async-start | bytes 8388608 | tf_op jit(solution)/shard_map/all_to_all | solution.py:238
  512.2 517.0 %all-gather.19.cloned.1.call-start = ((), (), s32[]{:S(2)}) async-start(), calls=%async_computation.19 | async-start | bytes 17301504 | tf_op jit(solution)/shard_map/all_gather | solution.py:143
  644.8 97.0 %all-to-all-start.1 = ((bf16[16,64,2048]{2,1,0:T(8,128)(2,1)}), bf16[16,64,2048]{2,1,0:T(8,128)(2,1)}, u32[]{:S(2)}, u32[]{:S(2)}) async-start(bf16[16,64,2048]{2,1,0:T(8,128)(2,1)} %bitcast.219), calls=%async_computation.1 | async-start | bytes 8388608 | tf_op jit(solution)/shard_map/all_to_all | solution.py:251
  651.6 790.0 %reduce-scatter.34.cloned.1.call-start = ((), (), s32[]{:S(2)}) async-start(), calls=%async_computation.35 | async-start | bytes 1081344
  768.5 674.5 %reduce-scatter.28.cloned.1.call-start = ((), (), s32[]{:S(2)}) async-start(), calls=%async_computation.32 | async-start | bytes 8650752 | tf_op jit(solution)/shard_map/reduce_scatter | solution.py:308
  779.7 668.0 %reduce-scatter.30.cloned.1.call-start = ((), (), s32[]{:S(2)}) async-start(), calls=%async_computation.33 | async-start | bytes 8650752 | tf_op jit(solution)/shard_map/reduce_scatter | solution.py:311
  811.8 239.2 %all-to-all-start.3 = ((bf16[16,64,2048]{2,1,0:T(8,128)(2,1)}), bf16[16,64,2048]{2,1,0:T(8,128)(2,1)}, u32[]{:S(2)}, u32[]{:S(2)}) async-start(bf16[16,64,2048]{2,1,0:T(8,128)(2,1)} %bitcast.218), calls=%async_computation.3 | async-start | bytes 8388608 | tf_op jit(solution)/shard_map/all_to_all | solution.py:306
  818.5 634.0 %reduce-scatter.32.cloned.1.call-start = ((), (), s32[]{:S(2)}) async-start(), calls=%async_computation.34 | async-start | bytes 8650752 | tf_op jit(solution)/shard_map/reduce_scatter | solution.py:314
  839.8 685.1 %reduce-scatter.16.cloned.1.call-start = ((), (), s32[]{:S(2)}) async-start(), calls=%async_computation.26 | async-start | bytes 5406720 | tf_op jit(solution)/shard_map/reduce_scatter | solution.py:432
  1029.2 17.0 slice-start.1
  1121.6 18.9 copy-start.26
  1147.4 80.7 %copy-start.48 = (f32[512]{0:T(512)S(1)}, f32[512]{0:T(512)}, u32[]{:S(2)}) copy-start(f32[512]{0:T(512)} %param.28) | copy-start | bytes 6148
  1147.4 85.0 %copy-start.2 = (bf16[128,2048]{1,0:T(8,128)(2,1)S(1)}, bf16[128,2048]{1,0:T(8,128)(2,1)}, u32[]{:S(2)}) copy-start(bf16[128,2048]{1,0:T(8,128)(2,1)} %param.22) | copy-start | bytes 1572868
  1147.4 85.0 %copy-start.30 = (f32[2048]{0:T(1024)S(1)}, f32[2048]{0:T(1024)}, u32[]{:S(2)}) copy-start(f32[2048]{0:T(1024)} %param.25) | copy-start | bytes 24580
  1147.4 85.0 %copy-start.46 = (f32[128]{0:T(128)S(1)}, f32[128]{0:T(128)}, u32[]{:S(2)}) copy-start(f32[128]{0:T(128)} %copy-done.45) | copy-start | bytes 1540
  1149.1 7.2 collective-permute-start.1
  1159.0 6.9 collective-permute-start.1
  1168.6 7.2 collective-permute-start.1
  1178.4 7.2 collective-permute-start.1
  1188.3 7.2 collective-permute-start.1
  1198.2 7.2 collective-permute-start.1
  1208.1 7.2 collective-permute-start.1
  1218.0 7.2 collective-permute-start.1
  1235.8 437.9 %reduce-scatter.18.cloned.1.call-start = ((), (), s32[]{:S(2)}) async-start(), calls=%async_computation.27 | async-start | bytes 8650752 | tf_op jit(solution)/shard_map/reduce_scatter | solution.py:433
  1276.0 659.7 %reduce-scatter.22.cloned.1.call-start = ((), (), s32[]{:S(2)}) async-start(), calls=%async_computation.29 | async-start | bytes 23789568 | tf_op jit(solution)/shard_map/reduce_scatter | solution.py:336
  1287.0 900.2 %reduce-scatter.24.cloned.1.call-start = ((), (), s32[]{:S(2)}) async-start(), calls=%async_computation.30 | async-start | bytes 23789568 | tf_op jit(solution)/shard_map/reduce_scatter | solution.py:337
  1297.6 1141.1 %reduce-scatter.26.cloned.1.call-start = ((), (), s32[]{:S(2)}) async-start(), calls=%async_computation.31 | async-start | bytes 23789568 | tf_op jit(solution)/shard_map/reduce_scatter | solution.py:338
  1309.3 1317.3 %reduce-scatter.20.cloned.1.call-start = ((), (), s32[]{:S(2)}) async-start(), calls=%async_computation.28 | async-start | bytes 17301504 | tf_op jit(solution)/shard_map/reduce_scatter | solution.py:434
  1318.5 17.7 copy-start.34
  1318.5 17.7 copy-start.36
  1318.5 1559.4 %reduce-scatter.14.cloned.1.call-start = ((), (), s32[]{:S(2)}) async-start(), calls=%async_computation.25 | async-start | bytes 25952256 | tf_op jit(solution)/shard_map/reduce_scatter | solution.py:431
  1361.5 70.2 %copy-start.61 = (f32[128]{0:T(128)S(1)}, f32[128]{0:T(128)}, u32[]{:S(2)}) copy-start(f32[128]{0:T(128)} %copy-done.60) | copy-start | bytes 1540
  (48 other events, 226.1 us)
Sparse Core Ops, SparseCore 0:
  9.6 37.2 all-gather.10
  48.4 152.5 all-gather.12
  203.1 65.0 all-gather.14
  269.6 103.9 all-gather.16
  375.0 74.5 all-gather.28
  451.0 74.4 all-gather.26
  527.0 74.4 all-gather.24
  603.1 141.0 all-gather.22
  745.7 141.0 all-gather.20
  888.1 141.0 all-gather.18
  1031.4 119.8 reduce-scatter.33
  1154.2 82.8 reduce-scatter.27
  1240.0 80.1 reduce-scatter.29
  1322.4 71.3 reduce-scatter.31
  1396.5 128.2 reduce-scatter.15
  1527.6 145.9 reduce-scatter.17
  1676.3 259.3 reduce-scatter.21
  1938.5 248.6 reduce-scatter.23
  2190.0 248.6 reduce-scatter.25
  2441.4 185.1 reduce-scatter.19
  2633.6 244.2 reduce-scatter.13
where the time goes:
time: 2890 us; the launch traced here: 2880 us
  waiting for transfers between devices  2160 us (75%)
  matrix products  356 us (12%)
  local copies, waits for them, and re-layouts  112 us (4%)
  other arithmetic  87 us (3%)
  starting transfers between devices  82.5 us (3%)
  blocking collectives  66.7 us (2%)
    reduce_scatter x1, waiting for transfers between devices, on_device(): lax.psum_scatter(sgate_term, ('shard', 'expert'), scatter_dimension=0, ti...  262 us
    reduce_scatter x1, waiting for transfers between devices, on_device(): lax.psum_scatter(sdown_term, ('shard', 'expert'), scatter_dimension=0, ti...  252 us
    reduce_scatter x1, waiting for transfers between devices, on_device(): lax.psum_scatter(sup_term, ('shard', 'expert'), scatter_dimension=0, tile...  251 us
    reduce_scatter x1, waiting for transfers between devices, on_device(): lax.psum_scatter(query_term, ('shard', 'expert'), scatter_dimension=0, ti...  251 us
    reduce_scatter x1, waiting for transfers between devices, on_device(): lax.psum_scatter(out_term, ('shard', 'expert'), scatter_dimension=0, tile...  188 us
    reduce_scatter x1, waiting for transfers between devices, on_device(): lax.psum_scatter(latent_up_term, ('shard', 'expert'), scatter_dimension=0...  149 us
    all_gather x1, waiting for transfers between devices, on_device(): lax.all_gather(shared_gate, 'shard', axis=0, tiled=True)  135 us
    all_to_all x1, waiting for transfers between devices, on_device(): lax.all_to_all(result, 'expert', split_axis=0, concat_axis=0, tiled=True)  90.1 us
  transfers between devices with their start and end apart: 41, of which 33 were waited for; matrix products, arithmetic and copies ran while one was open for 19% of the time, Pallas kernels for 0%

commit v1 on v0

v1 whole, which is shorter than its diff:
```python
import math

import jax
import jax.numpy as jnp
from jax import lax
from jax.sharding import PartitionSpec as P

HEADS = 16
QK_NOPE = 128
QK_ROPE = 64
V_HEAD = 128
KV_RANK = 512
TOP = 6
SEQ = 2048
WINDOW = 1024
TOK_DEV = 128
SEQ_DEVICES = SEQ // TOK_DEV


EPS = 1e-06
THETA = 10000.0
NEG = -1e30
HIGH = lax.Precision.HIGHEST


def matmul(left, right):
    return jnp.dot(left, right, preferred_element_type=jnp.float32)


def matmul_tn(left, right):
    return lax.dot_general(
        left, right, (((0,), (0,)), ((), ())), preferred_element_type=jnp.float32
    )


def matmul_nt(left, right):
    return lax.dot_general(
        left, right, (((1,), (1,)), ((), ())), preferred_element_type=jnp.float32
    )


def norm_scale(values, gain):
    return values * lax.rsqrt(jnp.mean(values * values, axis=-1, keepdims=True) + EPS) * gain


def rotary_tables(positions, width):
    half = width // 2
    freqs = THETA ** (-jnp.arange(half, dtype=jnp.float32) / half)
    angles = positions.astype(jnp.float32)[:, None] * freqs[None, :]
    return (jnp.cos(angles), jnp.sin(angles))


def rotate(values, cosine_part, sine_part):
    half = values.shape[-1] // 2
    first = values[..., :half]
    second = values[..., half:]
    return jnp.concatenate(
        [first * cosine_part - second * sine_part, second * cosine_part + first * sine_part],
        axis=-1,
    )


def unrotate(values, cosine_part, sine_part):
    half = values.shape[-1] // 2
    first = values[..., :half]
    second = values[..., half:]
    return jnp.concatenate(
        [first * cosine_part + second * sine_part, second * cosine_part - first * sine_part],
        axis=-1,
    )


def swish_parts(values):
    sigmoid_part = jax.nn.sigmoid(values)
    return (values * sigmoid_part, sigmoid_part * (1.0 + values * (1.0 - sigmoid_part)))


def plane_groups(plane):
    members = SEQ_DEVICES
    if plane == members:
        return None
    return [list(range(low, low + members)) for low in range(0, plane, members)]


def shard_ring(block):
    count = lax.axis_size("shard")
    me = lax.axis_index("shard")
    whole = jnp.zeros((count,) + block.shape, block.dtype)
    whole = lax.dynamic_update_index_in_dim(whole, block, me, 0)
    for step in range(1, count):
        moved = lax.ppermute(
            block, "shard", [(source, (source + step) % count) for source in range(count)]
        )
        whole = lax.dynamic_update_index_in_dim(whole, moved, (me - step) % count, 0)
    return whole


def shard_rows(block):
    whole = shard_ring(block)
    return whole.reshape((-1,) + block.shape[1:])


def shard_sum(values):
    count = lax.axis_size("shard")
    me = lax.axis_index("shard")
    blocks = values.reshape((count, -1) + values.shape[1:])
    total = lax.dynamic_index_in_dim(blocks, me, 0, keepdims=False)
    for step in range(1, count):
        outgoing = lax.dynamic_index_in_dim(blocks, (me + step) % count, 0, keepdims=False)
        moved = lax.ppermute(
            outgoing.astype(jnp.bfloat16),
            "shard",
            [(source, (source + step) % count) for source in range(count)],
        )
        total = total + moved.astype(jnp.float32)
    return total


def shared_rows_plane(block):
    plane = lax.axis_size("expert")
    count = lax.axis_size("shard")
    rows = block.shape[0] // plane
    mine = lax.dynamic_slice_in_dim(block, lax.axis_index("expert") * rows, rows, 0)
    pieces = shard_ring(mine)
    gathered = lax.all_gather(pieces, "expert", axis=1, tiled=False)
    return gathered.reshape((count * block.shape[0],) + block.shape[1:])


def on_device(
    tokens,
    document_lengths,
    routes,
    first_gain,
    query_weight,
    latent_down,
    latent_gain,
    latent_up,
    output_weight,
    second_gain,
    router_weight,
    shared_gate,
    shared_up,
    shared_down,
    expert_gate,
    expert_up,
    expert_down,
    cotangent,
):
    local_rows, width = tokens.shape
    shards = lax.axis_size("shard")
    plane = lax.axis_size("expert")
    everyone = ("shard", "expert")
    all_devices = shards * plane
    shard_at = lax.axis_index("shard")
    plane_at = lax.axis_index("expert")
    groups = plane_groups(plane)
    head_at = plane_at % SEQ_DEVICES
    sequence_at = (shard_at * plane + plane_at) // SEQ_DEVICES
    capacity = local_rows * TOP * 4 // (3 * plane)
    head_dim = QK_NOPE + QK_ROPE
    scale = 1.0 / math.sqrt(head_dim)
    own_at = head_at * local_rows

    def own_rows(values):
        return lax.dynamic_slice_in_dim(values, own_at, local_rows, 0)

    query_head = shard_rows(
        lax.dynamic_slice_in_dim(query_weight, head_at * head_dim, head_dim, 1)
    )
    full_down = shard_rows(latent_down)
    up_head = shard_rows(
        lax.dynamic_slice_in_dim(latent_up, head_at * (QK_NOPE + V_HEAD), QK_NOPE + V_HEAD, 1)
    )
    full_out = shared_rows_plane(output_weight)
    full_query = shared_rows_plane(query_weight)
    units = shared_down.shape[0] // plane
    gate_columns, up_columns = (
        jnp.concatenate(
            [
                lax.dynamic_slice_in_dim(
                    weight, index * shared_down.shape[0] + plane_at * units, units, 1
                )
                for index in range(shards)
            ],
            axis=1,
        )
        for weight in (shared_gate, shared_up)
    )
    gate_shared = shard_rows(gate_columns)
    up_shared = shard_rows(up_columns)
    down_shared = shard_rows(lax.dynamic_slice_in_dim(shared_down, plane_at * units, units, 0))
    gate_single = shard_rows(expert_gate[0])
    up_single = shard_rows(expert_up[0])
    down_single = shard_rows(expert_down[0])

    all_tokens = lax.all_gather(
        tokens, "expert", axis=0, tiled=True, axis_index_groups=groups
    ).astype(jnp.float32)
    normed_one = norm_scale(all_tokens, first_gain).astype(jnp.bfloat16)
    positions = jnp.arange(SEQ, dtype=jnp.int32)
    cosine_part, sine_part = rotary_tables(positions, QK_ROPE)
    sequence_count, entry_count = document_lengths.shape
    ends = jnp.cumsum(document_lengths, axis=1)
    picked = jnp.arange(sequence_count, dtype=jnp.int32)[:, None] == sequence_at
    row_ends = jnp.sum(jnp.where(picked, ends, 0), axis=0)
    documents = jnp.sum((positions[:, None] >= row_ends[None, :]).astype(jnp.int32), axis=1)
    real = (documents < entry_count - 1).astype(jnp.float32)
    allowed = (
        (documents[:, None] == documents[None, :])
        & (positions[None, :] <= positions[:, None])
        & (positions[None, :] > positions[:, None] - WINDOW)
    )
    query = matmul(normed_one, query_head)
    query_nope = query[:, :QK_NOPE].astype(jnp.bfloat16)
    query_rope = rotate(query[:, QK_NOPE:], cosine_part, sine_part).astype(jnp.bfloat16)
    compressed = matmul(normed_one, full_down)
    key_latent = norm_scale(compressed[:, :KV_RANK], latent_gain).astype(jnp.bfloat16)
    key_rope = rotate(compressed[:, KV_RANK:], cosine_part, sine_part).astype(jnp.bfloat16)
    keys_values = matmul(key_latent, up_head).astype(jnp.bfloat16)
    key_nope = keys_values[:, :QK_NOPE]
    value = keys_values[:, QK_NOPE:]

    def scores_of():
        raw = matmul_nt(query_nope, key_nope) + matmul_nt(query_rope, key_rope)
        return jnp.where(allowed, raw * scale, NEG)

    scores = scores_of()
    top_score = jnp.max(scores, axis=1, keepdims=True)
    expo = jnp.exp(scores - top_score)
    expo_total = jnp.sum(expo, axis=1, keepdims=True)
    log_total = top_score + jnp.log(expo_total)
    probs = expo / expo_total
    head_out = (matmul(probs.astype(jnp.bfloat16), value) * real[:, None]).astype(jnp.bfloat16)
    heads_out = lax.all_to_all(
        head_out.reshape(SEQ_DEVICES, local_rows, V_HEAD),
        "expert",
        split_axis=0,
        concat_axis=0,
        tiled=True,
        axis_index_groups=groups,
    )
    heads_out = heads_out.transpose(1, 0, 2).reshape(local_rows, HEADS * V_HEAD)

    hidden_rows = tokens.astype(jnp.float32)
    middle = hidden_rows + matmul(heads_out, full_out)
    second_normed = norm_scale(middle, second_gain).astype(jnp.bfloat16)

    all_normed = lax.all_gather(second_normed, "expert", axis=0, tiled=True)
    all_grads = lax.all_gather(cotangent, "expert", axis=0, tiled=True)
    all_routes = lax.all_gather(routes, "expert", axis=0, tiled=True)
    plane_rows = plane * local_rows
    logits = matmul(all_normed, router_weight)
    expert_ids = jnp.arange(plane, dtype=jnp.int32)
    choose = all_routes[:, :, None] == expert_ids[None, None, :]
    chosen = jnp.sum(jnp.where(choose, logits[:, None, :], 0.0), axis=2)
    chosen_top = jnp.max(chosen, axis=1, keepdims=True)
    chosen_exp = jnp.exp(chosen - chosen_top)
    gate_values = chosen_exp / jnp.sum(chosen_exp, axis=1, keepdims=True)
    here = all_routes == plane_at
    gate_here = jnp.sum(jnp.where(here, gate_values, 0.0), axis=1).reshape(plane, local_rows)
    marks = jnp.any(here, axis=1).reshape(plane, local_rows)
    ranks = jnp.cumsum(marks.astype(jnp.int32), axis=1) - 1
    picks = marks[:, None, :] & (
        ranks[:, None, :] == jnp.arange(capacity, dtype=jnp.int32)[None, :, None]
    )
    select = picks.astype(jnp.bfloat16)

    def to_slots(values):
        return (
            jnp.einsum(
                "bct,btd->bcd",
                select,
                values.reshape(plane, local_rows, width),
                preferred_element_type=jnp.float32,
            )
            .astype(jnp.bfloat16)
            .reshape(plane * capacity, width)
        )

    def to_tokens(values):
        return jnp.einsum(
            "bct,bcd->btd",
            select,
            values.reshape(plane, capacity, width),
            preferred_element_type=jnp.float32,
        ).reshape(plane_rows, width)

    slot_rows = to_slots(all_normed)
    slot_cotangent = to_slots(all_grads).astype(jnp.float32)
    slot_gate = jnp.sum(jnp.where(picks, gate_here[:, None, :], 0.0), axis=2).reshape(-1, 1)
    gate_pre = matmul(slot_rows, gate_single)
    up_pre = matmul(slot_rows, up_single)
    swished, slope = swish_parts(gate_pre)
    hidden = (swished * up_pre).astype(jnp.bfloat16)
    expert_out = matmul(hidden, down_single).astype(jnp.bfloat16).astype(jnp.float32)
    slot_gate_grad = jnp.sum(slot_cotangent * expert_out, axis=1).reshape(plane, capacity)
    slot_grad = (slot_gate * slot_cotangent).astype(jnp.bfloat16)
    hidden_grad = matmul_nt(slot_grad, down_single)
    gate_pre_grad = (hidden_grad * up_pre * slope).astype(jnp.bfloat16)
    up_pre_grad = (hidden_grad * swished).astype(jnp.bfloat16)
    row_back = (
        matmul_nt(gate_pre_grad, gate_single) + matmul_nt(up_pre_grad, up_single)
    ).astype(jnp.bfloat16)

    shared_pre = matmul(all_normed, gate_shared)
    shared_up_pre = matmul(all_normed, up_shared)
    shared_swished, shared_slope = swish_parts(shared_pre)
    shared_hidden = (shared_swished * shared_up_pre).astype(jnp.bfloat16)
    shared_hidden_grad = matmul_nt(all_grads, down_shared)
    shared_gate_back = (shared_hidden_grad * shared_up_pre * shared_slope).astype(jnp.bfloat16)
    shared_up_back = (shared_hidden_grad * shared_swished).astype(jnp.bfloat16)

    normed_part = (
        to_tokens(row_back)
        + matmul_nt(shared_gate_back, gate_shared)
        + matmul_nt(shared_up_back, up_shared)
    ).astype(jnp.bfloat16)
    token_gate_grad = jnp.sum(
        jnp.where(picks, slot_gate_grad[:, :, None], 0.0), axis=1
    ).reshape(plane_rows, 1)
    gate_high = token_gate_grad.astype(jnp.bfloat16)
    gate_low = (token_gate_grad - gate_high.astype(jnp.float32)).astype(jnp.bfloat16)
    at_me = (expert_ids == plane_at).astype(jnp.bfloat16)[None, :]
    back = lax.psum_scatter(
        jnp.concatenate([normed_part, gate_high * at_me, gate_low * at_me], axis=1),
        "expert",
        scatter_dimension=0,
        tiled=True,
    ).astype(jnp.float32)
    output_part = (
        to_tokens((slot_gate * expert_out).astype(jnp.bfloat16))
        + matmul(shared_hidden, down_shared)
    ).astype(jnp.bfloat16)
    output_sum = lax.psum_scatter(output_part, "expert", scatter_dimension=0, tiled=True)
    activations = (middle + output_sum.astype(jnp.float32)).astype(jnp.bfloat16)

    expert_down_grad = shard_sum(matmul_tn(hidden, slot_grad))[None]
    expert_gate_grad = shard_sum(matmul_tn(slot_rows, gate_pre_grad))[None]
    expert_up_grad = shard_sum(matmul_tn(slot_rows, up_pre_grad))[None]
    shared_down_grad = shard_sum(matmul_tn(shared_hidden, all_grads))
    shared_term = jnp.concatenate(
        [matmul_tn(all_normed, shared_gate_back), matmul_tn(all_normed, shared_up_back)], axis=1
    )

    def to_owners(term):
        moved = lax.all_to_all(
            term.astype(jnp.bfloat16).reshape(all_devices, -1, term.shape[1]),
            everyone,
            split_axis=0,
            concat_axis=0,
            tiled=True,
        )
        moved = moved.reshape(shards, plane, -1, term.shape[1]).astype(jnp.float32)
        return jnp.sum(moved, axis=0)

    def by_head(moved):
        heads = moved.reshape((plane // SEQ_DEVICES, HEADS) + moved.shape[1:]).sum(axis=0)
        return heads.transpose(1, 0, 2).reshape(moved.shape[1], -1)

    shared_moved = to_owners(shared_term).reshape(plane, -1, 2, shards, units)
    shared_moved = shared_moved.transpose(2, 1, 3, 0, 4)
    shared_moved = shared_moved.reshape(2, shared_moved.shape[1], -1)
    shared_gate_grad = shared_moved[0]
    shared_up_grad = shared_moved[1]

    grad_out = cotangent.astype(jnp.float32)
    gate_dense = back[:, width : width + plane] + back[:, width + plane :]
    own_start = plane_at * local_rows
    own_gates = lax.dynamic_slice_in_dim(gate_values, own_start, local_rows, 0)
    own_choose = routes[:, :, None] == expert_ids[None, None, :]
    gate_grad = jnp.sum(jnp.where(own_choose, gate_dense[:, None, :], 0.0), axis=2)
    chosen_grad = own_gates * (
        gate_grad - jnp.sum(own_gates * gate_grad, axis=1, keepdims=True)
    )
    logit_grad = jnp.sum(jnp.where(own_choose, chosen_grad[:, :, None], 0.0), axis=1)
    router_term = lax.dot_general(
        second_normed.astype(jnp.float32),
        logit_grad,
        (((0,), (0,)), ((), ())),
        precision=HIGH,
        preferred_element_type=jnp.float32,
    )
    normed_grad = back[:, :width] + lax.dot_general(
        logit_grad,
        router_weight.astype(jnp.float32),
        (((1,), (1,)), ((), ())),
        precision=HIGH,
        preferred_element_type=jnp.float32,
    )
    unused_two, second_back = jax.vjp(norm_scale, middle, second_gain)
    middle_norm_grad, second_term = second_back(normed_grad)
    middle_grad = grad_out + middle_norm_grad
    middle_low = middle_grad.astype(jnp.bfloat16)
    small_sums = lax.psum_scatter(
        jnp.concatenate([router_term, second_term[:, None]], axis=1),
        everyone,
        scatter_dimension=0,
        tiled=True,
    )
    router_weight_grad = small_sums[:, :plane]
    second_gain_grad = small_sums[:, plane]

    output_weight_grad = lax.psum_scatter(
        matmul_tn(heads_out, middle_low).astype(jnp.bfloat16),
        everyone,
        scatter_dimension=0,
        tiled=True,
    ).astype(jnp.float32)
    heads_grad = (matmul_nt(middle_low, full_out)).astype(jnp.bfloat16)
    heads_grad = heads_grad.reshape(local_rows, HEADS, V_HEAD).transpose(1, 0, 2)
    head_grad = lax.all_to_all(
        heads_grad, "expert", split_axis=0, concat_axis=0, tiled=True, axis_index_groups=groups
    ).reshape(SEQ, V_HEAD)
    head_grad = (head_grad.astype(jnp.float32) * real[:, None]).astype(jnp.bfloat16)
    again = jnp.exp(scores_of() - log_total)
    prob_grad = matmul_nt(head_grad, value)
    raw_grad = (
        again * (prob_grad - jnp.sum(again * prob_grad, axis=1, keepdims=True)) * scale
    ).astype(jnp.bfloat16)
    value_grad = matmul_tn(again.astype(jnp.bfloat16), head_grad)
    key_nope_grad = matmul_tn(raw_grad, query_nope)
    key_rope_grad = matmul_tn(raw_grad, query_rope)
    query_grad = jnp.concatenate(
        [
            matmul(raw_grad, key_nope),
            unrotate(matmul(raw_grad, key_rope), cosine_part, sine_part),
        ],
        axis=1,
    ).astype(jnp.bfloat16)
    pair_grad = jnp.concatenate([key_nope_grad, value_grad], axis=1).astype(jnp.bfloat16)
    latent_up_term = matmul_tn(key_latent, pair_grad)
    latent_up_grad = by_head(to_owners(latent_up_term))
    key_grad_part = jnp.concatenate([matmul_nt(pair_grad, up_head), key_rope_grad], axis=1)
    own_key_grad = lax.psum_scatter(
        key_grad_part.astype(jnp.bfloat16),
        "expert",
        scatter_dimension=0,
        tiled=True,
        axis_index_groups=groups,
    ).astype(jnp.float32)
    own_query_grad = lax.all_to_all(
        query_grad.reshape(SEQ_DEVICES, local_rows, head_dim),
        "expert",
        split_axis=0,
        concat_axis=0,
        tiled=True,
        axis_index_groups=groups,
    )
    own_query_grad = own_query_grad.transpose(1, 0, 2).reshape(local_rows, HEADS * head_dim)
    own_compressed = own_rows(compressed)
    unused_latent, latent_back = jax.vjp(norm_scale, own_compressed[:, :KV_RANK], latent_gain)
    latent_in_grad, latent_gain_term = latent_back(own_key_grad[:, :KV_RANK])
    rope_in_grad = unrotate(
        own_key_grad[:, KV_RANK:], own_rows(cosine_part), own_rows(sine_part)
    )
    compressed_grad = jnp.concatenate([latent_in_grad, rope_in_grad], axis=1).astype(jnp.bfloat16)
    down_columns = (KV_RANK + QK_ROPE) // SEQ_DEVICES
    column_grad = lax.all_to_all(
        compressed_grad.reshape(local_rows, SEQ_DEVICES, down_columns).transpose(1, 0, 2),
        "expert",
        split_axis=0,
        concat_axis=0,
        tiled=True,
        axis_index_groups=groups,
    ).reshape(SEQ, down_columns)
    normed_one_grad = matmul_nt(own_query_grad, full_query) + matmul_nt(
        compressed_grad, full_down
    )
    unused_one, first_back = jax.vjp(norm_scale, hidden_rows, first_gain)
    input_norm_grad, first_term = first_back(normed_one_grad)
    input_grad = middle_grad + input_norm_grad
    weight_term = matmul_tn(normed_one, jnp.concatenate([query_grad, column_grad], axis=1))
    weight_moved = to_owners(weight_term)
    query_weight_grad = by_head(weight_moved[:, :, :head_dim])
    latent_down_grad = by_head(weight_moved[:, :, head_dim:])
    gain_sums = lax.psum_scatter(
        jnp.concatenate(
            [
                first_term.reshape(all_devices, -1),
                latent_gain_term.reshape(all_devices, -1),
            ],
            axis=1,
        ),
        everyone,
        scatter_dimension=0,
        tiled=True,
    )[0]
    first_gain_grad = gain_sums[: width // all_devices]
    latent_gain_grad = gain_sums[width // all_devices :]
    return (
        activations,
        input_grad,
        first_gain_grad,
        query_weight_grad,
        latent_down_grad,
        latent_gain_grad,
        latent_up_grad,
        output_weight_grad,
        second_gain_grad,
        router_weight_grad,
        shared_gate_grad,
        shared_up_grad,
        shared_down_grad,
        expert_gate_grad,
        expert_up_grad,
        expert_down_grad,
    )


def solution(mesh):
    return jax.shard_map(
        on_device,
        mesh=mesh,
        in_specs=(
            P(("shard", "expert"), None),
            P(),
            P(("shard", "expert"), None),
            P(),
            P("shard", None),
            P("shard", None),
            P(),
            P("shard", None),
            P("shard", None),
            P(),
            P(),
            P("shard", None),
            P("shard", None),
            P("shard", None),
            P("expert", "shard", None),
            P("expert", "shard", None),
            P("expert", "shard", None),
            P(("shard", "expert"), None),
        ),
        out_specs=(
            P(("shard", "expert"), None),
            P(("shard", "expert"), None),
            P(("shard", "expert")),
            P(("shard", "expert"), None),
            P(("shard", "expert"), None),
            P(("shard", "expert")),
            P(("shard", "expert"), None),
            P(("shard", "expert"), None),
            P(("shard", "expert")),
            P(("shard", "expert"), None),
            P(("shard", "expert"), None),
            P(("shard", "expert"), None),
            P(("shard", "expert"), None),
            P("expert", "shard", None),
            P("expert", "shard", None),
            P("expert", "shard", None),
        ),
        check_vma=False,
    )
```

time: 2890 us -> 1380 us (0.48)
  waiting for transfers between devices: 2160 us -> 608 us
  local copies, waits for them, and re-layouts: 112 us -> 216 us
  matrix products: 356 us -> 313 us
    reduce_scatter x10 -> x3, waiting for transfers between devices: 1420 us -> 185 us  [the longest x1 104 us: on_device(): lax.psum_scatter(output_part, 'expert', scatter_dimension=0, tiled=True)]
    all_gather x10 -> x5, waiting for transfers between devices: 423 us -> 0.06 us  [the longest x2 0.04 us: shared_rows_plane(): gathered = lax.all_gather(pieces, 'expert', axis=1, tiled=False)]
    ppermute x16 -> x15, waiting for transfers between devices: 58.7 us -> 371 us  [the longest x11 188 us: shard_ring(): lax.ppermute(block, 'shard', [(source, (source + step) % count) for sourc...]
    all_to_all x4 -> x7, waiting for transfers between devices: 257 us -> 50.3 us  [the longest x1 26.1 us: on_device(): lax.all_to_all(head_out.reshape(SEQ_DEVICES, local_rows, V_HEAD), 'expert...]
    dynamic_update_slice x8 -> x19, local copies, waits for them, and re-layouts: 5.49 us -> 102 us  [the longest x10 52.3 us: shard_ring(): lax.dynamic_update_index_in_dim(whole, moved, (me - step) % count, 0)]
    dot_general x15 -> x5, matrix products: 109 us -> 24.2 us  [the longest x2 17.9 us: to_tokens(): jnp.einsum('bct,bcd->btd', select, values.reshape(plane, capacity, width)...]
    ppermute x16 -> x15, starting transfers between devices: 54.9 us -> 11.8 us  [the longest x11 8.99 us: shard_ring(): lax.ppermute(block, 'shard', [(source, (source + step) % count) for sourc...]
    dot_general x9 -> x13, matrix products: 74.3 us -> 113 us  [matmul_nt(): lax.dot_general(left, right, (((1,), (1,)), ((), ())), preferred_element_...]
  transfers between devices with their start and end apart: 41 -> 32, of which waited for: 33 -> 12; matrix products, arithmetic and copies ran while one was open for 19% -> 33% of each run, Pallas kernels for 0% -> 0%
where the time goes in v1:
time: 1380 us; the launch traced here: 1360 us
  waiting for transfers between devices  608 us (44%)
  matrix products  313 us (23%)
  local copies, waits for them, and re-layouts  216 us (16%)
  other arithmetic  83 us (6%)
  starting transfers between devices  68.1 us (5%)
  blocking collectives  59.1 us (4%)
  between operations  15.9 us (1%)
    ppermute x11, waiting for transfers between devices, shard_ring(): lax.ppermute(block, 'shard', [(source, (source + step) % count) for sourc...  188 us
    ppermute x4, waiting for transfers between devices, shard_sum(): lax.ppermute(outgoing.astype(jnp.bfloat16), 'shard', [(source, (source +...  183 us
    dot_general x13, matrix products, matmul_nt(): lax.dot_general(left, right, (((1,), (1,)), ((), ())), preferred_element_...  113 us
    reduce_scatter x1, waiting for transfers between devices, on_device(): lax.psum_scatter(output_part, 'expert', scatter_dimension=0, tiled=True)  104 us
    dot_general x14, matrix products, matmul(): return jnp.dot(left, right, preferred_element_type=jnp.float32)  99 us
    reduce_scatter x1, waiting for transfers between devices, on_device(): lax.psum_scatter(jnp.concatenate([normed_part, gate_high * at_me, gate_lo...  80.7 us
    dot_general x12, matrix products, matmul_tn(): lax.dot_general(left, right, (((0,), (0,)), ((), ())), preferred_element_...  74.6 us
    dynamic_update_slice x10, local copies, waits for them, and re-layouts, shard_ring(): lax.dynamic_update_index_in_dim(whole, moved, (me - step) % count, 0)  52.3 us
  transfers between devices with their start and end apart: 32, of which 12 were waited for; matrix products, arithmetic and copies ran while one was open for 33% of the time, Pallas kernels for 0%

profile of v1, /device:TPU:9, one launch (start us, length us, event | category | flops | bytes accessed | tf_op | source)
XLA Modules:
  0.0 1362.2 jit_solution(3165386699450417559)
XLA Ops:
  10.4 5.9 collective-permute-done.3
  31.2 38.4 %dynamic_update_slice.81 = bf16[2,1024,576]{1,0,2:T(2,128)(2,1)} dynamic-update-slice(bf16[2,1024,576]{1,0,2:T(2,128)(2,1)} %broadcast_in_dim.226, bf16[1,1024,576]{1,0,2:T(2,128)(2,1)S(1)} %copy.148, s32[]{:T(128)S(6)} %select_n.159, s32[]{:T(128)} %constant.217.clone.1, s32[]{:T(128)} %constant.217.clone.1) | dynamic-update-slice | bytes 2359300 | tf_op jit(solution)/shard_map/jit(dynamic_update_index_in_dim)/dynamic_update_slice | solution.py:89
  73.7 38.8 %dynamic_update_slice.82 = bf16[2,1024,576]{1,0,2:T(2,128)(2,1)} dynamic-update-slice(bf16[2,1024,576]{1,0,2:T(2,128)(2,1)} %dynamic_update_slice.81, bf16[1,1024,576]{1,0,2:T(2,128)(2,1)S(1)} %copy.149, s32[]{:T(128)S(6)} %select_n.161, s32[]{:T(128)} %constant.217.clone.1, s32[]{:T(128)} %constant.217.clone.1) | dynamic-update-slice | bytes 2359300 | tf_op jit(solution)/shard_map/jit(dynamic_update_index_in_dim)/dynamic_update_slice | solution.py:94
  115.0 6.0 fusion
  121.6 5.3 fusion.116
  128.4 4.9 fusion.118
  137.8 10.7 fusion.122
  148.5 8.3 fusion.8
  156.8 7.4 fusion.32
  165.3 9.2 all-to-all-start
  174.5 26.1 %all-to-all-done = bf16[16,128,128]{1,2,0:T(8,128)(2,1)S(1)} async-done(((bf16[16,128,128]{1,2,0:T(8,128)(2,1)}), bf16[16,128,128]{1,2,0:T(8,128)(2,1)S(1)}, u32[]{:S(2)}, u32[]{:S(2)}) %all-to-all-start) | async-done | bytes 524320 | tf_op jit(solution)/shard_map/all_to_all | solution.py:234
  200.6 4.9 multiply_reduce_fusion.4
  231.6 19.5 %all_gather.37 = s32[2048,6]{0,1:T(8,128)S(1)} all-gather(s32[128,6]{0,1:T(8,128)S(1)} %copy-done.55), channel_id=1, replica_groups=mesh['shard'=2,'expert'=16] {'expert'}, dimensions={0}, use_global_device_ids=true | all-gather | bytes 52224 | tf_op jit(solution)/shard_map/all_gather | solution.py:250
  252.2 31.7 %collective-permute-done.7 = bf16[1024,176]{1,0:T(8,128)(2,1)} collective-permute-done((bf16[1024,176]{1,0:T(8,128)(2,1)}, bf16[1024,176]{1,0:T(8,128)(2,1)}, u32[]{:S(2)}, u32[]{:S(2)}) %collective-permute-start.7) | collective-permute-done | bytes 360480 | tf_op jit(solution)/shard_map/ppermute | solution.py:91
  284.3 10.8 collective-permute-done.8
  296.4 129.9 %collective-permute-done.9 = bf16[88,2048]{1,0:T(8,128)(2,1)S(1)} collective-permute-done((bf16[88,2048]{1,0:T(8,128)(2,1)S(1)}, bf16[88,2048]{1,0:T(8,128)(2,1)S(1)}, u32[]{:S(2)}, u32[]{:S(2)}) %collective-permute-start.9) | collective-permute-done | bytes 360480 | tf_op jit(solution)/shard_map/ppermute | solution.py:91
  437.6 7.5 convolution_bitcast_fusion
  445.1 5.6 fusion.124
  452.0 4.8 convolution_convert_fusion.2
  459.3 12.0 fusion.125
  471.3 13.8 %fusion.17 = (bf16[1408,1024]{0,1:T(8,128)(2,1)}, f32[1024,1408]{1,0:T(8,128)}) fusion(f32[1024,1408]{1,0:T(8,128)S(1)} %fusion.125, bf16[1024,2048]{1,0:T(8,128)(2,1)S(1)} %bitcast.278, bf16[2048,1408]{1,0:T(8,128)(2,1)} %bitcast.23), kind=kOutput, calls=%fused_computation.35 | convolution fusion | flops 5914230784 | bytes 24379392 | tf_op jit(solution)/shard_map/dot_general | solution.py:27
  485.1 12.1 fusion.11
  502.7 13.4 multiply_convert_fusion.3
  516.1 12.0 fusion.127
  528.1 10.9 add_convert_fusion
  539.0 8.2 fusion.54
  550.2 4.7 multiply_convert_fusion.8
  554.8 8.3 fusion.128
  563.7 15.7 %fusion.4 = bf16[2048,2048]{1,0:T(8,128)(2,1)} fusion(f32[2048,2048]{1,0:T(8,128)} %fusion.128, f32[16,128,2048]{2,1,0:T(8,128)} %fusion.54, bf16[2048,176]{0,1:T(8,128)(2,1)} %get-tuple-element.128, bf16[2048,176]{1,0:T(8,128)(2,1)S(1)} %bitcast.288), kind=kOutput, calls=%fused_computation.7 | convolution fusion | flops 1488977920 | bytes 43384832 | tf_op jit(solution)/shard_map/dot_general | solution.py:37
  579.4 13.7 %concatenate.63 = bf16[2048,2080]{1,0:T(8,128)(2,1)} concatenate(bf16[2048,2048]{1,0:T(8,128)(2,1)} %fusion.4, bf16[2048,16]{1,0:T(8,128)(2,1)S(1)} %get-tuple-element.145, bf16[2048,16]{1,0:T(8,128)(2,1)S(1)} %get-tuple-element.144), dimensions={1} | concatenate | bytes 17039360 | tf_op jit(solution)/shard_map/concatenate | solution.py:325
  596.4 9.7 fusion.57
  606.2 13.3 fusion.5
  619.5 80.7 %reduce-scatter.12.cloned.1.call-done = bf16[128,2080]{1,0:T(8,128)(2,1)} async-done(((bf16[2048,2080]{1,0:T(8,128)(2,1)}), bf16[128,2080]{1,0:T(8,128)(2,1)}) %reduce-scatter.12.cloned.1.call-update) | async-done | bytes 532496 | tf_op jit(solution)/shard_map/reduce_scatter | solution.py:324
  704.8 104.4 %reduce-scatter.10.cloned.1.call-done = bf16[128,2048]{1,0:T(8,128)(2,1)} async-done(((bf16[2048,2048]{1,0:T(8,128)(2,1)}), bf16[128,2048]{1,0:T(8,128)(2,1)}) %reduce-scatter.10.cloned.1.call-update) | async-done | bytes 524304 | tf_op jit(solution)/shard_map/reduce_scatter | solution.py:334
  811.9 6.3 fusion.37
  819.1 5.2 all-to-all-start.1
  826.6 11.9 all-to-all-done.1
  838.8 8.9 fusion.33
  847.8 13.0 multiply_reduce_fusion
  860.9 8.4 multiply_convert_fusion
  884.8 9.7 collective-permute-done.10
  895.7 5.9 convolution_convert_fusion.7
  903.0 5.3 convolution_convert_fusion.6
  912.6 5.3 all-to-all-start.6
  917.9 6.4 copy.169
  924.3 5.7 convolution_convert_fusion
  930.0 11.8 fusion.29
  946.3 11.7 fusion.131
  958.1 6.7 fusion.27
  964.9 8.9 fusion.26
  974.9 5.1 fusion.24
  986.4 182.5 %collective-permute-done.11 = bf16[88,2048]{1,0:T(8,128)(2,1)S(1)} collective-permute-done((bf16[88,2048]{1,0:T(8,128)(2,1)S(1)}, bf16[88,2048]{1,0:T(8,128)(2,1)S(1)}, u32[]{:S(2)}, u32[]{:S(2)}) %collective-permute-start.11) | collective-permute-done | bytes 360480 | tf_op jit(solution)/shard_map/ppermute | solution.py:110
  1183.8 7.6 fusion.16
  1191.4 6.8 fusion.22
  1198.2 4.9 fusion.21
  1209.7 19.3 %all-to-all-start.5 = ((bf16[32,16,256]{2,1,0:T(8,128)(2,1)}), bf16[32,16,256]{2,1,0:T(8,128)(2,1)S(1)}, u32[]{:S(2)}, u32[]{:S(2)}) async-start(bf16[32,16,256]{2,1,0:T(8,128)(2,1)} %bitcast.61), calls=%async_computation.7 | async-start | bytes 524288 | tf_op jit(solution)/shard_map/all_to_all | solution.py:346
  1229.0 5.1 fusion.100
  1236.0 5.8 convolution_convert_fusion.9
  1247.6 6.2 all-to-all-start.3
  1262.6 5.3 all-to-all-start.2
  1272.3 7.7 convolution_convert_fusion.5
  1282.2 8.3 all-to-all-done.2
  1295.1 9.9 fusion.43
  1305.2 39.6 %all-reduce = f32[32,80]{1,0:T(8,128)S(1)} all-reduce(f32[32,80]{1,0:T(8,128)S(1)} %pad_maximum_fusion.15), channel_id=5, replica_groups=mesh['shard'=2,'expert'=16] {'shard','expert'}, use_global_device_ids=true, to_apply=%region_31.32.clone | all-reduce | flops 2560 | bytes 20480
  (404 shorter events, 192.6 us)
Async XLA Ops:
  7.2 437.9 %copy-start = (bf16[2048,16]{0,1:T(8,128)(2,1)S(1)}, bf16[2048,16]{0,1:T(8,128)(2,1)}, u32[]{:S(2)}) copy-start(bf16[2048,16]{0,1:T(8,128)(2,1)} %param.28) | copy-start | bytes 196612
  7.2 17.8 %copy-start.75 = (s32[2,4]{1,0:T(2,128)S(1)}, s32[2,4]{1,0:T(2,128)}, u32[]{:S(2)}) copy-start(s32[2,4]{1,0:T(2,128)} %param.19) | copy-start | bytes 100
  7.2 107.7 %all-gather.6.cloned.1.call-start = ((), (), s32[]{:S(2)}) async-start(), calls=%async_computation.12 | async-start | bytes 8912896 | tf_op jit(solution)/shard_map/all_gather | solution.py:196
  7.9 166.6 %all-gather.8.cloned.1.call-start = ((), (), s32[]{:S(2)}) async-start(), calls=%async_computation.13 | async-start | bytes 8912896 | tf_op jit(solution)/shard_map/all_gather | solution.py:125
  9.1 7.2 collective-permute-start.3
  17.1 420.5 %all-gather.12.cloned.1.call-start = ((), (), s32[]{:S(2)}) async-start(), calls=%async_computation.16 | async-start | bytes 8912896 | tf_op jit(solution)/shard_map/all_gather | solution.py:249
  18.9 50.7 %collective-permute-start.2 = (bf16[256,256]{1,0:T(8,128)(2,1)S(1)}, bf16[256,256]{1,0:T(8,128)(2,1)S(1)}, u32[]{:S(2)}, u32[]{:S(2)}) collective-permute-start(bf16[256,256]{1,0:T(8,128)(2,1)S(1)} %get-tuple-element.116), channel_id=1, source_target_pairs={{0,16},{16,0},{1,17},{17,1},{2,18},{18,2},{3,19},{19,3},{4,20},{20... | collective-permute-start | bytes 393224 | tf_op jit(solution)/shard_map/ppermute | solution.py:91
  23.5 46.0 %collective-permute-start = (bf16[1024,192]{1,0:T(8,128)(2,1)}, bf16[1024,192]{1,0:T(8,128)(2,1)S(1)}, u32[]{:S(2)}, u32[]{:S(2)}) collective-permute-start(bf16[1024,192]{1,0:T(8,128)(2,1)} %get-tuple-element.118), channel_id=1, source_target_pairs={{0,16},{16,0},{1,17},{17,1},{2,18},{18,2},{3,19},{19,3},{4,20},{20... | collective-permute-start | bytes 1179656 | tf_op jit(solution)/shard_map/ppermute | solution.py:91
  23.8 46.7 %collective-permute-start.1 = (bf16[1024,576]{0,1:T(8,128)(2,1)}, bf16[1024,576]{0,1:T(8,128)(2,1)}, u32[]{:S(2)}, u32[]{:S(2)}) collective-permute-start(bf16[1024,576]{0,1:T(8,128)(2,1)} %param.23), channel_id=1, source_target_pairs={{0,16},{16,0},{1,17},{17,1},{2,18},{18,2},{3,19},{19,3},{4,20},{20... | collective-permute-start | bytes 3538952 | tf_op jit(solution)/shard_map/ppermute | solution.py:91
  25.0 108.2 %copy-start.51 = (f32[2048]{0:T(1024)}, f32[2048]{0:T(1024)S(1)}, u32[]{:S(2)}) copy-start(f32[2048]{0:T(1024)S(1)} %iota_convert_fusion) | copy-start | bytes 24580
  25.4 131.4 %copy-start.63 = (f32[2048]{0:T(1024)}, f32[2048]{0:T(1024)S(1)}, u32[]{:S(2)}) copy-start(f32[2048]{0:T(1024)S(1)} %compare_convert_fusion) | copy-start | bytes 24580
  25.4 107.8 %copy-start.73 = (f32[32]{0:T(128)}, f32[32]{0:T(128)S(1)}, u32[]{:S(2)}) copy-start(f32[32]{0:T(128)S(1)} %multiply_power_fusion) | copy-start | bytes 388
  69.5 57.8 %copy-start.26 = (bf16[2,256,256]{2,1,0:T(8,128)(2,1)}, bf16[2,256,256]{2,1,0:T(8,128)(2,1)S(1)}, u32[]{:S(2)}) copy-start(bf16[2,256,256]{2,1,0:T(8,128)(2,1)S(1)} %bitcast_dynamic-update-slice_fusion.15) | copy-start | bytes 786436
  128.3 28.5 %copy-start.46 = (bf16[2048,256]{1,0:T(8,128)(2,1)}, bf16[2048,256]{1,0:T(8,128)(2,1)S(1)}, u32[]{:S(2)}) copy-start(bf16[2048,256]{1,0:T(8,128)(2,1)S(1)} %convolution_convert_fusion.4) | copy-start | bytes 3145732
  156.8 43.8 %copy-start.6 = (bf16[128,2048]{1,0:T(8,128)(2,1)S(1)}, bf16[128,2048]{1,0:T(8,128)(2,1)}, u32[]{:S(2)}) copy-start(bf16[128,2048]{1,0:T(8,128)(2,1)} %param.18) | copy-start | bytes 1572868
  165.3 35.3 %all-to-all-start = ((bf16[16,128,128]{1,2,0:T(8,128)(2,1)}), bf16[16,128,128]{1,2,0:T(8,128)(2,1)S(1)}, u32[]{:S(2)}, u32[]{:S(2)}) async-start(bf16[16,128,128]{1,2,0:T(8,128)(2,1)} %copy.150), calls=%async_computation | async-start | bytes 1048576 | tf_op jit(solution)/shard_map/all_to_all | solution.py:234
  174.5 270.7 %all-gather.10.cloned.1.call-start = ((), (), s32[]{:S(2)}) async-start(), calls=%async_computation.14 | async-start | bytes 8912896 | tf_op jit(solution)/shard_map/all_gather | solution.py:248
  207.6 492.6 %reduce-scatter.12.cloned.1.call-start = ((), (), s32[]{:S(2)}) async-start(), calls=%async_computation.17 | async-start | bytes 9469952 | tf_op jit(solution)/shard_map/reduce_scatter | solution.py:324
  207.9 218.5 %collective-permute-start.6 = (bf16[704,2048]{1,0:T(8,128)(2,1)}, bf16[704,2048]{1,0:T(8,128)(2,1)}, u32[]{:S(2)}, u32[]{:S(2)}) collective-permute-start(bf16[704,2048]{1,0:T(8,128)(2,1)} %bitcast.304), channel_id=1, source_target_pairs={{0,16},{16,0},{1,17},{17,1},{2,18},{18,2},{3,19},{19,3},{4,20},{20... | collective-permute-start | bytes 8650760 | tf_op jit(solution)/shard_map/ppermute | solution.py:91
  211.0 72.8 %collective-permute-start.7 = (bf16[1024,176]{1,0:T(8,128)(2,1)}, bf16[1024,176]{1,0:T(8,128)(2,1)}, u32[]{:S(2)}, u32[]{:S(2)}) collective-permute-start(bf16[1024,176]{1,0:T(8,128)(2,1)} %pad_maximum_fusion.6), channel_id=1, source_target_pairs={{0,16},{16,0},{1,17},{17,1},{2,18},{18,2},{3,19},{19,3},{4,20},{20... | collective-permute-start | bytes 1081352 | tf_op jit(solution)/shard_map/ppermute | solution.py:91
  214.6 80.5 %collective-permute-start.8 = (bf16[1024,176]{1,0:T(8,128)(2,1)}, bf16[1024,176]{1,0:T(8,128)(2,1)}, u32[]{:S(2)}, u32[]{:S(2)}) collective-permute-start(bf16[1024,176]{1,0:T(8,128)(2,1)} %pad_maximum_fusion.7), channel_id=1, source_target_pairs={{0,16},{16,0},{1,17},{17,1},{2,18},{18,2},{3,19},{19,3},{4,20},{20... | collective-permute-start | bytes 1081352 | tf_op jit(solution)/shard_map/ppermute | solution.py:91
  215.0 219.1 %collective-permute-start.5 = (bf16[1024,1408]{1,0:T(8,128)(2,1)}, bf16[1024,1408]{1,0:T(8,128)(2,1)}, u32[]{:S(2)}, u32[]{:S(2)}) collective-permute-start(bf16[1024,1408]{1,0:T(8,128)(2,1)} %bitcast.306), channel_id=1, source_target_pairs={{0,16},{16,0},{1,17},{17,1},{2,18},{18,2},{3,19},{19,3},{4,20},{20... | collective-permute-start | bytes 8650760 | tf_op jit(solution)/shard_map/ppermute | solution.py:91
  216.1 214.3 %collective-permute-start.4 = (bf16[1024,1408]{1,0:T(8,128)(2,1)}, bf16[1024,1408]{1,0:T(8,128)(2,1)}, u32[]{:S(2)}, u32[]{:S(2)}) collective-permute-start(bf16[1024,1408]{1,0:T(8,128)(2,1)} %bitcast.305), channel_id=1, source_target_pairs={{0,16},{16,0},{1,17},{17,1},{2,18},{18,2},{3,19},{19,3},{4,20},{20... | collective-permute-start | bytes 8650760 | tf_op jit(solution)/shard_map/ppermute | solution.py:91
  283.9 142.4 %collective-permute-start.9 = (bf16[88,2048]{1,0:T(8,128)(2,1)S(1)}, bf16[88,2048]{1,0:T(8,128)(2,1)S(1)}, u32[]{:S(2)}, u32[]{:S(2)}) collective-permute-start(bf16[88,2048]{1,0:T(8,128)(2,1)S(1)} %get-tuple-element.109), channel_id=1, source_target_pairs={{0,16},{16,0},{1,17},{17,1},{2,18},{18,2},{3,19},{19,3},{4,20},{20... | collective-permute-start | bytes 1081352 | tf_op jit(solution)/shard_map/ppermute | solution.py:91
  456.8 14.5 %copy-start.3 = (bf16[16,64,2048]{2,1,0:T(8,128)(2,1)}, bf16[16,64,2048]{2,1,0:T(8,128)(2,1)S(1)}, u32[]{:S(2)}) copy-start(bf16[16,64,2048]{2,1,0:T(8,128)(2,1)S(1)} %convolution_convert_fusion.2) | copy-start | bytes 12582916
  459.2 25.9 %copy-start.2 = (f32[16,64,2048]{2,1,0:T(8,128)}, f32[16,64,2048]{2,1,0:T(8,128)S(1)}, u32[]{:S(2)}) copy-start(f32[16,64,2048]{2,1,0:T(8,128)S(1)} %convert_convert_fusion) | copy-start | bytes 25165828
  516.1 31.1 %slice-start.4 = ((s8[8388608]{0:T(1024)(128)(4,1)}), s8[4194304]{0:T(1024)(128)(4,1)S(1)}, s32[]{:S(2)}) async-start(s8[8388608]{0:T(1024)(128)(4,1)} %bitcast.267), calls=%async_computation.26 | async-start | bytes 8388608
  528.1 19.0 %slice-start.5 = ((s8[8388608]{0:T(1024)(128)(4,1)}), s8[4194304]{0:T(1024)(128)(4,1)S(1)}, s32[]{:S(2)}) async-start(s8[8388608]{0:T(1024)(128)(4,1)} %bitcast.267), calls=%async_computation.27 | async-start | bytes 8388608
  593.1 216.1 %reduce-scatter.10.cloned.1.call-start = ((), (), s32[]{:S(2)}) async-start(), calls=%async_computation.15 | async-start | bytes 8912896 | tf_op jit(solution)/shard_map/reduce_scatter | solution.py:334
  619.4 82.1 %copy-start.56 = (s32[128,6]{0,1:T(8,128)S(1)}, s32[128,6]{0,1:T(8,128)}, u32[]{:S(2)}) copy-start(s32[128,6]{0,1:T(8,128)} %param.20) | copy-start | bytes 9220
  619.4 83.5 %copy-start.5 = (f32[128,2048]{1,0:T(8,128)S(1)}, f32[128,2048]{1,0:T(8,128)}, u32[]{:S(2)}) copy-start(f32[128,2048]{1,0:T(8,128)} %copy-done.4) | copy-start | bytes 3145732
  619.4 83.5 %copy-start.54 = (f32[2048]{0:T(1024)S(1)}, f32[2048]{0:T(1024)}, u32[]{:S(2)}) copy-start(f32[2048]{0:T(1024)} %param.27) | copy-start | bytes 24580
  619.4 83.5 %copy-start.72 = (f32[128]{0:T(128)S(1)}, f32[128]{0:T(128)}, u32[]{:S(2)}) copy-start(f32[128]{0:T(128)} %copy-done.71) | copy-start | bytes 1540
  619.5 85.3 %copy-start.77 = (f32[128]{0:T(128)S(1)}, f32[128]{0:T(128)}, u32[]{:S(2)}) copy-start(f32[128]{0:T(128)} %copy-done.76) | copy-start | bytes 1540
  811.9 26.6 %copy-start.64 = (f32[2048]{0:T(1024)S(1)}, f32[2048]{0:T(1024)}, u32[]{:S(2)}) copy-start(f32[2048]{0:T(1024)} %copy-done.63) | copy-start | bytes 24580
  819.1 19.3 %all-to-all-start.1 = ((bf16[16,128,128]{2,1,0:T(8,128)(2,1)}), bf16[16,128,128]{2,1,0:T(8,128)(2,1)S(1)}, u32[]{:S(2)}, u32[]{:S(2)}) async-start(bf16[16,128,128]{2,1,0:T(8,128)(2,1)} %bitcast.262), calls=%async_computation.3 | async-start | bytes 1048576 | tf_op jit(solution)/shard_map/all_to_all | solution.py:411
  824.3 378.8 %reduce-scatter.18.cloned.1.call-start = ((), (), s32[]{:S(2)}) async-start(), calls=%async_computation.21 | async-start | bytes 1081344
  826.1 415.8 %reduce-scatter.16.cloned.1.call-start = ((), (), s32[]{:S(2)}) async-start(), calls=%async_computation.20 | async-start | bytes 2785280
  838.8 22.0 %slice-start = ((s8[16777216]{0:T(1024)(128)(4,1)}), s8[4194304]{0:T(1024)(128)(4,1)S(1)}, s32[]{:S(2)}) async-start(s8[16777216]{0:T(1024)(128)(4,1)} %bitcast.264), calls=%async_computation.22 | async-start | bytes 8388608
  838.8 22.0 %slice-start.1 = ((s8[16777216]{0:T(1024)(128)(4,1)}), s8[4194304]{0:T(1024)(128)(4,1)S(1)}, s32[]{:S(2)}) async-start(s8[16777216]{0:T(1024)(128)(4,1)} %bitcast.264), calls=%async_computation.23 | async-start | bytes 8388608
  847.7 27.5 %copy-start.17 = (bf16[2048,128]{0,1:T(8,128)(2,1)}, bf16[2048,128]{0,1:T(8,128)(2,1)S(1)}, u32[]{:S(2)}) copy-start(bf16[2048,128]{0,1:T(8,128)(2,1)S(1)} %fusion.33) | copy-start | bytes 1572868
  877.7 17.7 %copy-start.7 = (bf16[128,2048]{1,0:T(8,128)(2,1)S(1)}, bf16[128,2048]{1,0:T(8,128)(2,1)}, u32[]{:S(2)}) copy-start(bf16[128,2048]{1,0:T(8,128)(2,1)} %param.18) | copy-start | bytes 1572868
  877.7 17.9 %copy-start.39 = (bf16[2048,176]{0,1:T(8,128)(2,1)S(1)}, bf16[2048,176]{0,1:T(8,128)(2,1)}, u32[]{:S(2)}) copy-start(bf16[2048,176]{0,1:T(8,128)(2,1)} %copy-done.38) | copy-start | bytes 2162692
  882.2 412.9 %all-gather.14.cloned.1.call-start = ((), (), s32[]{:S(2)}) async-start(), calls=%async_computation.18 | async-start | bytes 13369344 | tf_op jit(solution)/shard_map/all_gather | solution.py:125
  883.6 10.9 collective-permute-start.10
  912.6 257.3 %all-to-all-start.6 = ((bf16[32,64,352]{2,1,0:T(8,128)(2,1)}), bf16[32,64,352]{2,1,0:T(8,128)(2,1)}, u32[]{:S(2)}, u32[]{:S(2)}) async-start(bf16[32,64,352]{2,1,0:T(8,128)(2,1)} %pad_maximum_fusion.1), calls=%async_computation.9 | async-start | bytes 3145728 | tf_op jit(solution)/shard_map/all_to_all | solution.py:346
  917.9 435.6 %reduce-scatter.14.cloned.1.call-start = ((), (), s32[]{:S(2)}) async-start(), calls=%async_computation.19 | async-start | bytes 8650752 | tf_op jit(solution)/shard_map/reduce_scatter | solution.py:403
  964.8 15.3 %copy-start.14 = (f32[2,1024,1408]{2,1,0:T(8,128)}, f32[2,1024,1408]{2,1,0:T(8,128)S(1)}, u32[]{:S(2)}) copy-start(f32[2,1024,1408]{2,1,0:T(8,128)S(1)} %fusion.27) | copy-start | bytes 34603012
  964.9 18.6 %slice-start.8 = ((s8[8388608]{0:T(1024)(128)(4,1)}), s8[4194304]{0:T(1024)(128)(4,1)S(1)}, s32[]{:S(2)}) async-start(s8[8388608]{0:T(1024)(128)(4,1)} %bitcast.274), calls=%async_computation.30 | async-start | bytes 8388608
  973.7 210.1 %collective-permute-start.14 = (bf16[704,2048]{1,0:T(8,128)(2,1)}, bf16[704,2048]{1,0:T(8,128)(2,1)}, u32[]{:S(2)}, u32[]{:S(2)}) collective-permute-start(bf16[704,2048]{1,0:T(8,128)(2,1)} %fusion.26), channel_id=1, source_target_pairs={{0,16},{16,0},{1,17},{17,1},{2,18},{18,2},{3,19},{19,3},{4,20},{20... | collective-permute-start | bytes 8650760 | tf_op jit(solution)/shard_map/ppermute | solution.py:110
  980.1 211.3 %collective-permute-start.12 = (bf16[1024,1408]{1,0:T(8,128)(2,1)}, bf16[1024,1408]{1,0:T(8,128)(2,1)}, u32[]{:S(2)}, u32[]{:S(2)}) collective-permute-start(bf16[1024,1408]{1,0:T(8,128)(2,1)} %fusion.24), channel_id=1, source_target_pairs={{0,16},{16,0},{1,17},{17,1},{2,18},{18,2},{3,19},{19,3},{4,20},{20... | collective-permute-start | bytes 8650760 | tf_op jit(solution)/shard_map/ppermute | solution.py:110
  982.0 216.1 %collective-permute-start.13 = (bf16[1024,1408]{1,0:T(8,128)(2,1)}, bf16[1024,1408]{1,0:T(8,128)(2,1)}, u32[]{:S(2)}, u32[]{:S(2)}) collective-permute-start(bf16[1024,1408]{1,0:T(8,128)(2,1)} %fusion.25), channel_id=1, source_target_pairs={{0,16},{16,0},{1,17},{17,1},{2,18},{18,2},{3,19},{19,3},{4,20},{20... | collective-permute-start | bytes 8650760 | tf_op jit(solution)/shard_map/ppermute | solution.py:110
  985.3 183.6 %collective-permute-start.11 = (bf16[88,2048]{1,0:T(8,128)(2,1)S(1)}, bf16[88,2048]{1,0:T(8,128)(2,1)S(1)}, u32[]{:S(2)}, u32[]{:S(2)}) collective-permute-start(bf16[88,2048]{1,0:T(8,128)(2,1)S(1)} %fusion.77), channel_id=1, source_target_pairs={{0,16},{16,0},{1,17},{17,1},{2,18},{18,2},{3,19},{19,3},{4,20},{20... | collective-permute-start | bytes 1081352 | tf_op jit(solution)/shard_map/ppermute | solution.py:110
  1183.8 14.4 %slice-start.10 = ((s8[11534336]{0:T(1024)(128)(4,1)}), s8[4194304]{0:T(1024)(128)(4,1)S(1)}, s32[]{:S(2)}) async-start(s8[11534336]{0:T(1024)(128)(4,1)} %bitcast.292), calls=%async_computation.32 | async-start | bytes 8388608
  1183.8 14.4 %slice-start.11 = ((s8[11534336]{0:T(1024)(128)(4,1)}), s8[4194304]{0:T(1024)(128)(4,1)S(1)}, s32[]{:S(2)}) async-start(s8[11534336]{0:T(1024)(128)(4,1)} %bitcast.292), calls=%async_computation.33 | async-start | bytes 8388608
  1203.1 25.9 %copy-start.30 = (bf16[2048,32]{0,1:T(8,128)(2,1)S(1)}, bf16[2048,32]{0,1:T(8,128)(2,1)}, u32[]{:S(2)}) copy-start(bf16[2048,32]{0,1:T(8,128)(2,1)} %copy-done.29) | copy-start | bytes 393220
  1203.1 25.9 %copy-start.32 = (bf16[2048,32]{0,1:T(8,128)(2,1)S(1)}, bf16[2048,32]{0,1:T(8,128)(2,1)}, u32[]{:S(2)}) copy-start(bf16[2048,32]{0,1:T(8,128)(2,1)} %copy-done.31) | copy-start | bytes 393220
  1209.7 37.9 %all-to-all-start.5 = ((bf16[32,16,256]{2,1,0:T(8,128)(2,1)}), bf16[32,16,256]{2,1,0:T(8,128)(2,1)S(1)}, u32[]{:S(2)}, u32[]{:S(2)}) async-start(bf16[32,16,256]{2,1,0:T(8,128)(2,1)} %bitcast.61), calls=%async_computation.7 | async-start | bytes 524288 | tf_op jit(solution)/shard_map/all_to_all | solution.py:346
  1241.9 20.0 %copy-start.45 = (bf16[2048,128]{1,0:T(8,128)(2,1)}, bf16[2048,128]{1,0:T(8,128)(2,1)S(1)}, u32[]{:S(2)}) copy-start(bf16[2048,128]{1,0:T(8,128)(2,1)S(1)} %convolution_convert_fusion.9) | copy-start | bytes 1572868
  1247.6 24.7 %copy-start.62 = (f32[2048]{0:T(1024)S(1)}, f32[2048]{0:T(1024)}, u32[]{:S(2)}) copy-start(f32[2048]{0:T(1024)} %param.21) | copy-start | bytes 24580
  1247.6 24.7 %copy-start.68 = (f32[2048]{0:T(1024)S(1)}, f32[2048]{0:T(1024)}, u32[]{:S(2)}) copy-start(f32[2048]{0:T(1024)} %copy-done.67) | copy-start | bytes 24580
  1247.6 14.3 %all-to-all-start.3 = ((bf16[16,128,36]{1,2,0:T(8,128)(2,1)}), bf16[16,128,36]{1,2,0:T(8,128)(2,1)S(1)}, u32[]{:S(2)}, u32[]{:S(2)}) async-start(bf16[16,128,36]{1,2,0:T(8,128)(2,1)} %bitcast.54), calls=%async_computation.5 | async-start | bytes 327680 | tf_op jit(solution)/shard_map/all_to_all | solution.py:458
  1262.6 28.0 %all-to-all-start.2 = ((bf16[16,128,192]{1,2,0:T(8,128)(2,1)}), bf16[16,128,192]{1,2,0:T(8,128)(2,1)S(1)}, u32[]{:S(2)}, u32[]{:S(2)}) async-start(bf16[16,128,192]{1,2,0:T(8,128)(2,1)} %pad_maximum_fusion.3), calls=%async_computation.4 | async-start | bytes 1572864 | tf_op jit(solution)/shard_map/all_to_all | solution.py:441
  1290.6 57.9 %all-to-all-start.4 = ((bf16[32,64,228]{2,1,0:T(8,128)(2,1)}), bf16[32,64,228]{2,1,0:T(8,128)(2,1)}, u32[]{:S(2)}, u32[]{:S(2)}) async-start(bf16[32,64,228]{2,1,0:T(8,128)(2,1)} %bitcast.300), calls=%async_computation.6 | async-start | bytes 2097152 | tf_op jit(solution)/shard_map/all_to_all | solution.py:346
  (63 other events, 419.2 us)
Sparse Core Ops, SparseCore 0:
  10.2 75.8 all-gather.5
  88.9 73.1 all-gather.7
  164.2 84.5 all-gather.11
  251.4 73.2 all-gather.9
  593.3 106.9 reduce-scatter.11
  704.7 104.4 reduce-scatter.9
  828.1 122.6 reduce-scatter.17
  954.5 73.2 reduce-scatter.15
  1030.1 100.9 all-gather.13
  1133.2 135.6 reduce-scatter.13

commit v2 on v1

--- a/solution.py
+++ b/solution.py
@@ -1,8 +1,11 @@
+import functools
 import math
 
 import jax
 import jax.numpy as jnp
 from jax import lax
+from jax.experimental import pallas as pl
+from jax.experimental.pallas import tpu as pltpu
 from jax.sharding import PartitionSpec as P
 
 HEADS = 16
@@ -80,6 +83,459 @@
     if plane == members:
         return None
     return [list(range(low, low + members)) for low in range(0, plane, members)]
+
+
+MESH = pl.DeviceIdType.MESH
+INNER = 4
+PIECES = 2
+
+
+class Sender:
+    def __init__(self):
+        self.started = []
+
+    def start(self, there, copy):
+        @pl.when(there)
+        def _():
+            copy.start()
+
+        self.started.append((there, copy))
+
+    def finish(self):
+        for there, copy in self.started:
+            @pl.when(there)
+            def _():
+                copy.wait_send()
+
+
+def remote(source, target, send_sem, recv_sem, place):
+    return pltpu.make_async_remote_copy(
+        src_ref=source,
+        dst_ref=target,
+        send_sem=send_sem,
+        recv_sem=recv_sem,
+        device_id=place,
+        device_id_type=MESH,
+    )
+
+
+class Place:
+    def __init__(self, group):
+        self.me = lax.axis_index("expert")
+        self.shard = lax.axis_index("shard")
+        self.group = group
+        self.outer = group // INNER
+        self.local = lax.rem(self.me, group)
+        self.base = self.me - self.local
+        self.level = self.local // INNER
+        inner = lax.rem(self.local, INNER)
+        self.row_step = 2 - 4 * (inner // 2)
+        self.twin_step = 1 - 2 * lax.rem(inner, 2)
+        self.always = self.me >= 0
+        self.upper = self.level < self.outer - 1
+        self.lower = self.level > 0
+
+    def neighbours(self):
+        return [
+            (self.upper, {"expert": self.me + INNER}),
+            (self.lower, {"expert": self.me - INNER}),
+            (self.always, {"expert": self.me + self.row_step}),
+            (self.always, {"expert": self.me + self.twin_step}),
+        ]
+
+    def along(self, step):
+        below = (self.level >= step, self.local - step * INNER, self.upper, self.me + INNER, 0)
+        above = (self.level + step < self.outer, self.local + step * INNER, self.lower, self.me - INNER, 1)
+        return (below, above)
+
+
+def greet(peers):
+    barrier = pltpu.get_barrier_semaphore()
+    for there, peer in peers:
+        @pl.when(there)
+        def _():
+            pl.semaphore_signal(barrier, inc=1, device_id=peer, device_id_type=MESH)
+    pl.semaphore_wait(barrier, sum(there.astype(jnp.int32) for there, _ in peers))
+
+
+def gather_steps(place, own_ref, out_ref, copy_sem, send_sem, recv_sem, sender):
+    local = place.local
+    row, twin = local + place.row_step, local + place.twin_step
+
+    def push(kind, block, piece, target, source=None):
+        spot = out_ref.at[block, piece]
+        return remote(
+            spot if source is None else source.at[piece],
+            spot,
+            send_sem.at[kind, block, piece],
+            recv_sem.at[block, piece],
+            {"expert": target},
+        )
+
+    def arrive(there, block, piece):
+        @pl.when(there)
+        def _():
+            push(0, block, piece, place.me).wait_recv()
+
+    pieces = own_ref.shape[0]
+    row_at, twin_at = place.me + place.row_step, place.me + place.twin_step
+    keep = pltpu.make_async_copy(own_ref, out_ref.at[local], copy_sem)
+    keep.start()
+    for piece in range(pieces):
+        sender.start(place.upper, push(0, local, piece, place.me + INNER, own_ref))
+        sender.start(place.lower, push(1, local, piece, place.me - INNER, own_ref))
+        sender.start(place.always, push(2, local, piece, row_at, own_ref))
+        sender.start(place.always, push(3, local, piece, twin_at, own_ref))
+    yield
+    for step in range(1, place.outer + 1):
+        if step < place.outer:
+            for piece in range(pieces):
+                for there, block, onward, target, kind in place.along(step):
+                    arrive(there, block, piece)
+                    sender.start(there & onward, push(kind, block, piece, target))
+                    sender.start(there, push(2, block, piece, row_at))
+                    sender.start(there, push(3, block, piece, twin_at))
+        for piece in range(pieces):
+            for there, block, *_ in place.along(step - 1)[: 1 if step == 1 else 2]:
+                arrive(there, block + place.row_step, piece)
+                sender.start(there, push(3, block + place.row_step, piece, twin_at))
+        yield
+    for step in range(place.outer):
+        for piece in range(pieces):
+            for there, block, *_ in place.along(step)[: 1 if step == 0 else 2]:
+                arrive(there, block + place.twin_step, piece)
+                arrive(there, block + place.twin_step + place.row_step, piece)
+    keep.wait()
+    yield
+
+
+def add_into(target, first, *others):
+    rows = target.shape[0]
+    chunk = 32
+
+    def body(index, _):
+        at = pl.ds(pl.multiple_of(index * chunk, chunk), chunk)
+        total = first[at, :].astype(jnp.float32)
+        for other in others:
+            total = total + other[at, :].astype(jnp.float32)
+        target[at, :] = total.astype(target.dtype)
+        return 0
+
+    lax.fori_loop(0, rows // chunk, body, 0)
+
+
+def reduce_steps(place, part_ref, out_ref, scratch, sender):
+    (own_buf, twin_buf, row_buf, up_buf, down_buf, load_sem, twin_send, twin_recv, row_send, row_recv,
+     line_send, line_recv, out_buf, out_sem) = scratch
+    outer, local, level = place.outer, place.local, place.level
+    inner = lax.rem(local, INNER)
+    row_bit, core = inner // 2, lax.rem(inner, 2)
+    twin_at, row_at = {"expert": place.me + place.twin_step}, {"expert": place.me + place.row_step}
+    order = []
+    low, high = 0, outer - 1
+    while low <= high:
+        order.append(high)
+        if low != high:
+            order.append(low)
+        low, high = low + 1, high - 1
+
+    def slot(level_at, bit):
+        return level_at * 2 + bit
+
+    def block(level_at, bit, core_at):
+        return level_at * INNER + bit * 2 + core_at
+
+    other_bit, other_core = 1 - row_bit, 1 - core
+    loads, twins, rows = {}, {}, {}
+    for at in order:
+        for kind, bit in ((0, other_bit), (1, row_bit)):
+            where = slot(at, bit)
+            copy = remote(part_ref.at[block(at, bit, other_core)], twin_buf.at[where], twin_send.at[where],
+                          twin_recv.at[where], twin_at)
+            sender.start(place.always, copy)
+            load = pltpu.make_async_copy(part_ref.at[block(at, bit, core)], own_buf.at[where], load_sem.at[where])
+            load.start()
+            loads[at, kind] = load
+            twins[at, kind] = pltpu.make_async_remote_copy(
+                src_ref=part_ref.at[block(at, bit, other_core)], dst_ref=twin_buf.at[where],
+                send_sem=twin_send.at[where], recv_sem=twin_recv.at[where], device_id=twin_at, device_id_type=MESH)
+    yield
+    for at in order:
+        for kind, bit in ((0, other_bit), (1, row_bit)):
+            where = slot(at, bit)
+            loads[at, kind].wait()
+            twins[at, kind].wait_recv()
+            add_into(own_buf.at[where], own_buf.at[where], twin_buf.at[where])
+            if kind == 0:
+                copy = remote(own_buf.at[where], row_buf.at[at], row_send.at[at], row_recv.at[at], row_at)
+                sender.start(place.always, copy)
+                rows[at] = copy
+        yield
+    for at in order:
+        mine = own_buf.at[slot(at, row_bit)]
+        rows[at].wait_recv()
+
+        @pl.when(level == at)
+        def _():
+            add_into(mine, mine, row_buf.at[at])
+
+        up = remote(mine, up_buf.at[at], line_send.at[0, at], line_recv.at[0, at], {"expert": place.me + INNER})
+        down = remote(mine, down_buf.at[at], line_send.at[1, at], line_recv.at[1, at], {"expert": place.me - INNER})
+        for there, first, copy, buf in ((level < at, level == 0, up, up_buf), (level > at, level == outer - 1, down, down_buf)):
+            @pl.when(there & first)
+            def _():
+                add_into(mine, mine, row_buf.at[at])
+
+            @pl.when(there & ~first)
+            def _():
+                copy.wait_recv()
+                add_into(mine, mine, row_buf.at[at], buf.at[at])
+
+            sender.start(there, copy)
+        yield
+    for at in order:
+        @pl.when(level == at)
+        def _():
+            mine = own_buf.at[slot(at, row_bit)]
+            up = remote(mine, up_buf.at[at], line_send.at[0, at], line_recv.at[0, at], {"expert": place.me + INNER})
+            down = remote(mine, down_buf.at[at], line_send.at[1, at], line_recv.at[1, at], {"expert": place.me - INNER})
+            if at > 0:
+                up.wait_recv()
+            if at < outer - 1:
+                down.wait_recv()
+            if 0 < at < outer - 1:
+                add_into(out_buf, mine, up_buf.at[at], down_buf.at[at])
+            else:
+                add_into(out_buf, mine, up_buf.at[at] if at else down_buf.at[at])
+    done = pltpu.make_async_copy(out_buf, out_ref, out_sem)
+    done.start()
+    done.wait()
+    yield
+
+
+def reduce_scratch(group, rows, columns):
+    outer = group // INNER
+    bf = jnp.bfloat16
+    return [
+        pltpu.VMEM((2 * outer, rows, columns), bf),
+        pltpu.VMEM((2 * outer, rows, columns), bf),
+        pltpu.VMEM((outer, rows, columns), bf),
+        pltpu.VMEM((outer, rows, columns), bf),
+        pltpu.VMEM((outer, rows, columns), bf),
+        pltpu.SemaphoreType.DMA((2 * outer,)),
+        pltpu.SemaphoreType.DMA((2 * outer,)),
+        pltpu.SemaphoreType.DMA((2 * outer,)),
+        pltpu.SemaphoreType.DMA((outer,)),
+        pltpu.SemaphoreType.DMA((outer,)),
+        pltpu.SemaphoreType.DMA((2, outer)),
+        pltpu.SemaphoreType.DMA((2, outer)),
+        pltpu.VMEM((rows, columns), jnp.float32),
+        pltpu.SemaphoreType.DMA(()),
+    ]
+
+
+class HeadRows:
+    def __init__(self, started, received):
+        self.started, self.received = started, received
+
+    def wait(self):
+        for there, local, copy, keep in self.started:
+            @pl.when(there)
+            def _():
+                copy.wait_send()
+
+            @pl.when(local)
+            def _():
+                keep.wait()
+        for there, copy in self.received:
+            @pl.when(there)
+            def _():
+                copy.wait_recv()
+
+
+def head_rows(place, plane, shards, own_ref, out_ref, copy_sem, send_sem, recv_sem):
+    count = own_ref.shape[0]
+    number = place.shard * plane + place.me
+    sequences = plane // place.group
+    mine = place.shard * sequences + place.me // place.group
+    started, received = [], []
+    for index in range(count):
+        target = place.local * count + index
+        peer = {"shard": target // plane, "expert": lax.rem(target, plane)}
+        copy = remote(own_ref.at[index], out_ref.at[mine], send_sem.at[index], recv_sem.at[mine], peer)
+        keep = pltpu.make_async_copy(own_ref.at[index], out_ref.at[mine], copy_sem)
+
+        @pl.when(target != number)
+        def _():
+            copy.start()
+
+        @pl.when(target == number)
+        def _():
+            keep.start()
+
+        started.append((target != number, target == number, copy, keep))
+    for shard in range(shards):
+        for sequence in range(sequences):
+            source = shard * plane + sequence * place.group + number // count
+            slot = shard * sequences + sequence
+            peer = {"shard": source // plane, "expert": lax.rem(source, plane)}
+            copy = remote(own_ref.at[0], out_ref.at[slot], send_sem.at[0], recv_sem.at[slot], peer)
+            received.append((source != number, copy))
+    return HeadRows(started, received), []
+
+
+def bundle_kernel(group, shards, kinds, *refs):
+    count = len(kinds)
+    ins, outs, rest = refs[:count], refs[count : 2 * count], refs[2 * count :]
+    place = Place(group)
+    plane = lax.axis_size("expert")
+    peers = []
+    if "gather" in kinds or "reduce" in kinds:
+        peers += place.neighbours()
+    members = [{"expert": place.base + lax.rem(place.local + step, group)} for step in range(1, group)]
+    if "trade" in kinds:
+        peers = [(place.always, member) for member in members]
+    across = [{"shard": lax.rem(place.shard + step, shards)} for step in range(1, shards)]
+    if "swap" in kinds or "share" in kinds:
+        peers += [(place.always, peer) for peer in across]
+    everyone = []
+    if "owners" in kinds or "rows" in kinds:
+        total = shards * plane
+        number = place.shard * plane + place.me
+        for step in range(1, total):
+            target = lax.rem(number + step, total)
+            everyone.append((target, {"shard": target // plane, "expert": lax.rem(target, plane)}))
+        peers = [(place.always, peer) for _, peer in everyone]
+    greet(peers)
+    sender = Sender()
+    runs, waits = [], []
+    for kind, own, out in zip(kinds, ins, outs):
+        if kind == "gather":
+            copy_sem, send_sem, recv_sem, *rest = rest
+            runs.append(gather_steps(place, own, out, copy_sem, send_sem, recv_sem, sender))
+        elif kind == "reduce":
+            scratch, rest = rest[:14], rest[14:]
+            runs.append(reduce_steps(place, own, out, scratch, sender))
+        else:
+            copy_sem, send_sem, recv_sem, *rest = rest
+            if kind == "swap":
+                mine, source = place.shard, lambda target: own
+                targets = [(lax.rem(place.shard + step, shards), peer) for step, peer in enumerate(across, 1)]
+            elif kind == "share":
+                mine, source = place.shard, lambda target: own.at[target]
+                targets = [(lax.rem(place.shard + step, shards), peer) for step, peer in enumerate(across, 1)]
+            elif kind == "trade":
+                mine, source = place.local, lambda target: own.at[target]
+                targets = [(lax.rem(place.local + step, group), peer) for step, peer in enumerate(members, 1)]
+            elif kind == "owners":
+                mine, source = place.shard * plane + place.me, lambda target: own.at[target]
+                targets = everyone
+            else:
+                waits.append(head_rows(place, plane, shards, own, out, copy_sem, send_sem, recv_sem))
+                continue
+            keep = pltpu.make_async_copy(source(mine), out.at[mine], copy_sem)
+            keep.start()
+            total = len(targets) + 1
+            copies = []
+            for step, (target, peer) in enumerate(targets, 1):
+                copy = remote(source(target), out.at[mine], send_sem.at[step], recv_sem.at[step], peer)
+                copy.start()
+                copies.append(copy)
+            waits.append((keep, copies))
+    while runs:
+        runs = [run for run in runs if next(run, "end") != "end"]
+    for keep, copies in waits:
+        keep.wait()
+        for copy in copies:
+            copy.wait()
+    sender.finish()
+
+
+def bundle(number, group, shards, transfers, limit=48 * 2**20):
+    kinds, arrays, shapes, scratch = [], [], [], []
+    members = shards * lax.axis_size("expert")
+    for kind, array in transfers:
+        kinds.append(kind)
+        sems = [pltpu.SemaphoreType.DMA(())]
+        if kind == "gather":
+            pieces = PIECES if array.shape[0] % (16 * PIECES) == 0 else 1
+            array = array.reshape((pieces, array.shape[0] // pieces) + array.shape[1:])
+            shape = (group,) + array.shape
+            sems += [pltpu.SemaphoreType.DMA((4, group, pieces)), pltpu.SemaphoreType.DMA((group, pieces))]
+        elif kind == "reduce":
+            shape = array.shape[1:]
+            sems = reduce_scratch(group, *shape)
+        else:
+            total = {"swap": shards, "share": shards, "trade": group, "owners": members}.get(kind)
+            shape = ((total,) + array.shape) if kind == "swap" else array.shape
+            if kind == "rows":
+                total = max(array.shape[0], members // group)
+                shape = (members // group,) + array.shape[1:]
+            sems += [pltpu.SemaphoreType.DMA((total,)), pltpu.SemaphoreType.DMA((total,))]
+        arrays.append(array)
+        shapes.append(jax.ShapeDtypeStruct(shape, jnp.float32 if kind == "reduce" else array.dtype))
+        scratch += sems
+    outs = pl.pallas_call(
+        functools.partial(bundle_kernel, group, shards, tuple(kinds)),
+        out_shape=shapes,
+        in_specs=[pl.BlockSpec(memory_space=pl.ANY)] * len(arrays),
+        out_specs=[pl.BlockSpec(memory_space=pl.ANY)] * len(arrays),
+        scratch_shapes=scratch,
+        compiler_params=pltpu.CompilerParams(
+            collective_id=number, has_side_effects=True, vmem_limit_bytes=limit
+        ),
+        name="bundle_" + "_".join(kinds[:2]),
+    )(*arrays)
+    done = []
+    for (kind, array), out in zip(transfers, outs):
+        if kind == "gather":
+            out = out.reshape((group,) + array.shape)
+        done.append(out)
+    return done
+
+
+def tie(value, *awaited):
+    return lax.optimization_barrier((value,) + awaited)
+
+
+def other_blocks(pieces):
+    count = lax.axis_size("shard")
+    me = lax.axis_index("shard")
+    return [
+        lax.dynamic_index_in_dim(pieces, (me + step) % count, 0, keepdims=False)
+        for step in range(1, count)
+    ]
+
+
+def other_rows(pieces):
+    gathered = lax.all_gather(jnp.stack(other_blocks(pieces)), "expert", axis=1, tiled=True)
+    return [gathered[step] for step in range(gathered.shape[0])]
+
+
+def split_matmul(values, own, others):
+    count = len(others) + 1
+    me = lax.axis_index("shard")
+    parts = values.reshape(values.shape[0], count, -1)
+    total = 0.0
+    for step, block in enumerate([own] + others):
+        part = lax.dynamic_index_in_dim(parts, (me + step) % count, 1, keepdims=False)
+        total = total + matmul(part, block)
+    return total
+
+
+def split_matmul_nt(values, own, others):
+    count = len(others) + 1
+    me = lax.axis_index("shard")
+    whole = jnp.zeros((values.shape[0], count, own.shape[0]), jnp.float32)
+    for step, block in enumerate([own] + others):
+        whole = lax.dynamic_update_index_in_dim(
+            whole, matmul_nt(values, block), (me + step) % count, 1
+        )
+    return whole.reshape(values.shape[0], -1)
+
+
+def padded_rows(block):
+    return jnp.pad(block, ((0, -block.shape[0] % 16), (0, 0)))
 
 
 def shard_ring(block):
@@ -114,16 +570,6 @@
         )
         total = total + moved.astype(jnp.float32)
     return total
-
-
-def shared_rows_plane(block):
-    plane = lax.axis_size("expert")
-    count = lax.axis_size("shard")
-    rows = block.shape[0] // plane
-    mine = lax.dynamic_slice_in_dim(block, lax.axis_index("expert") * rows, rows, 0)
-    pieces = shard_ring(mine)
-    gathered = lax.all_gather(pieces, "expert", axis=1, tiled=False)
-    return gathered.reshape((count * block.shape[0],) + block.shape[1:])
 
 
 def on_device(
@@ -164,15 +610,30 @@
     def own_rows(values):
         return lax.dynamic_slice_in_dim(values, own_at, local_rows, 0)
 
-    query_head = shard_rows(
-        lax.dynamic_slice_in_dim(query_weight, head_at * head_dim, head_dim, 1)
-    )
-    full_down = shard_rows(latent_down)
-    up_head = shard_rows(
-        lax.dynamic_slice_in_dim(latent_up, head_at * (QK_NOPE + V_HEAD), QK_NOPE + V_HEAD, 1)
-    )
-    full_out = shared_rows_plane(output_weight)
-    full_query = shared_rows_plane(query_weight)
+    piece_rows = output_weight.shape[0] // plane
+    tokens_all, query_pieces, down_pieces, up_pieces, out_pieces = bundle(
+        1,
+        SEQ_DEVICES,
+        shards,
+        [
+            ("gather", tokens),
+            ("swap", lax.dynamic_slice_in_dim(query_weight, head_at * head_dim, head_dim, 1)),
+            ("swap", latent_down.T),
+            (
+                "swap",
+                lax.dynamic_slice_in_dim(
+                    latent_up, head_at * (QK_NOPE + V_HEAD), QK_NOPE + V_HEAD, 1
+                ),
+            ),
+            ("swap", lax.dynamic_slice_in_dim(output_weight, plane_at * piece_rows, piece_rows, 0)),
+        ],
+    )
+    query_head = query_pieces.reshape(width, head_dim)
+    full_down = down_pieces.transpose(0, 2, 1).reshape(width, KV_RANK + QK_ROPE)
+    up_head = up_pieces.reshape(KV_RANK, QK_NOPE + V_HEAD)
+    other_out = other_rows(out_pieces)
+    cotangent_late = tie(cotangent, other_out[0])[0]
+    all_grads = lax.all_gather(cotangent_late, "expert", axis=0, tiled=True)
     units = shared_down.shape[0] // plane
     gate_columns, up_columns = (
         jnp.concatenate(
@@ -186,16 +647,9 @@
         )
         for weight in (shared_gate, shared_up)
     )
-    gate_shared = shard_rows(gate_columns)
-    up_shared = shard_rows(up_columns)
-    down_shared = shard_rows(lax.dynamic_slice_in_dim(shared_down, plane_at * units, units, 0))
-    gate_single = shard_rows(expert_gate[0])
-    up_single = shard_rows(expert_up[0])
-    down_single = shard_rows(expert_down[0])
-
-    all_tokens = lax.all_gather(
-        tokens, "expert", axis=0, tiled=True, axis_index_groups=groups
-    ).astype(jnp.float32)
+    down_units = lax.dynamic_slice_in_dim(shared_down, plane_at * units, units, 0)
+
+    all_tokens = tokens_all.reshape(SEQ, width).astype(jnp.float32)
     normed_one = norm_scale(all_tokens, first_gain).astype(jnp.bfloat16)
     positions = jnp.arange(SEQ, dtype=jnp.int32)
     cosine_part, sine_part = rotary_tables(positions, QK_ROPE)
@@ -231,23 +685,44 @@
     log_total = top_score + jnp.log(expo_total)
     probs = expo / expo_total
     head_out = (matmul(probs.astype(jnp.bfloat16), value) * real[:, None]).astype(jnp.bfloat16)
-    heads_out = lax.all_to_all(
-        head_out.reshape(SEQ_DEVICES, local_rows, V_HEAD),
-        "expert",
-        split_axis=0,
-        concat_axis=0,
-        tiled=True,
-        axis_index_groups=groups,
+    gate_single = shard_rows(expert_gate[0])
+    head_out, gate_single = tie(head_out, gate_single)
+    heads_out, query_rows = bundle(
+        2,
+        SEQ_DEVICES,
+        shards,
+        [
+            ("trade", head_out.reshape(SEQ_DEVICES, local_rows, V_HEAD)),
+            ("swap", lax.dynamic_slice_in_dim(query_weight, plane_at * piece_rows, piece_rows, 0)),
+        ],
     )
     heads_out = heads_out.transpose(1, 0, 2).reshape(local_rows, HEADS * V_HEAD)
 
     hidden_rows = tokens.astype(jnp.float32)
-    middle = hidden_rows + matmul(heads_out, full_out)
+    middle = hidden_rows + split_matmul(heads_out, output_weight, other_out)
     second_normed = norm_scale(middle, second_gain).astype(jnp.bfloat16)
 
-    all_normed = lax.all_gather(second_normed, "expert", axis=0, tiled=True)
-    all_grads = lax.all_gather(cotangent, "expert", axis=0, tiled=True)
-    all_routes = lax.all_gather(routes, "expert", axis=0, tiled=True)
+    all_normed, all_routes, up_single, gate_shared, up_shared, down_shared = bundle(
+        3,
+        plane,
+        shards,
+        [
+            ("gather", second_normed),
+            ("gather", jnp.pad(routes.T, ((0, 2), (0, 0)))),
+            ("swap", expert_up[0]),
+            ("swap", gate_columns.T),
+            ("swap", up_columns.T),
+            ("swap", padded_rows(down_units)),
+        ],
+    )
+    all_normed = all_normed.reshape(-1, width)
+    all_routes = all_routes[:, :TOP].transpose(0, 2, 1).reshape(-1, TOP)
+    up_single = up_single.reshape(width, -1)
+    gate_shared = gate_shared.transpose(0, 2, 1).reshape(width, -1)
+    up_shared = up_shared.transpose(0, 2, 1).reshape(width, -1)
+    down_shared = down_shared[:, :units].reshape(-1, width)
+    down_single = shard_rows(expert_down[0])
+    other_query = other_rows(tie(query_rows, all_grads)[0])
     plane_rows = plane * local_rows
     logits = matmul(all_normed, router_weight)
     expert_ids = jnp.arange(plane, dtype=jnp.int32)
@@ -315,26 +790,43 @@
         + matmul_nt(shared_gate_back, gate_shared)
         + matmul_nt(shared_up_back, up_shared)
     ).astype(jnp.bfloat16)
-    token_gate_grad = jnp.sum(
-        jnp.where(picks, slot_gate_grad[:, :, None], 0.0), axis=1
-    ).reshape(plane_rows, 1)
-    gate_high = token_gate_grad.astype(jnp.bfloat16)
-    gate_low = (token_gate_grad - gate_high.astype(jnp.float32)).astype(jnp.bfloat16)
-    at_me = (expert_ids == plane_at).astype(jnp.bfloat16)[None, :]
-    back = lax.psum_scatter(
-        jnp.concatenate([normed_part, gate_high * at_me, gate_low * at_me], axis=1),
-        "expert",
-        scatter_dimension=0,
-        tiled=True,
-    ).astype(jnp.float32)
+    token_gate_grad = jnp.sum(jnp.where(picks, slot_gate_grad[:, :, None], 0.0), axis=1)
+    expert_down_term = matmul_tn(hidden, slot_grad)
+    back, gate_dense, down_blocks = bundle(
+        4,
+        plane,
+        shards,
+        [
+            ("reduce", normed_part.reshape(plane, local_rows, width)),
+            (
+                "trade",
+                jnp.broadcast_to(
+                    token_gate_grad.reshape(plane, 1, local_rows), (plane, 8, local_rows)
+                ),
+            ),
+            ("share", expert_down_term.astype(jnp.bfloat16).reshape(shards, -1, width)),
+        ],
+    )
+    gate_dense = gate_dense[:, 0].T
+
+    def sum_shards(term, blocks):
+        own = lax.dynamic_index_in_dim(
+            term.reshape((shards, -1) + term.shape[1:]), shard_at, 0, keepdims=False
+        )
+        for step in range(1, shards):
+            own = own + lax.dynamic_index_in_dim(
+                blocks, (shard_at + step) % shards, 0, keepdims=False
+            ).astype(jnp.float32)
+        return own
+
+    expert_down_grad = sum_shards(expert_down_term, down_blocks)[None]
     output_part = (
         to_tokens((slot_gate * expert_out).astype(jnp.bfloat16))
         + matmul(shared_hidden, down_shared)
     ).astype(jnp.bfloat16)
+    output_part = tie(output_part, back)[0]
     output_sum = lax.psum_scatter(output_part, "expert", scatter_dimension=0, tiled=True)
     activations = (middle + output_sum.astype(jnp.float32)).astype(jnp.bfloat16)
-
-    expert_down_grad = shard_sum(matmul_tn(hidden, slot_grad))[None]
     expert_gate_grad = shard_sum(matmul_tn(slot_rows, gate_pre_grad))[None]
     expert_up_grad = shard_sum(matmul_tn(slot_rows, up_pre_grad))[None]
     shared_down_grad = shard_sum(matmul_tn(shared_hidden, all_grads))
@@ -364,7 +856,6 @@
     shared_up_grad = shared_moved[1]
 
     grad_out = cotangent.astype(jnp.float32)
-    gate_dense = back[:, width : width + plane] + back[:, width + plane :]
     own_start = plane_at * local_rows
     own_gates = lax.dynamic_slice_in_dim(gate_values, own_start, local_rows, 0)
     own_choose = routes[:, :, None] == expert_ids[None, None, :]
@@ -380,7 +871,7 @@
         precision=HIGH,
         preferred_element_type=jnp.float32,
     )
-    normed_grad = back[:, :width] + lax.dot_general(
+    normed_grad = back + lax.dot_general(
         logit_grad,
         router_weight.astype(jnp.float32),
         (((1,), (1,)), ((), ())),
@@ -400,17 +891,13 @@
     router_weight_grad = small_sums[:, :plane]
     second_gain_grad = small_sums[:, plane]
 
-    output_weight_grad = lax.psum_scatter(
-        matmul_tn(heads_out, middle_low).astype(jnp.bfloat16),
-        everyone,
-        scatter_dimension=0,
-        tiled=True,
-    ).astype(jnp.float32)
-    heads_grad = (matmul_nt(middle_low, full_out)).astype(jnp.bfloat16)
+    heads_grad = split_matmul_nt(middle_low, output_weight, other_out).astype(jnp.bfloat16)
     heads_grad = heads_grad.reshape(local_rows, HEADS, V_HEAD).transpose(1, 0, 2)
-    head_grad = lax.all_to_all(
-        heads_grad, "expert", split_axis=0, concat_axis=0, tiled=True, axis_index_groups=groups
-    ).reshape(SEQ, V_HEAD)
+    (head_grad,) = bundle(5, SEQ_DEVICES, shards, [("trade", heads_grad)])
+    head_grad = head_grad.reshape(SEQ, V_HEAD)
+    all_middle = lax.all_gather(
+        tie(middle_low, head_grad)[0], "expert", axis=0, tiled=True, axis_index_groups=groups
+    )
     head_grad = (head_grad.astype(jnp.float32) * real[:, None]).astype(jnp.bfloat16)
     again = jnp.exp(scores_of() - log_total)
     prob_grad = matmul_nt(head_grad, value)
@@ -429,23 +916,24 @@
     ).astype(jnp.bfloat16)
     pair_grad = jnp.concatenate([key_nope_grad, value_grad], axis=1).astype(jnp.bfloat16)
     latent_up_term = matmul_tn(key_latent, pair_grad)
-    latent_up_grad = by_head(to_owners(latent_up_term))
-    key_grad_part = jnp.concatenate([matmul_nt(pair_grad, up_head), key_rope_grad], axis=1)
-    own_key_grad = lax.psum_scatter(
-        key_grad_part.astype(jnp.bfloat16),
-        "expert",
-        scatter_dimension=0,
-        tiled=True,
-        axis_index_groups=groups,
-    ).astype(jnp.float32)
-    own_query_grad = lax.all_to_all(
-        query_grad.reshape(SEQ_DEVICES, local_rows, head_dim),
-        "expert",
-        split_axis=0,
-        concat_axis=0,
-        tiled=True,
-        axis_index_groups=groups,
-    )
+    key_grad_part = jnp.concatenate(
+        [
+            matmul_nt(pair_grad, up_head),
+            key_rope_grad,
+            jnp.zeros((SEQ, -(KV_RANK + QK_ROPE) % 128), jnp.float32),
+        ],
+        axis=1,
+    ).astype(jnp.bfloat16)
+    own_key_grad, own_query_grad = bundle(
+        6,
+        SEQ_DEVICES,
+        shards,
+        [
+            ("reduce", key_grad_part.reshape(SEQ_DEVICES, local_rows, -1)),
+            ("trade", query_grad.reshape(SEQ_DEVICES, local_rows, head_dim)),
+        ],
+    )
+    own_key_grad = own_key_grad[:, : KV_RANK + QK_ROPE]
     own_query_grad = own_query_grad.transpose(1, 0, 2).reshape(local_rows, HEADS * head_dim)
     own_compressed = own_rows(compressed)
     unused_latent, latent_back = jax.vjp(norm_scale, own_compressed[:, :KV_RANK], latent_gain)
@@ -455,36 +943,63 @@
     )
     compressed_grad = jnp.concatenate([latent_in_grad, rope_in_grad], axis=1).astype(jnp.bfloat16)
     down_columns = (KV_RANK + QK_ROPE) // SEQ_DEVICES
-    column_grad = lax.all_to_all(
-        compressed_grad.reshape(local_rows, SEQ_DEVICES, down_columns).transpose(1, 0, 2),
-        "expert",
-        split_axis=0,
-        concat_axis=0,
-        tiled=True,
-        axis_index_groups=groups,
-    ).reshape(SEQ, down_columns)
-    normed_one_grad = matmul_nt(own_query_grad, full_query) + matmul_nt(
-        compressed_grad, full_down
-    )
+    def owner_blocks(term):
+        return term.astype(jnp.bfloat16).reshape(all_devices, -1, term.shape[1])
+
+    def owner_sum(moved):
+        blocks = moved.reshape((shards, plane) + moved.shape[1:]).astype(jnp.float32)
+        return by_head(jnp.sum(blocks, axis=0))
+
+    query_term = matmul_tn(normed_one, query_grad)
+    column_grad, query_moved, up_moved = bundle(
+        7,
+        SEQ_DEVICES,
+        shards,
+        [
+            (
+                "trade",
+                compressed_grad.reshape(local_rows, SEQ_DEVICES, down_columns).transpose(1, 0, 2),
+            ),
+            ("owners", owner_blocks(query_term)),
+            ("owners", owner_blocks(latent_up_term)),
+        ],
+    )
+    column_grad = column_grad.reshape(SEQ, down_columns)
+    query_weight_grad = owner_sum(query_moved)
+    latent_up_grad = owner_sum(up_moved)
+    normed_one_grad = split_matmul_nt(
+        own_query_grad, query_weight, other_query
+    ) + matmul_nt(compressed_grad, full_down)
     unused_one, first_back = jax.vjp(norm_scale, hidden_rows, first_gain)
     input_norm_grad, first_term = first_back(normed_one_grad)
     input_grad = middle_grad + input_norm_grad
-    weight_term = matmul_tn(normed_one, jnp.concatenate([query_grad, column_grad], axis=1))
-    weight_moved = to_owners(weight_term)
-    query_weight_grad = by_head(weight_moved[:, :, :head_dim])
-    latent_down_grad = by_head(weight_moved[:, :, head_dim:])
-    gain_sums = lax.psum_scatter(
-        jnp.concatenate(
-            [
-                first_term.reshape(all_devices, -1),
-                latent_gain_term.reshape(all_devices, -1),
-            ],
-            axis=1,
-        ),
-        everyone,
-        scatter_dimension=0,
-        tiled=True,
-    )[0]
+    down_term = matmul_tn(normed_one, column_grad)
+    out_term = matmul_tn(head_out, all_middle.reshape(SEQ, width)).astype(jnp.bfloat16)
+    gain_terms = jnp.concatenate(
+        [
+            first_term.reshape(all_devices, -1),
+            latent_gain_term.reshape(all_devices, -1),
+        ],
+        axis=1,
+    )
+    gain_columns = gain_terms.shape[1]
+    gain_terms = jnp.broadcast_to(
+        jnp.pad(gain_terms, ((0, 0), (0, -gain_columns % 128)))[:, None],
+        (all_devices, 8, gain_columns + -gain_columns % 128),
+    )
+    down_moved, gain_moved, out_moved = bundle(
+        8,
+        SEQ_DEVICES,
+        shards,
+        [
+            ("owners", owner_blocks(down_term)),
+            ("owners", gain_terms),
+            ("rows", out_term.reshape(-1, width // all_devices, width)),
+        ],
+    )
+    latent_down_grad = owner_sum(down_moved)
+    output_weight_grad = jnp.sum(out_moved.astype(jnp.float32), axis=0)
+    gain_sums = jnp.sum(gain_moved[:, 0, :gain_columns], axis=0)
     first_gain_grad = gain_sums[: width // all_devices]
     latent_gain_grad = gain_sums[width // all_devices :]
     return (

time: 1380 us -> 1020 us (0.74)
  waiting for transfers between devices: 608 us -> 52.5 us
  Pallas kernels: 0 us -> 414 us
  local copies, waits for them, and re-layouts: 216 us -> 109 us
  blocking collectives: 59.1 us -> 0 us
  starting transfers between devices: 68.1 us -> 9.31 us
  other arithmetic: 83 us -> 104 us
    pallas_call x0 -> x8, Pallas kernels: none -> 414 us  [bundle(): pl.pallas_call(functools.partial(bundle_kernel, group, shards, tuple(kind...]
    ppermute x4 -> x3, waiting for transfers between devices: 183 us -> 0.01 us  [shard_sum(): lax.ppermute(outgoing.astype(jnp.bfloat16), 'shard', [(source, (source +...]
    ppermute x11 -> x2, waiting for transfers between devices: 188 us -> 27.5 us  [shard_ring(): lax.ppermute(block, 'shard', [(source, (source + step) % count) for sourc...]
    reduce_scatter x1, waiting for transfers between devices: 104 us -> 0.02 us  [on_device(): lax.psum_scatter(output_part, 'expert', scatter_dimension=0, tiled=True)]
    reduce_scatter x2 -> x0, waiting for transfers between devices: 80.7 us -> none  [the longest x1 80.7 us: on_device(): lax.psum_scatter(jnp.concatenate([normed_part, gate_high * at_me, gate_lo...]
    all_to_all x4 -> x0, waiting for transfers between devices: 50.3 us -> none  [the longest x1 26.1 us: on_device(): lax.all_to_all(head_out.reshape(SEQ_DEVICES, local_rows, V_HEAD), 'expert...]
    dynamic_update_slice x9 -> x2, local copies, waits for them, and re-layouts: 50.1 us -> 0.85 us  [shard_ring(): whole = lax.dynamic_update_index_in_dim(whole, block, me, 0)]
    dynamic_update_slice x10 -> x2, local copies, waits for them, and re-layouts: 52.3 us -> 6.02 us  [shard_ring(): lax.dynamic_update_index_in_dim(whole, moved, (me - step) % count, 0)]
  transfers between devices with their start and end apart: 32 -> 12, of which waited for: 12 -> 2; matrix products, arithmetic and copies ran while one was open for 33% -> 37% of each run, Pallas kernels for 0% -> 24%
where the time goes in v2:
time: 1020 us; the launch traced here: 1010 us
  Pallas kernels  414 us (41%)
  matrix products  309 us (30%)
  local copies, waits for them, and re-layouts  109 us (11%)
  other arithmetic  104 us (10%)
  waiting for transfers between devices  52.5 us (5%)
  between operations  16.5 us (2%)
    pallas_call x8, Pallas kernels, bundle(): pl.pallas_call(functools.partial(bundle_kernel, group, shards, tuple(kind...  414 us
    dot_general x15, matrix products, matmul_nt(): lax.dot_general(left, right, (((1,), (1,)), ((), ())), preferred_element_...  113 us
    dot_general x15, matrix products, matmul(): return jnp.dot(left, right, preferred_element_type=jnp.float32)  94.5 us
    dot_general x13, matrix products, matmul_tn(): lax.dot_general(left, right, (((0,), (0,)), ((), ())), preferred_element_...  70.9 us
    unnamed x280, local copies, waits for them, and re-layouts  38.2 us
    ppermute x2, waiting for transfers between devices, shard_ring(): lax.ppermute(block, 'shard', [(source, (source + step) % count) for sourc...  27.5 us
    all_gather x1, waiting for transfers between devices, on_device(): lax.all_gather(tie(middle_low, head_grad)[0], 'expert', axis=0, tiled=Tru...  24.9 us
  transfers between devices with their start and end apart: 12, of which 2 were waited for; matrix products, arithmetic and copies ran while one was open for 37% of the time, Pallas kernels for 24%

profile of v2, /device:TPU:9, one launch (start us, length us, event | category | flops | bytes accessed | tf_op | source)
XLA Modules:
  0.0 1015.0 jit_solution(14043828552995357948)
XLA Ops:
  13.5 52.6 %bundle_gather_swap.1 = (bf16[16,2,64,2048]{3,2,1,0:T(8,128)(2,1)}, bf16[2,1024,192]{2,1,0:T(8,128)(2,1)S(1)}, bf16[2,576,1024]{2,1,0:T(8,128)(2,1)}, bf16[2,256...) custom-call(bf16[2,64,2048]{2,1,0:T(8,128)(2,1)S(1)} %bitcast.283, ...), custom_call_target="tpu_custom_call" | custom-call | tf_op jit(solution)/shard_map/bundle_gather_swap/pallas_call | solution.py:478
  70.6 6.0 multiply_reduce_fusion.1
  76.6 8.7 multiply_convert_fusion.1
  85.3 7.8 fusion.141
  99.6 6.3 fusion.140
  113.7 4.1 convolution_convert_fusion.3
  117.8 6.7 fusion.57
  128.2 11.9 %fusion.138 = (f32[2048]{0:T(1024)S(1)}, f32[2048,2048]{0,1:T(8,128)}) fusion(f32[2048,2048]{0,1:T(8,128)S(1)} %fusion.114, f32[2048,192]{0,1:T(8,128)} %copy-done.71, bf16[2048,256]{1,0:T(8,128)(2,1)} %convolution_convert_fusion.3, s32[2048]{0:T(1024)S(1)} %iota_add_fusion, s32[2048]{0:T(1024)S(1)} %convert_reduce_fusion.5), kind=kOutput, calls=%fused_computation.270 | convolution fusion | flops 1111488512 | bytes 34635776 | tf_op jit(solution)/shard_map/dot_general | solution.py:40
  147.8 9.3 fusion.7
  158.1 7.5 fusion.30
  165.7 27.5 %collective-permute-done = bf16[1024,1408]{1,0:T(8,128)(2,1)} collective-permute-done((bf16[1024,1408]{1,0:T(8,128)(2,1)}, bf16[1024,1408]{1,0:T(8,128)(2,1)}, u32[]{:S(2)}, u32[]{:S(2)}) %collective-permute-start) | collective-permute-done | bytes 2883616 | tf_op jit(solution)/shard_map/ppermute | solution.py:547
  195.5 15.4 %bundle_trade_swap.1 = (bf16[16,128,128]{2,1,0:T(8,128)(2,1)S(1)}, bf16[2,64,3072]{2,1,0:T(8,128)(2,1)S(1)}) custom-call(bf16[16,128,128]{2,1,0:T(8,128)(2,1)S(1)} %bitcast.287, bf16[64,3072]{1,0:T(8,128)(2,1)S(1)} %constant_dynamic-slice_fusion.9.refs_1_), custom_call_target="tpu_custom_call" | custom-call | tf_op jit(solution)/shard_map/bundle_trade_swap/pallas_call | solution.py:478
  215.9 3.8 bitcast_dynamic-update-slice_fusion
  223.8 92.7 %bundle_gather_gather.1 = (bf16[16,2,64,2048]{3,2,1,0:T(8,128)(2,1)}, s32[16,1,8,128]{3,2,1,0:T(8,128)S(1)}, bf16[2,1024,1408]{2,1,0:T(8,128)(2,1)}, bf16[2,176,...) custom-call(bf16[2,64,2048]{2,1,0:T(8,128)(2,1)S(1)} %bitcast.286, ...), custom_call_target="tpu_custom_call" | custom-call | tf_op jit(solution)/shard_map/bundle_gather_gather/pallas_call | solution.py:478
  317.4 5.7 fusion.142
  325.8 4.9 convolution_convert_fusion.2
  331.9 4.1 fusion.145
  335.9 4.0 fusion.144
  340.0 6.8 fusion.143
  349.3 9.1 multiply_convert_fusion.4
  358.4 4.8 convolution_convert_fusion.1
  363.2 12.6 %fusion.10 = (f32[1024]{0:T(1024)S(1)}, bf16[1024,2048]{1,0:T(8,128)(2,1)}) fusion(bf16[16,64,2048]{2,1,0:T(8,128)(2,1)S(1)} %convolution_convert_fusion.1, bf16[1024,1408]{1,0:T(8,128)(2,1)S(1)} %copy-done.110, bf16[1408,2048]{1,0:T(8,128)(2,1)} %bitcast.337), kind=kOutput, calls=%fused_computation.25 | convolution fusion | flops 5916064768 | bytes 17043456 | tf_op jit(solution)/shard_map/dot_general | solution.py:30
  379.6 14.5 %multiply_convert_fusion.2 = (bf16[1024,1408]{1,0:T(8,128)(2,1)}, bf16[1024,1408]{1,0:T(8,128)(2,1)}) fusion(f32[1024,1408]{1,0:T(8,128)} %copy-done.112, f32[1024,1408]{1,0:T(8,128)} %get-tuple-element.222, bf16[1024,2048]{1,0:T(8,128)(2,1)S(1)} %bitcast.347, bf16[1408,2048]{1,0:T(8,128)(2,1)} %bitcast.338), kind=kOutput, calls=%fused_computation.43 | convolution fusion | flops 5924323328 | bytes 27262976 | tf_op jit(solution)/shard_map/dot_general | solution.py:40
  394.1 10.6 %fusion.146 = f32[1024,2048]{1,0:T(8,128)} fusion(bf16[1024,1408]{1,0:T(8,128)(2,1)} %get-tuple-element.185, bf16[2048,1408]{1,0:T(8,128)(2,1)S(1)} %bitcast.346), kind=kOutput, calls=%fused_computation.278 | convolution fusion | flops 5905580032 | bytes 17039360 | tf_op jit(solution)/shard_map/dot_general | solution.py:40
  404.7 4.3 fusion.14
  409.0 9.8 fusion.139
  418.8 10.6 %add_convert_fusion = bf16[1024,2048]{1,0:T(8,128)(2,1)S(1)} fusion(f32[1024,2048]{1,0:T(8,128)} %fusion.146, bf16[1024,1408]{1,0:T(8,128)(2,1)} %get-tuple-element.184, bf16[2048,1408]{1,0:T(8,128)(2,1)S(1)} %bitcast.391), kind=kOutput, calls=%fused_computation.32 | convolution fusion | flops 5909774336 | bytes 21233664 | tf_op jit(solution)/shard_map/dot_general | solution.py:40
  429.4 8.1 fusion.88
  437.6 4.5 multiply_convert_fusion.6
  442.0 8.2 fusion.147
  450.3 15.4 %fusion.3 = bf16[2048,2048]{1,0:T(8,128)(2,1)} fusion(f32[2048,2048]{1,0:T(8,128)} %fusion.147, f32[16,128,2048]{2,1,0:T(8,128)} %fusion.88, bf16[2048,176]{0,1:T(8,128)(2,1)S(1)} %copy-done.61, bf16[2048,176]{0,1:T(8,128)(2,1)S(1)} %bitcast.361), kind=kOutput, calls=%fused_computation.5 | convolution fusion | flops 1488977920 | bytes 43384832 | tf_op jit(solution)/shard_map/dot_general | solution.py:40
  465.8 92.8 %bundle_reduce_trade.2 = (f32[128,2048]{1,0:T(8,128)S(1)}, f32[16,8,128]{2,1,0:T(8,128)S(1)}, bf16[2,704,2048]{2,1,0:T(8,128)(2,1)}) custom-call(bf16[16,128,2048]{2,1,0:T(8,128)(2,1)} %bitcast.320, f32[16,8,128]{2,1,0:T(8,128)S(1)} %broadcast_in_dim.194.refs_1_, bf16[2,704,2048]{2,1,0:T(8,128)(2,1)} %bitcast.336), custom_call_target="tpu_custom_call" | custom-call | tf_op jit(solution)/shard_map/bundle_reduce_trade/pallas_call | solution.py:478
  564.8 10.4 %fusion.91 = f32[16,128,2048]{2,1,0:T(8,128)} fusion(bf16[16,64,2048]{2,1,0:T(8,128)(2,1)} %bitcast.321, s32[16,128]{1,0:T(8,128)S(1)} %broadcast_add_fusion, pred[16,128]{1,0:T(8,128)(4,1)S(1)} %reduce_or.9), kind=kOutput, calls=%fused_computation.169 | convolution fusion | flops 537133056 | bytes 20981760 | tf_op jit(solution)/shard_map/bct,bcd->btd/dot_general | solution.py:756
  575.2 11.5 %fusion.4 = bf16[2048,2048]{1,0:T(8,128)(2,1)} fusion(f32[16,128,2048]{2,1,0:T(8,128)} %fusion.91, bf16[2048,176]{0,1:T(8,128)(2,1)S(1)} %copy-done.60, bf16[176,2048]{1,0:T(8,128)(2,1)S(1)} %bitcast.353), kind=kOutput, calls=%fused_computation.7 | convolution fusion | flops 1484783616 | bytes 26607616 | tf_op jit(solution)/shard_map/dot_general | solution.py:30
  589.6 8.6 fusion.1
  598.2 6.6 copy.294
  604.8 12.3 %copy.291 = bf16[2048,2048]{1,0:T(8,128)(2,1)} copy(bf16[2048,2048]{0,1:T(8,128)(2,1)} %bitcast.312) | data formatting | bytes 16777216 | tf_op jit(solution)/shard_map/dot_general | solution.py:34
  617.1 5.2 fusion.149
  630.3 4.7 all-to-all-start
  635.1 9.6 fusion.24
  650.4 3.7 fusion.55
  655.8 28.7 %bundle_trade.1 = bf16[16,128,128]{2,1,0:T(8,128)(2,1)S(1)} custom-call(bf16[16,128,128]{2,1,0:T(8,128)(2,1)S(1)} %bitcast.292), custom_call_target="tpu_custom_call" | custom-call | tf_op jit(solution)/shard_map/bundle_trade/pallas_call | solution.py:478
  684.5 11.7 %fusion.26 = f32[2,1024,1408]{2,1,0:T(8,128)} fusion(bf16[2,1024,1024]{2,1,0:T(8,128)(2,1)} %bitcast.349, bf16[1024,1408]{1,0:T(8,128)(2,1)} %get-tuple-element.185), kind=kOutput, calls=%fused_computation.58 | convolution fusion | flops 5905580032 | bytes 18612224 | tf_op jit(solution)/shard_map/dot_general | solution.py:34
  696.2 4.7 fusion.22
  702.0 13.4 %multiply_reduce_fusion = (f32[2048]{0:T(1024)S(1)}, f32[2048,2048]{0,1:T(8,128)}) fusion(f32[2048,2048]{0,1:T(8,128)} %get-tuple-element.218, f32[2048]{0:T(1024)S(1)} %log_add_fusion, bf16[2048,256]{1,0:T(8,128)(2,1)S(1)} %copy-done.65, bf16[2048,128]{1,0:T(8,128)(2,1)S(1)} %bitcast.284, f32[2048]{0:T(1024)S(1)} %copy-done.70), kind=kOutput, calls=%fused_computation.9 | convolution fusion | flops 1087109120 | bytes 34627584 | tf_op jit(solution)/shard_map/dot_general | solution.py:40
  715.9 8.4 multiply_convert_fusion
  724.3 3.2 copy-done.20
  731.3 6.2 fusion.113
  737.5 5.9 multiply_cosine_fusion
  748.8 8.8 fusion.31
  759.0 40.6 %bundle_reduce_trade.3 = (f32[128,640]{1,0:T(8,128)S(1)}, bf16[16,128,192]{2,1,0:T(8,128)(2,1)S(1)}) custom-call(bf16[16,128,640]{2,1,0:T(8,128)(2,1)S(1)} %maximum_maximum_fusion.refs_0_, bf16[16,128,192]{2,1,0:T(8,128)(2,1)S(1)} %pad_maximum_fusion.1.refs_1_), custom_call_target="tpu_custom_call" | custom-call | tf_op jit(solution)/shard_map/bundle_reduce_trade/pallas_call | solution.py:478
  810.8 62.8 %bundle_trade_owners.1 = (bf16[16,128,36]{2,1,0:T(8,128)(2,1)S(1)}, bf16[32,64,192]{2,1,0:T(8,128)(2,1)S(1)}, bf16[32,16,256]{2,1,0:T(8,128)(2,1)S(1)}) custom-call(bf16[16,128,36]{2,1,0:T(8,128)(2,1)S(1)} %bitcast.289, bf16[32,64,192]{2,1,0:T(8,128)(2,1)S(1)} %bitcast.288, bf16[32,16,256]{2,1,0:T(8,128)(2,1)S(1)} %bitcast.301), custom_call_target="tpu_custom_call" | custom-call | tf_op jit(solution)/shard_map/bundle_trade_owners/pallas_call | solution.py:478
  876.5 5.0 convolution_convert_fusion.9
  882.9 5.4 fusion.53
  888.3 7.5 convert_add_fusion
  903.6 4.0 reshape.454
  914.7 6.6 fusion.19
  921.3 6.6 fusion.20
  927.9 6.5 fusion.50
  937.1 3.7 fusion.73
  941.0 3.3 fusion.69
  944.3 24.9 %all-gather.11.cloned.1.call-done = bf16[2048,2048]{1,0:T(8,128)(2,1)} async-done(((bf16[128,2048]{1,0:T(8,128)(2,1)}), bf16[2048,2048]{1,0:T(8,128)(2,1)}) %all-gather.11.cloned.1.call-update) | async-done | bytes 8388624 | tf_op jit(solution)/shard_map/all_gather | solution.py:898
  969.2 4.8 convolution_convert_fusion.5
  974.0 28.9 %bundle_owners_owners.1 = (bf16[32,64,36]{2,1,0:T(8,128)(2,1)S(1)}, f32[32,8,128]{2,1,0:T(8,128)S(1)}, bf16[2,64,2048]{2,1,0:T(8,128)(2,1)S(1)}) custom-call(bf16[32,64,36]{2,1,0:T(8,128)(2,1)S(1)} %bitcast.291, f32[32,8,128]{2,1,0:T(8,128)S(1)} %broadcast_in_dim.206.refs_1_, bf16[2,64,2048]{2,1,0:T(8,128)(2,1)S(1)} %bitcast.290), custom_call_target="tpu_custom_call" | custom-call | tf_op jit(solution)/shard_map/bundle_owners_owners/pallas_call | solution.py:478
  (442 shorter events, 133.1 us)
Async XLA Ops:
  7.2 212.5 %all-gather.5.cloned.1.call-start = ((), (), s32[]{:S(2)}) async-start(), calls=%async_computation.3 | async-start | bytes 4456448 | tf_op jit(solution)/shard_map/all_gather | solution.py:511
  66.1 47.6 %copy-start.14 = (bf16[2,256,256]{2,1,0:T(8,128)(2,1)}, bf16[2,256,256]{2,1,0:T(8,128)(2,1)S(1)}, u32[]{:S(2)}) copy-start(bf16[2,256,256]{2,1,0:T(8,128)(2,1)S(1)} %get-tuple-element.49) | copy-start | bytes 786436
  66.9 291.5 %all-gather.7.cloned.1.call-start = ((), (), s32[]{:S(2)}) async-start(), calls=%async_computation.4 | async-start | bytes 8912896 | tf_op jit(solution)/shard_map/all_gather | solution.py:636
  67.0 148.9 %collective-permute-start.1 = (bf16[704,2048]{1,0:T(8,128)(2,1)}, bf16[704,2048]{1,0:T(8,128)(2,1)}, u32[]{:S(2)}, u32[]{:S(2)}) collective-permute-start(bf16[704,2048]{1,0:T(8,128)(2,1)} %bitcast.358), channel_id=1, source_target_pairs={{0,16},{16,0},{1,17},{17,1},{2,18},{18,2},{3,19},{19,3},{4,20},{20... | collective-permute-start | bytes 8650760 | tf_op jit(solution)/shard_map/ppermute | solution.py:547
  68.3 124.9 %collective-permute-start = (bf16[1024,1408]{1,0:T(8,128)(2,1)}, bf16[1024,1408]{1,0:T(8,128)(2,1)}, u32[]{:S(2)}, u32[]{:S(2)}) collective-permute-start(bf16[1024,1408]{1,0:T(8,128)(2,1)} %bitcast.357), channel_id=1, source_target_pairs={{0,16},{16,0},{1,17},{17,1},{2,18},{18,2},{3,19},{19,3},{4,20},{20... | collective-permute-start | bytes 8650760 | tf_op jit(solution)/shard_map/ppermute | solution.py:547
  68.5 827.3 %reduce-scatter.7.cloned.1.call-start = ((), (), s32[]{:S(2)}) async-start(), calls=%async_computation.8 | async-start | bytes 1081344
  68.6 49.2 %copy-start.100 = (f32[32]{0:T(128)}, f32[32]{0:T(128)S(1)}, u32[]{:S(2)}) copy-start(f32[32]{0:T(128)S(1)} %multiply_power_fusion) | copy-start | bytes 388
  68.6 49.1 %copy-start.80 = (f32[2048]{0:T(1024)}, f32[2048]{0:T(1024)S(1)}, u32[]{:S(2)}) copy-start(f32[2048]{0:T(1024)S(1)} %iota_convert_fusion) | copy-start | bytes 24580
  70.6 14.8 %copy-start.27 = (bf16[2,72,8,1024]{3,2,0,1:T(8,128)(2,1)}, bf16[2,72,8,1024]{3,2,0,1:T(8,128)(2,1)S(1)}, u32[]{:S(2)}) copy-start(bf16[2,72,8,1024]{3,2,0,1:T(8,128)(2,1)S(1)} %copy.314) | copy-start | bytes 7077892
  85.3 10.1 copy-start.102
  128.2 11.9 %copy-start.82 = (s32[128,6]{0,1:T(8,128)S(1)}, s32[128,6]{0,1:T(8,128)}, u32[]{:S(2)}) copy-start(s32[128,6]{0,1:T(8,128)} %param.20) | copy-start | bytes 9220
  140.1 18.0 %copy-start.84 = (f32[2048]{0:T(1024)}, f32[2048]{0:T(1024)S(1)}, u32[]{:S(2)}) copy-start(f32[2048]{0:T(1024)S(1)} %get-tuple-element.217) | copy-start | bytes 24580
  147.8 10.3 %copy-start.64 = (bf16[2048,256]{1,0:T(8,128)(2,1)S(1)}, bf16[2048,256]{1,0:T(8,128)(2,1)}, u32[]{:S(2)}) copy-start(bf16[2048,256]{1,0:T(8,128)(2,1)} %convolution_convert_fusion.3) | copy-start | bytes 3145732
  147.8 45.4 %slice-start.10 = ((s8[5767168]{0:T(1024)(128)(4,1)}), s8[1572864]{0:T(1024)(128)(4,1)S(1)}, s32[]{:S(2)}) async-start(s8[5767168]{0:T(1024)(128)(4,1)} %bitcast.339), calls=%async_computation.19 | async-start | bytes 3145728
  158.1 35.1 %slice-start.11 = ((s8[5767168]{0:T(1024)(128)(4,1)}), s8[4194304]{0:T(1024)(128)(4,1)S(1)}, s32[]{:S(2)}) async-start(s8[5767168]{0:T(1024)(128)(4,1)} %bitcast.339), calls=%async_computation.20 | async-start | bytes 8388608
  165.7 29.8 %copy-start.8 = (bf16[2048,128]{1,0:T(8,128)(2,1)}, bf16[2048,128]{1,0:T(8,128)(2,1)S(1)}, u32[]{:S(2)}) copy-start(bf16[2048,128]{1,0:T(8,128)(2,1)S(1)} %fusion.30) | copy-start | bytes 1572868
  195.4 15.4 %copy-start.34 = (bf16[2,1024,1408]{2,1,0:T(8,128)(2,1)}, bf16[2,1024,1408]{2,1,0:T(8,128)(2,1)S(1)}, u32[]{:S(2)}) copy-start(bf16[2,1024,1408]{2,1,0:T(8,128)(2,1)S(1)} %bitcast_dynamic-update-slice_fusion.1) | copy-start | bytes 17301508
  219.7 97.8 %copy-start.67 = (bf16[2048,16]{0,1:T(8,128)(2,1)S(1)}, bf16[2048,16]{0,1:T(8,128)(2,1)}, u32[]{:S(2)}) copy-start(bf16[2048,16]{0,1:T(8,128)(2,1)} %param.28) | copy-start | bytes 196612
  223.0 100.1 %copy-start.6 = (bf16[128,2048]{1,0:T(8,128)(2,1)}, bf16[128,2048]{1,0:T(8,128)(2,1)S(1)}, u32[]{:S(2)}) copy-start(bf16[128,2048]{1,0:T(8,128)(2,1)S(1)} %multiply_convert_fusion.10) | copy-start | bytes 1572868
  325.8 111.8 %copy-start.45 = (bf16[2,88,2048]{2,1,0:T(8,128)(2,1)}, bf16[2,88,2048]{2,1,0:T(8,128)(2,1)S(1)}, u32[]{:S(2)}) copy-start(bf16[2,88,2048]{2,1,0:T(8,128)(2,1)S(1)} %slice.96) | copy-start | bytes 2162692
  330.8 16.0 %copy-start.22 = (bf16[16,64,2048]{2,1,0:T(8,128)(2,1)}, bf16[16,64,2048]{2,1,0:T(8,128)(2,1)S(1)}, u32[]{:S(2)}) copy-start(bf16[16,64,2048]{2,1,0:T(8,128)(2,1)S(1)} %convolution_convert_fusion.2) | copy-start | bytes 12582916
  335.9 13.4 %slice-start.16 = ((s8[5767168]{0:T(1024)(128)(4,1)}), s8[4194304]{0:T(1024)(128)(4,1)S(1)}, s32[]{:S(2)}) async-start(s8[5767168]{0:T(1024)(128)(4,1)} %bitcast.386), calls=%async_computation.25 | async-start | bytes 8388608
  363.2 12.7 %copy-start.18 = (bf16[16,64,2048]{2,1,0:T(8,128)(2,1)}, bf16[16,64,2048]{2,1,0:T(8,128)(2,1)S(1)}, u32[]{:S(2)}) copy-start(bf16[16,64,2048]{2,1,0:T(8,128)(2,1)S(1)} %convolution_convert_fusion.1) | copy-start | bytes 12582916
  363.2 12.7 %copy-start.88 = (f32[16,128]{1,0:T(8,128)S(1)}, f32[16,128]{1,0:T(8,128)}, u32[]{:S(2)}) copy-start(f32[16,128]{1,0:T(8,128)} %get-tuple-element.180) | copy-start | bytes 24580
  376.5 17.6 %slice-start.14 = ((s8[5767168]{0:T(1024)(128)(4,1)}), s8[4194304]{0:T(1024)(128)(4,1)S(1)}, s32[]{:S(2)}) async-start(s8[5767168]{0:T(1024)(128)(4,1)} %bitcast.344), calls=%async_computation.23 | async-start | bytes 8388608
  379.6 14.5 %slice-start.15 = ((s8[5767168]{0:T(1024)(128)(4,1)}), s8[1572864]{0:T(1024)(128)(4,1)S(1)}, s32[]{:S(2)}) async-start(s8[5767168]{0:T(1024)(128)(4,1)} %bitcast.344), calls=%async_computation.24 | async-start | bytes 3145728
  394.0 10.6 %copy-start.19 = (bf16[16,64,2048]{2,1,0:T(8,128)(2,1)S(1)}, bf16[16,64,2048]{2,1,0:T(8,128)(2,1)}, u32[]{:S(2)}) copy-start(bf16[16,64,2048]{2,1,0:T(8,128)(2,1)} %copy-done.18) | copy-start | bytes 12582916
  394.0 10.6 %copy-start.42 = (bf16[1024,2048]{1,0:T(8,128)(2,1)S(1)}, bf16[1024,2048]{1,0:T(8,128)(2,1)}, u32[]{:S(2)}) copy-start(bf16[1024,2048]{1,0:T(8,128)(2,1)} %get-tuple-element.224) | copy-start | bytes 12582916
  404.7 14.1 %slice-start.18 = ((s8[5767168]{0:T(1024)(128)(4,1)}), s8[4194304]{0:T(1024)(128)(4,1)S(1)}, s32[]{:S(2)}) async-start(s8[5767168]{0:T(1024)(128)(4,1)} %bitcast.389), calls=%async_computation.27 | async-start | bytes 8388608
  409.0 9.8 slice-start.19
  409.0 28.6 %slice-start.6 = ((s8[8388608]{0:T(1024)(128)(4,1)}), s8[4194304]{0:T(1024)(128)(4,1)S(1)}, s32[]{:S(2)}) async-start(s8[8388608]{0:T(1024)(128)(4,1)} %bitcast.326), calls=%async_computation.15 | async-start | bytes 8388608
  418.8 18.7 %slice-start.7 = ((s8[8388608]{0:T(1024)(128)(4,1)}), s8[4194304]{0:T(1024)(128)(4,1)S(1)}, s32[]{:S(2)}) async-start(s8[8388608]{0:T(1024)(128)(4,1)} %bitcast.326), calls=%async_computation.16 | async-start | bytes 8388608
  465.7 92.9 %copy-start.83 = (s32[128,6]{0,1:T(8,128)S(1)}, s32[128,6]{0,1:T(8,128)}, u32[]{:S(2)}) copy-start(s32[128,6]{0,1:T(8,128)} %param.20) | copy-start | bytes 9220
  465.7 92.9 %copy-start.98 = (f32[128]{0:T(128)S(1)}, f32[128]{0:T(128)}, u32[]{:S(2)}) copy-start(f32[128]{0:T(128)} %dynamic-slice) | copy-start | bytes 1540
  465.7 94.4 %copy-start.7 = (bf16[128,2048]{1,0:T(8,128)(2,1)S(1)}, bf16[128,2048]{1,0:T(8,128)(2,1)}, u32[]{:S(2)}) copy-start(bf16[128,2048]{1,0:T(8,128)(2,1)} %copy-done.6) | copy-start | bytes 1572868
  465.7 94.7 %copy-start.24 = (f32[128,2048]{1,0:T(8,128)S(1)}, f32[128,2048]{1,0:T(8,128)}, u32[]{:S(2)}) copy-start(f32[128,2048]{1,0:T(8,128)} %copy-done.23) | copy-start | bytes 3145732
  465.8 94.7 %copy-start.68 = (bf16[2048,16]{0,1:T(8,128)(2,1)S(1)}, bf16[2048,16]{0,1:T(8,128)(2,1)}, u32[]{:S(2)}) copy-start(bf16[2048,16]{0,1:T(8,128)(2,1)} %param.28) | copy-start | bytes 196612
  465.8 94.7 %copy-start.79 = (f32[2048]{0:T(1024)S(1)}, f32[2048]{0:T(1024)}, u32[]{:S(2)}) copy-start(f32[2048]{0:T(1024)} %param.27) | copy-start | bytes 24580
  465.8 94.7 %copy-start.92 = (f32[128]{0:T(128)S(1)}, f32[128]{0:T(128)}, u32[]{:S(2)}) copy-start(f32[128]{0:T(128)} %copy-done.91) | copy-start | bytes 1540
  563.7 364.2 %all-gather.9.cloned.1.call-start = ((), (), s32[]{:S(2)}) async-start(), calls=%async_computation.6 | async-start | bytes 6684672 | tf_op jit(solution)/shard_map/all_gather | solution.py:511
  564.6 376.4 %reduce-scatter.5.cloned.1.call-start = ((), (), s32[]{:S(2)}) async-start(), calls=%async_computation.5 | async-start | bytes 8912896 | tf_op jit(solution)/shard_map/reduce_scatter | solution.py:828
  564.8 10.4 %copy-start.46 = (bf16[2,88,2048]{2,1,0:T(8,128)(2,1)S(1)}, bf16[2,88,2048]{2,1,0:T(8,128)(2,1)}, u32[]{:S(2)}) copy-start(bf16[2,88,2048]{2,1,0:T(8,128)(2,1)} %copy-done.45) | copy-start | bytes 2162692
  564.8 10.4 %copy-start.60 = (bf16[2048,176]{0,1:T(8,128)(2,1)S(1)}, bf16[2048,176]{0,1:T(8,128)(2,1)}, u32[]{:S(2)}) copy-start(bf16[2048,176]{0,1:T(8,128)(2,1)} %get-tuple-element.194) | copy-start | bytes 2162692
  589.6 210.1 %copy-start.99 = (f32[128]{0:T(128)}, f32[128]{0:T(128)S(1)}, u32[]{:S(2)}) copy-start(f32[128]{0:T(128)S(1)} %fusion.123) | copy-start | bytes 1540
  623.2 275.5 %collective-permute-start.2 = (bf16[88,2048]{1,0:T(8,128)(2,1)}, bf16[88,2048]{1,0:T(8,128)(2,1)}, u32[]{:S(2)}, u32[]{:S(2)}) collective-permute-start(bf16[88,2048]{1,0:T(8,128)(2,1)} %fusion.99), channel_id=1, source_target_pairs={{0,16},{16,0},{1,17},{17,1},{2,18},{18,2},{3,19},{19,3},{4,20},{20... | collective-permute-start | bytes 1081352 | tf_op jit(solution)/shard_map/ppermute | solution.py:566
  630.3 270.3 %all-to-all-start = ((bf16[32,64,352]{2,1,0:T(8,128)(2,1)}), bf16[32,64,352]{2,1,0:T(8,128)(2,1)}, u32[]{:S(2)}, u32[]{:S(2)}) async-start(bf16[32,64,352]{2,1,0:T(8,128)(2,1)} %pad_maximum_fusion), calls=%async_computation.1 | async-start | bytes 3145728 | tf_op jit(solution)/shard_map/all_to_all | solution.py:838
  635.0 334.1 %all-gather.11.cloned.1.call-start = ((), (), s32[]{:S(2)}) async-start(), calls=%async_computation.7 | async-start | bytes 8912896 | tf_op jit(solution)/shard_map/all_gather | solution.py:898
  646.6 268.2 %collective-permute-start.4 = (bf16[1024,1408]{1,0:T(8,128)(2,1)}, bf16[1024,1408]{1,0:T(8,128)(2,1)}, u32[]{:S(2)}, u32[]{:S(2)}) collective-permute-start(bf16[1024,1408]{1,0:T(8,128)(2,1)} %fusion.23), channel_id=1, source_target_pairs={{0,16},{16,0},{1,17},{17,1},{2,18},{18,2},{3,19},{19,3},{4,20},{20... | collective-permute-start | bytes 8650760 | tf_op jit(solution)/shard_map/ppermute | solution.py:566
  696.2 19.2 %slice-start = ((s8[16777216]{0:T(1024)(128)(4,1)}), s8[4194304]{0:T(1024)(128)(4,1)S(1)}, s32[]{:S(2)}) async-start(s8[16777216]{0:T(1024)(128)(4,1)} %bitcast.308), calls=%async_computation.9 | async-start | bytes 8388608
  700.9 14.5 %slice-start.1 = ((s8[16777216]{0:T(1024)(128)(4,1)}), s8[4194304]{0:T(1024)(128)(4,1)S(1)}, s32[]{:S(2)}) async-start(s8[16777216]{0:T(1024)(128)(4,1)} %bitcast.308), calls=%async_computation.10 | async-start | bytes 8388608
  700.9 14.5 %slice-start.2 = ((s8[16777216]{0:T(1024)(128)(4,1)}), s8[4194304]{0:T(1024)(128)(4,1)S(1)}, s32[]{:S(2)}) async-start(s8[16777216]{0:T(1024)(128)(4,1)} %bitcast.308), calls=%async_computation.11 | async-start | bytes 8388608
  700.9 15.0 %slice-start.3 = ((s8[16777216]{0:T(1024)(128)(4,1)}), s8[4194304]{0:T(1024)(128)(4,1)S(1)}, s32[]{:S(2)}) async-start(s8[16777216]{0:T(1024)(128)(4,1)} %bitcast.308), calls=%async_computation.12 | async-start | bytes 8388608
  700.9 220.4 %collective-permute-start.3 = (bf16[1024,1408]{1,0:T(8,128)(2,1)}, bf16[1024,1408]{1,0:T(8,128)(2,1)}, u32[]{:S(2)}, u32[]{:S(2)}) collective-permute-start(bf16[1024,1408]{1,0:T(8,128)(2,1)} %fusion.22), channel_id=1, source_target_pairs={{0,16},{16,0},{1,17},{17,1},{2,18},{18,2},{3,19},{19,3},{4,20},{20... | collective-permute-start | bytes 8650760 | tf_op jit(solution)/shard_map/ppermute | solution.py:566
  715.9 11.6 %copy-start.39 = (bf16[2048,32]{1,0:T(8,128)(2,1)S(1)}, bf16[2048,32]{1,0:T(8,128)(2,1)}, u32[]{:S(2)}) copy-start(bf16[2048,32]{1,0:T(8,128)(2,1)} %copy-done.38) | copy-start | bytes 393220
  715.9 11.6 %copy-start.41 = (bf16[2048,32]{1,0:T(8,128)(2,1)S(1)}, bf16[2048,32]{1,0:T(8,128)(2,1)}, u32[]{:S(2)}) copy-start(bf16[2048,32]{1,0:T(8,128)(2,1)} %copy-done.40) | copy-start | bytes 393220
  731.3 12.2 %copy-start.21 = (bf16[2048,2048]{0,1:T(8,128)(2,1)S(1)}, bf16[2048,2048]{0,1:T(8,128)(2,1)}, u32[]{:S(2)}) copy-start(bf16[2048,2048]{0,1:T(8,128)(2,1)} %copy-done.20) | copy-start | bytes 25165828
  731.3 12.2 %copy-start.66 = (bf16[2048,256]{1,0:T(8,128)(2,1)S(1)}, bf16[2048,256]{1,0:T(8,128)(2,1)}, u32[]{:S(2)}) copy-start(bf16[2048,256]{1,0:T(8,128)(2,1)} %convolution_convert_fusion.3) | copy-start | bytes 3145732
  746.3 54.3 %slice-start.8 = ((s8[8388608]{0:T(1024)(128)(4,1)}), s8[4194304]{0:T(1024)(128)(4,1)S(1)}, s32[]{:S(2)}) async-start(s8[8388608]{0:T(1024)(128)(4,1)} %bitcast.331), calls=%async_computation.17 | async-start | bytes 8388608
  748.7 9.6 copy-start.53
  748.8 51.9 %slice-start.9 = ((s8[8388608]{0:T(1024)(128)(4,1)}), s8[4194304]{0:T(1024)(128)(4,1)S(1)}, s32[]{:S(2)}) async-start(s8[8388608]{0:T(1024)(128)(4,1)} %bitcast.331), calls=%async_computation.18 | async-start | bytes 8388608
  757.6 42.1 %copy-start.90 = (f32[512]{0:T(512)S(1)}, f32[512]{0:T(512)}, u32[]{:S(2)}) copy-start(f32[512]{0:T(512)} %param.24) | copy-start | bytes 6148
  888.3 10.4 %copy-start.55 = (f32[176,2048]{1,0:T(8,128)S(1)}, f32[176,2048]{1,0:T(8,128)}, u32[]{:S(2)}) copy-start(f32[176,2048]{1,0:T(8,128)} %copy-done.54) | copy-start | bytes 4325380
  937.1 32.1 %copy-start.9 = (bf16[2048,128]{1,0:T(8,128)(2,1)S(1)}, bf16[2048,128]{1,0:T(8,128)(2,1)}, u32[]{:S(2)}) copy-start(bf16[2048,128]{1,0:T(8,128)(2,1)} %copy-done.8) | copy-start | bytes 1572868
  969.2 38.5 %copy-start.1 = (bf16[256,4096]{1,0:T(8,128)(2,1)S(1)}, bf16[256,4096]{1,0:T(8,128)(2,1)}, u32[]{:S(2)}) copy-start(bf16[256,4096]{1,0:T(8,128)(2,1)} %param.25) | copy-start | bytes 6291460
  (81 other events, 388.0 us)
Sparse Core Ops, SparseCore 0:
  67.0 50.4 all-gather.4
  119.7 72.7 all-gather.6
  563.8 120.6 reduce-scatter.6
  686.9 73.8 all-gather.8
  765.2 127.2 reduce-scatter.4
  894.7 74.4 all-gather.10

commit v3 on v2

--- a/solution.py
+++ b/solution.py
@@ -17,6 +17,7 @@
 SEQ = 2048
 WINDOW = 1024
 TOK_DEV = 128
+STEP_SENDERS = 4
 SEQ_DEVICES = SEQ // TOK_DEV
 
 
@@ -225,111 +226,118 @@
 
 
 def reduce_steps(place, part_ref, out_ref, scratch, sender):
-    (own_buf, twin_buf, row_buf, up_buf, down_buf, load_sem, twin_send, twin_recv, row_send, row_recv,
-     line_send, line_recv, out_buf, out_sem) = scratch
+    (own_buf, twin_buf, row_buf, line_buf, load_sem, twin_send, twin_recv, row_send, row_recv, line_send, line_recv,
+     out_buf, out_sem) = scratch
     outer, local, level = place.outer, place.local, place.level
+    pieces = part_ref.shape[1]
     inner = lax.rem(local, INNER)
     row_bit, core = inner // 2, lax.rem(inner, 2)
     twin_at, row_at = {"expert": place.me + place.twin_step}, {"expert": place.me + place.row_step}
     order = []
     low, high = 0, outer - 1
     while low <= high:
-        order.append(high)
-        if low != high:
-            order.append(low)
+        order += [high] if low == high else [high, low]
         low, high = low + 1, high - 1
-
-    def slot(level_at, bit):
-        return level_at * 2 + bit
-
-    def block(level_at, bit, core_at):
-        return level_at * INNER + bit * 2 + core_at
-
-    other_bit, other_core = 1 - row_bit, 1 - core
-    loads, twins, rows = {}, {}, {}
-    for at in order:
-        for kind, bit in ((0, other_bit), (1, row_bit)):
-            where = slot(at, bit)
-            copy = remote(part_ref.at[block(at, bit, other_core)], twin_buf.at[where], twin_send.at[where],
-                          twin_recv.at[where], twin_at)
-            sender.start(place.always, copy)
-            load = pltpu.make_async_copy(part_ref.at[block(at, bit, core)], own_buf.at[where], load_sem.at[where])
-            load.start()
-            loads[at, kind] = load
-            twins[at, kind] = pltpu.make_async_remote_copy(
-                src_ref=part_ref.at[block(at, bit, other_core)], dst_ref=twin_buf.at[where],
-                send_sem=twin_send.at[where], recv_sem=twin_recv.at[where], device_id=twin_at, device_id_type=MESH)
+    units = [(at, piece) for at in order for piece in range(pieces)]
+    bits = (1 - row_bit, row_bit)
+
+    def loading(at, piece, bit):
+        where = at * 2 + bit
+        return pltpu.make_async_copy(
+            part_ref.at[at * INNER + bit * 2 + core, piece], own_buf.at[where, piece], load_sem.at[where, piece]
+        )
+
+    def to_twin(at, piece, bit):
+        where = at * 2 + bit
+        return remote(
+            part_ref.at[at * INNER + bit * 2 + 1 - core, piece],
+            twin_buf.at[where, piece],
+            twin_send.at[where, piece],
+            twin_recv.at[where, piece],
+            twin_at,
+        )
+
+    def to_row(at, piece):
+        return remote(
+            own_buf.at[at * 2 + bits[0], piece], row_buf.at[at, piece], row_send.at[at, piece], row_recv.at[at, piece], row_at
+        )
+
+    def mine(at, piece):
+        return own_buf.at[at * 2 + row_bit, piece]
+
+    def to_line(side, at, piece):
+        return remote(
+            mine(at, piece),
+            line_buf.at[side, at, piece],
+            line_send.at[side, at, piece],
+            line_recv.at[side, at, piece],
+            {"expert": place.me + (INNER if side == 0 else -INNER)},
+        )
+
+    for at, piece in units:
+        for bit in bits:
+            sender.start(place.always, to_twin(at, piece, bit))
+            loading(at, piece, bit).start()
     yield
-    for at in order:
-        for kind, bit in ((0, other_bit), (1, row_bit)):
-            where = slot(at, bit)
-            loads[at, kind].wait()
-            twins[at, kind].wait_recv()
-            add_into(own_buf.at[where], own_buf.at[where], twin_buf.at[where])
-            if kind == 0:
-                copy = remote(own_buf.at[where], row_buf.at[at], row_send.at[at], row_recv.at[at], row_at)
-                sender.start(place.always, copy)
-                rows[at] = copy
-        yield
-    for at in order:
-        mine = own_buf.at[slot(at, row_bit)]
-        rows[at].wait_recv()
-
+    for at, piece in units:
+        for bit in bits:
+            where = at * 2 + bit
+            loading(at, piece, bit).wait()
+            to_twin(at, piece, bit).wait_recv()
+            add_into(own_buf.at[where, piece], own_buf.at[where, piece], twin_buf.at[where, piece])
+            if bit is bits[0]:
+                sender.start(place.always, to_row(at, piece))
+    yield
+    for at, piece in units:
+        to_row(at, piece).wait_recv()
+        spot, row = mine(at, piece), row_buf.at[at, piece]
+        for side, there, first in ((0, level < at, level == 0), (1, level > at, level == outer - 1)):
+            line = to_line(side, at, piece)
+
+            @pl.when(there & first)
+            def _():
+                add_into(spot, spot, row)
+
+            @pl.when(there & ~first)
+            def _():
+                line.wait_recv()
+                add_into(spot, spot, row, line_buf.at[side, at, piece])
+
+            sender.start(there, line)
+    yield
+    for at, piece in units:
         @pl.when(level == at)
         def _():
-            add_into(mine, mine, row_buf.at[at])
-
-        up = remote(mine, up_buf.at[at], line_send.at[0, at], line_recv.at[0, at], {"expert": place.me + INNER})
-        down = remote(mine, down_buf.at[at], line_send.at[1, at], line_recv.at[1, at], {"expert": place.me - INNER})
-        for there, first, copy, buf in ((level < at, level == 0, up, up_buf), (level > at, level == outer - 1, down, down_buf)):
-            @pl.when(there & first)
-            def _():
-                add_into(mine, mine, row_buf.at[at])
-
-            @pl.when(there & ~first)
-            def _():
-                copy.wait_recv()
-                add_into(mine, mine, row_buf.at[at], buf.at[at])
-
-            sender.start(there, copy)
-        yield
-    for at in order:
-        @pl.when(level == at)
-        def _():
-            mine = own_buf.at[slot(at, row_bit)]
-            up = remote(mine, up_buf.at[at], line_send.at[0, at], line_recv.at[0, at], {"expert": place.me + INNER})
-            down = remote(mine, down_buf.at[at], line_send.at[1, at], line_recv.at[1, at], {"expert": place.me - INNER})
-            if at > 0:
-                up.wait_recv()
-            if at < outer - 1:
-                down.wait_recv()
-            if 0 < at < outer - 1:
-                add_into(out_buf, mine, up_buf.at[at], down_buf.at[at])
-            else:
-                add_into(out_buf, mine, up_buf.at[at] if at else down_buf.at[at])
+            parts = [mine(at, piece), row_buf.at[at, piece]]
+            for side, there in ((0, at > 0), (1, at < outer - 1)):
+                if there:
+                    to_line(side, at, piece).wait_recv()
+                    parts.append(line_buf.at[side, at, piece])
+            add_into(out_buf.at[piece], *parts)
     done = pltpu.make_async_copy(out_buf, out_ref, out_sem)
     done.start()
     done.wait()
     yield
 
 
-def reduce_scratch(group, rows, columns):
+def reduce_scratch(group, pieces, rows, columns):
     outer = group // INNER
     bf = jnp.bfloat16
+    pair, single, line = (2 * outer, pieces), (outer, pieces), (2, outer, pieces)
+    block = (rows, columns)
     return [
-        pltpu.VMEM((2 * outer, rows, columns), bf),
-        pltpu.VMEM((2 * outer, rows, columns), bf),
-        pltpu.VMEM((outer, rows, columns), bf),
-        pltpu.VMEM((outer, rows, columns), bf),
-        pltpu.VMEM((outer, rows, columns), bf),
-        pltpu.SemaphoreType.DMA((2 * outer,)),
-        pltpu.SemaphoreType.DMA((2 * outer,)),
-        pltpu.SemaphoreType.DMA((2 * outer,)),
-        pltpu.SemaphoreType.DMA((outer,)),
-        pltpu.SemaphoreType.DMA((outer,)),
-        pltpu.SemaphoreType.DMA((2, outer)),
-        pltpu.SemaphoreType.DMA((2, outer)),
-        pltpu.VMEM((rows, columns), jnp.float32),
+        pltpu.VMEM(pair + block, bf),
+        pltpu.VMEM(pair + block, bf),
+        pltpu.VMEM(single + block, bf),
+        pltpu.VMEM(line + block, bf),
+        pltpu.SemaphoreType.DMA(pair),
+        pltpu.SemaphoreType.DMA(pair),
+        pltpu.SemaphoreType.DMA(pair),
+        pltpu.SemaphoreType.DMA(single),
+        pltpu.SemaphoreType.DMA(single),
+        pltpu.SemaphoreType.DMA(line),
+        pltpu.SemaphoreType.DMA(line),
+        pltpu.VMEM((pieces,) + block, jnp.float32),
         pltpu.SemaphoreType.DMA(()),
     ]
 
@@ -414,7 +422,7 @@
             copy_sem, send_sem, recv_sem, *rest = rest
             runs.append(gather_steps(place, own, out, copy_sem, send_sem, recv_sem, sender))
         elif kind == "reduce":
-            scratch, rest = rest[:14], rest[14:]
+            scratch, rest = rest[:13], rest[13:]
             runs.append(reduce_steps(place, own, out, scratch, sender))
         else:
             copy_sem, send_sem, recv_sem, *rest = rest
@@ -463,6 +471,8 @@
             shape = (group,) + array.shape
             sems += [pltpu.SemaphoreType.DMA((4, group, pieces)), pltpu.SemaphoreType.DMA((group, pieces))]
         elif kind == "reduce":
+            pieces = 2 * PIECES
+            array = array.reshape(group, pieces, array.shape[1] // pieces, array.shape[2])
             shape = array.shape[1:]
             sems = reduce_scratch(group, *shape)
         else:
@@ -490,8 +500,256 @@
     for (kind, array), out in zip(transfers, outs):
         if kind == "gather":
             out = out.reshape((group,) + array.shape)
+        if kind == "reduce":
+            out = out.reshape(array.shape[1:])
         done.append(out)
     return done
+
+
+def pieces_of(size, most):
+    return [(at, min(most, size - at)) for at in range(0, size, most)]
+
+
+def expert_kernel(
+    pick_ref, place_ref, gate_ref, rows_in, grads_in, gate_w, up_w, down_w, shared_gate_w, shared_up_w, shared_down_w,
+    back_ref, out_ref, rows_ref, grad_ref, hidden_ref, gate_back_ref, up_back_ref, score_ref,
+    shared_hidden_ref, shared_gate_back_ref, shared_up_back_ref, slot_cotangent,
+):
+    width = rows_in.shape[1]
+    hidden_width = gate_w.shape[1]
+    low = jnp.bfloat16
+    gate = gate_ref[...]
+    pick = pick_ref[0]
+
+    def pick_step(index, _):
+        at = pl.ds(pl.multiple_of(index * 512, 512), 512)
+        rows_ref[:, at] = matmul(pick, rows_in[:, at]).astype(low)
+        picked = matmul(pick, grads_in[:, at])
+        slot_cotangent[:, at] = picked.astype(low)
+        grad_ref[:, at] = (gate * picked).astype(low)
+        return 0
+
+    lax.fori_loop(0, width // 512, pick_step, 0)
+    shared_pre = matmul(rows_in[...], shared_gate_w[...])
+    shared_up = matmul(rows_in[...], shared_up_w[...])
+    swished, slope = swish_parts(shared_pre)
+    shared_hidden_ref[...] = (swished * shared_up).astype(low)
+    shared_grad = matmul_nt(grads_in[...], shared_down_w[...])
+    shared_gate_back_ref[...] = (shared_grad * shared_up * slope).astype(low)
+    shared_up_back_ref[...] = (shared_grad * swished).astype(low)
+    for at, size in pieces_of(hidden_width, 512):
+        columns = slice(at, at + size)
+        gate_pre = matmul(rows_ref[...], gate_w[:, columns])
+        up_pre = matmul(rows_ref[...], up_w[:, columns])
+        swished, slope = swish_parts(gate_pre)
+        hidden_ref[:, columns] = (swished * up_pre).astype(low)
+        hidden_grad = matmul_nt(grad_ref[...], down_w[columns, :])
+        gate_back_ref[:, columns] = (hidden_grad * up_pre * slope).astype(low)
+        up_back_ref[:, columns] = (hidden_grad * swished).astype(low)
+    place = place_ref[0]
+
+    def out_step(index, score):
+        at = pl.ds(pl.multiple_of(index * 512, 512), 512)
+        expert_out = matmul(hidden_ref[...], down_w[:, at]).astype(low).astype(jnp.float32)
+        score = score + jnp.sum(expert_out * slot_cotangent[:, at].astype(jnp.float32), axis=1, keepdims=True)
+        out = matmul(place, (gate * expert_out).astype(low)) + matmul(shared_hidden_ref[...], shared_down_w[:, at])
+        out_ref[:, at] = out.astype(low)
+        row_back = matmul_nt(gate_back_ref[...], gate_w[at, :]) + matmul_nt(up_back_ref[...], up_w[at, :])
+        back = (
+            matmul(place, row_back.astype(low))
+            + matmul_nt(shared_gate_back_ref[...], shared_gate_w[at, :])
+            + matmul_nt(shared_up_back_ref[...], shared_up_w[at, :])
+        )
+        back_ref[:, at] = back.astype(low)
+        return score
+
+    score = lax.fori_loop(0, width // 512, out_step, jnp.zeros((pick.shape[0], 1), jnp.float32))
+    score_ref[...] = jnp.broadcast_to(score, score_ref.shape)
+
+
+def expert_pass(pick, place, slot_gate, rows, grads, gate_w, up_w, down_w, shared_gate_w, shared_up_w, shared_down_w):
+    steps, slots, tokens = pick.shape
+    width, hidden_width = gate_w.shape
+    shared_width = shared_gate_w.shape[1]
+    low = jnp.bfloat16
+    whole = lambda shape: pl.BlockSpec(shape, lambda i: (0, 0), pipeline_mode=pl.Buffered(1))
+    by_step = lambda r, c: pl.BlockSpec((r, c), lambda i: (i, 0))
+    total = steps * slots
+    out_shape = [
+        jax.ShapeDtypeStruct((steps * tokens, width), low),
+        jax.ShapeDtypeStruct((steps * tokens, width), low),
+        jax.ShapeDtypeStruct((total, width), low),
+        jax.ShapeDtypeStruct((total, width), low),
+        jax.ShapeDtypeStruct((total, hidden_width), low),
+        jax.ShapeDtypeStruct((total, hidden_width), low),
+        jax.ShapeDtypeStruct((total, hidden_width), low),
+        jax.ShapeDtypeStruct((total, 128), jnp.float32),
+        jax.ShapeDtypeStruct((steps * tokens, shared_width), low),
+        jax.ShapeDtypeStruct((steps * tokens, shared_width), low),
+        jax.ShapeDtypeStruct((steps * tokens, shared_width), low),
+    ]
+    return pl.pallas_call(
+        expert_kernel,
+        grid=(steps,),
+        out_shape=out_shape,
+        in_specs=[
+            pl.BlockSpec((1, slots, tokens), lambda i: (i, 0, 0)),
+            pl.BlockSpec((1, tokens, slots), lambda i: (i, 0, 0)),
+            by_step(slots, 1),
+            by_step(tokens, width),
+            by_step(tokens, width),
+            whole(gate_w.shape), whole(up_w.shape), whole(down_w.shape),
+            whole(shared_gate_w.shape), whole(shared_up_w.shape), whole(shared_down_w.shape),
+        ],
+        out_specs=[
+            by_step(tokens, width), by_step(tokens, width), by_step(slots, width), by_step(slots, width),
+            by_step(slots, hidden_width), by_step(slots, hidden_width), by_step(slots, hidden_width), by_step(slots, 128),
+            by_step(tokens, shared_width), by_step(tokens, shared_width), by_step(tokens, shared_width),
+        ],
+        scratch_shapes=[pltpu.VMEM((slots, width), low)],
+        compiler_params=pltpu.CompilerParams(vmem_limit_bytes=60 * 2**20, dimension_semantics=("arbitrary",)),
+        name="experts",
+    )(pick, place, slot_gate, rows, grads, gate_w, up_w, down_w, shared_gate_w, shared_up_w, shared_down_w)
+
+
+QUERIES = 256
+KEYS = WINDOW + QUERIES
+
+
+def score_block(step, scale, query, keys, query_docs, key_docs):
+    raw = matmul_nt(query, keys) * scale
+    row = lax.broadcasted_iota(jnp.int32, raw.shape, 0) + WINDOW
+    column = lax.broadcasted_iota(jnp.int32, raw.shape, 1)
+    allowed = (query_docs == key_docs) & (column <= row) & (column > row - WINDOW)
+    return jnp.where(allowed, raw, NEG)
+
+
+def attend_kernel(scale, last, query_ref, key_ref, value_ref, docs_ref, row_docs_ref, out_ref, total_ref):
+    step = pl.program_id(0)
+    at = pl.ds(pl.multiple_of(step * QUERIES, QUERIES), KEYS)
+    scores = score_block(step, scale, query_ref[...], key_ref[at, :], docs_ref[...], row_docs_ref[:, at])
+    top = jnp.max(scores, axis=1, keepdims=True)
+    expo = jnp.exp(scores - top)
+    total = jnp.sum(expo, axis=1, keepdims=True)
+    probs = (expo / total).astype(jnp.bfloat16)
+    real = jnp.where(docs_ref[...] < last, 1.0, 0.0)
+    out_ref[...] = (matmul(probs, value_ref[at, :]) * real).astype(jnp.bfloat16)
+    total_ref[...] = jnp.broadcast_to(top + jnp.log(total), total_ref.shape)
+
+
+def attend_back_kernel(
+    scale, last, query_ref, key_ref, value_ref, docs_ref, row_docs_ref, total_ref, grad_ref,
+    query_grad_ref, key_grad_ref, value_grad_ref, key_sum, value_sum,
+):
+    step = pl.program_id(0)
+
+    @pl.when(step == 0)
+    def _():
+        key_sum[...] = jnp.zeros_like(key_sum)
+        value_sum[...] = jnp.zeros_like(value_sum)
+
+    at = pl.ds(pl.multiple_of(step * QUERIES, QUERIES), KEYS)
+    query, keys, grad = query_ref[...], key_ref[at, :], grad_ref[...]
+    grad = jnp.where(docs_ref[...] < last, grad, jnp.zeros((), grad.dtype))
+    scores = score_block(step, scale, query, keys, docs_ref[...], row_docs_ref[:, at])
+    probs = jnp.exp(scores - total_ref[:, :1])
+    prob_grad = matmul_nt(grad, value_ref[at, :])
+    inner = jnp.sum(probs * prob_grad, axis=1, keepdims=True)
+    raw_grad = (probs * (prob_grad - inner) * scale).astype(jnp.bfloat16)
+    query_grad_ref[...] = matmul(raw_grad, keys)
+    key_sum[at, :] += matmul_tn(raw_grad, query)
+    value_sum[at, :] += matmul_tn(probs.astype(jnp.bfloat16), grad)
+
+    @pl.when(step == pl.num_programs(0) - 1)
+    def _():
+        key_grad_ref[...] = key_sum[WINDOW:, :]
+        value_grad_ref[...] = value_sum[WINDOW:, :]
+
+
+def attend(scale, last, query, keys, value, docs, row_docs):
+    rows, head_dim = query.shape
+    whole = lambda a: pl.BlockSpec(a.shape, lambda i: (0, 0))
+    by_step = lambda c: pl.BlockSpec((QUERIES, c), lambda i: (i, 0))
+    return pl.pallas_call(
+        functools.partial(attend_kernel, scale, last),
+        grid=(rows // QUERIES,),
+        out_shape=[jax.ShapeDtypeStruct((rows, V_HEAD), jnp.bfloat16), jax.ShapeDtypeStruct((rows, 128), jnp.float32)],
+        in_specs=[by_step(head_dim), whole(keys), whole(value), by_step(1), whole(row_docs)],
+        out_specs=[by_step(V_HEAD), by_step(128)],
+        compiler_params=pltpu.CompilerParams(vmem_limit_bytes=48 * 2**20, dimension_semantics=("arbitrary",)),
+        name="attend",
+    )(query, keys, value, docs, row_docs)
+
+
+def attend_back(scale, last, query, keys, value, docs, row_docs, totals, grad):
+    rows, head_dim = query.shape
+    whole = lambda a: pl.BlockSpec(a.shape, lambda i: (0, 0))
+    by_step = lambda c: pl.BlockSpec((QUERIES, c), lambda i: (i, 0))
+    full = lambda c: pl.BlockSpec((rows, c), lambda i: (0, 0))
+    return pl.pallas_call(
+        functools.partial(attend_back_kernel, scale, last),
+        grid=(rows // QUERIES,),
+        out_shape=[
+            jax.ShapeDtypeStruct((rows, head_dim), jnp.float32),
+            jax.ShapeDtypeStruct((rows, head_dim), jnp.float32),
+            jax.ShapeDtypeStruct((rows, V_HEAD), jnp.float32),
+        ],
+        in_specs=[by_step(head_dim), whole(keys), whole(value), by_step(1), whole(row_docs), by_step(128), by_step(V_HEAD)],
+        out_specs=[by_step(head_dim), full(head_dim), full(V_HEAD)],
+        scratch_shapes=[pltpu.VMEM(keys.shape, jnp.float32), pltpu.VMEM(value.shape, jnp.float32)],
+        compiler_params=pltpu.CompilerParams(vmem_limit_bytes=48 * 2**20, dimension_semantics=("arbitrary",)),
+        name="attend_back",
+    )(query, keys, value, docs, row_docs, totals, grad)
+
+
+def front_kernel(tokens_ref, first_gain_ref, packed_ref, up_ref, latent_gain_ref, turn_ref, sway_ref,
+                 normed_ref, query_ref, key_ref, value_ref, latent_ref, compressed_ref):
+    low = jnp.bfloat16
+    values = tokens_ref[...].astype(jnp.float32)
+    r = lax.rsqrt(jnp.mean(values * values, axis=1, keepdims=True) + EPS)
+    normed = (values * r * first_gain_ref[...]).astype(low)
+    normed_ref[...] = normed
+    rest = QK_NOPE + 4 * QK_ROPE
+    first = matmul(normed, packed_ref[:, :rest])
+    latent = matmul(normed, packed_ref[:, rest:])
+    query_ref[:, :QK_NOPE] = first[:, :QK_NOPE].astype(low)
+    plain = first[:, QK_NOPE : QK_NOPE + 2 * QK_ROPE]
+    turned = (plain * turn_ref[...] + first[:, QK_NOPE + 2 * QK_ROPE :] * sway_ref[...]).astype(low)
+    query_ref[:, QK_NOPE:] = turned[:, :QK_ROPE]
+    compressed_ref[...] = latent
+    r = lax.rsqrt(jnp.mean(latent * latent, axis=1, keepdims=True) + EPS)
+    key_latent = (latent * r * latent_gain_ref[...]).astype(low)
+    latent_ref[...] = key_latent
+    both = matmul(key_latent, up_ref[...]).astype(low)
+    key_ref[:, :QK_NOPE] = both[:, :QK_NOPE]
+    key_ref[:, QK_NOPE:] = turned[:, QK_ROPE:]
+    value_ref[...] = both[:, QK_NOPE:]
+
+
+def front(tokens, first_gain, packed, up_head, latent_gain, turn, sway):
+    rows, width = tokens.shape
+    step = 256
+    low = jnp.bfloat16
+    whole = lambda a: pl.BlockSpec(a.shape, lambda i: (0, 0))
+    by_step = lambda c: pl.BlockSpec((step, c), lambda i: (i, 0))
+    head_dim = QK_NOPE + QK_ROPE
+    return pl.pallas_call(
+        front_kernel,
+        grid=(rows // step,),
+        out_shape=[
+            jax.ShapeDtypeStruct((rows, width), low),
+            jax.ShapeDtypeStruct((rows, head_dim), low),
+            jax.ShapeDtypeStruct((rows, head_dim), low),
+            jax.ShapeDtypeStruct((rows, V_HEAD), low),
+            jax.ShapeDtypeStruct((rows, KV_RANK), low),
+            jax.ShapeDtypeStruct((rows, KV_RANK), jnp.float32),
+        ],
+        in_specs=[by_step(width), whole(first_gain), whole(packed), whole(up_head), whole(latent_gain),
+                  by_step(2 * QK_ROPE), by_step(2 * QK_ROPE)],
+        out_specs=[by_step(width), by_step(head_dim), by_step(head_dim), by_step(V_HEAD), by_step(KV_RANK), by_step(KV_RANK)],
+        compiler_params=pltpu.CompilerParams(vmem_limit_bytes=48 * 2**20, dimension_semantics=("arbitrary",)),
+        name="front",
+    )(tokens, first_gain, packed, up_head, latent_gain, turn, sway)
 
 
 def tie(value, *awaited):
@@ -611,14 +869,28 @@
         return lax.dynamic_slice_in_dim(values, own_at, local_rows, 0)
 
     piece_rows = output_weight.shape[0] // plane
-    tokens_all, query_pieces, down_pieces, up_pieces, out_pieces = bundle(
+    half = QK_ROPE // 2
+    query_columns = lax.dynamic_slice_in_dim(query_weight, head_at * head_dim, head_dim, 1)
+    query_turn, key_turn = query_columns[:, QK_NOPE:], latent_down[:, KV_RANK:]
+    packed_half = jnp.concatenate(
+        [
+            query_columns,
+            key_turn,
+            query_turn[:, half:],
+            query_turn[:, :half],
+            key_turn[:, half:],
+            key_turn[:, :half],
+            latent_down[:, :KV_RANK],
+        ],
+        axis=1,
+    )
+    tokens_all, packed, up_pieces, out_pieces = bundle(
         1,
         SEQ_DEVICES,
         shards,
         [
             ("gather", tokens),
-            ("swap", lax.dynamic_slice_in_dim(query_weight, head_at * head_dim, head_dim, 1)),
-            ("swap", latent_down.T),
+            ("swap", packed_half),
             (
                 "swap",
                 lax.dynamic_slice_in_dim(
@@ -628,8 +900,7 @@
             ("swap", lax.dynamic_slice_in_dim(output_weight, plane_at * piece_rows, piece_rows, 0)),
         ],
     )
-    query_head = query_pieces.reshape(width, head_dim)
-    full_down = down_pieces.transpose(0, 2, 1).reshape(width, KV_RANK + QK_ROPE)
+    packed = packed.reshape(width, -1)
     up_head = up_pieces.reshape(KV_RANK, QK_NOPE + V_HEAD)
     other_out = other_rows(out_pieces)
     cotangent_late = tie(cotangent, other_out[0])[0]
@@ -649,8 +920,6 @@
     )
     down_units = lax.dynamic_slice_in_dim(shared_down, plane_at * units, units, 0)
 
-    all_tokens = tokens_all.reshape(SEQ, width).astype(jnp.float32)
-    normed_one = norm_scale(all_tokens, first_gain).astype(jnp.bfloat16)
     positions = jnp.arange(SEQ, dtype=jnp.int32)
     cosine_part, sine_part = rotary_tables(positions, QK_ROPE)
     sequence_count, entry_count = document_lengths.shape
@@ -658,33 +927,16 @@
     picked = jnp.arange(sequence_count, dtype=jnp.int32)[:, None] == sequence_at
     row_ends = jnp.sum(jnp.where(picked, ends, 0), axis=0)
     documents = jnp.sum((positions[:, None] >= row_ends[None, :]).astype(jnp.int32), axis=1)
-    real = (documents < entry_count - 1).astype(jnp.float32)
-    allowed = (
-        (documents[:, None] == documents[None, :])
-        & (positions[None, :] <= positions[:, None])
-        & (positions[None, :] > positions[:, None] - WINDOW)
-    )
-    query = matmul(normed_one, query_head)
-    query_nope = query[:, :QK_NOPE].astype(jnp.bfloat16)
-    query_rope = rotate(query[:, QK_NOPE:], cosine_part, sine_part).astype(jnp.bfloat16)
-    compressed = matmul(normed_one, full_down)
-    key_latent = norm_scale(compressed[:, :KV_RANK], latent_gain).astype(jnp.bfloat16)
-    key_rope = rotate(compressed[:, KV_RANK:], cosine_part, sine_part).astype(jnp.bfloat16)
-    keys_values = matmul(key_latent, up_head).astype(jnp.bfloat16)
-    key_nope = keys_values[:, :QK_NOPE]
-    value = keys_values[:, QK_NOPE:]
-
-    def scores_of():
-        raw = matmul_nt(query_nope, key_nope) + matmul_nt(query_rope, key_rope)
-        return jnp.where(allowed, raw * scale, NEG)
-
-    scores = scores_of()
-    top_score = jnp.max(scores, axis=1, keepdims=True)
-    expo = jnp.exp(scores - top_score)
-    expo_total = jnp.sum(expo, axis=1, keepdims=True)
-    log_total = top_score + jnp.log(expo_total)
-    probs = expo / expo_total
-    head_out = (matmul(probs.astype(jnp.bfloat16), value) * real[:, None]).astype(jnp.bfloat16)
+    turn = jnp.tile(jnp.concatenate([cosine_part, cosine_part], axis=1), (1, 2))
+    sway = jnp.tile(jnp.concatenate([-sine_part, sine_part], axis=1), (1, 2))
+    normed_one, query, keys, value, key_latent, compressed = front(
+        tokens_all.reshape(SEQ, width), first_gain[None], packed, up_head, latent_gain[None], turn, sway
+    )
+    ahead = ((WINDOW, 0), (0, 0))
+    keys, value = jnp.pad(keys, ahead), jnp.pad(value, ahead)
+    docs = documents[:, None]
+    row_docs = jnp.pad(docs, ahead, constant_values=-1).T
+    head_out, log_total = attend(scale, entry_count - 1, query, keys, value, docs, row_docs)
     gate_single = shard_rows(expert_gate[0])
     head_out, gate_single = tie(head_out, gate_single)
     heads_out, query_rows = bundle(
@@ -738,58 +990,44 @@
     picks = marks[:, None, :] & (
         ranks[:, None, :] == jnp.arange(capacity, dtype=jnp.int32)[None, :, None]
     )
-    select = picks.astype(jnp.bfloat16)
-
-    def to_slots(values):
-        return (
-            jnp.einsum(
-                "bct,btd->bcd",
-                select,
-                values.reshape(plane, local_rows, width),
-                preferred_element_type=jnp.float32,
-            )
-            .astype(jnp.bfloat16)
-            .reshape(plane * capacity, width)
-        )
-
-    def to_tokens(values):
-        return jnp.einsum(
-            "bct,bcd->btd",
-            select,
-            values.reshape(plane, capacity, width),
-            preferred_element_type=jnp.float32,
-        ).reshape(plane_rows, width)
-
-    slot_rows = to_slots(all_normed)
-    slot_cotangent = to_slots(all_grads).astype(jnp.float32)
+    senders = STEP_SENDERS
+    steps = plane // senders
+    pick = jnp.einsum(
+        "sbct,bd->sbcdt",
+        picks.reshape(steps, senders, capacity, local_rows).astype(jnp.bfloat16),
+        jnp.eye(senders, dtype=jnp.bfloat16),
+    ).reshape(steps, senders * capacity, senders * local_rows)
     slot_gate = jnp.sum(jnp.where(picks, gate_here[:, None, :], 0.0), axis=2).reshape(-1, 1)
-    gate_pre = matmul(slot_rows, gate_single)
-    up_pre = matmul(slot_rows, up_single)
-    swished, slope = swish_parts(gate_pre)
-    hidden = (swished * up_pre).astype(jnp.bfloat16)
-    expert_out = matmul(hidden, down_single).astype(jnp.bfloat16).astype(jnp.float32)
-    slot_gate_grad = jnp.sum(slot_cotangent * expert_out, axis=1).reshape(plane, capacity)
-    slot_grad = (slot_gate * slot_cotangent).astype(jnp.bfloat16)
-    hidden_grad = matmul_nt(slot_grad, down_single)
-    gate_pre_grad = (hidden_grad * up_pre * slope).astype(jnp.bfloat16)
-    up_pre_grad = (hidden_grad * swished).astype(jnp.bfloat16)
-    row_back = (
-        matmul_nt(gate_pre_grad, gate_single) + matmul_nt(up_pre_grad, up_single)
-    ).astype(jnp.bfloat16)
-
-    shared_pre = matmul(all_normed, gate_shared)
-    shared_up_pre = matmul(all_normed, up_shared)
-    shared_swished, shared_slope = swish_parts(shared_pre)
-    shared_hidden = (shared_swished * shared_up_pre).astype(jnp.bfloat16)
-    shared_hidden_grad = matmul_nt(all_grads, down_shared)
-    shared_gate_back = (shared_hidden_grad * shared_up_pre * shared_slope).astype(jnp.bfloat16)
-    shared_up_back = (shared_hidden_grad * shared_swished).astype(jnp.bfloat16)
-
-    normed_part = (
-        to_tokens(row_back)
-        + matmul_nt(shared_gate_back, gate_shared)
-        + matmul_nt(shared_up_back, up_shared)
-    ).astype(jnp.bfloat16)
+    lanes = ((0, 0), (0, -(shards * units) % 128))
+    (
+        normed_part,
+        output_part,
+        slot_rows,
+        slot_grad,
+        hidden,
+        gate_pre_grad,
+        up_pre_grad,
+        slot_gate_grad,
+        shared_hidden,
+        shared_gate_back,
+        shared_up_back,
+    ) = expert_pass(
+        pick,
+        pick.transpose(0, 2, 1),
+        slot_gate,
+        all_normed,
+        all_grads,
+        gate_single,
+        up_single,
+        down_single,
+        jnp.pad(gate_shared, lanes),
+        jnp.pad(up_shared, lanes),
+        jnp.pad(down_shared, lanes[::-1]),
+    )
+    slot_gate_grad = slot_gate_grad[:, 0].reshape(plane, capacity)
+    shared_hidden = shared_hidden[:, : shards * units]
+    shared_gate_back = shared_gate_back[:, : shards * units]
+    shared_up_back = shared_up_back[:, : shards * units]
     token_gate_grad = jnp.sum(jnp.where(picks, slot_gate_grad[:, :, None], 0.0), axis=1)
     expert_down_term = matmul_tn(hidden, slot_grad)
     back, gate_dense, down_blocks = bundle(
@@ -820,10 +1058,6 @@
         return own
 
     expert_down_grad = sum_shards(expert_down_term, down_blocks)[None]
-    output_part = (
-        to_tokens((slot_gate * expert_out).astype(jnp.bfloat16))
-        + matmul(shared_hidden, down_shared)
-    ).astype(jnp.bfloat16)
     output_part = tie(output_part, back)[0]
     output_sum = lax.psum_scatter(output_part, "expert", scatter_dimension=0, tiled=True)
     activations = (middle + output_sum.astype(jnp.float32)).astype(jnp.bfloat16)
@@ -882,15 +1116,6 @@
     middle_norm_grad, second_term = second_back(normed_grad)
     middle_grad = grad_out + middle_norm_grad
     middle_low = middle_grad.astype(jnp.bfloat16)
-    small_sums = lax.psum_scatter(
-        jnp.concatenate([router_term, second_term[:, None]], axis=1),
-        everyone,
-        scatter_dimension=0,
-        tiled=True,
-    )
-    router_weight_grad = small_sums[:, :plane]
-    second_gain_grad = small_sums[:, plane]
-
     heads_grad = split_matmul_nt(middle_low, output_weight, other_out).astype(jnp.bfloat16)
     heads_grad = heads_grad.reshape(local_rows, HEADS, V_HEAD).transpose(1, 0, 2)
     (head_grad,) = bundle(5, SEQ_DEVICES, shards, [("trade", heads_grad)])
@@ -898,22 +1123,14 @@
     all_middle = lax.all_gather(
         tie(middle_low, head_grad)[0], "expert", axis=0, tiled=True, axis_index_groups=groups
     )
-    head_grad = (head_grad.astype(jnp.float32) * real[:, None]).astype(jnp.bfloat16)
-    again = jnp.exp(scores_of() - log_total)
-    prob_grad = matmul_nt(head_grad, value)
-    raw_grad = (
-        again * (prob_grad - jnp.sum(again * prob_grad, axis=1, keepdims=True)) * scale
-    ).astype(jnp.bfloat16)
-    value_grad = matmul_tn(again.astype(jnp.bfloat16), head_grad)
-    key_nope_grad = matmul_tn(raw_grad, query_nope)
-    key_rope_grad = matmul_tn(raw_grad, query_rope)
+    query_raw, keys_grad, value_grad = attend_back(
+        scale, entry_count - 1, query, keys, value, docs, row_docs, log_total, head_grad
+    )
     query_grad = jnp.concatenate(
-        [
-            matmul(raw_grad, key_nope),
-            unrotate(matmul(raw_grad, key_rope), cosine_part, sine_part),
-        ],
+        [query_raw[:, :QK_NOPE], unrotate(query_raw[:, QK_NOPE:], cosine_part, sine_part)],
         axis=1,
     ).astype(jnp.bfloat16)
+    key_nope_grad, key_rope_grad = keys_grad[:, :QK_NOPE], keys_grad[:, QK_NOPE:]
     pair_grad = jnp.concatenate([key_nope_grad, value_grad], axis=1).astype(jnp.bfloat16)
     latent_up_term = matmul_tn(key_latent, pair_grad)
     key_grad_part = jnp.concatenate(
@@ -924,6 +1141,17 @@
         ],
         axis=1,
     ).astype(jnp.bfloat16)
+    query_term = matmul_tn(normed_one, query_grad)
+    query_moved, up_moved = (
+        lax.all_to_all(
+            term.astype(jnp.bfloat16).reshape(all_devices, -1, term.shape[1]),
+            everyone,
+            split_axis=0,
+            concat_axis=0,
+            tiled=True,
+        )
+        for term in (query_term, latent_up_term)
+    )
     own_key_grad, own_query_grad = bundle(
         6,
         SEQ_DEVICES,
@@ -936,7 +1164,7 @@
     own_key_grad = own_key_grad[:, : KV_RANK + QK_ROPE]
     own_query_grad = own_query_grad.transpose(1, 0, 2).reshape(local_rows, HEADS * head_dim)
     own_compressed = own_rows(compressed)
-    unused_latent, latent_back = jax.vjp(norm_scale, own_compressed[:, :KV_RANK], latent_gain)
+    unused_latent, latent_back = jax.vjp(norm_scale, own_compressed, latent_gain)
     latent_in_grad, latent_gain_term = latent_back(own_key_grad[:, :KV_RANK])
     rope_in_grad = unrotate(
         own_key_grad[:, KV_RANK:], own_rows(cosine_part), own_rows(sine_part)
@@ -950,58 +1178,60 @@
         blocks = moved.reshape((shards, plane) + moved.shape[1:]).astype(jnp.float32)
         return by_head(jnp.sum(blocks, axis=0))
 
-    query_term = matmul_tn(normed_one, query_grad)
-    column_grad, query_moved, up_moved = bundle(
-        7,
-        SEQ_DEVICES,
-        shards,
-        [
-            (
-                "trade",
-                compressed_grad.reshape(local_rows, SEQ_DEVICES, down_columns).transpose(1, 0, 2),
-            ),
-            ("owners", owner_blocks(query_term)),
-            ("owners", owner_blocks(latent_up_term)),
-        ],
+    column_grad = lax.all_to_all(
+        compressed_grad.reshape(local_rows, SEQ_DEVICES, down_columns).transpose(1, 0, 2),
+        "expert",
+        split_axis=0,
+        concat_axis=0,
+        tiled=True,
+        axis_index_groups=groups,
     )
     column_grad = column_grad.reshape(SEQ, down_columns)
     query_weight_grad = owner_sum(query_moved)
     latent_up_grad = owner_sum(up_moved)
-    normed_one_grad = split_matmul_nt(
-        own_query_grad, query_weight, other_query
-    ) + matmul_nt(compressed_grad, full_down)
+    packed_rope = packed[:, head_dim : head_dim + QK_ROPE]
+    packed_latent = packed[:, QK_NOPE + 4 * QK_ROPE :]
+    normed_one_grad = (
+        split_matmul_nt(own_query_grad, query_weight, other_query)
+        + matmul_nt(compressed_grad[:, :KV_RANK], packed_latent)
+        + matmul_nt(compressed_grad[:, KV_RANK:], packed_rope)
+    )
     unused_one, first_back = jax.vjp(norm_scale, hidden_rows, first_gain)
     input_norm_grad, first_term = first_back(normed_one_grad)
     input_grad = middle_grad + input_norm_grad
     down_term = matmul_tn(normed_one, column_grad)
     out_term = matmul_tn(head_out, all_middle.reshape(SEQ, width)).astype(jnp.bfloat16)
-    gain_terms = jnp.concatenate(
+    small_terms = jnp.concatenate(
         [
+            router_term.reshape(all_devices, -1),
+            second_term.reshape(all_devices, -1),
             first_term.reshape(all_devices, -1),
             latent_gain_term.reshape(all_devices, -1),
         ],
         axis=1,
     )
-    gain_columns = gain_terms.shape[1]
-    gain_terms = jnp.broadcast_to(
-        jnp.pad(gain_terms, ((0, 0), (0, -gain_columns % 128)))[:, None],
-        (all_devices, 8, gain_columns + -gain_columns % 128),
-    )
+    small_count = small_terms.shape[1]
+    small_terms = jnp.pad(small_terms, ((0, 0), (0, -small_count % 1024)))
+    small_terms = small_terms.reshape(all_devices, -1, 128)
     down_moved, gain_moved, out_moved = bundle(
         8,
         SEQ_DEVICES,
         shards,
         [
             ("owners", owner_blocks(down_term)),
-            ("owners", gain_terms),
+            ("owners", small_terms),
             ("rows", out_term.reshape(-1, width // all_devices, width)),
         ],
     )
     latent_down_grad = owner_sum(down_moved)
     output_weight_grad = jnp.sum(out_moved.astype(jnp.float32), axis=0)
-    gain_sums = jnp.sum(gain_moved[:, 0, :gain_columns], axis=0)
-    first_gain_grad = gain_sums[: width // all_devices]
-    latent_gain_grad = gain_sums[width // all_devices :]
+    small_sums = jnp.sum(gain_moved, axis=0).reshape(-1)[:small_count]
+    own_width = width // all_devices
+    at_second = own_width * plane
+    router_weight_grad = small_sums[:at_second].reshape(own_width, plane)
+    second_gain_grad = small_sums[at_second : at_second + own_width]
+    first_gain_grad = small_sums[at_second + own_width : at_second + 2 * own_width]
+    latent_gain_grad = small_sums[at_second + 2 * own_width :]
     return (
         activations,
         input_grad,

time: 1020 us -> 969 us (0.950)
  matrix products: 309 us -> 104 us
  Pallas kernels: 414 us -> 527 us
  waiting for transfers between devices: 52.5 us -> 99 us
  other arithmetic: 104 us -> 59.4 us
  starting transfers between devices: 9.31 us -> 32.5 us
  local copies, waits for them, and re-layouts: 109 us -> 125 us
    pallas_call x0 -> x4, Pallas kernels: none -> 123 us  [the longest x1 81.5 us: expert_pass(): pl.pallas_call(expert_kernel, grid=(steps,), out_shape=out_shape, in_spec...]
    dot_general x15 -> x7, matrix products: 113 us -> 22.2 us  [matmul_nt(): lax.dot_general(left, right, (((1,), (1,)), ((), ())), preferred_element_...]
    dot_general x15 -> x3, matrix products: 94.5 us -> 13.8 us  [matmul(): return jnp.dot(left, right, preferred_element_type=jnp.float32)]
    ppermute x2, waiting for transfers between devices: 27.5 us -> 64.1 us  [shard_ring(): lax.ppermute(block, 'shard', [(source, (source + step) % count) for sourc...]
    all_to_all x0 -> x3, waiting for transfers between devices: none -> 34.1 us  [the longest x2 26.9 us: on_device(): lax.all_to_all(term.astype(jnp.bfloat16).reshape(all_devices, -1, term.sh...]
    convert_element_type x6 -> x0, other arithmetic: 33 us -> none  [the longest x2 17.3 us: on_device(): normed_one = norm_scale(all_tokens, first_gain).astype(jnp.bfloat16)]
    dot_general x4 -> x0, matrix products: 28.3 us -> none  [the longest x2 18.5 us: to_tokens(): jnp.einsum('bct,bcd->btd', select, values.reshape(plane, capacity, width)...]
    all_gather x1, waiting for transfers between devices: 24.9 us -> 0.01 us  [on_device(): lax.all_gather(tie(middle_low, head_grad)[0], 'expert', axis=0, tiled=Tru...]
  transfers between devices with their start and end apart: 12 -> 14, of which waited for: 2 -> 5; matrix products, arithmetic and copies ran while one was open for 37% -> 27% of each run, Pallas kernels for 24% -> 51%
where the time goes in v3:
time: 969 us; the launch traced here: 962 us
  Pallas kernels  527 us (54%)
  local copies, waits for them, and re-layouts  125 us (13%)
  matrix products  104 us (11%)
  waiting for transfers between devices  99 us (10%)
  other arithmetic  59.4 us (6%)
  starting transfers between devices  32.5 us (3%)
  between operations  15.4 us (2%)
    pallas_call x7, Pallas kernels, bundle(): pl.pallas_call(functools.partial(bundle_kernel, group, shards, tuple(kind...  403 us
    pallas_call x1, Pallas kernels, expert_pass(): pl.pallas_call(expert_kernel, grid=(steps,), out_shape=out_shape, in_spec...  81.5 us
    ppermute x2, waiting for transfers between devices, shard_ring(): lax.ppermute(block, 'shard', [(source, (source + step) % count) for sourc...  64.1 us
    dot_general x10, matrix products, matmul_tn(): lax.dot_general(left, right, (((0,), (0,)), ((), ())), preferred_element_...  64 us
    all_to_all x2, waiting for transfers between devices, on_device(): lax.all_to_all(term.astype(jnp.bfloat16).reshape(all_devices, -1, term.sh...  26.9 us
    unnamed x141, local copies, waits for them, and re-layouts  24.1 us
    dot_general x7, matrix products, matmul_nt(): lax.dot_general(left, right, (((1,), (1,)), ((), ())), preferred_element_...  22.2 us
  transfers between devices with their start and end apart: 14, of which 5 were waited for; matrix products, arithmetic and copies ran while one was open for 27% of the time, Pallas kernels for 51%

profile of v3, /device:TPU:9, one launch (start us, length us, event | category | flops | bytes accessed | tf_op | source)
XLA Modules:
  0.0 961.8 jit_solution(7796606280487820722)
XLA Ops:
  14.3 2.1 constant_dynamic-slice_fusion.1
  16.3 4.9 concatenate.59.refs_1_
  23.7 70.5 %bundle_gather_swap.1 = (bf16[16,2,64,2048]{3,2,1,0:T(8,128)(2,1)}, bf16[2,1024,896]{2,1,0:T(8,128)(2,1)}, bf16[2,256,256]{2,1,0:T(8,128)(2,1)S(1)}, bf16[2,64,2048]{2,1,0:T(8,128)(2,1)S(1)}) custom-call(bf16[2,64,2048]{2,1,0:T(8,128)(2,1)S(1)} %bitcast.233, bf16[1024,896]{1,0:T(8,128)(2,1)S(1)} %copy-done.6, ...), custom_call_target="tpu_custom_call" | custom-call | tf_op jit(solution)/shard_map/bundle_gather_swap/pallas_call | solution.py:488
  96.7 3.7 fusion.19
  107.9 17.7 %front.1 = (bf16[2048,2048]{1,0:T(8,128)(2,1)}, bf16[2048,192]{1,0:T(8,128)(2,1)S(1)}, bf16[2048,192]{1,0:T(8,128)(2,1)S(1)}, bf16[2048,128]{1,0:T(8,128)(2,1)S(...) custom-call(bf16[2048,2048]{1,0:T(8,128)(2,1)} %bitcast.265, f32[1,2048]{1,0:T(1,128)S(1)} %bitcast.254, ...), custom_call_target="tpu_custom_call" | custom-call | tf_op jit(solution)/shard_map/front/pallas_call | solution.py:736
  130.9 8.6 attend.1
  139.9 1.9 copy-done.42
  143.4 16.3 %collective-permute-done = bf16[1024,1408]{1,0:T(8,128)(2,1)} collective-permute-done((bf16[1024,1408]{1,0:T(8,128)(2,1)}, bf16[1024,1408]{1,0:T(8,128)(2,1)}, u32[]{:S(2)}, u32[]{:S(2)}) %collective-permute-start) | collective-permute-done | bytes 2883616 | tf_op jit(solution)/shard_map/ppermute | solution.py:805
  159.7 2.3 bitcast_dynamic-update-slice_fusion.1
  162.1 2.5 copy-done.30
  164.6 28.1 %bundle_trade_swap.1 = (bf16[16,128,128]{2,1,0:T(8,128)(2,1)S(1)}, bf16[2,64,3072]{2,1,0:T(8,128)(2,1)S(1)}) custom-call(bf16[16,128,128]{2,1,0:T(8,128)(2,1)S(1)} %bitcast.235, bf16[64,3072]{1,0:T(8,128)(2,1)S(1)} %constant_dynamic-slice_fusion.10.refs_1_), custom_call_target="tpu_custom_call" | custom-call | tf_op jit(solution)/shard_map/bundle_trade_swap/pallas_call | solution.py:488
  200.4 3.3 broadcast_in_dim.172
  206.4 4.0 fusion.54
  210.5 47.8 %collective-permute-done.1 = bf16[704,2048]{1,0:T(8,128)(2,1)} collective-permute-done((bf16[704,2048]{1,0:T(8,128)(2,1)}, bf16[704,2048]{1,0:T(8,128)(2,1)}, u32[]{:S(2)}, u32[]{:S(2)}) %collective-permute-start.1) | collective-permute-done | bytes 2883616 | tf_op jit(solution)/shard_map/ppermute | solution.py:805
  258.3 3.8 bitcast_dynamic-update-slice_fusion
  262.0 3.3 multiply_reduce_fusion.2
  266.4 92.1 %bundle_gather_gather.1 = (bf16[16,2,64,2048]{3,2,1,0:T(8,128)(2,1)}, s32[16,1,8,128]{3,2,1,0:T(8,128)S(1)}, bf16[2,1024,1408]{2,1,0:T(8,128)(2,1)}, bf16[2,176,...) custom-call(bf16[2,64,2048]{2,1,0:T(8,128)(2,1)S(1)} %bitcast.234, ...), custom_call_target="tpu_custom_call" | custom-call | tf_op jit(solution)/shard_map/bundle_gather_gather/pallas_call | solution.py:488
  358.5 6.4 fusion.83
  369.4 2.3 reshape.361.pick_ref
  371.7 2.3 copy.261
  375.3 2.4 pad.40.shared_gate_w
  379.0 2.4 pad.41.shared_up_w
  382.6 81.5 %experts.1 = (bf16[2048,2048]{1,0:T(8,128)(2,1)}, bf16[2048,2048]{1,0:T(8,128)(2,1)}, bf16[1024,2048]{1,0:T(8,128)(2,1)}, bf16[1024,2048]{1,0:T(8,128)(2,1)}, bf...) custom-call(bf16[4,256,512]{2,1,0:T(8,128)(2,1)} %reshape.361.pick_r, ...), custom_call_target="tpu_custom_call" | custom-call | tf_op jit(solution)/shard_map/experts/pallas_call | solution.py:591
  465.7 12.2 %fusion.82 = (bf16[1408,2048]{1,0:T(8,128)(2,1)}, f32[1408,2048]{1,0:T(8,128)}) fusion(bf16[1024,1408]{1,0:T(8,128)(2,1)} %get-tuple-element.85, bf16[1024,2048]{1,0:T(8,128)(2,1)} %get-tuple-element.86), kind=kOutput, calls=%fused_computation.189 | convolution fusion | flops 5908463616 | bytes 24379392 | tf_op jit(solution)/shard_map/dot_general | solution.py:35
  477.9 94.9 %bundle_reduce_trade.2 = (f32[4,32,2048]{2,1,0:T(8,128)S(1)}, f32[16,8,128]{2,1,0:T(8,128)S(1)}, bf16[2,704,2048]{2,1,0:T(8,128)(2,1)}) custom-call(bf16[16,4,32,2048]{3,2,1,0:T(8,128)(2,1)} %bitcast.266, f32[16,8,128]{2,1,0:T(8,128)S(1)} %broadcast_in_dim.176.refs_1_, bf16[2,704,2048]{2,1,0:T(8,128)(2,1)} %bitcast.275), custom_call_target="tpu_custom_call" | custom-call | tf_op jit(solution)/shard_map/bundle_reduce_trade/pallas_call | solution.py:488
  574.3 12.6 %copy.282 = bf16[2048,2048]{1,0:T(8,128)(2,1)} copy(bf16[2048,2048]{0,1:T(8,128)(2,1)} %bitcast.258) | data formatting | bytes 16777216 | tf_op jit(solution)/shard_map/dot_general | solution.py:35
  588.4 2.2 multiply_reduce_fusion
  593.6 3.8 fusion.16
  599.0 24.5 %bundle_trade.1 = bf16[16,128,128]{2,1,0:T(8,128)(2,1)S(1)} custom-call(bf16[16,128,128]{2,1,0:T(8,128)(2,1)S(1)} %bitcast.239), custom_call_target="tpu_custom_call" | custom-call | tf_op jit(solution)/shard_map/bundle_trade/pallas_call | solution.py:488
  623.6 12.0 %fusion.86 = f32[2048,1408]{1,0:T(8,128)} fusion(bf16[1024,2048]{1,0:T(8,128)(2,1)} %get-tuple-element.108, bf16[1024,1408]{1,0:T(8,128)(2,1)} %get-tuple-element.110), kind=kOutput, calls=%fused_computation.193 | convolution fusion | flops 5905580032 | bytes 18612224 | tf_op jit(solution)/shard_map/dot_general | solution.py:35
  635.6 15.5 %attend_back.1 = (f32[2048,192]{1,0:T(8,128)}, f32[2048,192]{1,0:T(8,128)}, f32[2048,128]{1,0:T(8,128)S(1)}) custom-call(bf16[2048,192]{1,0:T(8,128)(2,1)S(1)} %copy-done.11, bf16[3072,192]{1,0:T(8,128)(2,1)} %copy-done.2, bf16[3072,128]{1,0:T(8,128)(2,1)S(1)} %pad.36.value_ref, s32[2048,1]{1,0:T(8,128)S(1)} %copy-done.5, ...), custom_call_target="tpu_custom_call" | custom-call | tf_op jit(solution)/shard_map/attend_back/pallas_call | solution.py:689
  652.5 2.1 slice.204
  654.6 4.6 fusion.5
  660.0 6.9 fusion.85
  670.1 4.8 fusion.21
  676.7 60.0 %bundle_reduce_trade.3 = (f32[4,32,640]{2,1,0:T(8,128)S(1)}, bf16[16,128,192]{2,1,0:T(8,128)(2,1)S(1)}) custom-call(bf16[16,4,32,640]{3,2,1,0:T(8,128)(2,1)S(1)} %maximum_maximum_fusion.refs_0_, bf16[16,128,192]{2,1,0:T(8,128)(2,1)S(1)} %pad_maximum_fusion.3.refs_1_), custom_call_target="tpu_custom_call" | custom-call | tf_op jit(solution)/shard_map/bundle_reduce_trade/pallas_call | solution.py:488
  740.9 8.2 all-to-all-start
  749.0 3.3 convolution_convert_fusion.6
  752.3 7.2 all-to-all-done
  759.5 5.1 all-to-all-start.2
  764.6 6.2 convolution_convert_fusion
  770.9 2.2 copy.278
  773.1 15.5 %all-to-all-done.2 = bf16[32,16,256]{2,1,0:T(8,128)(2,1)} async-done(((bf16[32,16,256]{2,1,0:T(8,128)(2,1)}), bf16[32,16,256]{2,1,0:T(8,128)(2,1)}, u32[]{:S(2)}, u32[]{:S(2)}) %all-to-all-start.2) | async-done | bytes 262176 | tf_op jit(solution)/shard_map/all_to_all | solution.py:1146
  788.5 7.5 all-to-all-start.1
  796.0 6.0 convolution_convert_fusion.5
  802.1 5.7 convolution_convert_fusion.4
  809.6 11.4 %all-to-all-done.1 = bf16[32,64,192]{2,1,0:T(8,128)(2,1)} async-done(((bf16[32,64,192]{2,1,0:T(8,128)(2,1)}), bf16[32,64,192]{2,1,0:T(8,128)(2,1)}, u32[]{:S(2)}, u32[]{:S(2)}) %all-to-all-start.1) | async-done | bytes 786464 | tf_op jit(solution)/shard_map/all_to_all | solution.py:1146
  821.1 5.8 all-to-all-start.3
  826.9 5.4 fusion.43
  836.5 2.5 reshape.376
  841.5 5.7 fusion.14
  847.1 7.5 convert_add_fusion
  864.4 3.0 convert_reduce_fusion
  867.4 3.9 reshape.388
  877.1 6.5 fusion.2
  883.7 6.6 fusion.3
  890.2 5.4 fusion.11
  895.6 2.6 copy.293
  898.2 2.8 convolution_add_fusion.1
  901.0 2.6 fusion.29
  903.9 3.4 fusion.25
  907.3 4.8 convolution_convert_fusion.1
  912.1 33.5 %bundle_owners_owners.1 = (bf16[32,64,36]{2,1,0:T(8,128)(2,1)S(1)}, f32[32,16,128]{2,1,0:T(8,128)S(1)}, bf16[2,64,2048]{2,1,0:T(8,128)(2,1)S(1)}) custom-call(bf16[32,64,36]{2,1,0:T(8,128)(2,1)S(1)} %bitcast.238, f32[32,16,128]{2,1,0:T(8,128)S(1)} %bitcast.246, bf16[2,64,2048]{2,1,0:T(8,128)(2,1)S(1)} %bitcast.237), custom_call_target="tpu_custom_call" | custom-call | tf_op jit(solution)/shard_map/bundle_owners_owners/pallas_call | solution.py:488
  951.5 1.9 reshape.402
  (288 shorter events, 98.0 us)
Async XLA Ops:
  7.2 14.1 %copy-start = (bf16[256,4096]{1,0:T(8,128)(2,1)S(1)}, bf16[256,4096]{1,0:T(8,128)(2,1)}, u32[]{:S(2)}) copy-start(bf16[256,4096]{1,0:T(8,128)(2,1)} %param.25) | copy-start | bytes 6291460
  7.2 3.5 slice-start.2
  7.2 4.9 slice-start.3
  7.2 185.5 %all-gather.7.cloned.1.call-start = ((), (), s32[]{:S(2)}) async-start(), calls=%async_computation.6 | async-start | bytes 8912896 | tf_op jit(solution)/shard_map/all_gather | solution.py:907
  8.0 254.1 %all-gather.5.cloned.1.call-start = ((), (), s32[]{:S(2)}) async-start(), calls=%async_computation.5 | async-start | bytes 4456448 | tf_op jit(solution)/shard_map/all_gather | solution.py:769
  12.1 10.2 %copy-start.3 = (bf16[128,2048]{1,0:T(8,128)(2,1)S(1)}, bf16[128,2048]{1,0:T(8,128)(2,1)}, u32[]{:S(2)}) copy-start(bf16[128,2048]{1,0:T(8,128)(2,1)} %param.18) | copy-start | bytes 1572868
  94.3 13.6 %copy-start.13 = (bf16[2,256,256]{2,1,0:T(8,128)(2,1)}, bf16[2,256,256]{2,1,0:T(8,128)(2,1)S(1)}, u32[]{:S(2)}) copy-start(bf16[2,256,256]{2,1,0:T(8,128)(2,1)S(1)} %get-tuple-element.66) | copy-start | bytes 786436
  95.1 795.2 %all-gather.9.cloned.1.call-start = ((), (), s32[]{:S(2)}) async-start(), calls=%async_computation.8 | async-start | bytes 6684672 | tf_op jit(solution)/shard_map/all_gather | solution.py:769
  95.3 64.4 %collective-permute-start = (bf16[1024,1408]{1,0:T(8,128)(2,1)}, bf16[1024,1408]{1,0:T(8,128)(2,1)}, u32[]{:S(2)}, u32[]{:S(2)}) collective-permute-start(bf16[1024,1408]{1,0:T(8,128)(2,1)} %bitcast.286), channel_id=1, source_target_pairs={{0,16},{16,0},{1,17},{17,1},{2,18},{18,2},{3,19},{19,3},{4,20},{20... | collective-permute-start | bytes 8650760 | tf_op jit(solution)/shard_map/ppermute | solution.py:805
  102.3 5.6 copy-start.25
  102.3 5.6 copy-start.27
  107.9 18.7 %copy-start.53 = (s32[2,4]{1,0:T(2,128)S(1)}, s32[2,4]{1,0:T(2,128)}, u32[]{:S(2)}) copy-start(s32[2,4]{1,0:T(2,128)} %param.19) | copy-start | bytes 100
  126.6 13.3 %copy-start.2 = (bf16[3072,192]{1,0:T(8,128)(2,1)}, bf16[3072,192]{1,0:T(8,128)(2,1)S(1)}, u32[]{:S(2)}) copy-start(bf16[3072,192]{1,0:T(8,128)(2,1)S(1)} %pad.35.key_ref) | copy-start | bytes 3538948
  139.4 2.8 copy-start.15
  139.4 25.1 %copy-start.7 = (bf16[2048,128]{1,0:T(8,128)(2,1)}, bf16[2048,128]{1,0:T(8,128)(2,1)S(1)}, u32[]{:S(2)}) copy-start(bf16[2048,128]{1,0:T(8,128)(2,1)S(1)} %get-tuple-element.71) | copy-start | bytes 1572868
  162.1 37.2 %copy-start.52 = (s32[128,6]{0,1:T(8,128)S(1)}, s32[128,6]{0,1:T(8,128)}, u32[]{:S(2)}) copy-start(s32[128,6]{0,1:T(8,128)} %param.20) | copy-start | bytes 9220
  193.5 710.4 %reduce-scatter.2.cloned.1.call-start = ((), (), s32[]{:S(2)}) async-start(), calls=%async_computation.7 | async-start | bytes 8912896 | tf_op jit(solution)/shard_map/reduce_scatter | solution.py:1062
  193.8 64.5 %collective-permute-start.1 = (bf16[704,2048]{1,0:T(8,128)(2,1)}, bf16[704,2048]{1,0:T(8,128)(2,1)}, u32[]{:S(2)}, u32[]{:S(2)}) collective-permute-start(bf16[704,2048]{1,0:T(8,128)(2,1)} %bitcast.287), channel_id=1, source_target_pairs={{0,16},{16,0},{1,17},{17,1},{2,18},{18,2},{3,19},{19,3},{4,20},{20... | collective-permute-start | bytes 8650760 | tf_op jit(solution)/shard_map/ppermute | solution.py:805
  199.2 4.4 copy-start.43
  210.5 51.6 %copy-start.47 = (bf16[128,16,128]{0,2,1:T(8,128)(2,1)S(1)}, bf16[128,16,128]{0,2,1:T(8,128)(2,1)}, u32[]{:S(2)}) copy-start(bf16[128,16,128]{0,2,1:T(8,128)(2,1)} %copy.254) | copy-start | bytes 1572868
  262.0 3.4 copy-start.51
  265.4 99.6 %copy-start.56 = (f32[128]{0:T(128)}, f32[128]{0:T(128)S(1)}, u32[]{:S(2)}) copy-start(f32[128]{0:T(128)S(1)} %get-tuple-element.225) | copy-start | bytes 1540
  265.4 93.1 %copy-start.50 = (bf16[2048,16]{0,1:T(8,128)(2,1)S(1)}, bf16[2048,16]{0,1:T(8,128)(2,1)}, u32[]{:S(2)}) copy-start(bf16[2048,16]{0,1:T(8,128)(2,1)} %param.28) | copy-start | bytes 196612
  358.5 6.5 copy-start.17
  358.5 6.5 copy-start.19
  358.5 6.5 copy-start.21
  365.2 8.8 copy-start.20
  369.4 8.3 copy-start.18
  375.3 6.1 copy-start.22
  572.8 334.4 %all-gather.11.cloned.1.call-start = ((), (), s32[]{:S(2)}) async-start(), calls=%async_computation.9 | async-start | bytes 8912896 | tf_op jit(solution)/shard_map/all_gather | solution.py:1123
  574.0 12.8 %copy-start.54 = (f32[128]{0:T(128)}, f32[128]{0:T(128)S(1)}, u32[]{:S(2)}) copy-start(f32[128]{0:T(128)S(1)} %multiply_reduce_fusion.5) | copy-start | bytes 1540
  574.2 16.4 %copy-start.57 = (f32[128]{0:T(128)S(1)}, f32[128]{0:T(128)}, u32[]{:S(2)}) copy-start(f32[128]{0:T(128)} %copy-done.56) | copy-start | bytes 1540
  593.5 5.2 copy-start.33
  593.5 3.9 copy-start.31
  623.5 12.0 %copy-start.5 = (s32[2048,1]{1,0:T(8,128)S(1)}, s32[2048,1]{1,0:T(8,128)}, u32[]{:S(2)}) copy-start(s32[2048,1]{1,0:T(8,128)} %copy.253.docs_ref) | copy-start | bytes 24580
  623.5 12.0 %copy-start.11 = (bf16[2048,192]{1,0:T(8,128)(2,1)S(1)}, bf16[2048,192]{1,0:T(8,128)(2,1)}, u32[]{:S(2)}) copy-start(bf16[2048,192]{1,0:T(8,128)(2,1)} %copy-done.9) | copy-start | bytes 2359300
  623.5 12.0 %copy-start.16 = (f32[2048,128]{1,0:T(8,128)S(1)}, f32[2048,128]{1,0:T(8,128)}, u32[]{:S(2)}) copy-start(f32[2048,128]{1,0:T(8,128)} %copy-done.15) | copy-start | bytes 3145732
  651.0 9.0 copy-start.58
  651.0 9.0 copy-start.59
  652.5 22.7 %copy-start.46 = (bf16[2048,128]{1,0:T(8,128)(2,1)}, bf16[2048,128]{1,0:T(8,128)(2,1)S(1)}, u32[]{:S(2)}) copy-start(bf16[2048,128]{1,0:T(8,128)(2,1)S(1)} %slice.206) | copy-start | bytes 1572868
  659.3 217.8 %collective-permute-start.4 = (bf16[1024,1408]{1,0:T(8,128)(2,1)}, bf16[1024,1408]{1,0:T(8,128)(2,1)}, u32[]{:S(2)}, u32[]{:S(2)}) collective-permute-start(bf16[1024,1408]{1,0:T(8,128)(2,1)} %fusion.5), channel_id=1, source_target_pairs={{0,16},{16,0},{1,17},{17,1},{2,18},{18,2},{3,19},{19,3},{4,20},{20... | collective-permute-start | bytes 8650760 | tf_op jit(solution)/shard_map/ppermute | solution.py:824
  666.9 8.0 copy-start.34
  666.9 3.1 copy-start.41
  668.7 214.9 %collective-permute-start.3 = (bf16[1024,1408]{1,0:T(8,128)(2,1)}, bf16[1024,1408]{1,0:T(8,128)(2,1)}, u32[]{:S(2)}, u32[]{:S(2)}) collective-permute-start(bf16[1024,1408]{1,0:T(8,128)(2,1)} %fusion.4), channel_id=1, source_target_pairs={{0,16},{16,0},{1,17},{17,1},{2,18},{18,2},{3,19},{19,3},{4,20},{20... | collective-permute-start | bytes 8650760 | tf_op jit(solution)/shard_map/ppermute | solution.py:824
  669.5 5.7 copy-start.14
  669.6 6.4 copy-start.45
  676.0 61.9 %copy-start.55 = (f32[128]{0:T(128)S(1)}, f32[128]{0:T(128)}, u32[]{:S(2)}) copy-start(f32[128]{0:T(128)} %copy-done.54) | copy-start | bytes 1540
  740.9 18.6 %all-to-all-start = ((bf16[16,128,36]{1,2,0:T(8,128)(2,1)}), bf16[16,128,36]{1,2,0:T(8,128)(2,1)S(1)}, u32[]{:S(2)}, u32[]{:S(2)}) async-start(bf16[16,128,36]{1,2,0:T(8,128)(2,1)} %bitcast.303), calls=%async_computation.1 | async-start | bytes 327680 | tf_op jit(solution)/shard_map/all_to_all | solution.py:1181
  759.5 29.0 %all-to-all-start.2 = ((bf16[32,16,256]{2,1,0:T(8,128)(2,1)}), bf16[32,16,256]{2,1,0:T(8,128)(2,1)}, u32[]{:S(2)}, u32[]{:S(2)}) async-start(bf16[32,16,256]{2,1,0:T(8,128)(2,1)} %bitcast.308), calls=%async_computation.3 | async-start | bytes 524288 | tf_op jit(solution)/shard_map/all_to_all | solution.py:1146
  788.5 32.5 %all-to-all-start.1 = ((bf16[32,64,192]{2,1,0:T(8,128)(2,1)}), bf16[32,64,192]{2,1,0:T(8,128)(2,1)}, u32[]{:S(2)}, u32[]{:S(2)}) async-start(bf16[32,64,192]{2,1,0:T(8,128)(2,1)} %bitcast.281), calls=%async_computation.2 | async-start | bytes 2097152 | tf_op jit(solution)/shard_map/all_to_all | solution.py:1146
  796.0 6.1 copy-start.60
  821.1 43.3 %all-to-all-start.3 = ((bf16[32,64,352]{2,1,0:T(8,128)(2,1)}), bf16[32,64,352]{2,1,0:T(8,128)(2,1)}, u32[]{:S(2)}, u32[]{:S(2)}) async-start(bf16[32,64,352]{2,1,0:T(8,128)(2,1)} %pad_maximum_fusion), calls=%async_computation.4 | async-start | bytes 3145728 | tf_op jit(solution)/shard_map/all_to_all | solution.py:1072
  833.6 23.7 %collective-permute-start.2 = (bf16[88,2048]{1,0:T(8,128)(2,1)S(1)}, bf16[88,2048]{1,0:T(8,128)(2,1)}, u32[]{:S(2)}, u32[]{:S(2)}) collective-permute-start(bf16[88,2048]{1,0:T(8,128)(2,1)S(1)} %fusion.51), channel_id=1, source_target_pairs={{0,16},{16,0},{1,17},{17,1},{2,18},{18,2},{3,19},{19,3},{4,20},{20... | collective-permute-start | bytes 1081352 | tf_op jit(solution)/shard_map/ppermute | solution.py:824
  841.5 13.3 %slice-start = ((s8[8388608]{0:T(1024)(128)(4,1)}), s8[4194304]{0:T(1024)(128)(4,1)S(1)}, s32[]{:S(2)}) async-start(s8[8388608]{0:T(1024)(128)(4,1)} %bitcast.263), calls=%async_computation.10 | async-start | bytes 8388608
  847.1 7.6 slice-start.1
  854.7 2.6 copy-start.39
  883.6 6.6 copy-start.48
  895.6 5.4 copy-start.26
  898.2 5.5 copy-start.49
  898.2 5.7 copy-start.29
  898.2 5.7 copy-start.35
  903.6 3.7 copy-start.8
  907.2 4.8 copy-start.12
  907.2 47.8 %copy-start.1 = (bf16[256,4096]{1,0:T(8,128)(2,1)S(1)}, bf16[256,4096]{1,0:T(8,128)(2,1)}, u32[]{:S(2)}) copy-start(bf16[256,4096]{1,0:T(8,128)(2,1)} %param.25) | copy-start | bytes 6291460
  (15 other events, 20.2 us)
Sparse Core Ops, SparseCore 0:
  10.2 102.4 all-gather.6
  115.5 51.0 all-gather.4
  193.6 62.6 all-gather.8
  572.9 113.1 reduce-scatter.1
  688.1 95.0 all-gather.10

commit v4 on v3

--- a/solution.py
+++ b/solution.py
@@ -178,10 +178,13 @@
         def _():
             push(0, block, piece, place.me).wait_recv()
 
-    pieces = own_ref.shape[0]
+    pieces = out_ref.shape[1]
+    if own_ref is None:
+        own_ref = out_ref.at[local]
+    else:
+        keep = pltpu.make_async_copy(own_ref, out_ref.at[local], copy_sem)
+        keep.start()
     row_at, twin_at = place.me + place.row_step, place.me + place.twin_step
-    keep = pltpu.make_async_copy(own_ref, out_ref.at[local], copy_sem)
-    keep.start()
     for piece in range(pieces):
         sender.start(place.upper, push(0, local, piece, place.me + INNER, own_ref))
         sender.start(place.lower, push(1, local, piece, place.me - INNER, own_ref))
@@ -206,7 +209,8 @@
             for there, block, *_ in place.along(step)[: 1 if step == 0 else 2]:
                 arrive(there, block + place.twin_step, piece)
                 arrive(there, block + place.twin_step + place.row_step, piece)
-    keep.wait()
+    if copy_sem is not None:
+        keep.wait()
     yield
 
 
@@ -511,27 +515,61 @@
 
 
 def expert_kernel(
-    pick_ref, place_ref, gate_ref, rows_in, grads_in, gate_w, up_w, down_w, shared_gate_w, shared_up_w, shared_down_w,
+    me_ref, routes_ref, router_ref, rows_in, grads_in, gate_w, up_w, down_w, shared_gate_w, shared_up_w, shared_down_w,
     back_ref, out_ref, rows_ref, grad_ref, hidden_ref, gate_back_ref, up_back_ref, score_ref,
-    shared_hidden_ref, shared_gate_back_ref, shared_up_back_ref, slot_cotangent,
+    shared_hidden_ref, shared_gate_back_ref, shared_up_back_ref, slot_cotangent, pick_buf, gate_buf,
 ):
     width = rows_in.shape[1]
     hidden_width = gate_w.shape[1]
+    shards, own_width, _ = shared_gate_w.shape
+    senders, _, rows = routes_ref.shape
+    capacity = pick_buf.shape[0] // senders
+    experts = router_ref.shape[0]
     low = jnp.bfloat16
-    gate = gate_ref[...]
-    pick = pick_ref[0]
+    me = me_ref[0, 0]
+
+    @pl.when(pl.program_id(0) == 0)
+    def _():
+        pick_buf[...] = jnp.zeros_like(pick_buf)
+
+    logits = matmul_nt(router_ref[...], rows_in[...])
+    names = lax.broadcasted_iota(jnp.int32, (experts, rows), 0)
+    earlier = lax.broadcasted_iota(jnp.int32, (rows, rows), 0) <= lax.broadcasted_iota(jnp.int32, (rows, rows), 1)
+    earlier = jnp.where(earlier, 1.0, 0.0).astype(low)
+    slot_names = lax.broadcasted_iota(jnp.int32, (capacity, rows), 0).astype(jnp.float32)
+    picks = []
+    for sender in range(senders):
+        routed = routes_ref[sender]
+        chosen = jnp.zeros((experts, rows), jnp.float32)
+        for choice in range(TOP):
+            chosen = chosen + jnp.where(routed[choice : choice + 1] == names, 1.0, 0.0)
+        logit = jnp.where(chosen > 0.0, logits[:, sender * rows : (sender + 1) * rows], NEG)
+        expo = jnp.exp(logit - jnp.max(logit, axis=0, keepdims=True)) * chosen
+        dense = expo / jnp.sum(expo, axis=0, keepdims=True)
+        gate_row = jnp.sum(jnp.where(names == me, dense, 0.0), axis=0, keepdims=True)
+        mark = jnp.sum(jnp.where(routed == me, 1.0, 0.0), axis=0, keepdims=True)
+        rank = matmul(jnp.broadcast_to(mark, (8, rows)).astype(low), earlier)[:1] - 1.0
+        pick = jnp.where((slot_names == rank) & (mark > 0.0), 1.0, 0.0)
+        picks.append(pick)
+        at = slice(sender * capacity, (sender + 1) * capacity)
+        pick_buf[at, sender * rows : (sender + 1) * rows] = pick.astype(low)
+        gate_buf[at, :] = jnp.sum(pick * gate_row, axis=1, keepdims=True)
+    gate = gate_buf[...]
 
     def pick_step(index, _):
         at = pl.ds(pl.multiple_of(index * 512, 512), 512)
-        rows_ref[:, at] = matmul(pick, rows_in[:, at]).astype(low)
-        picked = matmul(pick, grads_in[:, at])
+        rows_ref[:, at] = matmul(pick_buf[...], rows_in[:, at]).astype(low)
+        picked = matmul(pick_buf[...], grads_in[:, at])
         slot_cotangent[:, at] = picked.astype(low)
         grad_ref[:, at] = (gate * picked).astype(low)
         return 0
 
     lax.fori_loop(0, width // 512, pick_step, 0)
-    shared_pre = matmul(rows_in[...], shared_gate_w[...])
-    shared_up = matmul(rows_in[...], shared_up_w[...])
+    shared_pre, shared_up = 0.0, 0.0
+    for shard in range(shards):
+        part = rows_in[:, shard * own_width : (shard + 1) * own_width]
+        shared_pre = shared_pre + matmul(part, shared_gate_w[shard])
+        shared_up = shared_up + matmul(part, shared_up_w[shard])
     swished, slope = swish_parts(shared_pre)
     shared_hidden_ref[...] = (swished * shared_up).astype(low)
     shared_grad = matmul_nt(grads_in[...], shared_down_w[...])
@@ -546,77 +584,108 @@
         hidden_grad = matmul_nt(grad_ref[...], down_w[columns, :])
         gate_back_ref[:, columns] = (hidden_grad * up_pre * slope).astype(low)
         up_back_ref[:, columns] = (hidden_grad * swished).astype(low)
-    place = place_ref[0]
 
     def out_step(index, score):
         at = pl.ds(pl.multiple_of(index * 512, 512), 512)
+        shard = index * 512 // own_width
+        within = pl.ds(pl.multiple_of(index * 512 - shard * own_width, 512), 512)
         expert_out = matmul(hidden_ref[...], down_w[:, at]).astype(low).astype(jnp.float32)
         score = score + jnp.sum(expert_out * slot_cotangent[:, at].astype(jnp.float32), axis=1, keepdims=True)
-        out = matmul(place, (gate * expert_out).astype(low)) + matmul(shared_hidden_ref[...], shared_down_w[:, at])
-        out_ref[:, at] = out.astype(low)
+        out = matmul_tn(pick_buf[...], (gate * expert_out).astype(low))
+        out_ref[:, at] = (out + matmul(shared_hidden_ref[...], shared_down_w[:, at])).astype(low)
         row_back = matmul_nt(gate_back_ref[...], gate_w[at, :]) + matmul_nt(up_back_ref[...], up_w[at, :])
         back = (
-            matmul(place, row_back.astype(low))
-            + matmul_nt(shared_gate_back_ref[...], shared_gate_w[at, :])
-            + matmul_nt(shared_up_back_ref[...], shared_up_w[at, :])
+            matmul_tn(pick_buf[...], row_back.astype(low))
+            + matmul_nt(shared_gate_back_ref[...], shared_gate_w[shard, within, :])
+            + matmul_nt(shared_up_back_ref[...], shared_up_w[shard, within, :])
         )
         back_ref[:, at] = back.astype(low)
         return score
 
-    score = lax.fori_loop(0, width // 512, out_step, jnp.zeros((pick.shape[0], 1), jnp.float32))
-    score_ref[...] = jnp.broadcast_to(score, score_ref.shape)
-
-
-def expert_pass(pick, place, slot_gate, rows, grads, gate_w, up_w, down_w, shared_gate_w, shared_up_w, shared_down_w):
-    steps, slots, tokens = pick.shape
+    score = lax.fori_loop(0, width // 512, out_step, jnp.zeros((gate.shape[0], 1), jnp.float32))
+    for sender in range(senders):
+        own = score[sender * capacity : (sender + 1) * capacity]
+        total = jnp.sum(picks[sender] * own, axis=0, keepdims=True)
+        score_ref[sender] = jnp.broadcast_to(total, score_ref.shape[1:])
+
+
+def expert_pass(me, routes, router, rows, grads, gate_w, up_w, down_w, shared_gate_w, shared_up_w, shared_down_w, capacity):
+    plane, _, local = routes.shape
+    senders = STEP_SENDERS
+    tokens, slots = senders * local, senders * capacity
+    steps = plane // senders
     width, hidden_width = gate_w.shape
-    shared_width = shared_gate_w.shape[1]
+    units = shared_gate_w.shape[2]
     low = jnp.bfloat16
-    whole = lambda shape: pl.BlockSpec(shape, lambda i: (0, 0), pipeline_mode=pl.Buffered(1))
-    by_step = lambda r, c: pl.BlockSpec((r, c), lambda i: (i, 0))
+
+    def whole(array):
+        return pl.BlockSpec(array.shape, lambda i: (0,) * array.ndim, pipeline_mode=pl.Buffered(1))
+
+    def by_step(r, c):
+        return pl.BlockSpec((r, c), lambda i: (i, 0))
+
     total = steps * slots
-    out_shape = [
-        jax.ShapeDtypeStruct((steps * tokens, width), low),
-        jax.ShapeDtypeStruct((steps * tokens, width), low),
-        jax.ShapeDtypeStruct((total, width), low),
-        jax.ShapeDtypeStruct((total, width), low),
-        jax.ShapeDtypeStruct((total, hidden_width), low),
-        jax.ShapeDtypeStruct((total, hidden_width), low),
-        jax.ShapeDtypeStruct((total, hidden_width), low),
-        jax.ShapeDtypeStruct((total, 128), jnp.float32),
-        jax.ShapeDtypeStruct((steps * tokens, shared_width), low),
-        jax.ShapeDtypeStruct((steps * tokens, shared_width), low),
-        jax.ShapeDtypeStruct((steps * tokens, shared_width), low),
-    ]
+    shape = jax.ShapeDtypeStruct
+    route_block = pl.BlockSpec((senders, 8, local), lambda i: (i, 0, 0))
     return pl.pallas_call(
         expert_kernel,
         grid=(steps,),
-        out_shape=out_shape,
+        out_shape=[
+            shape((steps * tokens, width), low),
+            shape((steps * tokens, width), low),
+            shape((total, width), low),
+            shape((total, width), low),
+            shape((total, hidden_width), low),
+            shape((total, hidden_width), low),
+            shape((total, hidden_width), low),
+            shape((plane, 8, local), jnp.float32),
+            shape((steps * tokens, units), low),
+            shape((steps * tokens, units), low),
+            shape((steps * tokens, units), low),
+        ],
         in_specs=[
-            pl.BlockSpec((1, slots, tokens), lambda i: (i, 0, 0)),
-            pl.BlockSpec((1, tokens, slots), lambda i: (i, 0, 0)),
-            by_step(slots, 1),
+            pl.BlockSpec(memory_space=pltpu.SMEM),
+            route_block,
+            whole(router),
             by_step(tokens, width),
             by_step(tokens, width),
-            whole(gate_w.shape), whole(up_w.shape), whole(down_w.shape),
-            whole(shared_gate_w.shape), whole(shared_up_w.shape), whole(shared_down_w.shape),
+            whole(gate_w),
+            whole(up_w),
+            whole(down_w),
+            whole(shared_gate_w),
+            whole(shared_up_w),
+            whole(shared_down_w),
         ],
         out_specs=[
-            by_step(tokens, width), by_step(tokens, width), by_step(slots, width), by_step(slots, width),
-            by_step(slots, hidden_width), by_step(slots, hidden_width), by_step(slots, hidden_width), by_step(slots, 128),
-            by_step(tokens, shared_width), by_step(tokens, shared_width), by_step(tokens, shared_width),
+            by_step(tokens, width),
+            by_step(tokens, width),
+            by_step(slots, width),
+            by_step(slots, width),
+            by_step(slots, hidden_width),
+            by_step(slots, hidden_width),
+            by_step(slots, hidden_width),
+            route_block,
+            by_step(tokens, units),
+            by_step(tokens, units),
+            by_step(tokens, units),
         ],
-        scratch_shapes=[pltpu.VMEM((slots, width), low)],
-        compiler_params=pltpu.CompilerParams(vmem_limit_bytes=60 * 2**20, dimension_semantics=("arbitrary",)),
+        scratch_shapes=[
+            pltpu.VMEM((slots, width), low),
+            pltpu.VMEM((slots, tokens), low),
+            pltpu.VMEM((slots, 1), jnp.float32),
+        ],
+        compiler_params=pltpu.CompilerParams(
+            vmem_limit_bytes=60 * 2**20, dimension_semantics=("arbitrary",)
+        ),
         name="experts",
-    )(pick, place, slot_gate, rows, grads, gate_w, up_w, down_w, shared_gate_w, shared_up_w, shared_down_w)
+    )(me, routes, router, rows, grads, gate_w, up_w, down_w, shared_gate_w, shared_up_w, shared_down_w)
 
 
 QUERIES = 256
 KEYS = WINDOW + QUERIES
 
 
-def score_block(step, scale, query, keys, query_docs, key_docs):
+def score_block(scale, query, keys, query_docs, key_docs):
     raw = matmul_nt(query, keys) * scale
     row = lax.broadcasted_iota(jnp.int32, raw.shape, 0) + WINDOW
     column = lax.broadcasted_iota(jnp.int32, raw.shape, 1)
@@ -624,19 +693,6 @@
     return jnp.where(allowed, raw, NEG)
 
 
-def attend_kernel(scale, last, query_ref, key_ref, value_ref, docs_ref, row_docs_ref, out_ref, total_ref):
-    step = pl.program_id(0)
-    at = pl.ds(pl.multiple_of(step * QUERIES, QUERIES), KEYS)
-    scores = score_block(step, scale, query_ref[...], key_ref[at, :], docs_ref[...], row_docs_ref[:, at])
-    top = jnp.max(scores, axis=1, keepdims=True)
-    expo = jnp.exp(scores - top)
-    total = jnp.sum(expo, axis=1, keepdims=True)
-    probs = (expo / total).astype(jnp.bfloat16)
-    real = jnp.where(docs_ref[...] < last, 1.0, 0.0)
-    out_ref[...] = (matmul(probs, value_ref[at, :]) * real).astype(jnp.bfloat16)
-    total_ref[...] = jnp.broadcast_to(top + jnp.log(total), total_ref.shape)
-
-
 def attend_back_kernel(
     scale, last, query_ref, key_ref, value_ref, docs_ref, row_docs_ref, total_ref, grad_ref,
     query_grad_ref, key_grad_ref, value_grad_ref, key_sum, value_sum,
@@ -651,7 +707,7 @@
     at = pl.ds(pl.multiple_of(step * QUERIES, QUERIES), KEYS)
     query, keys, grad = query_ref[...], key_ref[at, :], grad_ref[...]
     grad = jnp.where(docs_ref[...] < last, grad, jnp.zeros((), grad.dtype))
-    scores = score_block(step, scale, query, keys, docs_ref[...], row_docs_ref[:, at])
+    scores = score_block(scale, query, keys, docs_ref[...], row_docs_ref[:, at])
     probs = jnp.exp(scores - total_ref[:, :1])
     prob_grad = matmul_nt(grad, value_ref[at, :])
     inner = jnp.sum(probs * prob_grad, axis=1, keepdims=True)
@@ -664,21 +720,6 @@
     def _():
         key_grad_ref[...] = key_sum[WINDOW:, :]
         value_grad_ref[...] = value_sum[WINDOW:, :]
-
-
-def attend(scale, last, query, keys, value, docs, row_docs):
-    rows, head_dim = query.shape
-    whole = lambda a: pl.BlockSpec(a.shape, lambda i: (0, 0))
-    by_step = lambda c: pl.BlockSpec((QUERIES, c), lambda i: (i, 0))
-    return pl.pallas_call(
-        functools.partial(attend_kernel, scale, last),
-        grid=(rows // QUERIES,),
-        out_shape=[jax.ShapeDtypeStruct((rows, V_HEAD), jnp.bfloat16), jax.ShapeDtypeStruct((rows, 128), jnp.float32)],
-        in_specs=[by_step(head_dim), whole(keys), whole(value), by_step(1), whole(row_docs)],
-        out_specs=[by_step(V_HEAD), by_step(128)],
-        compiler_params=pltpu.CompilerParams(vmem_limit_bytes=48 * 2**20, dimension_semantics=("arbitrary",)),
-        name="attend",
-    )(query, keys, value, docs, row_docs)
 
 
 def attend_back(scale, last, query, keys, value, docs, row_docs, totals, grad):
@@ -702,98 +743,322 @@
     )(query, keys, value, docs, row_docs, totals, grad)
 
 
-def front_kernel(tokens_ref, first_gain_ref, packed_ref, up_ref, latent_gain_ref, turn_ref, sway_ref,
-                 normed_ref, query_ref, key_ref, value_ref, latent_ref, compressed_ref):
+class Swaps:
+    def __init__(self, place, shards, sender):
+        self.place, self.shards, self.sender = place, shards, sender
+
+    def start(self, source, target, send_sem, recv_sem, keep=None):
+        place, shards = self.place, self.shards
+        arrivals = []
+        for step in range(1, shards):
+            other = lax.rem(place.shard + step, shards)
+            self.sender.start(
+                place.always,
+                remote(source, target(place.shard), send_sem.at[step], recv_sem.at[place.shard], {"shard": other}),
+            )
+            arrivals.append(
+                remote(source, target(other), send_sem.at[step], recv_sem.at[other], {"shard": other})
+            )
+        if keep is not None:
+            copy = pltpu.make_async_copy(source, target(place.shard), keep)
+            copy.start()
+
+        def wait():
+            for arrival in arrivals:
+                arrival.wait_recv()
+            if keep is not None:
+                copy.wait()
+
+        return wait
+
+
+def drain(run):
+    for _ in run:
+        pass
+
+
+def forward_kernel(shards, plane, scale, last, *refs):
+    (tokens, cotangent, query_cols, down_half, up_half, out_half, query_half, gate_half, wide_half, narrow_half,
+     shared_gate, shared_up, shared_down, routes, first_gain, latent_gain, second_gain, turn, sway, docs, row_docs,
+     all_normed, all_grads, all_routes, full_down, full_out, full_query, full_gate, full_up, full_narrow,
+     full_shared_gate, full_shared_up, full_shared_down, normed_one,
+     query, keys, value, key_latent, compressed, head_out, log_total, middle,
+     token_buf, normed_buf, query_buf, up_buf, down_buf, out_buf, heads_buf, second_buf,
+     swap_send, swap_recv, keep_sem, gather_send, gather_recv, gather_keep, piece_send, piece_recv,
+     trade_send, trade_recv, load_sem) = refs
     low = jnp.bfloat16
-    values = tokens_ref[...].astype(jnp.float32)
-    r = lax.rsqrt(jnp.mean(values * values, axis=1, keepdims=True) + EPS)
-    normed = (values * r * first_gain_ref[...]).astype(low)
-    normed_ref[...] = normed
-    rest = QK_NOPE + 4 * QK_ROPE
-    first = matmul(normed, packed_ref[:, :rest])
-    latent = matmul(normed, packed_ref[:, rest:])
-    query_ref[:, :QK_NOPE] = first[:, :QK_NOPE].astype(low)
-    plain = first[:, QK_NOPE : QK_NOPE + 2 * QK_ROPE]
-    turned = (plain * turn_ref[...] + first[:, QK_NOPE + 2 * QK_ROPE :] * sway_ref[...]).astype(low)
-    query_ref[:, QK_NOPE:] = turned[:, :QK_ROPE]
-    compressed_ref[...] = latent
-    r = lax.rsqrt(jnp.mean(latent * latent, axis=1, keepdims=True) + EPS)
-    key_latent = (latent * r * latent_gain_ref[...]).astype(low)
-    latent_ref[...] = key_latent
-    both = matmul(key_latent, up_ref[...]).astype(low)
-    key_ref[:, :QK_NOPE] = both[:, :QK_NOPE]
-    key_ref[:, QK_NOPE:] = turned[:, QK_ROPE:]
-    value_ref[...] = both[:, QK_NOPE:]
-
-
-def front(tokens, first_gain, packed, up_head, latent_gain, turn, sway):
-    rows, width = tokens.shape
-    step = 256
-    low = jnp.bfloat16
-    whole = lambda a: pl.BlockSpec(a.shape, lambda i: (0, 0))
-    by_step = lambda c: pl.BlockSpec((step, c), lambda i: (i, 0))
+    group = SEQ_DEVICES
+    place, wide = Place(group), Place(plane)
+    width = tokens.shape[-1]
+    rows = docs.shape[0] // group
+    sender = Sender()
+    members = [lax.rem(place.local + step, group) for step in range(1, group)]
+    peers = [(place.always, {"expert": place.base + member}) for member in members]
+    if plane != group:
+        peers += [
+            (wide.upper & ~place.upper, {"expert": place.me + INNER}),
+            (wide.lower & ~place.lower, {"expert": place.me - INNER}),
+        ]
+    others = [lax.rem(place.shard + step, shards) for step in range(1, shards)]
+    peers += [(place.always, {"shard": other}) for other in others]
+    greet(peers)
+
+    swaps = Swaps(place, shards, sender)
+    numbers = iter(range(16))
+
+    def swap(source, target, keep=False):
+        at = next(numbers)
+        return swaps.start(
+            source, target, swap_send.at[at], swap_recv.at[at], keep_sem.at[at] if keep else None
+        )
+
+    at_piece = lambda ref: ref.at[wide.me]
+    got_query = swap(query_cols, lambda shard: query_buf.at[shard], True)
+    got_down = swap(at_piece(down_half), lambda shard: full_down.at[shard, wide.me])
+    got_up = swap(up_half, lambda shard: up_buf.at[shard], True)
+    token_run = gather_steps(
+        place, tokens, token_buf, gather_keep.at[0], gather_send.at[0], gather_recv.at[0], sender
+    )
+    next(token_run)
+    got_out = swap(at_piece(out_half), lambda shard: full_out.at[shard, wide.me])
+    got_wq = swap(at_piece(query_half), lambda shard: full_query.at[shard, wide.me])
+    owns = [
+        pltpu.make_async_copy(half, full.at[place.shard], load_sem.at[index])
+        for index, (half, full) in enumerate(((down_half, full_down), (out_half, full_out), (query_half, full_query)))
+    ]
+    for own in owns:
+        own.start()
+
+    def piece_gathers(kind, full):
+        return [
+            gather_steps(
+                wide, None, full.at[other], None, piece_send.at[kind, step], piece_recv.at[kind, step], sender
+            )
+            for step, other in enumerate(others)
+        ]
+
+    next(token_run)
+    got_down()
+    down_runs = piece_gathers(0, full_down)
+    for run in down_runs:
+        next(run)
+    next(token_run)
+    for run in down_runs:
+        next(run)
+    got_query()
+    got_up()
+    waits = [
+        swap(gate_half, lambda shard: full_gate.at[shard], True),
+        swap(wide_half, lambda shard: full_up.at[shard], True),
+    ]
+    drain(token_run)
+    got_out()
+    got_wq()
+    waits += [
+        swap(shared_gate, lambda shard: full_shared_gate.at[shard], True),
+        swap(shared_up, lambda shard: full_shared_up.at[shard], True),
+        swap(shared_down, lambda shard: full_shared_down.at[shard], True),
+        swap(narrow_half, lambda shard: full_narrow.at[shard], True),
+    ]
+    for run in down_runs:
+        drain(run)
+    for own in owns:
+        own.wait()
+    route_run = gather_steps(
+        wide, routes, all_routes, gather_keep.at[1], gather_send.at[1], gather_recv.at[1], sender
+    )
+    next(route_run)
+    out_runs = piece_gathers(1, full_out)
+    for run in out_runs:
+        next(run)
+    load_down = pltpu.make_async_copy(full_down, down_buf, load_sem.at[0])
+    load_down.start()
+    load_down.wait()
+
+    keys[:WINDOW, :] = jnp.zeros((WINDOW, keys.shape[1]), low)
+    value[:WINDOW, :] = jnp.zeros((WINDOW, value.shape[1]), low)
+    tile = 2 * rows
+    own_width = width // shards
+
+    def whole_dot(at, weight_of):
+        total = 0.0
+        for shard in range(shards):
+            total = total + matmul(normed_buf[at, shard * own_width : (shard + 1) * own_width], weight_of(shard))
+        return total
+
+    def front_tile(index, _):
+        at = pl.ds(pl.multiple_of(index * tile, tile), tile)
+        values = token_buf[pl.ds(index * 2, 2)].reshape(tile, width).astype(jnp.float32)
+        root = lax.rsqrt(jnp.mean(values * values, axis=1, keepdims=True) + EPS)
+        normed_buf[at, :] = (values * root * first_gain[...]).astype(low)
+        first = whole_dot(at, lambda shard: query_buf[shard])
+        latent = whole_dot(at, lambda shard: down_buf[shard].reshape(own_width, -1))
+        turn_at, sway_at = turn[at, :], sway[at, :]
+        end = QK_NOPE + QK_ROPE
+        query[at, :QK_NOPE] = first[:, :QK_NOPE].astype(low)
+        query[at, QK_NOPE:] = (first[:, QK_NOPE:end] * turn_at + first[:, end:] * sway_at).astype(low)
+        end = KV_RANK + QK_ROPE
+        key_rope = (latent[:, KV_RANK:end] * turn_at + latent[:, end:] * sway_at).astype(low)
+        latent = latent[:, :KV_RANK]
+        compressed[at, :] = latent
+        root = lax.rsqrt(jnp.mean(latent * latent, axis=1, keepdims=True) + EPS)
+        normed_latent = (latent * root * latent_gain[...]).astype(low)
+        key_latent[at, :] = normed_latent
+        up_rows = KV_RANK // shards
+        both = 0.0
+        for shard in range(shards):
+            both = both + matmul(normed_latent[:, shard * up_rows : (shard + 1) * up_rows], up_buf[shard])
+        both = both.astype(low)
+        later = pl.ds(pl.multiple_of(index * tile + WINDOW, tile), tile)
+        keys[later, :QK_NOPE] = both[:, :QK_NOPE]
+        keys[later, QK_NOPE:] = key_rope
+        value[later, :] = both[:, QK_NOPE:]
+        return 0
+
+    tiles = group // 2
+    for part in range(2):
+        lax.fori_loop(part * tiles // 2, (part + 1) * tiles // 2, front_tile, 0)
+        for run in out_runs + [route_run]:
+            next(run, None)
+    save = pltpu.make_async_copy(normed_buf, normed_one, load_sem.at[1])
+    save.start()
+    for run in out_runs + [route_run]:
+        next(run, None)
+
+    def attend_tile(index, _):
+        at = pl.ds(pl.multiple_of(index * QUERIES, QUERIES), QUERIES)
+        window = pl.ds(pl.multiple_of(index * QUERIES, QUERIES), KEYS)
+        scores = score_block(scale, query[at, :], keys[window, :], docs[at, :], row_docs[:, window])
+        top = jnp.max(scores, axis=1, keepdims=True)
+        expo = jnp.exp(scores - top)
+        total = jnp.sum(expo, axis=1, keepdims=True)
+        probs = (expo / total).astype(low)
+        real = jnp.where(docs[at, :] < last, 1.0, 0.0)
+        head_out[at, :] = (matmul(probs, value[window, :]) * real).astype(low)
+        log_total[at, :] = jnp.broadcast_to(top + jnp.log(total), (QUERIES, log_total.shape[1]))
+        return 0
+
+    blocks = docs.shape[0] // QUERIES
+    lax.fori_loop(0, blocks // 2, attend_tile, 0)
+    for run in out_runs + [route_run]:
+        drain(run)
+    load_out = pltpu.make_async_copy(full_out, out_buf, load_sem.at[0])
+    load_out.start()
+    lax.fori_loop(blocks // 2, blocks, attend_tile, 0)
+
+    def head_at(member):
+        return head_out.at[pl.ds(pl.multiple_of(member * rows, rows), rows), :]
+
+    def lands(head):
+        return heads_buf.at[:, pl.ds(pl.multiple_of(head * V_HEAD, V_HEAD), V_HEAD)]
+
+    keep = pltpu.make_async_copy(head_at(place.local), lands(place.local), load_sem.at[2])
+    keep.start()
+    for step, member in enumerate(members):
+        sender.start(
+            place.always,
+            remote(
+                head_at(member), lands(place.local), trade_send.at[step], trade_recv.at[place.local],
+                {"expert": place.base + member},
+            ),
+        )
+    for step, member in enumerate(members):
+        remote(
+            head_at(member), lands(member), trade_send.at[step], trade_recv.at[member], {"expert": place.base + member}
+        ).wait_recv()
+    keep.wait()
+    load_out.wait()
+
+    for at, size in pieces_of(width, 512):
+        columns = slice(at, at + size)
+        total = token_buf[place.local].reshape(rows, width)[:, columns].astype(jnp.float32)
+        for shard in range(shards):
+            weight = out_buf[shard, :, :, :, columns].reshape(own_width, size)
+            total = total + matmul(heads_buf[:, shard * own_width : (shard + 1) * own_width], weight)
+        middle[:, columns] = total
+    values = middle[...]
+    root = lax.rsqrt(jnp.mean(values * values, axis=1, keepdims=True) + EPS)
+    second_buf[...] = (values * root * second_gain[...]).astype(low).reshape(second_buf.shape)
+
+    normed_run = gather_steps(
+        wide, second_buf, all_normed, gather_keep.at[2], gather_send.at[2], gather_recv.at[2], sender
+    )
+    grad_run = gather_steps(
+        wide, cotangent, all_grads, gather_keep.at[3], gather_send.at[3], gather_recv.at[3], sender
+    )
+    wq_runs = piece_gathers(2, full_query)
+    runs = [normed_run, grad_run] + wq_runs
+    while runs:
+        runs = [run for run in runs if next(run, "end") != "end"]
+    save.wait()
+    for wait in waits:
+        wait()
+    sender.finish()
+
+
+def forward_pass(scale, last, tokens, cotangent, blocks, routes, gains, tables):
+    shards, plane = lax.axis_size("shard"), lax.axis_size("expert")
+    local, width = tokens.shape
+    low, shape = jnp.bfloat16, jax.ShapeDtypeStruct
+    pieces = (PIECES, local // PIECES, width)
+    any_space, vmem = pl.BlockSpec(memory_space=pl.ANY), pl.BlockSpec(memory_space=pltpu.VMEM)
     head_dim = QK_NOPE + QK_ROPE
+    query_cols, down_half, up_half, out_half, query_half = blocks[:5]
+    out_shape = [
+        shape((plane,) + pieces, low),
+        shape((plane,) + pieces, low),
+        shape((plane, 1) + routes.shape, jnp.int32),
+    ]
+    out_shape += [shape((shards,) + block.shape, low) for block in (down_half, out_half, query_half) + blocks[5:]]
+    out_shape += [
+        shape((SEQ, width), low),
+        shape((SEQ, head_dim), low),
+        shape((SEQ + WINDOW, head_dim), low),
+        shape((SEQ + WINDOW, V_HEAD), low),
+        shape((SEQ, KV_RANK), low),
+        shape((SEQ, KV_RANK), jnp.float32),
+        shape((SEQ, V_HEAD), low),
+        shape((SEQ, 128), jnp.float32),
+        shape((local, width), jnp.float32),
+    ]
+    hbm_out = 13
+    own_width = width // shards
+    dma = pltpu.SemaphoreType.DMA
     return pl.pallas_call(
-        front_kernel,
-        grid=(rows // step,),
-        out_shape=[
-            jax.ShapeDtypeStruct((rows, width), low),
-            jax.ShapeDtypeStruct((rows, head_dim), low),
-            jax.ShapeDtypeStruct((rows, head_dim), low),
-            jax.ShapeDtypeStruct((rows, V_HEAD), low),
-            jax.ShapeDtypeStruct((rows, KV_RANK), low),
-            jax.ShapeDtypeStruct((rows, KV_RANK), jnp.float32),
+        functools.partial(forward_kernel, shards, plane, scale, last),
+        out_shape=out_shape,
+        in_specs=[any_space] * (3 + len(blocks)) + [vmem] * (len(gains) + len(tables)),
+        out_specs=[any_space] * hbm_out + [vmem] * (len(out_shape) - hbm_out),
+        scratch_shapes=[
+            pltpu.VMEM((SEQ_DEVICES,) + pieces, low),
+            pltpu.VMEM((SEQ, width), low),
+            pltpu.VMEM((shards,) + query_cols.shape, low),
+            pltpu.VMEM((shards,) + up_half.shape, low),
+            pltpu.VMEM((shards,) + down_half.shape, low),
+            pltpu.VMEM((shards,) + out_half.shape, low),
+            pltpu.VMEM((local, HEADS * V_HEAD), low),
+            pltpu.VMEM(pieces, low),
+            dma((12, shards)),
+            dma((12, shards)),
+            dma((12,)),
+            dma((4, 4, plane, PIECES)),
+            dma((4, plane, PIECES)),
+            dma((4,)),
+            dma((3, shards, 4, plane, 1)),
+            dma((3, shards, plane, 1)),
+            dma((SEQ_DEVICES,)),
+            dma((SEQ_DEVICES,)),
+            dma((4,)),
         ],
-        in_specs=[by_step(width), whole(first_gain), whole(packed), whole(up_head), whole(latent_gain),
-                  by_step(2 * QK_ROPE), by_step(2 * QK_ROPE)],
-        out_specs=[by_step(width), by_step(head_dim), by_step(head_dim), by_step(V_HEAD), by_step(KV_RANK), by_step(KV_RANK)],
-        compiler_params=pltpu.CompilerParams(vmem_limit_bytes=48 * 2**20, dimension_semantics=("arbitrary",)),
-        name="front",
-    )(tokens, first_gain, packed, up_head, latent_gain, turn, sway)
+        compiler_params=pltpu.CompilerParams(
+            collective_id=1, has_side_effects=True, vmem_limit_bytes=60 * 2**20
+        ),
+        name="forward",
+    )(tokens.reshape(pieces), cotangent.reshape(pieces), *blocks, routes[None], *gains, *tables)
 
 
 def tie(value, *awaited):
     return lax.optimization_barrier((value,) + awaited)
-
-
-def other_blocks(pieces):
-    count = lax.axis_size("shard")
-    me = lax.axis_index("shard")
-    return [
-        lax.dynamic_index_in_dim(pieces, (me + step) % count, 0, keepdims=False)
-        for step in range(1, count)
-    ]
-
-
-def other_rows(pieces):
-    gathered = lax.all_gather(jnp.stack(other_blocks(pieces)), "expert", axis=1, tiled=True)
-    return [gathered[step] for step in range(gathered.shape[0])]
-
-
-def split_matmul(values, own, others):
-    count = len(others) + 1
-    me = lax.axis_index("shard")
-    parts = values.reshape(values.shape[0], count, -1)
-    total = 0.0
-    for step, block in enumerate([own] + others):
-        part = lax.dynamic_index_in_dim(parts, (me + step) % count, 1, keepdims=False)
-        total = total + matmul(part, block)
-    return total
-
-
-def split_matmul_nt(values, own, others):
-    count = len(others) + 1
-    me = lax.axis_index("shard")
-    whole = jnp.zeros((values.shape[0], count, own.shape[0]), jnp.float32)
-    for step, block in enumerate([own] + others):
-        whole = lax.dynamic_update_index_in_dim(
-            whole, matmul_nt(values, block), (me + step) % count, 1
-        )
-    return whole.reshape(values.shape[0], -1)
-
-
-def padded_rows(block):
-    return jnp.pad(block, ((0, -block.shape[0] % 16), (0, 0)))
 
 
 def shard_ring(block):
@@ -872,45 +1137,23 @@
     half = QK_ROPE // 2
     query_columns = lax.dynamic_slice_in_dim(query_weight, head_at * head_dim, head_dim, 1)
     query_turn, key_turn = query_columns[:, QK_NOPE:], latent_down[:, KV_RANK:]
-    packed_half = jnp.concatenate(
-        [
-            query_columns,
-            key_turn,
-            query_turn[:, half:],
-            query_turn[:, :half],
-            key_turn[:, half:],
-            key_turn[:, :half],
-            latent_down[:, :KV_RANK],
-        ],
-        axis=1,
-    )
-    tokens_all, packed, up_pieces, out_pieces = bundle(
-        1,
-        SEQ_DEVICES,
-        shards,
-        [
-            ("gather", tokens),
-            ("swap", packed_half),
-            (
-                "swap",
-                lax.dynamic_slice_in_dim(
-                    latent_up, head_at * (QK_NOPE + V_HEAD), QK_NOPE + V_HEAD, 1
-                ),
-            ),
-            ("swap", lax.dynamic_slice_in_dim(output_weight, plane_at * piece_rows, piece_rows, 0)),
-        ],
-    )
-    packed = packed.reshape(width, -1)
-    up_head = up_pieces.reshape(KV_RANK, QK_NOPE + V_HEAD)
-    other_out = other_rows(out_pieces)
-    cotangent_late = tie(cotangent, other_out[0])[0]
-    all_grads = lax.all_gather(cotangent_late, "expert", axis=0, tiled=True)
+    query_cols = jnp.concatenate(
+        [query_columns, query_turn[:, half:], query_turn[:, :half]], axis=1
+    )
+    down_half = jnp.concatenate(
+        [latent_down, key_turn[:, half:], key_turn[:, :half]], axis=1
+    )
     units = shared_down.shape[0] // plane
+    unit_pad = -units % 16
+    padded_units = units + unit_pad
     gate_columns, up_columns = (
         jnp.concatenate(
             [
-                lax.dynamic_slice_in_dim(
-                    weight, index * shared_down.shape[0] + plane_at * units, units, 1
+                jnp.pad(
+                    lax.dynamic_slice_in_dim(
+                        weight, index * shared_down.shape[0] + plane_at * units, units, 1
+                    ),
+                    ((0, 0), (0, unit_pad)),
                 )
                 for index in range(shards)
             ],
@@ -919,6 +1162,10 @@
         for weight in (shared_gate, shared_up)
     )
     down_units = lax.dynamic_slice_in_dim(shared_down, plane_at * units, units, 0)
+    down_units = jnp.pad(down_units, ((0, unit_pad), (0, 0)))
+
+    def plane_pieces(weight):
+        return weight.reshape(plane, 1, -1, weight.shape[1])
 
     positions = jnp.arange(SEQ, dtype=jnp.int32)
     cosine_part, sine_part = rotary_tables(positions, QK_ROPE)
@@ -927,78 +1174,65 @@
     picked = jnp.arange(sequence_count, dtype=jnp.int32)[:, None] == sequence_at
     row_ends = jnp.sum(jnp.where(picked, ends, 0), axis=0)
     documents = jnp.sum((positions[:, None] >= row_ends[None, :]).astype(jnp.int32), axis=1)
-    turn = jnp.tile(jnp.concatenate([cosine_part, cosine_part], axis=1), (1, 2))
-    sway = jnp.tile(jnp.concatenate([-sine_part, sine_part], axis=1), (1, 2))
-    normed_one, query, keys, value, key_latent, compressed = front(
-        tokens_all.reshape(SEQ, width), first_gain[None], packed, up_head, latent_gain[None], turn, sway
-    )
-    ahead = ((WINDOW, 0), (0, 0))
-    keys, value = jnp.pad(keys, ahead), jnp.pad(value, ahead)
+    turn = jnp.concatenate([cosine_part, cosine_part], axis=1)
+    sway = jnp.concatenate([-sine_part, sine_part], axis=1)
     docs = documents[:, None]
-    row_docs = jnp.pad(docs, ahead, constant_values=-1).T
-    head_out, log_total = attend(scale, entry_count - 1, query, keys, value, docs, row_docs)
-    gate_single = shard_rows(expert_gate[0])
-    head_out, gate_single = tie(head_out, gate_single)
-    heads_out, query_rows = bundle(
-        2,
-        SEQ_DEVICES,
-        shards,
-        [
-            ("trade", head_out.reshape(SEQ_DEVICES, local_rows, V_HEAD)),
-            ("swap", lax.dynamic_slice_in_dim(query_weight, plane_at * piece_rows, piece_rows, 0)),
-        ],
-    )
-    heads_out = heads_out.transpose(1, 0, 2).reshape(local_rows, HEADS * V_HEAD)
-
+    row_docs = jnp.pad(docs, ((WINDOW, 0), (0, 0)), constant_values=-1).T
+    route_rows = jnp.pad(routes.T, ((0, 8 - TOP), (0, 0)), constant_values=-1)
+    (
+        all_normed,
+        all_grads,
+        all_routes,
+        full_down,
+        full_out,
+        full_query,
+        gate_single,
+        up_single,
+        down_single,
+        gate_shared,
+        up_shared,
+        down_shared,
+        normed_one,
+        query,
+        keys,
+        value,
+        key_latent,
+        compressed,
+        head_out,
+        log_total,
+        middle,
+    ) = forward_pass(
+        scale,
+        entry_count - 1,
+        tokens,
+        cotangent,
+        (
+            query_cols,
+            plane_pieces(down_half),
+            lax.dynamic_slice_in_dim(
+                latent_up, head_at * (QK_NOPE + V_HEAD), QK_NOPE + V_HEAD, 1
+            ),
+            plane_pieces(output_weight),
+            plane_pieces(query_weight),
+            expert_gate[0],
+            expert_up[0],
+            expert_down[0],
+            gate_columns,
+            up_columns,
+            down_units,
+        ),
+        route_rows,
+        (first_gain[None], latent_gain[None], second_gain[None]),
+        (turn, sway, docs, row_docs),
+    )
+    all_normed = all_normed.reshape(-1, width)
+    all_grads = all_grads.reshape(-1, width)
+    full_out = full_out.reshape(-1, width)
+    full_query = full_query.reshape(width, -1)
+    full_down = full_down.reshape(width, -1)
     hidden_rows = tokens.astype(jnp.float32)
-    middle = hidden_rows + split_matmul(heads_out, output_weight, other_out)
     second_normed = norm_scale(middle, second_gain).astype(jnp.bfloat16)
-
-    all_normed, all_routes, up_single, gate_shared, up_shared, down_shared = bundle(
-        3,
-        plane,
-        shards,
-        [
-            ("gather", second_normed),
-            ("gather", jnp.pad(routes.T, ((0, 2), (0, 0)))),
-            ("swap", expert_up[0]),
-            ("swap", gate_columns.T),
-            ("swap", up_columns.T),
-            ("swap", padded_rows(down_units)),
-        ],
-    )
-    all_normed = all_normed.reshape(-1, width)
-    all_routes = all_routes[:, :TOP].transpose(0, 2, 1).reshape(-1, TOP)
-    up_single = up_single.reshape(width, -1)
-    gate_shared = gate_shared.transpose(0, 2, 1).reshape(width, -1)
-    up_shared = up_shared.transpose(0, 2, 1).reshape(width, -1)
-    down_shared = down_shared[:, :units].reshape(-1, width)
-    down_single = shard_rows(expert_down[0])
-    other_query = other_rows(tie(query_rows, all_grads)[0])
-    plane_rows = plane * local_rows
-    logits = matmul(all_normed, router_weight)
     expert_ids = jnp.arange(plane, dtype=jnp.int32)
-    choose = all_routes[:, :, None] == expert_ids[None, None, :]
-    chosen = jnp.sum(jnp.where(choose, logits[:, None, :], 0.0), axis=2)
-    chosen_top = jnp.max(chosen, axis=1, keepdims=True)
-    chosen_exp = jnp.exp(chosen - chosen_top)
-    gate_values = chosen_exp / jnp.sum(chosen_exp, axis=1, keepdims=True)
-    here = all_routes == plane_at
-    gate_here = jnp.sum(jnp.where(here, gate_values, 0.0), axis=1).reshape(plane, local_rows)
-    marks = jnp.any(here, axis=1).reshape(plane, local_rows)
-    ranks = jnp.cumsum(marks.astype(jnp.int32), axis=1) - 1
-    picks = marks[:, None, :] & (
-        ranks[:, None, :] == jnp.arange(capacity, dtype=jnp.int32)[None, :, None]
-    )
-    senders = STEP_SENDERS
-    steps = plane // senders
-    pick = jnp.einsum(
-        "sbct,bd->sbcdt",
-        picks.reshape(steps, senders, capacity, local_rows).astype(jnp.bfloat16),
-        jnp.eye(senders, dtype=jnp.bfloat16),
-    ).reshape(steps, senders * capacity, senders * local_rows)
-    slot_gate = jnp.sum(jnp.where(picks, gate_here[:, None, :], 0.0), axis=2).reshape(-1, 1)
-    lanes = ((0, 0), (0, -(shards * units) % 128))
     (
         normed_part,
         output_part,
@@ -1007,28 +1241,25 @@
         hidden,
         gate_pre_grad,
         up_pre_grad,
-        slot_gate_grad,
+        token_scores,
         shared_hidden,
         shared_gate_back,
         shared_up_back,
     ) = expert_pass(
-        pick,
-        pick.transpose(0, 2, 1),
-        slot_gate,
+        plane_at.astype(jnp.int32).reshape(1, 1),
+        all_routes[:, 0],
+        router_weight.T,
         all_normed,
         all_grads,
-        gate_single,
-        up_single,
-        down_single,
-        jnp.pad(gate_shared, lanes),
-        jnp.pad(up_shared, lanes),
-        jnp.pad(down_shared, lanes[::-1]),
-    )
-    slot_gate_grad = slot_gate_grad[:, 0].reshape(plane, capacity)
-    shared_hidden = shared_hidden[:, : shards * units]
-    shared_gate_back = shared_gate_back[:, : shards * units]
-    shared_up_back = shared_up_back[:, : shards * units]
-    token_gate_grad = jnp.sum(jnp.where(picks, slot_gate_grad[:, :, None], 0.0), axis=1)
+        gate_single.reshape(width, -1),
+        up_single.reshape(width, -1),
+        down_single.reshape(-1, width),
+        gate_shared,
+        up_shared,
+        down_shared.reshape(-1, width),
+        capacity,
+    )
+    plane_rows = plane * local_rows
     expert_down_term = matmul_tn(hidden, slot_grad)
     back, gate_dense, down_blocks = bundle(
         4,
@@ -1036,12 +1267,7 @@
         shards,
         [
             ("reduce", normed_part.reshape(plane, local_rows, width)),
-            (
-                "trade",
-                jnp.broadcast_to(
-                    token_gate_grad.reshape(plane, 1, local_rows), (plane, 8, local_rows)
-                ),
-            ),
+            ("trade", token_scores),
             ("share", expert_down_term.astype(jnp.bfloat16).reshape(shards, -1, width)),
         ],
     )
@@ -1063,7 +1289,8 @@
     activations = (middle + output_sum.astype(jnp.float32)).astype(jnp.bfloat16)
     expert_gate_grad = shard_sum(matmul_tn(slot_rows, gate_pre_grad))[None]
     expert_up_grad = shard_sum(matmul_tn(slot_rows, up_pre_grad))[None]
-    shared_down_grad = shard_sum(matmul_tn(shared_hidden, all_grads))
+    shared_down_term = matmul_tn(shared_hidden, all_grads).reshape(shards, padded_units, width)
+    shared_down_grad = shard_sum(shared_down_term[:, :units].reshape(-1, width))
     shared_term = jnp.concatenate(
         [matmul_tn(all_normed, shared_gate_back), matmul_tn(all_normed, shared_up_back)], axis=1
     )
@@ -1083,16 +1310,18 @@
         heads = moved.reshape((plane // SEQ_DEVICES, HEADS) + moved.shape[1:]).sum(axis=0)
         return heads.transpose(1, 0, 2).reshape(moved.shape[1], -1)
 
-    shared_moved = to_owners(shared_term).reshape(plane, -1, 2, shards, units)
+    shared_moved = to_owners(shared_term).reshape(plane, -1, 2, shards, padded_units)[..., :units]
     shared_moved = shared_moved.transpose(2, 1, 3, 0, 4)
     shared_moved = shared_moved.reshape(2, shared_moved.shape[1], -1)
     shared_gate_grad = shared_moved[0]
     shared_up_grad = shared_moved[1]
 
     grad_out = cotangent.astype(jnp.float32)
-    own_start = plane_at * local_rows
-    own_gates = lax.dynamic_slice_in_dim(gate_values, own_start, local_rows, 0)
     own_choose = routes[:, :, None] == expert_ids[None, None, :]
+    own_logits = matmul(second_normed, router_weight)
+    chosen = jnp.sum(jnp.where(own_choose, own_logits[:, None, :], 0.0), axis=2)
+    chosen_exp = jnp.exp(chosen - jnp.max(chosen, axis=1, keepdims=True))
+    own_gates = chosen_exp / jnp.sum(chosen_exp, axis=1, keepdims=True)
     gate_grad = jnp.sum(jnp.where(own_choose, gate_dense[:, None, :], 0.0), axis=2)
     chosen_grad = own_gates * (
         gate_grad - jnp.sum(own_gates * gate_grad, axis=1, keepdims=True)
@@ -1116,7 +1345,7 @@
     middle_norm_grad, second_term = second_back(normed_grad)
     middle_grad = grad_out + middle_norm_grad
     middle_low = middle_grad.astype(jnp.bfloat16)
-    heads_grad = split_matmul_nt(middle_low, output_weight, other_out).astype(jnp.bfloat16)
+    heads_grad = matmul_nt(middle_low, full_out).astype(jnp.bfloat16)
     heads_grad = heads_grad.reshape(local_rows, HEADS, V_HEAD).transpose(1, 0, 2)
     (head_grad,) = bundle(5, SEQ_DEVICES, shards, [("trade", heads_grad)])
     head_grad = head_grad.reshape(SEQ, V_HEAD)
@@ -1133,6 +1362,10 @@
     key_nope_grad, key_rope_grad = keys_grad[:, :QK_NOPE], keys_grad[:, QK_NOPE:]
     pair_grad = jnp.concatenate([key_nope_grad, value_grad], axis=1).astype(jnp.bfloat16)
     latent_up_term = matmul_tn(key_latent, pair_grad)
+    up_half = lax.dynamic_slice_in_dim(
+        latent_up, head_at * (QK_NOPE + V_HEAD), QK_NOPE + V_HEAD, 1
+    )
+    up_head = shard_rows(up_half)
     key_grad_part = jnp.concatenate(
         [
             matmul_nt(pair_grad, up_head),
@@ -1189,12 +1422,8 @@
     column_grad = column_grad.reshape(SEQ, down_columns)
     query_weight_grad = owner_sum(query_moved)
     latent_up_grad = owner_sum(up_moved)
-    packed_rope = packed[:, head_dim : head_dim + QK_ROPE]
-    packed_latent = packed[:, QK_NOPE + 4 * QK_ROPE :]
-    normed_one_grad = (
-        split_matmul_nt(own_query_grad, query_weight, other_query)
-        + matmul_nt(compressed_grad[:, :KV_RANK], packed_latent)
-        + matmul_nt(compressed_grad[:, KV_RANK:], packed_rope)
+    normed_one_grad = matmul_nt(own_query_grad, full_query) + matmul_nt(
+        compressed_grad, full_down[:, : KV_RANK + QK_ROPE]
     )
     unused_one, first_back = jax.vjp(norm_scale, hidden_rows, first_gain)
     input_norm_grad, first_term = first_back(normed_one_grad)

time: 969 us -> 1450 us (1.50)
  Pallas kernels: 527 us -> 1150 us
  waiting for transfers between devices: 99 us -> 20.5 us
  local copies, waits for them, and re-layouts: 125 us -> 85 us
    pallas_call x3 -> x2, Pallas kernels: 108 us -> 917 us  [the longest x1 832 us: forward_pass(): pl.pallas_call(functools.partial(forward_kernel, shards, plane, scale, la...]
    pallas_call x7 -> x4, Pallas kernels: 403 us -> 214 us  [bundle(): pl.pallas_call(functools.partial(bundle_kernel, group, shards, tuple(kind...]
    ppermute x2 -> x1, waiting for transfers between devices: 64.1 us -> 0.01 us  [shard_ring(): lax.ppermute(block, 'shard', [(source, (source + step) % count) for sourc...]
    all_to_all x2, waiting for transfers between devices: 26.9 us -> 11 us  [on_device(): lax.all_to_all(term.astype(jnp.bfloat16).reshape(all_devices, -1, term.sh...]
  transfers between devices with their start and end apart: 14 -> 10, of which waited for: 5 -> 4; matrix products, arithmetic and copies ran while one was open for 27% -> 12% of each run, Pallas kernels for 51% -> 7%
where the time goes in v4:
time: 1450 us; the launch traced here: 1440 us
  Pallas kernels  1150 us (79%)
  matrix products  92.7 us (6%)
  local copies, waits for them, and re-layouts  85 us (6%)
  other arithmetic  56.1 us (4%)
  starting transfers between devices  21.9 us (2%)
  waiting for transfers between devices  20.5 us (1%)
  between operations  15.5 us (1%)
    pallas_call x1, Pallas kernels, forward_pass(): pl.pallas_call(functools.partial(forward_kernel, shards, plane, scale, la...  832 us
    pallas_call x4, Pallas kernels, bundle(): pl.pallas_call(functools.partial(bundle_kernel, group, shards, tuple(kind...  214 us
    pallas_call x1, Pallas kernels, expert_pass(): pl.pallas_call(expert_kernel, grid=(steps,), out_shape=[shape((steps * to...  84.4 us
    dot_general x10, matrix products, matmul_tn(): lax.dot_general(left, right, (((0,), (0,)), ((), ())), preferred_element_...  70.1 us
  transfers between devices with their start and end apart: 10, of which 4 were waited for; matrix products, arithmetic and copies ran while one was open for 12% of the time, Pallas kernels for 7%

profile of v4, /device:TPU:9, one launch (start us, length us, event | category | flops | bytes accessed | tf_op | source)
XLA Modules:
  0.0 1437.6 jit_solution(3445478810438029808)
XLA Ops:
  10.4 1.4 constant_dynamic-slice_fusion.8
  12.8 1.4 copy.134
  16.2 1.9 constant_dynamic-slice_fusion.4
  22.0 3.7 fusion.11
  27.0 1.9 pad_maximum_fusion.2
  29.7 1.6 bitcast_dynamic-update-slice_fusion.1
  31.3 832.3 %forward.1 = (bf16[16,2,64,2048]{3,2,1,0:T(8,128)(2,1)}, bf16[16,2,64,2048]{3,2,1,0:T(8,128)(2,1)}, s32[16,1,8,128]{3,2,1,0:T(8,128)}, bf16[2,16,1,64,640]{4,3,2...) custom-call(bf16[2,64,2048]{2,1,0:T(8,128)(2,1)} %bitcast.185, ...), custom_call_target="tpu_custom_call" | custom-call | tf_op jit(solution)/shard_map/forward/pallas_call | solution.py:1027
  863.6 84.4 %experts.1 = (bf16[2048,2048]{1,0:T(8,128)(2,1)}, bf16[2048,2048]{1,0:T(8,128)(2,1)}, bf16[1024,2048]{1,0:T(8,128)(2,1)}, bf16[1024,2048]{1,0:T(8,128)(2,1)}, bf...) custom-call(s32[1,1]{1,0:T(1,128)} %bitcast.15.me_ref, ...), custom_call_target="tpu_custom_call" | custom-call | tf_op jit(solution)/shard_map/experts/pallas_call | solution.py:630
  948.0 12.2 fusion.58
  960.2 93.0 %bundle_reduce_trade.2 = (f32[4,32,2048]{2,1,0:T(8,128)S(1)}, f32[16,8,128]{2,1,0:T(8,128)S(1)}, bf16[2,704,2048]{2,1,0:T(8,128)(2,1)}) custom-call(bf16[16,4,32,2048]{3,2,1,0:T(8,128)(2,1)} %bitcast.171, f32[16,8,128]{2,1,0:T(8,128)S(1)} %copy-done.7, bf16[2,704,2048]{2,1,0:T(8,128)(2,1)} %bitcast.183), custom_call_target="tpu_custom_call" | custom-call | tf_op jit(solution)/shard_map/bundle_reduce_trade/pallas_call | solution.py:492
  1056.1 1.5 multiply_reduce_fusion
  1058.9 7.3 convolution_convert_fusion.2
  1066.8 15.8 %bundle_trade.1 = bf16[16,128,128]{2,1,0:T(8,128)(2,1)S(1)} custom-call(bf16[16,128,128]{2,1,0:T(8,128)(2,1)S(1)} %bitcast.157), custom_call_target="tpu_custom_call" | custom-call | tf_op jit(solution)/shard_map/bundle_trade/pallas_call | solution.py:492
  1082.6 12.5 fusion.61
  1095.2 4.7 fusion.3
  1099.9 6.8 fusion.60
  1106.7 4.2 copy-done.12
  1111.0 1.9 fusion.2
  1112.8 1.5 collective-permute-start.2
  1114.3 1.6 copy.153
  1115.9 5.5 fusion.39
  1124.7 15.0 %attend_back.1 = (f32[2048,192]{1,0:T(8,128)}, f32[2048,192]{1,0:T(8,128)}, f32[2048,128]{1,0:T(8,128)S(1)}) custom-call(bf16[2048,192]{1,0:T(8,128)(2,1)S(1)} %copy-done.1, bf16[3072,192]{1,0:T(8,128)(2,1)} %get-tuple-element.80.key_ref, bf16[3072,128]{1,0:T(8,128)(2,1)S(1)} %copy-done.5, s32[2048,1]{1,0:T(8,128)S(1)} %copy-done, s32[1,3072]{1,0:T(1,128)S(1)} %copy-done.6, ...), custom_call_target="tpu_custom_call" | custom-call | tf_op jit(solution)/shard_map/attend_back/pallas_call | solution.py:730
  1140.7 2.1 slice.156
  1142.8 2.1 slice.154
  1144.9 12.5 copy.148
  1158.3 4.8 fusion.13
  1164.1 5.5 convolution_convert_fusion
  1169.6 1.4 copy.144
  1175.0 7.1 convolution_convert_fusion.6
  1182.1 6.9 convolution_convert_fusion.5
  1189.3 1.6 bitcast_dynamic-update-slice_fusion
  1190.9 1.7 convolution_convert_fusion.4
  1193.3 71.4 %bundle_reduce_trade.3 = (f32[4,32,640]{2,1,0:T(8,128)S(1)}, bf16[16,128,192]{2,1,0:T(8,128)(2,1)S(1)}) custom-call(bf16[16,4,32,640]{3,2,1,0:T(8,128)(2,1)S(1)} %maximum_maximum_fusion.refs_0_, bf16[16,128,192]{2,1,0:T(8,128)(2,1)S(1)} %pad_maximum_fusion.4.refs_1_), custom_call_target="tpu_custom_call" | custom-call | tf_op jit(solution)/shard_map/bundle_reduce_trade/pallas_call | solution.py:492
  1268.9 5.4 all-to-all-start
  1274.4 3.1 convolution_convert_fusion.7
  1277.5 3.3 all-to-all-done
  1280.8 4.3 all-to-all-start.2
  1285.3 7.3 convert_add_fusion
  1292.6 1.4 all-to-all-done.2
  1294.0 4.6 all-to-all-start.1
  1298.7 3.4 pad_maximum_fusion
  1302.7 9.0 fusion.59
  1311.8 2.1 fusion.21
  1314.2 9.6 all-to-all-done.1
  1323.8 4.8 all-to-all-start.3
  1328.6 2.2 bitcast_add_fusion.2
  1330.9 5.6 convolution_convert_fusion.3
  1339.4 1.5 convert_reduce_fusion.1
  1340.9 1.6 copy.145
  1342.5 2.5 reshape.379
  1345.0 6.5 fusion
  1351.6 6.5 fusion.1
  1358.1 6.2 all-to-all-done.3
  1364.2 1.5 convert_reduce_fusion
  1365.7 4.8 reshape.383
  1370.5 2.3 slice_bitcast_fusion
  1372.9 1.7 fusion.55
  1374.5 1.6 copy.151
  1376.2 2.8 squeeze.44
  1378.9 2.8 copy.152
  1381.8 2.7 squeeze.45
  1384.4 3.2 fusion.17
  1387.6 4.9 convolution_convert_fusion.1
  1392.5 33.8 %bundle_owners_owners.1 = (bf16[32,64,36]{2,1,0:T(8,128)(2,1)S(1)}, f32[32,16,128]{2,1,0:T(8,128)S(1)}, bf16[2,64,2048]{2,1,0:T(8,128)(2,1)S(1)}) custom-call(bf16[32,64,36]{2,1,0:T(8,128)(2,1)S(1)} %bitcast.156, f32[32,16,128]{2,1,0:T(8,128)S(1)} %bitcast.162, bf16[2,64,2048]{2,1,0:T(8,128)(2,1)S(1)} %bitcast.155), custom_call_target="tpu_custom_call" | custom-call | tf_op jit(solution)/shard_map/bundle_owners_owners/pallas_call | solution.py:492
  (208 shorter events, 39.9 us)
Async XLA Ops:
  7.2 5.5 copy-start.30
  7.2 1377.2 %reduce-scatter.2.cloned.1.call-start = ((), (), s32[]{:S(2)}) async-start(), calls=%async_computation.5 | async-start | bytes 8912896 | tf_op jit(solution)/shard_map/reduce_scatter | solution.py:1288
  10.4 11.6 copy-start.43
  10.4 11.6 copy-start.54
  10.4 3.8 copy-start.48
  25.7 3.2 copy-start.17
  25.8 3.2 copy-start.18
  948.0 12.2 copy-start.7
  1053.3 2.1 copy-start.8
  1053.3 2.3 copy-start.37
  1053.3 2.3 copy-start.40
  1053.3 5.2 copy-start.15
  1053.4 334.2 %all-gather.2.cloned.1.call-start = ((), (), s32[]{:S(2)}) async-start(), calls=%async_computation.6 | async-start | bytes 8912896 | tf_op jit(solution)/shard_map/all_gather | solution.py:1352
  1054.2 135.1 %collective-permute-start = (bf16[256,256]{1,0:T(8,128)(2,1)S(1)}, bf16[256,256]{1,0:T(8,128)(2,1)}, u32[]{:S(2)}, u32[]{:S(2)}) collective-permute-start(bf16[256,256]{1,0:T(8,128)(2,1)S(1)} %copy-done.38), channel_id=1, source_target_pairs={{0,16},{16,0},{1,17},{17,1},{2,18},{18,2},{3,19},{19,3},{4,20},{20... | collective-permute-start | bytes 393224 | tf_op jit(solution)/shard_map/ppermute | solution.py:1070
  1056.1 2.8 copy-start.45
  1057.6 8.6 copy-start.52
  1058.9 7.3 copy-start.16
  1082.6 17.2 %copy-start.57 = (bf16[1024,1408]{1,0:T(8,128)(2,1)S(1)}, bf16[1024,1408]{1,0:T(8,128)(2,1)}, u32[]{:S(2)}) copy-start(bf16[1024,1408]{1,0:T(8,128)(2,1)} %get-tuple-element.103) | copy-start | bytes 8650756
  1095.2 4.7 copy-start.56
  1099.8 245.2 %collective-permute-start.3 = (bf16[1024,1408]{1,0:T(8,128)(2,1)}, bf16[1024,1408]{1,0:T(8,128)(2,1)}, u32[]{:S(2)}, u32[]{:S(2)}) collective-permute-start(bf16[1024,1408]{1,0:T(8,128)(2,1)} %fusion.3), channel_id=1, source_target_pairs={{0,16},{16,0},{1,17},{17,1},{2,18},{18,2},{3,19},{19,3},{4,20},{20... | collective-permute-start | bytes 8650760 | tf_op jit(solution)/shard_map/ppermute | solution.py:1089
  1106.7 4.3 copy-start.12
  1106.7 7.6 copy-start.31
  1112.8 238.7 %collective-permute-start.2 = (bf16[1024,1408]{1,0:T(8,128)(2,1)}, bf16[1024,1408]{1,0:T(8,128)(2,1)}, u32[]{:S(2)}, u32[]{:S(2)}) collective-permute-start(bf16[1024,1408]{1,0:T(8,128)(2,1)} %fusion.2), channel_id=1, source_target_pairs={{0,16},{16,0},{1,17},{17,1},{2,18},{18,2},{3,19},{19,3},{4,20},{20... | collective-permute-start | bytes 8650760 | tf_op jit(solution)/shard_map/ppermute | solution.py:1089
  1115.9 7.6 copy-start
  1115.9 7.5 copy-start.1
  1115.9 7.5 copy-start.5
  1115.9 7.5 copy-start.6
  1121.5 1.2 copy-start.19
  1123.4 205.2 %collective-permute-start.1 = (bf16[88,2048]{1,0:T(8,128)(2,1)}, bf16[88,2048]{1,0:T(8,128)(2,1)}, u32[]{:S(2)}, u32[]{:S(2)}) collective-permute-start(bf16[88,2048]{1,0:T(8,128)(2,1)} %fusion.43), channel_id=1, source_target_pairs={{0,16},{16,0},{1,17},{17,1},{2,18},{18,2},{3,19},{19,3},{4,20},{20... | collective-permute-start | bytes 1081352 | tf_op jit(solution)/shard_map/ppermute | solution.py:1089
  1123.5 1.2 copy-start.2
  1144.9 12.5 copy-start.4
  1144.9 13.4 copy-start.20
  1144.9 13.4 copy-start.44
  1144.9 13.4 copy-start.55
  1158.3 4.8 copy-start.22
  1164.1 7.0 copy-start.9
  1164.1 7.0 copy-start.41
  1164.1 7.0 copy-start.46
  1169.6 3.5 copy-start.50
  1175.0 7.1 copy-start.59
  1182.0 6.9 copy-start.23
  1182.1 6.9 copy-start.26
  1182.1 6.9 copy-start.28
  1182.1 8.8 copy-start.24
  1182.1 8.8 copy-start.29
  1189.0 3.6 copy-start.21
  1193.3 71.5 %copy-start.51 = (f32[512]{0:T(512)S(1)}, f32[512]{0:T(512)}, u32[]{:S(2)}) copy-start(f32[512]{0:T(512)} %param.24) | copy-start | bytes 6148
  1266.8 18.2 %copy-start.13 = (bf16[128,2048]{1,0:T(8,128)(2,1)S(1)}, bf16[128,2048]{1,0:T(8,128)(2,1)}, u32[]{:S(2)}) copy-start(bf16[128,2048]{1,0:T(8,128)(2,1)} %param.18) | copy-start | bytes 1572868
  1268.9 11.9 all-to-all-start
  1280.8 11.8 copy-start.33
  1280.8 13.2 all-to-all-start.2
  1294.0 8.0 copy-start.32
  1294.0 29.8 %all-to-all-start.1 = ((bf16[32,64,192]{2,1,0:T(8,128)(2,1)}), bf16[32,64,192]{2,1,0:T(8,128)(2,1)}, u32[]{:S(2)}, u32[]{:S(2)}) async-start(bf16[32,64,192]{2,1,0:T(8,128)(2,1)} %bitcast.187), calls=%async_computation.2 | async-start | bytes 2097152 | tf_op jit(solution)/shard_map/all_to_all | solution.py:1379
  1302.7 9.1 copy-start.36
  1302.7 9.1 copy-start.49
  1302.7 9.1 copy-start.58
  1311.8 2.3 copy-start.39
  1311.8 2.3 copy-start.47
  1313.9 16.9 %copy-start.34 = (bf16[16,128,36]{1,2,0:T(8,128)(2,1)S(1)}, bf16[16,128,36]{1,2,0:T(8,128)(2,1)}, u32[]{:S(2)}) copy-start(bf16[16,128,36]{1,2,0:T(8,128)(2,1)} %copy-done.33) | copy-start | bytes 442372
  1323.8 40.4 %all-to-all-start.3 = ((bf16[32,64,384]{2,1,0:T(8,128)(2,1)}), bf16[32,64,384]{2,1,0:T(8,128)(2,1)S(1)}, u32[]{:S(2)}, u32[]{:S(2)}) async-start(bf16[32,64,384]{2,1,0:T(8,128)(2,1)} %pad_maximum_fusion), calls=%async_computation.4 | async-start | bytes 3145728 | tf_op jit(solution)/shard_map/all_to_all | solution.py:1299
  1376.2 8.3 copy-start.11
  1376.2 8.3 copy-start.14
  1376.2 8.3 copy-start.42
  1376.2 8.3 copy-start.53
  (6 other events, 5.5 us)
Sparse Core Ops, SparseCore 0:
  1053.5 103.6 reduce-scatter.1
  1159.3 99.6 all-gather.1

commit v5 on v4

--- a/solution.py
+++ b/solution.py
@@ -77,13 +77,6 @@
 def swish_parts(values):
     sigmoid_part = jax.nn.sigmoid(values)
     return (values * sigmoid_part, sigmoid_part * (1.0 + values * (1.0 - sigmoid_part)))
-
-
-def plane_groups(plane):
-    members = SEQ_DEVICES
-    if plane == members:
-        return None
-    return [list(range(low, low + members)) for low in range(0, plane, members)]
 
 
 MESH = pl.DeviceIdType.MESH
@@ -445,8 +438,10 @@
             else:
                 waits.append(head_rows(place, plane, shards, own, out, copy_sem, send_sem, recv_sem))
                 continue
-            keep = pltpu.make_async_copy(source(mine), out.at[mine], copy_sem)
-            keep.start()
+            keep = None
+            if kind != "share":
+                keep = pltpu.make_async_copy(source(mine), out.at[mine], copy_sem)
+                keep.start()
             total = len(targets) + 1
             copies = []
             for step, (target, peer) in enumerate(targets, 1):
@@ -457,7 +452,8 @@
     while runs:
         runs = [run for run in runs if next(run, "end") != "end"]
     for keep, copies in waits:
-        keep.wait()
+        if keep is not None:
+            keep.wait()
         for copy in copies:
             copy.wait()
     sender.finish()
@@ -515,10 +511,39 @@
 
 
 def expert_kernel(
-    me_ref, routes_ref, router_ref, rows_in, grads_in, gate_w, up_w, down_w, shared_gate_w, shared_up_w, shared_down_w,
-    back_ref, out_ref, rows_ref, grad_ref, hidden_ref, gate_back_ref, up_back_ref, score_ref,
-    shared_hidden_ref, shared_gate_back_ref, shared_up_back_ref, slot_cotangent, pick_buf, gate_buf,
+    me_ref, routes_ref, router_ref, rows_in, grads_in, *rest
 ):
+    weights, rest = rest[:12], rest[12:]
+    (back_ref, out_ref, rows_ref, grad_ref, hidden_ref, gate_back_ref, up_back_ref, score_ref,
+     shared_hidden_ref, shared_gate_back_ref, shared_up_back_ref, slot_cotangent, pick_buf, gate_buf,
+     gate_w, up_w, down_w, shared_gate_w, shared_up_w, shared_down_w, weight_sem) = rest
+    targets = (shared_gate_w, shared_up_w, shared_down_w, gate_w, up_w, down_w)
+    shard_at = me_ref[0, 1]
+    loads = []
+    for index, target in enumerate(targets):
+        own, got = weights[2 * index], weights[2 * index + 1]
+        count = got.shape[0]
+        for step in range(count):
+            at = lax.rem(shard_at + step, count)
+            block = own.shape[0]
+            spot = target.at[at] if len(target.shape) == 3 else target.at[pl.ds(pl.multiple_of(at * block, 16), block), :]
+            source = own if step == 0 else got.at[at]
+            loads.append(pltpu.make_async_copy(source, spot, weight_sem.at[index, step]))
+
+    def when_first(action):
+        @pl.when(pl.program_id(0) == 0)
+        def _():
+            action()
+
+    def start_loads():
+        for load in loads:
+            load.start()
+
+    def wait_loads():
+        for load in loads:
+            load.wait()
+
+    when_first(start_loads)
     width = rows_in.shape[1]
     hidden_width = gate_w.shape[1]
     shards, own_width, _ = shared_gate_w.shape
@@ -565,6 +590,7 @@
         return 0
 
     lax.fori_loop(0, width // 512, pick_step, 0)
+    when_first(wait_loads)
     shared_pre, shared_up = 0.0, 0.0
     for shard in range(shards):
         part = rows_in[:, shard * own_width : (shard + 1) * own_width]
@@ -609,13 +635,14 @@
         score_ref[sender] = jnp.broadcast_to(total, score_ref.shape[1:])
 
 
-def expert_pass(me, routes, router, rows, grads, gate_w, up_w, down_w, shared_gate_w, shared_up_w, shared_down_w, capacity):
+def expert_pass(me, routes, router, rows, grads, weights, capacity):
     plane, _, local = routes.shape
     senders = STEP_SENDERS
     tokens, slots = senders * local, senders * capacity
     steps = plane // senders
-    width, hidden_width = gate_w.shape
-    units = shared_gate_w.shape[2]
+    shards = weights[1].shape[0]
+    width, hidden_width = rows.shape[1], weights[6].shape[1]
+    units = weights[0].shape[1]
     low = jnp.bfloat16
 
     def whole(array):
@@ -649,13 +676,8 @@
             whole(router),
             by_step(tokens, width),
             by_step(tokens, width),
-            whole(gate_w),
-            whole(up_w),
-            whole(down_w),
-            whole(shared_gate_w),
-            whole(shared_up_w),
-            whole(shared_down_w),
-        ],
+        ]
+        + [pl.BlockSpec(memory_space=pl.ANY)] * len(weights),
         out_specs=[
             by_step(tokens, width),
             by_step(tokens, width),
@@ -673,12 +695,19 @@
             pltpu.VMEM((slots, width), low),
             pltpu.VMEM((slots, tokens), low),
             pltpu.VMEM((slots, 1), jnp.float32),
+            pltpu.VMEM((width, hidden_width), low),
+            pltpu.VMEM((width, hidden_width), low),
+            pltpu.VMEM((hidden_width, width), low),
+            pltpu.VMEM((shards, width // shards, units), low),
+            pltpu.VMEM((shards, width // shards, units), low),
+            pltpu.VMEM((units, width), low),
+            pltpu.SemaphoreType.DMA((6, shards)),
         ],
         compiler_params=pltpu.CompilerParams(
             vmem_limit_bytes=60 * 2**20, dimension_semantics=("arbitrary",)
         ),
         name="experts",
-    )(me, routes, router, rows, grads, gate_w, up_w, down_w, shared_gate_w, shared_up_w, shared_down_w)
+    )(me, routes, router, rows, grads, *weights)
 
 
 QUERIES = 256
@@ -691,56 +720,6 @@
     column = lax.broadcasted_iota(jnp.int32, raw.shape, 1)
     allowed = (query_docs == key_docs) & (column <= row) & (column > row - WINDOW)
     return jnp.where(allowed, raw, NEG)
-
-
-def attend_back_kernel(
-    scale, last, query_ref, key_ref, value_ref, docs_ref, row_docs_ref, total_ref, grad_ref,
-    query_grad_ref, key_grad_ref, value_grad_ref, key_sum, value_sum,
-):
-    step = pl.program_id(0)
-
-    @pl.when(step == 0)
-    def _():
-        key_sum[...] = jnp.zeros_like(key_sum)
-        value_sum[...] = jnp.zeros_like(value_sum)
-
-    at = pl.ds(pl.multiple_of(step * QUERIES, QUERIES), KEYS)
-    query, keys, grad = query_ref[...], key_ref[at, :], grad_ref[...]
-    grad = jnp.where(docs_ref[...] < last, grad, jnp.zeros((), grad.dtype))
-    scores = score_block(scale, query, keys, docs_ref[...], row_docs_ref[:, at])
-    probs = jnp.exp(scores - total_ref[:, :1])
-    prob_grad = matmul_nt(grad, value_ref[at, :])
-    inner = jnp.sum(probs * prob_grad, axis=1, keepdims=True)
-    raw_grad = (probs * (prob_grad - inner) * scale).astype(jnp.bfloat16)
-    query_grad_ref[...] = matmul(raw_grad, keys)
-    key_sum[at, :] += matmul_tn(raw_grad, query)
-    value_sum[at, :] += matmul_tn(probs.astype(jnp.bfloat16), grad)
-
-    @pl.when(step == pl.num_programs(0) - 1)
-    def _():
-        key_grad_ref[...] = key_sum[WINDOW:, :]
-        value_grad_ref[...] = value_sum[WINDOW:, :]
-
-
-def attend_back(scale, last, query, keys, value, docs, row_docs, totals, grad):
-    rows, head_dim = query.shape
-    whole = lambda a: pl.BlockSpec(a.shape, lambda i: (0, 0))
-    by_step = lambda c: pl.BlockSpec((QUERIES, c), lambda i: (i, 0))
-    full = lambda c: pl.BlockSpec((rows, c), lambda i: (0, 0))
-    return pl.pallas_call(
-        functools.partial(attend_back_kernel, scale, last),
-        grid=(rows // QUERIES,),
-        out_shape=[
-            jax.ShapeDtypeStruct((rows, head_dim), jnp.float32),
-            jax.ShapeDtypeStruct((rows, head_dim), jnp.float32),
-            jax.ShapeDtypeStruct((rows, V_HEAD), jnp.float32),
-        ],
-        in_specs=[by_step(head_dim), whole(keys), whole(value), by_step(1), whole(row_docs), by_step(128), by_step(V_HEAD)],
-        out_specs=[by_step(head_dim), full(head_dim), full(V_HEAD)],
-        scratch_shapes=[pltpu.VMEM(keys.shape, jnp.float32), pltpu.VMEM(value.shape, jnp.float32)],
-        compiler_params=pltpu.CompilerParams(vmem_limit_bytes=48 * 2**20, dimension_semantics=("arbitrary",)),
-        name="attend_back",
-    )(query, keys, value, docs, row_docs, totals, grad)
 
 
 class Swaps:
@@ -772,6 +751,15 @@
         return wait
 
 
+def whole_weight(place, others, own_ref, full_ref, buf, sem):
+    copies = [pltpu.make_async_copy(own_ref, buf.at[place.shard], sem.at[0])]
+    for step, other in enumerate(others, 1):
+        copies.append(pltpu.make_async_copy(full_ref.at[other], buf.at[other], sem.at[step]))
+    for copy in copies:
+        copy.start()
+    return copies
+
+
 def drain(run):
     for _ in run:
         pass
@@ -782,10 +770,10 @@
      shared_gate, shared_up, shared_down, routes, first_gain, latent_gain, second_gain, turn, sway, docs, row_docs,
      all_normed, all_grads, all_routes, full_down, full_out, full_query, full_gate, full_up, full_narrow,
      full_shared_gate, full_shared_up, full_shared_down, normed_one,
-     query, keys, value, key_latent, compressed, head_out, log_total, middle,
-     token_buf, normed_buf, query_buf, up_buf, down_buf, out_buf, heads_buf, second_buf,
+     query, keys, value, key_latent, compressed, head_out, log_total, middle, up_buf,
+     token_buf, normed_buf, query_buf, down_buf, out_buf, heads_buf, second_buf,
      swap_send, swap_recv, keep_sem, gather_send, gather_recv, gather_keep, piece_send, piece_recv,
-     trade_send, trade_recv, load_sem) = refs
+     trade_send, trade_recv, load_sem, whole_sem) = refs
     low = jnp.bfloat16
     group = SEQ_DEVICES
     place, wide = Place(group), Place(plane)
@@ -822,13 +810,6 @@
     next(token_run)
     got_out = swap(at_piece(out_half), lambda shard: full_out.at[shard, wide.me])
     got_wq = swap(at_piece(query_half), lambda shard: full_query.at[shard, wide.me])
-    owns = [
-        pltpu.make_async_copy(half, full.at[place.shard], load_sem.at[index])
-        for index, (half, full) in enumerate(((down_half, full_down), (out_half, full_out), (query_half, full_query)))
-    ]
-    for own in owns:
-        own.start()
-
     def piece_gathers(kind, full):
         return [
             gather_steps(
@@ -848,22 +829,20 @@
     got_query()
     got_up()
     waits = [
-        swap(gate_half, lambda shard: full_gate.at[shard], True),
-        swap(wide_half, lambda shard: full_up.at[shard], True),
+        swap(gate_half, lambda shard: full_gate.at[shard]),
+        swap(wide_half, lambda shard: full_up.at[shard]),
     ]
     drain(token_run)
     got_out()
     got_wq()
     waits += [
-        swap(shared_gate, lambda shard: full_shared_gate.at[shard], True),
-        swap(shared_up, lambda shard: full_shared_up.at[shard], True),
-        swap(shared_down, lambda shard: full_shared_down.at[shard], True),
-        swap(narrow_half, lambda shard: full_narrow.at[shard], True),
+        swap(shared_gate, lambda shard: full_shared_gate.at[shard]),
+        swap(shared_up, lambda shard: full_shared_up.at[shard]),
+        swap(shared_down, lambda shard: full_shared_down.at[shard]),
+        swap(narrow_half, lambda shard: full_narrow.at[shard]),
     ]
     for run in down_runs:
         drain(run)
-    for own in owns:
-        own.wait()
     route_run = gather_steps(
         wide, routes, all_routes, gather_keep.at[1], gather_send.at[1], gather_recv.at[1], sender
     )
@@ -871,9 +850,8 @@
     out_runs = piece_gathers(1, full_out)
     for run in out_runs:
         next(run)
-    load_down = pltpu.make_async_copy(full_down, down_buf, load_sem.at[0])
-    load_down.start()
-    load_down.wait()
+    for copy in whole_weight(place, others, down_half, full_down, down_buf, whole_sem.at[0]):
+        copy.wait()
 
     keys[:WINDOW, :] = jnp.zeros((WINDOW, keys.shape[1]), low)
     value[:WINDOW, :] = jnp.zeros((WINDOW, value.shape[1]), low)
@@ -893,10 +871,11 @@
         normed_buf[at, :] = (values * root * first_gain[...]).astype(low)
         first = whole_dot(at, lambda shard: query_buf[shard])
         latent = whole_dot(at, lambda shard: down_buf[shard].reshape(own_width, -1))
-        turn_at, sway_at = turn[at, :], sway[at, :]
+        turn_at, sway_at = turn[at, :QK_ROPE], sway[at, :QK_ROPE]
         end = QK_NOPE + QK_ROPE
         query[at, :QK_NOPE] = first[:, :QK_NOPE].astype(low)
-        query[at, QK_NOPE:] = (first[:, QK_NOPE:end] * turn_at + first[:, end:] * sway_at).astype(low)
+        query[at, QK_NOPE:end] = (first[:, QK_NOPE:end] * turn_at + first[:, end:] * sway_at).astype(low)
+        query[at, end:] = jnp.zeros((tile, QK_ROPE), low)
         end = KV_RANK + QK_ROPE
         key_rope = (latent[:, KV_RANK:end] * turn_at + latent[:, end:] * sway_at).astype(low)
         latent = latent[:, :KV_RANK]
@@ -911,15 +890,20 @@
         both = both.astype(low)
         later = pl.ds(pl.multiple_of(index * tile + WINDOW, tile), tile)
         keys[later, :QK_NOPE] = both[:, :QK_NOPE]
-        keys[later, QK_NOPE:] = key_rope
+        keys[later, QK_NOPE : QK_NOPE + QK_ROPE] = key_rope
+        keys[later, QK_NOPE + QK_ROPE :] = key_rope
         value[later, :] = both[:, QK_NOPE:]
         return 0
 
     tiles = group // 2
+    grad_run = gather_steps(
+        wide, cotangent, all_grads, gather_keep.at[3], gather_send.at[3], gather_recv.at[3], sender
+    )
     for part in range(2):
         lax.fori_loop(part * tiles // 2, (part + 1) * tiles // 2, front_tile, 0)
         for run in out_runs + [route_run]:
             next(run, None)
+    next(grad_run)
     save = pltpu.make_async_copy(normed_buf, normed_one, load_sem.at[1])
     save.start()
     for run in out_runs + [route_run]:
@@ -942,8 +926,8 @@
     lax.fori_loop(0, blocks // 2, attend_tile, 0)
     for run in out_runs + [route_run]:
         drain(run)
-    load_out = pltpu.make_async_copy(full_out, out_buf, load_sem.at[0])
-    load_out.start()
+    load_out = whole_weight(place, others, out_half, full_out, out_buf, whole_sem.at[1])
+    next(grad_run)
     lax.fori_loop(blocks // 2, blocks, attend_tile, 0)
 
     def head_at(member):
@@ -967,7 +951,8 @@
             head_at(member), lands(member), trade_send.at[step], trade_recv.at[member], {"expert": place.base + member}
         ).wait_recv()
     keep.wait()
-    load_out.wait()
+    for copy in load_out:
+        copy.wait()
 
     for at, size in pieces_of(width, 512):
         columns = slice(at, at + size)
@@ -982,9 +967,6 @@
 
     normed_run = gather_steps(
         wide, second_buf, all_normed, gather_keep.at[2], gather_send.at[2], gather_recv.at[2], sender
-    )
-    grad_run = gather_steps(
-        wide, cotangent, all_grads, gather_keep.at[3], gather_send.at[3], gather_recv.at[3], sender
     )
     wq_runs = piece_gathers(2, full_query)
     runs = [normed_run, grad_run] + wq_runs
@@ -1012,17 +994,17 @@
     out_shape += [shape((shards,) + block.shape, low) for block in (down_half, out_half, query_half) + blocks[5:]]
     out_shape += [
         shape((SEQ, width), low),
-        shape((SEQ, head_dim), low),
-        shape((SEQ + WINDOW, head_dim), low),
+        shape((SEQ, head_dim + QK_ROPE), low),
+        shape((SEQ + WINDOW, head_dim + QK_ROPE), low),
         shape((SEQ + WINDOW, V_HEAD), low),
         shape((SEQ, KV_RANK), low),
         shape((SEQ, KV_RANK), jnp.float32),
         shape((SEQ, V_HEAD), low),
         shape((SEQ, 128), jnp.float32),
         shape((local, width), jnp.float32),
+        shape((shards,) + up_half.shape, low),
     ]
     hbm_out = 13
-    own_width = width // shards
     dma = pltpu.SemaphoreType.DMA
     return pl.pallas_call(
         functools.partial(forward_kernel, shards, plane, scale, last),
@@ -1033,7 +1015,6 @@
             pltpu.VMEM((SEQ_DEVICES,) + pieces, low),
             pltpu.VMEM((SEQ, width), low),
             pltpu.VMEM((shards,) + query_cols.shape, low),
-            pltpu.VMEM((shards,) + up_half.shape, low),
             pltpu.VMEM((shards,) + down_half.shape, low),
             pltpu.VMEM((shards,) + out_half.shape, low),
             pltpu.VMEM((local, HEADS * V_HEAD), low),
@@ -1049,6 +1030,7 @@
             dma((SEQ_DEVICES,)),
             dma((SEQ_DEVICES,)),
             dma((4,)),
+            dma((2, shards)),
         ],
         compiler_params=pltpu.CompilerParams(
             collective_id=1, has_side_effects=True, vmem_limit_bytes=60 * 2**20
@@ -1057,42 +1039,487 @@
     )(tokens.reshape(pieces), cotangent.reshape(pieces), *blocks, routes[None], *gains, *tables)
 
 
-def tie(value, *awaited):
-    return lax.optimization_barrier((value,) + awaited)
-
-
-def shard_ring(block):
-    count = lax.axis_size("shard")
-    me = lax.axis_index("shard")
-    whole = jnp.zeros((count,) + block.shape, block.dtype)
-    whole = lax.dynamic_update_index_in_dim(whole, block, me, 0)
-    for step in range(1, count):
-        moved = lax.ppermute(
-            block, "shard", [(source, (source + step) % count) for source in range(count)]
+class Everyone:
+    def __init__(self, place, plane, shards, source, got, send_sem, recv_sem, keep_sem):
+        self.total = shards * plane
+        self.plane = plane
+        self.number = place.shard * plane + place.me
+        self.source, self.got = source, got
+        self.send_sem, self.recv_sem = send_sem, recv_sem
+        self.keep = pltpu.make_async_copy(source(self.number), got.at[self.number], keep_sem)
+
+    def copy(self, step, arriving):
+        other = lax.rem(self.number + step, self.total)
+        spot = other if arriving else self.number
+        return remote(
+            self.source(other),
+            self.got.at[spot],
+            self.send_sem.at[step],
+            self.recv_sem.at[spot],
+            {"shard": other // self.plane, "expert": lax.rem(other, self.plane)},
         )
-        whole = lax.dynamic_update_index_in_dim(whole, moved, (me - step) % count, 0)
-    return whole
-
-
-def shard_rows(block):
-    whole = shard_ring(block)
-    return whole.reshape((-1,) + block.shape[1:])
-
-
-def shard_sum(values):
-    count = lax.axis_size("shard")
-    me = lax.axis_index("shard")
-    blocks = values.reshape((count, -1) + values.shape[1:])
-    total = lax.dynamic_index_in_dim(blocks, me, 0, keepdims=False)
-    for step in range(1, count):
-        outgoing = lax.dynamic_index_in_dim(blocks, (me + step) % count, 0, keepdims=False)
-        moved = lax.ppermute(
-            outgoing.astype(jnp.bfloat16),
-            "shard",
-            [(source, (source + step) % count) for source in range(count)],
+
+    def start(self):
+        self.keep.start()
+
+        def body(step, _):
+            self.copy(step, False).start()
+            return 0
+
+        lax.fori_loop(1, self.total, body, 0)
+
+    def wait(self):
+        self.keep.wait()
+
+        def body(step, _):
+            self.copy(step, True).wait_recv()
+            return 0
+
+        lax.fori_loop(1, self.total, body, 0)
+
+    def finish(self):
+        def body(step, _):
+            self.copy(step, False).wait_send()
+            return 0
+
+        lax.fori_loop(1, self.total, body, 0)
+
+
+def greet_everyone(place, plane, shards):
+    barrier = pltpu.get_barrier_semaphore()
+    total = shards * plane
+    number = place.shard * plane + place.me
+
+    def body(step, _):
+        other = lax.rem(number + step, total)
+        pl.semaphore_signal(
+            barrier,
+            inc=1,
+            device_id={"shard": other // plane, "expert": lax.rem(other, plane)},
+            device_id_type=MESH,
         )
-        total = total + moved.astype(jnp.float32)
-    return total
+        return 0
+
+    lax.fori_loop(1, total, body, 0)
+    pl.semaphore_wait(barrier, total - 1)
+
+
+def norm_back(values, gain, grad):
+    root = lax.rsqrt(jnp.mean(values * values, axis=1, keepdims=True) + EPS)
+    weighted = grad * gain
+    inner = jnp.mean(weighted * values, axis=1, keepdims=True)
+    scaled = values * root
+    return root * (weighted - scaled * (root * inner)), jnp.sum(grad * scaled, axis=0, keepdims=True)
+
+
+def two_parts(values):
+    high = values.astype(jnp.bfloat16)
+    return high, (values - high.astype(jnp.float32)).astype(jnp.bfloat16)
+
+
+def swapped_halves(pair):
+    return pltpu.roll(pair, QK_ROPE // 2, 1)
+
+
+def backward_kernel(shards, plane, scale, last, *refs):
+    (back, scores, routes, middle, cotangent, tokens, first_gain, second_gain, latent_gain, router,
+     query, keys, value, docs, row_docs, log_total, turn, sway, key_latent, up_head, head_out,
+     compressed, full_out, full_query, full_down, normed_one, out_half, query_half, down_half, gate_send, up_send, narrow_send, shared_term,
+     input_grad, query_out, up_out, down_out, out_out, small_out,
+     gate_got, up_got, narrow_got, shared_got, mid_all,
+     stream_buf, wq_buf, wd_buf, own_columns, own_compressed, heads_sum, mid_buf, low_buf, heads_buf, grad_buf, key_sum, value_sum,
+     part_buf, trade_buf, trade_got, pair_buf, query_term, query_got, up_term, up_got_buf, own_query, low_grad, low_all,
+     down_rows, down_got, out_rows, out_got, small_buf, small_got, key_got, *sems) = refs
+    (load_sem, whole_sem, stream_sem, swap_send, swap_recv, trade_send, trade_recv, gather_send, gather_recv, gather_keep,
+     all_send, all_recv, all_keep, rows_send, rows_recv, rows_keep, *reduce_scratch_refs) = sems
+    low = jnp.bfloat16
+    group = SEQ_DEVICES
+    place = Place(group)
+    local, width = middle.shape
+    total = shards * plane
+    sender = Sender()
+    greet_everyone(place, plane, shards)
+    members = [lax.rem(place.local + step, group) for step in range(1, group)]
+    others = [lax.rem(place.shard + step, shards) for step in range(1, shards)]
+
+    shares = []
+    for number, (source, got) in enumerate(((gate_send, gate_got), (up_send, up_got), (narrow_send, narrow_got))):
+        for step, other in enumerate(others, 1):
+            sender.start(
+                place.always,
+                remote(source.at[other], got.at[place.shard], swap_send.at[number, step],
+                       swap_recv.at[number, place.shard], {"shard": other}),
+            )
+            shares.append(
+                remote(source.at[other], got.at[other], swap_send.at[number, step], swap_recv.at[number, other],
+                       {"shard": other})
+            )
+    numbers = iter(range(16))
+
+    def load(source, target):
+        copy = pltpu.make_async_copy(source, target, load_sem.at[next(numbers)])
+        copy.start()
+        return copy
+
+    own_lanes = pl.ds(pl.multiple_of(place.local * 128, 128), 128)
+    got_wd = whole_weight(place, others, down_half, full_down, wd_buf, whole_sem)
+    got_columns = load(normed_one.at[:, :, :, own_lanes], own_columns)
+    tile = stream_buf.shape[-1]
+    tiles = [slice(at, at + tile) for at in range(0, width, tile)]
+
+    def streamed(buf, count, sources):
+        def copies(index):
+            half = index % 2
+            return [
+                (there, pltpu.make_async_copy(source, target, stream_sem.at[half, number]))
+                for there, source, target, number in sources(index, buf.at[half])
+            ]
+
+        def start(index):
+            for there, copy in copies(index):
+                @pl.when(there)
+                def _():
+                    copy.start()
+
+        start(0)
+        for index in range(count):
+            if index + 1 < count:
+                start(index + 1)
+            for there, copy in copies(index):
+                @pl.when(there)
+                def _():
+                    copy.wait()
+            yield index, buf.at[index % 2]
+
+    own_at = pl.ds(pl.multiple_of(place.local * local, local), local)
+    per_shard = group // shards
+
+    def columns_of(array):
+        def sources(index, target):
+            return [
+                (place.always, array.at[pl.ds(shard * per_shard, per_shard), :, :, tiles[index]], target.at[shard], shard)
+                for shard in range(shards)
+            ]
+
+        return sources
+
+    def out_columns(index, target):
+        found = []
+        for shard in range(shards):
+            mine = place.shard == shard
+            found.append((mine, out_half.at[:, :, :, tiles[index]], target.at[shard], shard))
+            found.append((~mine, full_out.at[shard, :, :, :, tiles[index]], target.at[shard], shard))
+        return found
+
+    row_tile = wq_buf.shape[1]
+    own_rows = width // shards
+
+    def query_rows(index, target):
+        shard = index * row_tile // own_rows
+        rows = slice(index * row_tile - shard * own_rows, (index + 1) * row_tile - shard * own_rows)
+        mine = place.shard == shard
+        return [(mine, query_half.at[rows], target, 0), (~mine, full_query.at[shard, rows], target, 0)]
+
+    got_compressed = load(compressed.at[own_at, :], own_compressed)
+
+    def everyone(index, source, got):
+        return Everyone(place, plane, shards, source, got, all_send.at[index], all_recv.at[index], all_keep.at[index])
+
+    experts = router.shape[0]
+    values = middle[...]
+    root = lax.rsqrt(jnp.mean(values * values, axis=1, keepdims=True) + EPS)
+    second_normed = (values * root * second_gain[...]).astype(low)
+    logits = matmul_nt(router[...], second_normed)
+    names = lax.broadcasted_iota(jnp.int32, (experts, local), 0)
+    chosen = jnp.zeros((experts, local), jnp.float32)
+    for choice in range(TOP):
+        chosen = chosen + jnp.where(routes[choice : choice + 1, :] == names, 1.0, 0.0)
+    logits = jnp.where(chosen > 0.0, logits, NEG)
+    gates = jnp.exp(logits - jnp.max(logits, axis=0, keepdims=True)) * chosen
+    gates = gates / jnp.sum(gates, axis=0, keepdims=True)
+    gate_grad = jnp.concatenate([scores[index, :1, :] for index in range(experts)], axis=0)
+    logit_grad = gates * (gate_grad - jnp.sum(gates * gate_grad, axis=0, keepdims=True))
+    high, rest = two_parts(logit_grad)
+    router_term = matmul(high, second_normed) + matmul(rest, second_normed)
+    grad = back[...] + matmul_tn(high, router[...]) + matmul_tn(rest, router[...])
+    row_grad, second_term = norm_back(values, second_gain[...], grad)
+    mid_buf[...] = cotangent[...].astype(jnp.float32) + row_grad
+    low_buf[...] = mid_buf[...].astype(low).reshape(low_buf.shape)
+
+    for index, piece in streamed(stream_buf, len(tiles), out_columns):
+        part = matmul_nt(low_buf[:, :, tiles[index]].reshape(local, tile), piece[...].reshape(-1, tile))
+        heads_sum[...] = part if index == 0 else heads_sum[...] + part
+    heads_buf[...] = heads_sum[...].astype(low)
+
+    def lands(member):
+        return heads_buf.at[:, pl.ds(pl.multiple_of(member * V_HEAD, V_HEAD), V_HEAD)]
+
+    def head_trade(step, member, source):
+        spot = pl.ds(pl.multiple_of(source * local, local), local)
+        return remote(lands(member), grad_buf.at[spot, :], trade_send.at[0, step], trade_recv.at[0, source],
+                      {"expert": place.base + member})
+
+    keep_head = pltpu.make_async_copy(lands(place.local), grad_buf.at[own_at, :], load_sem.at[next(numbers)])
+    keep_head.start()
+    for step, member in enumerate(members):
+        sender.start(place.always, head_trade(step, member, place.local))
+    mid_run = gather_steps(place, low_buf, mid_all, gather_keep.at[0], gather_send.at[0], gather_recv.at[0], sender)
+    for step, member in enumerate(members):
+        head_trade(step, member, member).wait_recv()
+    keep_head.wait()
+    next(mid_run)
+    shared_trade = everyone(0, lambda target: shared_term.at[target], shared_got)
+    shared_trade.start()
+
+    key_sum[...] = jnp.zeros_like(key_sum)
+    value_sum[...] = jnp.zeros_like(value_sum)
+
+    def attend_tile(index, _):
+        at = pl.ds(pl.multiple_of(index * QUERIES, QUERIES), QUERIES)
+        window = pl.ds(pl.multiple_of(index * QUERIES, QUERIES), KEYS)
+        tile, key_tile = query[at, :], keys[window, :]
+        head_grad = jnp.where(docs[at, :] < last, grad_buf[at, :], jnp.zeros((), low))
+        scores_at = score_block(scale, tile, key_tile, docs[at, :], row_docs[:, window])
+        probs = jnp.exp(scores_at - log_total[at, :1])
+        prob_grad = matmul_nt(head_grad, value[window, :])
+        inner = jnp.sum(probs * prob_grad, axis=1, keepdims=True)
+        raw_grad = (probs * (prob_grad - inner) * scale).astype(low)
+        grads = matmul(raw_grad, key_tile)
+        trade_buf[at, :QK_NOPE] = grads[:, :QK_NOPE].astype(low)
+        pair = grads[:, QK_NOPE:]
+        trade_buf[at, QK_NOPE:] = (pair * turn[at, :] - swapped_halves(pair) * sway[at, :]).astype(low)
+        key_sum[window, :] += matmul_tn(raw_grad, tile)
+        value_sum[window, :] += matmul_tn(probs.astype(low), head_grad)
+        return 0
+
+    blocks = docs.shape[0] // QUERIES
+    for index in range(blocks // 2):
+        attend_tile(jnp.int32(index), 0)
+    next(mid_run)
+    for index in range(blocks // 2, blocks):
+        attend_tile(jnp.int32(index), 0)
+    next(mid_run)
+
+    lane = lax.broadcasted_iota(jnp.int32, (QUERIES, 2 * QK_ROPE), 1)
+
+    def key_tile(index, _):
+        at = pl.ds(pl.multiple_of(index * QUERIES, QUERIES), QUERIES)
+        later = pl.ds(pl.multiple_of(index * QUERIES + WINDOW, QUERIES), QUERIES)
+        key_rope = pltpu.roll(key_sum[later, QK_NOPE:], QK_ROPE, 1).astype(low)
+        trade_buf[at, QK_NOPE:] = jnp.where(lane < QK_ROPE, trade_buf[at, QK_NOPE:], key_rope)
+        pair_buf[at, :QK_NOPE] = key_sum[later, :QK_NOPE].astype(low)
+        pair_buf[at, QK_NOPE:] = value_sum[later, :].astype(low)
+        part = matmul_nt(pair_buf[at, :], up_head[...]).astype(low)
+        per = QUERIES // local
+        part_buf[pl.ds(index * per, per)] = part.reshape((per,) + part_buf.shape[1:])
+        return 0
+
+    for index in range(blocks):
+        key_tile(jnp.int32(index), 0)
+
+    def token_trade(step, member, source):
+        spot = pl.ds(pl.multiple_of(member * local, local), local)
+        return remote(trade_buf.at[spot, :], trade_got.at[source], trade_send.at[1, step], trade_recv.at[1, source],
+                      {"expert": place.base + member})
+
+    reduce_run = reduce_steps(place, part_buf, key_got, reduce_scratch_refs, sender)
+    next(reduce_run)
+    keep_token = pltpu.make_async_copy(trade_buf.at[own_at, :], trade_got.at[place.local], load_sem.at[next(numbers)])
+    keep_token.start()
+    for step, member in enumerate(members):
+        sender.start(place.always, token_trade(step, member, place.local))
+
+    for index, piece in streamed(stream_buf, len(tiles), columns_of(normed_one)):
+        term = matmul_tn(trade_buf[...], piece[...].reshape(SEQ, tile))
+        per = tile // query_term.shape[1]
+        query_term[index * per : (index + 1) * per] = term.T.astype(low).reshape((per,) + query_term.shape[1:])
+    up_term[...] = matmul_tn(key_latent[...], pair_buf[...]).astype(low).reshape(up_term.shape)
+    next(reduce_run)
+    query_trade = everyone(1, lambda target: query_term.at[target], query_got)
+    query_trade.start()
+    up_trade = everyone(2, lambda target: up_term.at[target], up_got_buf)
+    up_trade.start()
+    next(reduce_run)
+    drain(reduce_run)
+    for step, member in enumerate(members):
+        token_trade(step, member, member).wait_recv()
+    keep_token.wait()
+
+    got_compressed.wait()
+    head_dim = QK_NOPE + QK_ROPE
+    rope = jnp.zeros((local, 2 * QK_ROPE), jnp.float32)
+    for head in range(group):
+        own_query[:, head * head_dim : (head + 1) * head_dim] = trade_got[head, :, :head_dim]
+        rope = rope + trade_got[head, :, QK_NOPE:].astype(jnp.float32)
+    lane = lax.broadcasted_iota(jnp.int32, rope.shape, 1)
+    rope = jnp.where(lane < QK_ROPE, pltpu.roll(rope, QK_ROPE, 1), rope)
+    rope = rope * turn[own_at, :] - swapped_halves(rope) * sway[own_at, :]
+    latent_grad, latent_term = norm_back(own_compressed[...], latent_gain[...], key_got[...].reshape(local, KV_RANK))
+    low_grad[0, 0, :, :KV_RANK] = latent_grad.astype(low)
+    low_grad[0, 0, :, KV_RANK:] = jnp.where(lane < QK_ROPE, rope, 0.0).astype(low)
+    low_run = gather_steps(place, low_grad.at[0], low_all, gather_keep.at[1], gather_send.at[1], gather_recv.at[1], sender)
+    next(low_run)
+    for copy in got_wd:
+        copy.wait()
+    for index, piece in streamed(wq_buf, width // row_tile, query_rows):
+        rows = slice(index * row_tile, (index + 1) * row_tile)
+        shard = index * row_tile // own_rows
+        within = slice(rows.start - shard * own_rows, rows.stop - shard * own_rows)
+        term = matmul_nt(own_query[...], piece[...])
+        input_grad[:, rows] = term + matmul_nt(low_grad[0, 0], wd_buf[shard, within, :])
+    next(low_run)
+    row_grad, first_term = norm_back(tokens[...].astype(jnp.float32), first_gain[...], input_grad[...])
+    input_grad[...] = mid_buf[...] + row_grad
+    next(low_run)
+    drain(mid_run)
+    per_lane = width // 128
+    for block in range(per_lane):
+        columns = slice(block * 128, (block + 1) * 128)
+        small_buf[block, :experts, :] = router_term[:, columns]
+        small_buf[block, experts : experts + 1, :] = second_term[:, columns]
+        small_buf[block, experts + 1 : experts + 2, :] = first_term[:, columns]
+        at = block // (per_lane * 128 // KV_RANK) * 128
+        small_buf[block, experts + 2 : experts + 3, :] = latent_term[:, at : at + 128]
+        small_buf[block, experts + 3 :, :] = jnp.zeros((small_buf.shape[1] - experts - 3, 128), jnp.float32)
+    small_trade = everyone(3, lambda target: small_buf.at[target // (total // per_lane)], small_got)
+    small_trade.start()
+    drain(low_run)
+    got_columns.wait()
+    down = matmul_tn(own_columns[...].reshape(SEQ, -1), low_all[...].reshape(SEQ, -1))
+    down_rows[...] = down.astype(low).reshape(down_rows.shape)
+    down_trade = head_rows(place, plane, shards, down_rows, down_got, rows_keep.at[0], rows_send.at[0], rows_recv.at[0])[0]
+    for index, piece in streamed(stream_buf, len(tiles), columns_of(mid_all)):
+        term = matmul_tn(head_out[...], piece[...].reshape(SEQ, tile)).astype(low)
+        out_rows[:, :, tiles[index]] = term.reshape(out_rows.shape[:2] + (tile,))
+    out_trade = head_rows(place, plane, shards, out_rows, out_got, rows_keep.at[1], rows_send.at[1], rows_recv.at[1])[0]
+
+    sequences = total // group
+    query_trade.wait()
+    up_trade.wait()
+    for head in range(group):
+        query_sum, up_sum = 0.0, 0.0
+        for sequence in range(sequences):
+            query_sum = query_sum + query_got[sequence * group + head].astype(jnp.float32)
+            up_sum = up_sum + up_got_buf[sequence * group + head].astype(jnp.float32)
+        query_out[:, head * head_dim : (head + 1) * head_dim] = query_sum[:, :head_dim]
+        both = QK_NOPE + V_HEAD
+        up_out[:, head * both : (head + 1) * both] = up_sum
+    small_trade.wait()
+    small_out[...] = small_got[0]
+
+    def small_sum(source, _):
+        small_out[...] += small_got[source]
+        return 0
+
+    lax.fori_loop(1, total, small_sum, 0)
+    down_trade.wait()
+    out_trade.wait()
+    down_sum, out_sum = 0.0, 0.0
+    for sequence in range(sequences):
+        down_sum = down_sum + down_got[sequence].astype(jnp.float32)
+        out_sum = out_sum + out_got[sequence].astype(jnp.float32)
+    down_out[...] = down_sum[:, : down_out.shape[1]]
+    out_out[...] = out_sum
+    shared_trade.wait()
+    for share in shares:
+        share.wait_recv()
+    for trade in (shared_trade, query_trade, up_trade, small_trade):
+        trade.finish()
+    sender.finish()
+
+
+def backward_pass(scale, last, small, tables, saved, weights, sends):
+    shards, plane = lax.axis_size("shard"), lax.axis_size("expert")
+    total = shards * plane
+    low, shape = jnp.bfloat16, jax.ShapeDtypeStruct
+    local, width = small[3].shape
+    head_dim = QK_NOPE + QK_ROPE
+    vmem, any_space = pl.BlockSpec(memory_space=pltpu.VMEM), pl.BlockSpec(memory_space=pl.ANY)
+    inputs = list(small) + list(tables) + list(saved)
+    hbm = list(weights) + list(sends)
+    gate_send, up_send, narrow_send, shared_term = sends
+    experts = small[9].shape[0]
+    small_rows = experts + 3 + -(experts + 3) % 8
+    own_width = width // total
+    out_shape = [
+        shape((local, width), jnp.float32),
+        shape((own_width, HEADS * head_dim), jnp.float32),
+        shape((KV_RANK // total, HEADS * (QK_NOPE + V_HEAD)), jnp.float32),
+        shape((own_width, KV_RANK + QK_ROPE), jnp.float32),
+        shape((own_width, width), jnp.float32),
+        shape((small_rows, 128), jnp.float32),
+        shape(gate_send.shape, low),
+        shape(up_send.shape, low),
+        shape(narrow_send.shape, low),
+        shape(shared_term.shape, low),
+        shape((SEQ_DEVICES, PIECES, local // PIECES, width), low),
+    ]
+    hbm_out = 5
+    dma, scratch = pltpu.SemaphoreType.DMA, pltpu.VMEM
+    pieces = (PIECES, local // PIECES)
+    down_width = weights[3].shape[2]
+    row_count = 128 // own_width
+    sequences = total // SEQ_DEVICES
+    wide_head = 2 * QK_NOPE
+    return pl.pallas_call(
+        functools.partial(backward_kernel, shards, plane, scale, last),
+        out_shape=out_shape,
+        in_specs=[vmem] * len(inputs) + [any_space] * len(hbm),
+        out_specs=[vmem] * (len(out_shape) - hbm_out) + [any_space] * hbm_out,
+        scratch_shapes=[
+            scratch((2, shards, SEQ_DEVICES // shards) + pieces + (512,), low),
+            scratch((2, 256, HEADS * head_dim), low),
+            scratch((shards, width // shards, down_width), low),
+            scratch((SEQ_DEVICES,) + pieces + (128,), low),
+            scratch((local, KV_RANK), jnp.float32),
+            scratch((local, width), jnp.float32),
+            scratch((local, width), jnp.float32),
+            scratch(pieces + (width,), low),
+            scratch((local, width), low),
+            scratch((SEQ, V_HEAD), low),
+            scratch((SEQ + WINDOW, wide_head), jnp.float32),
+            scratch((SEQ + WINDOW, V_HEAD), jnp.float32),
+            scratch((SEQ_DEVICES,) + pieces + (KV_RANK,), low),
+            scratch((SEQ, wide_head), low),
+            scratch((SEQ_DEVICES, local, wide_head), low),
+            scratch((SEQ, wide_head), low),
+            scratch((total, own_width, wide_head), low),
+            scratch((total, own_width, wide_head), low),
+            scratch((total, KV_RANK // total, wide_head), low),
+            scratch((total, KV_RANK // total, wide_head), low),
+            scratch((local, HEADS * head_dim), low),
+            scratch((1, 1, local, down_width), low),
+            scratch((SEQ_DEVICES, 1, local, down_width), low),
+            scratch((row_count, own_width, down_width), low),
+            scratch((sequences, own_width, down_width), low),
+            scratch((row_count, own_width, width), low),
+            scratch((sequences, own_width, width), low),
+            scratch((width // 128, small_rows, 128), jnp.float32),
+            scratch((total, small_rows, 128), jnp.float32),
+            scratch(pieces + (KV_RANK,), jnp.float32),
+            dma((8,)),
+            dma((shards,)),
+            dma((2, shards)),
+            dma((3, shards)),
+            dma((3, shards)),
+            dma((2, SEQ_DEVICES)),
+            dma((2, SEQ_DEVICES)),
+            dma((2, 4, SEQ_DEVICES, PIECES)),
+            dma((2, SEQ_DEVICES, PIECES)),
+            dma((2,)),
+            dma((4, total)),
+            dma((4, total)),
+            dma((4,)),
+            dma((2, max(row_count, sequences))),
+            dma((2, max(row_count, sequences))),
+            dma((2,)),
+        ]
+        + reduce_scratch(SEQ_DEVICES, PIECES, local // PIECES, KV_RANK),
+        compiler_params=pltpu.CompilerParams(
+            collective_id=3, has_side_effects=True, vmem_limit_bytes=62 * 2**20
+        ),
+        name="backward",
+    )(*inputs, *hbm)
 
 
 def on_device(
@@ -1122,7 +1549,6 @@
     all_devices = shards * plane
     shard_at = lax.axis_index("shard")
     plane_at = lax.axis_index("expert")
-    groups = plane_groups(plane)
     head_at = plane_at % SEQ_DEVICES
     sequence_at = (shard_at * plane + plane_at) // SEQ_DEVICES
     capacity = local_rows * TOP * 4 // (3 * plane)
@@ -1174,8 +1600,8 @@
     picked = jnp.arange(sequence_count, dtype=jnp.int32)[:, None] == sequence_at
     row_ends = jnp.sum(jnp.where(picked, ends, 0), axis=0)
     documents = jnp.sum((positions[:, None] >= row_ends[None, :]).astype(jnp.int32), axis=1)
-    turn = jnp.concatenate([cosine_part, cosine_part], axis=1)
-    sway = jnp.concatenate([-sine_part, sine_part], axis=1)
+    turn = jnp.tile(cosine_part, (1, 4))
+    sway = jnp.tile(jnp.concatenate([-sine_part, sine_part], axis=1), (1, 2))
     docs = documents[:, None]
     row_docs = jnp.pad(docs, ((WINDOW, 0), (0, 0)), constant_values=-1).T
     route_rows = jnp.pad(routes.T, ((0, 8 - TOP), (0, 0)), constant_values=-1)
@@ -1201,6 +1627,7 @@
         head_out,
         log_total,
         middle,
+        up_head,
     ) = forward_pass(
         scale,
         entry_count - 1,
@@ -1227,12 +1654,8 @@
     )
     all_normed = all_normed.reshape(-1, width)
     all_grads = all_grads.reshape(-1, width)
-    full_out = full_out.reshape(-1, width)
-    full_query = full_query.reshape(width, -1)
-    full_down = full_down.reshape(width, -1)
-    hidden_rows = tokens.astype(jnp.float32)
-    second_normed = norm_scale(middle, second_gain).astype(jnp.bfloat16)
-    expert_ids = jnp.arange(plane, dtype=jnp.int32)
+    blocked = (SEQ_DEVICES, PIECES, local_rows // PIECES, width)
+    shard_blocked = (shards, SEQ_DEVICES // shards) + blocked[1:]
     (
         normed_part,
         output_part,
@@ -1246,32 +1669,42 @@
         shared_gate_back,
         shared_up_back,
     ) = expert_pass(
-        plane_at.astype(jnp.int32).reshape(1, 1),
+        jnp.stack([plane_at, shard_at]).astype(jnp.int32)[None],
         all_routes[:, 0],
         router_weight.T,
         all_normed,
         all_grads,
-        gate_single.reshape(width, -1),
-        up_single.reshape(width, -1),
-        down_single.reshape(-1, width),
-        gate_shared,
-        up_shared,
-        down_shared.reshape(-1, width),
+        (
+            gate_columns,
+            gate_shared,
+            up_columns,
+            up_shared,
+            down_units,
+            down_shared,
+            expert_gate[0],
+            gate_single,
+            expert_up[0],
+            up_single,
+            expert_down[0],
+            down_single,
+        ),
         capacity,
     )
-    plane_rows = plane * local_rows
     expert_down_term = matmul_tn(hidden, slot_grad)
-    back, gate_dense, down_blocks = bundle(
-        4,
-        plane,
-        shards,
-        [
-            ("reduce", normed_part.reshape(plane, local_rows, width)),
-            ("trade", token_scores),
-            ("share", expert_down_term.astype(jnp.bfloat16).reshape(shards, -1, width)),
-        ],
-    )
-    gate_dense = gate_dense[:, 0].T
+    transfers = [
+        ("reduce", normed_part.reshape(plane, local_rows, width)),
+        ("trade", token_scores),
+        ("share", expert_down_term.astype(jnp.bfloat16).reshape(shards, -1, width)),
+    ]
+    output_transfer = ("reduce", output_part.reshape(plane, local_rows, width))
+    if plane == SEQ_DEVICES:
+        back, scores, down_blocks, output_sum = bundle(
+            2, plane, shards, transfers + [output_transfer], 56 * 2**20
+        )
+    else:
+        back, scores, down_blocks = bundle(2, plane, shards, transfers, 56 * 2**20)
+        (output_sum,) = bundle(4, plane, shards, [output_transfer], 56 * 2**20)
+    activations = (middle + output_sum).astype(jnp.bfloat16)
 
     def sum_shards(term, blocks):
         own = lax.dynamic_index_in_dim(
@@ -1284,183 +1717,80 @@
         return own
 
     expert_down_grad = sum_shards(expert_down_term, down_blocks)[None]
-    output_part = tie(output_part, back)[0]
-    output_sum = lax.psum_scatter(output_part, "expert", scatter_dimension=0, tiled=True)
-    activations = (middle + output_sum.astype(jnp.float32)).astype(jnp.bfloat16)
-    expert_gate_grad = shard_sum(matmul_tn(slot_rows, gate_pre_grad))[None]
-    expert_up_grad = shard_sum(matmul_tn(slot_rows, up_pre_grad))[None]
-    shared_down_term = matmul_tn(shared_hidden, all_grads).reshape(shards, padded_units, width)
-    shared_down_grad = shard_sum(shared_down_term[:, :units].reshape(-1, width))
+    gate_term = matmul_tn(slot_rows, gate_pre_grad)
+    up_term = matmul_tn(slot_rows, up_pre_grad)
+    shared_down_term = matmul_tn(shared_hidden, all_grads)
     shared_term = jnp.concatenate(
         [matmul_tn(all_normed, shared_gate_back), matmul_tn(all_normed, shared_up_back)], axis=1
+    ).astype(jnp.bfloat16)
+
+    def for_shards(term):
+        return term.astype(jnp.bfloat16).reshape((shards, -1) + term.shape[1:])
+
+    (
+        input_grad,
+        query_weight_grad,
+        latent_up_grad,
+        latent_down_grad,
+        output_weight_grad,
+        small_sums,
+        gate_blocks,
+        up_blocks,
+        shared_blocks,
+        shared_moved,
+        _,
+    ) = backward_pass(
+        scale,
+        entry_count - 1,
+        (
+            back,
+            scores,
+            route_rows,
+            middle,
+            cotangent,
+            tokens,
+            first_gain[None],
+            second_gain[None],
+            latent_gain[None],
+            router_weight.T,
+        ),
+        (query, keys, value, docs, row_docs, log_total, turn, sway),
+        (key_latent, up_head.reshape(KV_RANK, -1), head_out),
+        (
+            compressed,
+            full_out.reshape(shard_blocked),
+            full_query.reshape((shards,) + query_weight.shape),
+            full_down.reshape((shards,) + down_half.shape),
+            normed_one.reshape(blocked),
+            output_weight.reshape(shard_blocked[1:]),
+            query_weight,
+            down_half,
+        ),
+        (
+            for_shards(gate_term),
+            for_shards(up_term),
+            for_shards(shared_down_term),
+            shared_term.reshape(all_devices, -1, shared_term.shape[1]),
+        ),
     )
-
-    def to_owners(term):
-        moved = lax.all_to_all(
-            term.astype(jnp.bfloat16).reshape(all_devices, -1, term.shape[1]),
-            everyone,
-            split_axis=0,
-            concat_axis=0,
-            tiled=True,
-        )
-        moved = moved.reshape(shards, plane, -1, term.shape[1]).astype(jnp.float32)
-        return jnp.sum(moved, axis=0)
-
-    def by_head(moved):
-        heads = moved.reshape((plane // SEQ_DEVICES, HEADS) + moved.shape[1:]).sum(axis=0)
-        return heads.transpose(1, 0, 2).reshape(moved.shape[1], -1)
-
-    shared_moved = to_owners(shared_term).reshape(plane, -1, 2, shards, padded_units)[..., :units]
-    shared_moved = shared_moved.transpose(2, 1, 3, 0, 4)
+    expert_gate_grad = sum_shards(gate_term, gate_blocks)[None]
+    expert_up_grad = sum_shards(up_term, up_blocks)[None]
+    shared_down_grad = sum_shards(shared_down_term, shared_blocks)[:units]
+    shared_moved = shared_moved.astype(jnp.float32).reshape(shards, plane, -1, 2, shards, padded_units)
+    shared_moved = jnp.sum(shared_moved, axis=0)[..., :units].transpose(2, 1, 3, 0, 4)
     shared_moved = shared_moved.reshape(2, shared_moved.shape[1], -1)
     shared_gate_grad = shared_moved[0]
     shared_up_grad = shared_moved[1]
-
-    grad_out = cotangent.astype(jnp.float32)
-    own_choose = routes[:, :, None] == expert_ids[None, None, :]
-    own_logits = matmul(second_normed, router_weight)
-    chosen = jnp.sum(jnp.where(own_choose, own_logits[:, None, :], 0.0), axis=2)
-    chosen_exp = jnp.exp(chosen - jnp.max(chosen, axis=1, keepdims=True))
-    own_gates = chosen_exp / jnp.sum(chosen_exp, axis=1, keepdims=True)
-    gate_grad = jnp.sum(jnp.where(own_choose, gate_dense[:, None, :], 0.0), axis=2)
-    chosen_grad = own_gates * (
-        gate_grad - jnp.sum(own_gates * gate_grad, axis=1, keepdims=True)
+    own_width = width // all_devices
+    number = shard_at * plane + plane_at
+    own_small = lax.dynamic_slice_in_dim(small_sums, number * own_width % 128, own_width, 1)
+    router_weight_grad = own_small[:plane].T
+    second_gain_grad = own_small[plane]
+    first_gain_grad = own_small[plane + 1]
+    latent_width = KV_RANK // all_devices
+    latent_gain_grad = lax.dynamic_slice_in_dim(
+        small_sums[plane + 2], number * latent_width % 128, latent_width, 0
     )
-    logit_grad = jnp.sum(jnp.where(own_choose, chosen_grad[:, :, None], 0.0), axis=1)
-    router_term = lax.dot_general(
-        second_normed.astype(jnp.float32),
-        logit_grad,
-        (((0,), (0,)), ((), ())),
-        precision=HIGH,
-        preferred_element_type=jnp.float32,
-    )
-    normed_grad = back + lax.dot_general(
-        logit_grad,
-        router_weight.astype(jnp.float32),
-        (((1,), (1,)), ((), ())),
-        precision=HIGH,
-        preferred_element_type=jnp.float32,
-    )
-    unused_two, second_back = jax.vjp(norm_scale, middle, second_gain)
-    middle_norm_grad, second_term = second_back(normed_grad)
-    middle_grad = grad_out + middle_norm_grad
-    middle_low = middle_grad.astype(jnp.bfloat16)
-    heads_grad = matmul_nt(middle_low, full_out).astype(jnp.bfloat16)
-    heads_grad = heads_grad.reshape(local_rows, HEADS, V_HEAD).transpose(1, 0, 2)
-    (head_grad,) = bundle(5, SEQ_DEVICES, shards, [("trade", heads_grad)])
-    head_grad = head_grad.reshape(SEQ, V_HEAD)
-    all_middle = lax.all_gather(
-        tie(middle_low, head_grad)[0], "expert", axis=0, tiled=True, axis_index_groups=groups
-    )
-    query_raw, keys_grad, value_grad = attend_back(
-        scale, entry_count - 1, query, keys, value, docs, row_docs, log_total, head_grad
-    )
-    query_grad = jnp.concatenate(
-        [query_raw[:, :QK_NOPE], unrotate(query_raw[:, QK_NOPE:], cosine_part, sine_part)],
-        axis=1,
-    ).astype(jnp.bfloat16)
-    key_nope_grad, key_rope_grad = keys_grad[:, :QK_NOPE], keys_grad[:, QK_NOPE:]
-    pair_grad = jnp.concatenate([key_nope_grad, value_grad], axis=1).astype(jnp.bfloat16)
-    latent_up_term = matmul_tn(key_latent, pair_grad)
-    up_half = lax.dynamic_slice_in_dim(
-        latent_up, head_at * (QK_NOPE + V_HEAD), QK_NOPE + V_HEAD, 1
-    )
-    up_head = shard_rows(up_half)
-    key_grad_part = jnp.concatenate(
-        [
-            matmul_nt(pair_grad, up_head),
-            key_rope_grad,
-            jnp.zeros((SEQ, -(KV_RANK + QK_ROPE) % 128), jnp.float32),
-        ],
-        axis=1,
-    ).astype(jnp.bfloat16)
-    query_term = matmul_tn(normed_one, query_grad)
-    query_moved, up_moved = (
-        lax.all_to_all(
-            term.astype(jnp.bfloat16).reshape(all_devices, -1, term.shape[1]),
-            everyone,
-            split_axis=0,
-            concat_axis=0,
-            tiled=True,
-        )
-        for term in (query_term, latent_up_term)
-    )
-    own_key_grad, own_query_grad = bundle(
-        6,
-        SEQ_DEVICES,
-        shards,
-        [
-            ("reduce", key_grad_part.reshape(SEQ_DEVICES, local_rows, -1)),
-            ("trade", query_grad.reshape(SEQ_DEVICES, local_rows, head_dim)),
-        ],
-    )
-    own_key_grad = own_key_grad[:, : KV_RANK + QK_ROPE]
-    own_query_grad = own_query_grad.transpose(1, 0, 2).reshape(local_rows, HEADS * head_dim)
-    own_compressed = own_rows(compressed)
-    unused_latent, latent_back = jax.vjp(norm_scale, own_compressed, latent_gain)
-    latent_in_grad, latent_gain_term = latent_back(own_key_grad[:, :KV_RANK])
-    rope_in_grad = unrotate(
-        own_key_grad[:, KV_RANK:], own_rows(cosine_part), own_rows(sine_part)
-    )
-    compressed_grad = jnp.concatenate([latent_in_grad, rope_in_grad], axis=1).astype(jnp.bfloat16)
-    down_columns = (KV_RANK + QK_ROPE) // SEQ_DEVICES
-    def owner_blocks(term):
-        return term.astype(jnp.bfloat16).reshape(all_devices, -1, term.shape[1])
-
-    def owner_sum(moved):
-        blocks = moved.reshape((shards, plane) + moved.shape[1:]).astype(jnp.float32)
-        return by_head(jnp.sum(blocks, axis=0))
-
-    column_grad = lax.all_to_all(
-        compressed_grad.reshape(local_rows, SEQ_DEVICES, down_columns).transpose(1, 0, 2),
-        "expert",
-        split_axis=0,
-        concat_axis=0,
-        tiled=True,
-        axis_index_groups=groups,
-    )
-    column_grad = column_grad.reshape(SEQ, down_columns)
-    query_weight_grad = owner_sum(query_moved)
-    latent_up_grad = owner_sum(up_moved)
-    normed_one_grad = matmul_nt(own_query_grad, full_query) + matmul_nt(
-        compressed_grad, full_down[:, : KV_RANK + QK_ROPE]
-    )
-    unused_one, first_back = jax.vjp(norm_scale, hidden_rows, first_gain)
-    input_norm_grad, first_term = first_back(normed_one_grad)
-    input_grad = middle_grad + input_norm_grad
-    down_term = matmul_tn(normed_one, column_grad)
-    out_term = matmul_tn(head_out, all_middle.reshape(SEQ, width)).astype(jnp.bfloat16)
-    small_terms = jnp.concatenate(
-        [
-            router_term.reshape(all_devices, -1),
-            second_term.reshape(all_devices, -1),
-            first_term.reshape(all_devices, -1),
-            latent_gain_term.reshape(all_devices, -1),
-        ],
-        axis=1,
-    )
-    small_count = small_terms.shape[1]
-    small_terms = jnp.pad(small_terms, ((0, 0), (0, -small_count % 1024)))
-    small_terms = small_terms.reshape(all_devices, -1, 128)
-    down_moved, gain_moved, out_moved = bundle(
-        8,
-        SEQ_DEVICES,
-        shards,
-        [
-            ("owners", owner_blocks(down_term)),
-            ("owners", small_terms),
-            ("rows", out_term.reshape(-1, width // all_devices, width)),
-        ],
-    )
-    latent_down_grad = owner_sum(down_moved)
-    output_weight_grad = jnp.sum(out_moved.astype(jnp.float32), axis=0)
-    small_sums = jnp.sum(gain_moved, axis=0).reshape(-1)[:small_count]
-    own_width = width // all_devices
-    at_second = own_width * plane
-    router_weight_grad = small_sums[:at_second].reshape(own_width, plane)
-    second_gain_grad = small_sums[at_second : at_second + own_width]
-    first_gain_grad = small_sums[at_second + own_width : at_second + 2 * own_width]
-    latent_gain_grad = small_sums[at_second + 2 * own_width :]
     return (
         activations,
         input_grad,

time: 1450 us -> 845 us (0.58)
  Pallas kernels: 1150 us -> 708 us
  matrix products: 92.7 us -> 44.4 us
  local copies, waits for them, and re-layouts: 85 us -> 47.9 us
  starting transfers between devices: 21.9 us -> 0 us
  waiting for transfers between devices: 20.5 us -> 0 us
  other arithmetic: 56.1 us -> 37.9 us
    pallas_call x1, Pallas kernels: 832 us -> 276 us  [forward_pass(): pl.pallas_call(functools.partial(forward_kernel, shards, plane, scale, la...]
    pallas_call x1, Pallas kernels: 15 us -> 239 us  [backward_pass(): pl.pallas_call(functools.partial(backward_kernel, shards, plane, scale, l...]
    pallas_call x4 -> x1, Pallas kernels: 214 us -> 110 us  [bundle(): pl.pallas_call(functools.partial(bundle_kernel, group, shards, tuple(kind...]
    dot_general x10 -> x6, matrix products: 70.1 us -> 44.4 us  [matmul_tn(): lax.dot_general(left, right, (((0,), (0,)), ((), ())), preferred_element_...]
    dot_general x7 -> x0, matrix products: 22.6 us -> none  [the longest x4 20 us: matmul_nt(): lax.dot_general(left, right, (((1,), (1,)), ((), ())), preferred_element_...]
    all_to_all x4 -> x0, waiting for transfers between devices: 20.5 us -> none  [the longest x2 11 us: on_device(): lax.all_to_all(term.astype(jnp.bfloat16).reshape(all_devices, -1, term.sh...]
    all_to_all x4 -> x0, starting transfers between devices: 19.1 us -> none  [the longest x2 8.91 us: on_device(): lax.all_to_all(term.astype(jnp.bfloat16).reshape(all_devices, -1, term.sh...]
  transfers between devices with their start and end apart: 10 -> 0, of which waited for: 4 -> 0; matrix products, arithmetic and copies ran while one was open for 12% -> 0% of each run, Pallas kernels for 7% -> 0%
where the time goes in v5:
time: 845 us; the launch traced here: 840 us
  Pallas kernels  708 us (84%)
  local copies, waits for them, and re-layouts  47.9 us (6%)
  matrix products  44.4 us (5%)
  other arithmetic  37.9 us (4%)
    pallas_call x1, Pallas kernels, forward_pass(): pl.pallas_call(functools.partial(forward_kernel, shards, plane, scale, la...  276 us
    pallas_call x1, Pallas kernels, backward_pass(): pl.pallas_call(functools.partial(backward_kernel, shards, plane, scale, l...  239 us
    pallas_call x1, Pallas kernels, bundle(): pl.pallas_call(functools.partial(bundle_kernel, group, shards, tuple(kind...  110 us
    pallas_call x1, Pallas kernels, expert_pass(): pl.pallas_call(expert_kernel, grid=(steps,), out_shape=[shape((steps * to...  83.5 us
    dot_general x6, matrix products, matmul_tn(): lax.dot_general(left, right, (((0,), (0,)), ((), ())), preferred_element_...  44.4 us
    add x3, other arithmetic, sum_shards(): own + lax.dynamic_index_in_dim(blocks, (shard_at + step) % shards, 0, kee...  19.2 us

profile of v5, /device:TPU:9, one launch (start us, length us, event | category | flops | bytes accessed | tf_op | source)
XLA Modules:
  0.0 839.6 jit_solution(4821916763536275949)
XLA Ops:
  0.7 1.2 constant_dynamic-slice_fusion.1
  1.9 1.4 constant_dynamic-slice_fusion.9
  3.3 0.0 copy-start.4
  3.3 1.1 pad_maximum_fusion.2.refs_2_
  4.4 0.8 reduce_window_sum.11
  5.2 0.1 select_reduce_fusion
  5.3 0.1 convert_reduce_fusion
  5.4 1.4 copy.89.refs_19_.refs_13_
  6.8 1.6 constant_dynamic-slice_fusion.8.refs_4_
  8.3 0.6 pad_bitcast_fusion.refs_20_.refs_14_
  9.0 1.9 constant_dynamic-slice_fusion.5
  10.9 1.0 fusion.8.refs_10_.rest_0_
  11.9 1.0 fusion.9.refs_11_.rest_2_
  13.0 1.0 constant_dynamic-slice_fusion.3
  14.0 0.8 pad.29.refs_12_.rest_4_
  14.8 0.7 copy.85
  15.5 0.1 fusion.13
  15.6 1.3 pad_maximum_fusion.1.refs_28_
  17.0 1.0 fusion.10
  18.0 0.0 copy-start.11
  18.0 0.1 tile.24
  18.1 1.3 copy.88.refs_18_.refs_17_
  19.4 0.1 tile.22
  19.5 1.3 copy.87.refs_17_.refs_16_
  20.9 0.6 fusion.14
  21.5 276.1 %forward.1 = (bf16[16,2,64,2048]{3,2,1,0:T(8,128)(2,1)}, bf16[16,2,64,2048]{3,2,1,0:T(8,128)(2,1)}, s32[16,1,8,128]{3,2,1,0:T(8,128)}, bf16[2,16,1,64,640]{4,3,2...) custom-call(bf16[2,64,2048]{2,1,0:T(8,128)(2,1)} %bitcast.119, ...), custom_call_target="tpu_custom_call" | custom-call | tf_op jit(solution)/shard_map/forward/pallas_call | solution.py:1009
  297.6 0.6 add_bitcast_fusion.me_ref
  298.2 83.5 %experts.1 = (bf16[2048,2048]{1,0:T(8,128)(2,1)}, bf16[2048,2048]{1,0:T(8,128)(2,1)}, bf16[1024,2048]{1,0:T(8,128)(2,1)}, bf16[1024,2048]{1,0:T(8,128)(2,1)}, bf...) custom-call(s32[1,2]{1,0:T(1,128)} %add_bitcast_fusion.me_ref, ...), custom_call_target="tpu_custom_call" | custom-call | tf_op jit(solution)/shard_map/experts/pallas_call | solution.py:657
  381.7 12.2 %fusion.15 = (bf16[1408,2048]{1,0:T(8,128)(2,1)}, f32[1408,2048]{1,0:T(8,128)}) fusion(bf16[1024,1408]{1,0:T(8,128)(2,1)} %get-tuple-element.75, bf16[1024,2048]{1,0:T(8,128)(2,1)} %get-tuple-element.76), kind=kOutput, calls=%fused_computation.53 | convolution fusion | flops 5908463616 | bytes 24379392 | tf_op jit(solution)/shard_map/dot_general | solution.py:35
  393.9 109.9 %bundle_reduce_trade.1 = (f32[4,32,2048]{2,1,0:T(8,128)}, f32[16,8,128]{2,1,0:T(8,128)}, bf16[2,704,2048]{2,1,0:T(8,128)(2,1)}, f32[4,32,2048]{2,1,0:T(8,128)}) custom-call(bf16[16,4,32,2048]{3,2,1,0:T(8,128)(2,1)} %bitcast.106, f32[16,8,128]{2,1,0:T(8,128)} %get-tuple-element.74.refs_1_, bf16[2,704,2048]{2,1,0:T(8,128)(2,1)} %bitcast.110, ...), custom_call_target="tpu_custom_call" | custom-call | tf_op jit(solution)/shard_map/bundle_reduce_trade/pallas_call | solution.py:488
  503.8 7.3 convert_add_fusion
  511.2 12.4 %copy.90 = bf16[2048,2048]{1,0:T(8,128)(2,1)} copy(bf16[2048,2048]{0,1:T(8,128)(2,1)} %bitcast.90) | data formatting | bytes 16777216 | tf_op jit(solution)/shard_map/dot_general | solution.py:35
  523.6 0.0 slice-start
  523.6 5.9 convolution_convert_fusion.1
  529.5 0.1 copy-done.15
  529.6 2.5 convolution_convert_fusion
  532.1 1.8 pad_maximum_fusion.refs_32_
  534.0 0.0 copy-start.12
  534.0 2.7 fusion.18
  536.7 0.7 copy-done.14
  537.4 10.6 %fusion.17 = (bf16[2048,1408]{1,0:T(8,128)(2,1)}, f32[2048,1408]{1,0:T(8,128)}) fusion(bf16[1024,2048]{1,0:T(8,128)(2,1)S(1)} %copy-done.12, bf16[1024,1408]{1,0:T(8,128)(2,1)S(1)} %copy-done.14), kind=kOutput, calls=%fused_computation.55 | convolution fusion | flops 5908463616 | bytes 24379392 | tf_op jit(solution)/shard_map/dot_general | solution.py:35
  547.9 10.6 %fusion.16 = (bf16[2048,1408]{1,0:T(8,128)(2,1)}, f32[2048,1408]{1,0:T(8,128)}) fusion(bf16[1024,2048]{1,0:T(8,128)(2,1)S(1)} %copy-done.12, bf16[1024,1408]{1,0:T(8,128)(2,1)S(1)} %copy-done.13), kind=kOutput, calls=%fused_computation.54 | convolution fusion | flops 5908463616 | bytes 24379392 | tf_op jit(solution)/shard_map/dot_general | solution.py:35
  558.5 238.7 %backward.1 = (f32[128,2048]{1,0:T(8,128)}, f32[64,3072]{1,0:T(8,128)}, f32[16,4096]{1,0:T(8,128)}, f32[64,576]{1,0:T(8,128)}, f32[64,2048]{1,0:T(8,128)}, /*ind...) custom-call(f32[128,2048]{1,0:T(8,128)} %bitcast.121, ...), custom_call_target="tpu_custom_call" | custom-call | tf_op jit(solution)/shard_map/backward/pallas_call | solution.py:1464
  797.2 7.1 convert_add_fusion.1
  804.2 1.8 copy-done.2
  806.0 4.8 convert_add_fusion.2
  810.8 1.9 fusion.7
  812.7 7.1 reshape.197
  819.8 5.7 reduce_sum.29
  825.5 0.9 slice_bitcast_fusion
  826.5 0.7 fusion.12
  827.2 0.6 copy.96
  827.8 1.4 squeeze.48
  829.3 0.6 copy.97
  829.9 1.4 squeeze.49
  831.4 0.7 dynamic-slice_bitcast_fusion
  832.0 0.6 dynamic-slice_bitcast_fusion.1
  832.6 0.6 fusion.11
  833.2 2.1 fusion.6
  835.3 1.0 copy.107
  836.3 0.9 copy.108
  837.2 0.7 copy.109
  837.9 0.7 copy.110
  838.6 0.8 copy.111
  (37 shorter events, 0.1 us)
Async XLA Ops:
  3.3 11.5 %copy-start.4 = (bf16[1024,576]{0,1:T(8,128)(2,1)S(1)}, bf16[1024,576]{0,1:T(8,128)(2,1)}, u32[]{:S(2)}) copy-start(bf16[1024,576]{0,1:T(8,128)(2,1)} %param.23) | copy-start | bytes 3538948
  18.0 2.9 copy-start.11
  511.2 12.4 %copy-start.16 = (bf16[2048,192]{1,0:T(8,128)(2,1)S(1)}, bf16[2048,192]{1,0:T(8,128)(2,1)}, u32[]{:S(2)}) copy-start(bf16[2048,192]{1,0:T(8,128)(2,1)} %get-tuple-element.97) | copy-start | bytes 2359300
  523.6 5.9 copy-start
  523.6 6.0 copy-start.15
  523.6 10.3 %slice-start = ((s8[8388608]{0:T(1024)(128)(4,1)}), s8[4194304]{0:T(1024)(128)(4,1)S(1)}, s32[]{:S(2)}) async-start(s8[8388608]{0:T(1024)(128)(4,1)} %bitcast.86), calls=%async_computation | async-start | bytes 8388608
  529.6 4.3 slice-start.1
  532.1 1.8 copy-start.3
  534.0 2.7 copy-start.12
  534.0 3.4 copy-start.14
  537.4 10.6 %copy-start.13 = (bf16[1024,1408]{1,0:T(8,128)(2,1)S(1)}, bf16[1024,1408]{1,0:T(8,128)(2,1)}, u32[]{:S(2)}) copy-start(bf16[1024,1408]{1,0:T(8,128)(2,1)} %get-tuple-element.94) | copy-start | bytes 8650756
  797.1 8.9 %copy-start.2 = (f32[2048,1408]{1,0:T(8,128)S(1)}, f32[2048,1408]{1,0:T(8,128)}, u32[]{:S(2)}) copy-start(f32[2048,1408]{1,0:T(8,128)} %get-tuple-element.130) | copy-start | bytes 34603012
  827.2 4.2 copy-start.10
  827.2 6.0 copy-start.1
  829.9 5.4 copy-start.5
  829.9 8.0 copy-start.8
  831.3 5.0 copy-start.6
  831.3 5.8 copy-start.9
  832.6 5.9 copy-start.7

commit v6 on v5

--- a/solution.py
+++ b/solution.py
@@ -222,7 +222,7 @@
     lax.fori_loop(0, rows // chunk, body, 0)
 
 
-def reduce_steps(place, part_ref, out_ref, scratch, sender):
+def reduce_steps(place, part_ref, out_ref, scratch, sender, fine=False):
     (own_buf, twin_buf, row_buf, line_buf, load_sem, twin_send, twin_recv, row_send, row_recv, line_send, line_recv,
      out_buf, out_sem) = scratch
     outer, local, level = place.outer, place.local, place.level
@@ -284,7 +284,10 @@
             add_into(own_buf.at[where, piece], own_buf.at[where, piece], twin_buf.at[where, piece])
             if bit is bits[0]:
                 sender.start(place.always, to_row(at, piece))
-    yield
+        if fine:
+            yield
+    if not fine:
+        yield
     for at, piece in units:
         to_row(at, piece).wait_recv()
         spot, row = mine(at, piece), row_buf.at[at, piece]
@@ -301,7 +304,10 @@
                 add_into(spot, spot, row, line_buf.at[side, at, piece])
 
             sender.start(there, line)
-    yield
+        if fine:
+            yield
+    if not fine:
+        yield
     for at, piece in units:
         @pl.when(level == at)
         def _():
@@ -1037,6 +1043,245 @@
         ),
         name="forward",
     )(tokens.reshape(pieces), cotangent.reshape(pieces), *blocks, routes[None], *gains, *tables)
+
+
+def sums_kernel(shards, plane, *refs):
+    (normed_part, output_part, token_scores, slot_rows, slot_grad, hidden, gate_back, up_back, all_normed, all_grads,
+     shared_hidden, shared_gate_back, shared_up_back,
+     back, output_sum, scores, down_got, down_own, gate_own, up_own, gate_send, up_send, narrow_own, narrow_send,
+     shared_term,
+     down_send, pair_buf, stream_buf, wide_buf, own_stage, send_stage, down_stage,
+     load_sem, stream_sem, stage_sem, score_send, score_recv, swap_send, swap_recv, *reduces) = refs
+    low = jnp.bfloat16
+    place = Place(plane)
+    sender = Sender()
+    members = [lax.rem(place.me + step, plane) for step in range(1, plane)]
+    others = [lax.rem(place.shard + step, shards) for step in range(1, shards)]
+    greet([(place.always, {"expert": member}) for member in members] + [(place.always, {"shard": other}) for other in others])
+    count = 13
+    back_run = reduce_steps(place, normed_part, back, reduces[:count], sender, True)
+    output_run = iter(())
+    if len(reduces) > count:
+        output_run = reduce_steps(place, output_part, output_sum, reduces[count:], sender, True)
+    next(back_run)
+    keep = pltpu.make_async_copy(token_scores.at[place.me], scores.at[place.me], load_sem.at[0])
+    keep.start()
+
+    def score_trade(step, member, source):
+        return remote(token_scores.at[member], scores.at[source], score_send.at[step], score_recv.at[source],
+                      {"expert": member})
+
+    for step, member in enumerate(members):
+        sender.start(place.always, score_trade(step, member, place.me))
+    load_hidden = pltpu.make_async_copy(hidden, pair_buf.at[0], load_sem.at[1])
+    load_hidden.start()
+    load_up = pltpu.make_async_copy(up_back, pair_buf.at[1], load_sem.at[2])
+    load_up.start()
+    width = slot_rows.shape[1]
+    tile = stream_buf.shape[-1]
+    tiles = [slice(at, at + tile) for at in range(0, width, tile)]
+    hidden_width = hidden.shape[1]
+    own_hidden, own_width = hidden_width // shards, width // shards
+
+    def streamed(source, buf, sem):
+        copies = [
+            pltpu.make_async_copy(source.at[:, columns], buf.at[index % 2], sem.at[index % 2])
+            for index, columns in enumerate(tiles)
+        ]
+        copies[0].start()
+        for index, copy in enumerate(copies):
+            if index + 1 < len(copies):
+                copies[index + 1].start()
+            copy.wait()
+            yield index, buf.at[index % 2]
+
+    def down_chunks():
+        load_hidden.wait()
+        before = None
+        for index, piece in streamed(slot_grad, stream_buf, stream_sem.at[0]):
+            term = matmul_tn(pair_buf[0], piece[...])
+            if before is not None:
+                before.wait()
+            for shard in range(shards):
+                part = term[shard * own_hidden : (shard + 1) * own_hidden]
+
+                @pl.when(place.shard == shard)
+                def _():
+                    down_stage[...] = part
+
+                @pl.when(place.shard != shard)
+                def _():
+                    down_send[shard, :, tiles[index]] = part.astype(low)
+
+            before = pltpu.make_async_copy(down_stage, down_own.at[:, tiles[index]], stage_sem.at[0])
+            before.start()
+            yield
+        before.wait()
+        for step, other in enumerate(others, 1):
+            sender.start(
+                place.always,
+                remote(down_send.at[other], down_got.at[place.shard], swap_send.at[step], swap_recv.at[place.shard],
+                       {"shard": other}),
+            )
+
+    def gate_chunks():
+        load_gate = pltpu.make_async_copy(gate_back, pair_buf.at[0], load_sem.at[1])
+        load_gate.start()
+        load_gate.wait()
+        load_up.wait()
+        before = []
+        for index, piece in streamed(slot_rows, stream_buf, stream_sem.at[0]):
+            shard = index * tile // own_width
+            within = pl.ds(index * tile - shard * own_width, tile)
+            mine = place.shard == shard
+            after = []
+            for matrix, (own, send) in enumerate(((gate_own, gate_send), (up_own, up_send))):
+                term = matmul_tn(piece[...], pair_buf[matrix])
+                for there, copy in before[2 * matrix : 2 * matrix + 2]:
+                    @pl.when(there)
+                    def _():
+                        copy.wait()
+
+                to_own = pltpu.make_async_copy(own_stage.at[matrix], own.at[within], stage_sem.at[1 + matrix])
+                to_send = pltpu.make_async_copy(send_stage.at[matrix], send.at[shard, within], stage_sem.at[3 + matrix])
+
+                @pl.when(mine)
+                def _():
+                    own_stage[matrix] = term
+                    to_own.start()
+
+                @pl.when(~mine)
+                def _():
+                    send_stage[matrix] = term.astype(low)
+                    to_send.start()
+
+                after += [(mine, to_own), (~mine, to_send)]
+                yield
+            before = after
+        for there, copy in before:
+            @pl.when(there)
+            def _():
+                copy.wait()
+
+    def shared_chunks():
+        units = shared_hidden.shape[1]
+        per = tile // shared_term.shape[1]
+        for index, piece in streamed(all_normed, wide_buf, stream_sem.at[1]):
+            both = [matmul_tn(piece[...], grads[...]).astype(low) for grads in (shared_gate_back, shared_up_back)]
+            spot = slice(index * per, (index + 1) * per)
+            shape = (per, shared_term.shape[1], units)
+            shared_term[spot, :, :units] = both[0].reshape(shape)
+            shared_term[spot, :, units:] = both[1].reshape(shape)
+            yield
+        own_units = units // shards
+        for index, piece in streamed(all_grads, wide_buf, stream_sem.at[1]):
+            term = matmul_tn(shared_hidden[...], piece[...])
+            for shard in range(shards):
+                part = term[shard * own_units : (shard + 1) * own_units]
+                narrow_send[shard, :, tiles[index]] = part.astype(low)
+
+                @pl.when(place.shard == shard)
+                def _():
+                    narrow_own[:, tiles[index]] = part
+
+            yield
+
+    def chunks():
+        yield from down_chunks()
+        yield from gate_chunks()
+        yield from shared_chunks()
+
+    work = chunks()
+    units = plane // INNER * normed_part.shape[1]
+    next(work)
+    for _ in range(units):
+        next(back_run)
+    next(output_run, None)
+    for index in range(8):
+        next(work)
+    for index in range(units):
+        next(work, None)
+        next(back_run)
+    for index in range(units):
+        next(work, None)
+        next(output_run, None)
+    drain(back_run)
+    drain(work)
+    drain(output_run)
+    for step, member in enumerate(members):
+        score_trade(step, member, member).wait_recv()
+    keep.wait()
+    for step, other in enumerate(others, 1):
+        remote(down_send.at[other], down_got.at[other], swap_send.at[step], swap_recv.at[other], {"shard": other}).wait_recv()
+    sender.finish()
+
+
+def sums_pass(normed_part, output_part, token_scores, expert_terms, plane_terms, shared_terms):
+    shards, plane = lax.axis_size("shard"), lax.axis_size("expert")
+    low, shape = jnp.bfloat16, jax.ShapeDtypeStruct
+    slot_rows, slot_grad, hidden, gate_back, up_back = expert_terms
+    local, width = normed_part.shape[1:]
+    slots, hidden_width = hidden.shape
+    units = shared_terms[0].shape[1]
+    count = 2 * PIECES
+    pieces = (plane, count, local // count, width)
+    own_width, own_hidden = width // shards, hidden_width // shards
+    any_space, vmem = pl.BlockSpec(memory_space=pl.ANY), pl.BlockSpec(memory_space=pltpu.VMEM)
+    reduces = 2 if plane == SEQ_DEVICES else 1
+    out_shape = [
+        shape(pieces[1:], jnp.float32),
+        shape(pieces[1:], jnp.float32),
+        shape(token_scores.shape, jnp.float32),
+        shape((shards, own_hidden, width), low),
+        shape((own_hidden, width), jnp.float32),
+        shape((own_width, hidden_width), jnp.float32),
+        shape((own_width, hidden_width), jnp.float32),
+        shape((shards, own_width, hidden_width), low),
+        shape((shards, own_width, hidden_width), low),
+        shape((units // shards, width), jnp.float32),
+        shape((shards, units // shards, width), low),
+        shape((shards * plane, width // (shards * plane), 2 * units), low),
+    ]
+    dma, scratch = pltpu.SemaphoreType.DMA, pltpu.VMEM
+    tile = 256
+    outs = pl.pallas_call(
+        functools.partial(sums_kernel, shards, plane),
+        out_shape=out_shape,
+        in_specs=[any_space] * 10 + [vmem] * 3,
+        out_specs=[any_space] * 9 + [vmem] * 3,
+        scratch_shapes=[
+            scratch((shards, own_hidden, width), low),
+            scratch((2, slots, hidden_width), low),
+            scratch((2, slots, tile), low),
+            scratch((2, plane * local, tile), low),
+            scratch((2, tile, hidden_width), jnp.float32),
+            scratch((2, tile, hidden_width), low),
+            scratch((own_hidden, tile), jnp.float32),
+            dma((3,)),
+            dma((2, 2)),
+            dma((5,)),
+            dma((plane,)),
+            dma((plane,)),
+            dma((shards,)),
+            dma((shards,)),
+        ]
+        + reduces * reduce_scratch(plane, count, local // count, width),
+        compiler_params=pltpu.CompilerParams(
+            collective_id=2, has_side_effects=True, vmem_limit_bytes=63 * 2**20
+        ),
+        name="sums",
+    )(
+        normed_part.reshape(pieces),
+        output_part.reshape(pieces),
+        token_scores,
+        *expert_terms,
+        *plane_terms,
+        *shared_terms,
+    )
+    output_sum = outs[1].reshape(local, width)
+    if reduces == 1:
+        (output_sum,) = bundle(4, plane, shards, [("reduce", output_part)], 56 * 2**20)
+    return (outs[0].reshape(local, width), output_sum) + tuple(outs[2:])
 
 
 class Everyone:
@@ -1690,42 +1935,35 @@
         ),
         capacity,
     )
-    expert_down_term = matmul_tn(hidden, slot_grad)
-    transfers = [
-        ("reduce", normed_part.reshape(plane, local_rows, width)),
-        ("trade", token_scores),
-        ("share", expert_down_term.astype(jnp.bfloat16).reshape(shards, -1, width)),
-    ]
-    output_transfer = ("reduce", output_part.reshape(plane, local_rows, width))
-    if plane == SEQ_DEVICES:
-        back, scores, down_blocks, output_sum = bundle(
-            2, plane, shards, transfers + [output_transfer], 56 * 2**20
-        )
-    else:
-        back, scores, down_blocks = bundle(2, plane, shards, transfers, 56 * 2**20)
-        (output_sum,) = bundle(4, plane, shards, [output_transfer], 56 * 2**20)
+    (
+        back,
+        output_sum,
+        scores,
+        down_blocks,
+        down_own,
+        gate_own,
+        up_own,
+        gate_send,
+        up_send,
+        shared_down_own,
+        shared_down_send,
+        shared_term,
+    ) = sums_pass(
+        normed_part.reshape(plane, local_rows, width),
+        output_part.reshape(plane, local_rows, width),
+        token_scores,
+        (slot_rows, slot_grad, hidden, gate_pre_grad, up_pre_grad),
+        (all_normed, all_grads),
+        (shared_hidden, shared_gate_back, shared_up_back),
+    )
     activations = (middle + output_sum).astype(jnp.bfloat16)
 
-    def sum_shards(term, blocks):
-        own = lax.dynamic_index_in_dim(
-            term.reshape((shards, -1) + term.shape[1:]), shard_at, 0, keepdims=False
-        )
+    def sum_shards(own, blocks):
         for step in range(1, shards):
             own = own + lax.dynamic_index_in_dim(
                 blocks, (shard_at + step) % shards, 0, keepdims=False
             ).astype(jnp.float32)
         return own
-
-    expert_down_grad = sum_shards(expert_down_term, down_blocks)[None]
-    gate_term = matmul_tn(slot_rows, gate_pre_grad)
-    up_term = matmul_tn(slot_rows, up_pre_grad)
-    shared_down_term = matmul_tn(shared_hidden, all_grads)
-    shared_term = jnp.concatenate(
-        [matmul_tn(all_normed, shared_gate_back), matmul_tn(all_normed, shared_up_back)], axis=1
-    ).astype(jnp.bfloat16)
-
-    def for_shards(term):
-        return term.astype(jnp.bfloat16).reshape((shards, -1) + term.shape[1:])
 
     (
         input_grad,
@@ -1766,16 +2004,12 @@
             query_weight,
             down_half,
         ),
-        (
-            for_shards(gate_term),
-            for_shards(up_term),
-            for_shards(shared_down_term),
-            shared_term.reshape(all_devices, -1, shared_term.shape[1]),
-        ),
+        (gate_send, up_send, shared_down_send, shared_term),
     )
-    expert_gate_grad = sum_shards(gate_term, gate_blocks)[None]
-    expert_up_grad = sum_shards(up_term, up_blocks)[None]
-    shared_down_grad = sum_shards(shared_down_term, shared_blocks)[:units]
+    expert_gate_grad = sum_shards(gate_own, gate_blocks)[None]
+    expert_up_grad = sum_shards(up_own, up_blocks)[None]
+    expert_down_grad = sum_shards(down_own, down_blocks)[None]
+    shared_down_grad = sum_shards(shared_down_own, shared_blocks)[:units]
     shared_moved = shared_moved.astype(jnp.float32).reshape(shards, plane, -1, 2, shards, padded_units)
     shared_moved = jnp.sum(shared_moved, axis=0)[..., :units].transpose(2, 1, 3, 0, 4)
     shared_moved = shared_moved.reshape(2, shared_moved.shape[1], -1)

time: 845 us -> 804 us (0.951)
  matrix products: 44.4 us -> 0 us
  Pallas kernels: 708 us -> 729 us
  local copies, waits for them, and re-layouts: 47.9 us -> 35.2 us
    dot_general x6 -> x0, matrix products: 44.4 us -> none  [matmul_tn(): lax.dot_general(left, right, (((0,), (0,)), ((), ())), preferred_element_...]
    pallas_call x1, Pallas kernels: 110 us -> 131 us  [sums_pass(): pl.pallas_call(functools.partial(sums_kernel, shards, plane), out_shape=o...]
    add x3 -> x1, other arithmetic: 19.2 us -> 0.93 us  [sum_shards(): own + lax.dynamic_index_in_dim(blocks, (shard_at + step) % shards, 0, kee...]
    broadcast_in_dim x0 -> x3, other arithmetic: none -> 17.4 us  [the longest x1 7.36 us: on_device(): expert_down_grad = sum_shards(down_own, down_blocks)[None]]
    dot_general x1 -> x0, local copies, waits for them, and re-layouts: 12.4 us -> none  [matmul_tn(): lax.dot_general(left, right, (((0,), (0,)), ((), ())), preferred_element_...]
where the time goes in v6:
time: 804 us; the launch traced here: 799 us
  Pallas kernels  729 us (91%)
  local copies, waits for them, and re-layouts  35.2 us (4%)
  other arithmetic  33.2 us (4%)
    pallas_call x1, Pallas kernels, forward_pass(): pl.pallas_call(functools.partial(forward_kernel, shards, plane, scale, la...  276 us
    pallas_call x1, Pallas kernels, backward_pass(): pl.pallas_call(functools.partial(backward_kernel, shards, plane, scale, l...  239 us
    pallas_call x1, Pallas kernels, sums_pass(): pl.pallas_call(functools.partial(sums_kernel, shards, plane), out_shape=o...  131 us
    pallas_call x1, Pallas kernels, expert_pass(): pl.pallas_call(expert_kernel, grid=(steps,), out_shape=[shape((steps * to...  83.5 us

profile of v6, /device:TPU:9, one launch (start us, length us, event | category | flops | bytes accessed | tf_op | source)
XLA Modules:
  0.0 799.0 jit_solution(127180152183490364)
XLA Ops:
  0.6 0.0 copy-start.4
  0.7 1.3 constant_dynamic-slice_fusion.1
  2.0 1.4 constant_dynamic-slice_fusion.9
  3.4 1.1 pad_maximum_fusion.1.refs_2_
  4.4 0.8 reduce_window_sum.11
  5.3 0.1 select_reduce_fusion
  5.4 0.1 convert_reduce_fusion
  5.5 1.4 copy.76.refs_19_.refs_13_
  6.8 1.6 constant_dynamic-slice_fusion.8.refs_4_
  8.4 0.6 pad_bitcast_fusion.refs_20_.refs_14_
  9.0 1.9 constant_dynamic-slice_fusion.5
  10.9 1.0 fusion.8.refs_10_.rest_0_
  12.0 1.0 fusion.9.refs_11_.rest_2_
  13.0 1.0 constant_dynamic-slice_fusion.3
  14.0 0.8 pad.29.refs_12_.rest_4_
  14.8 0.0 copy-done.4
  14.8 0.7 copy.72
  15.5 0.1 fusion.13
  15.6 0.0 copy-start.12
  15.7 1.3 pad_maximum_fusion.refs_28_
  17.0 1.0 fusion.10
  18.0 0.1 tile.24
  18.1 1.3 copy.75.refs_18_.refs_17_
  19.5 0.1 tile.22
  19.6 1.3 copy.74.refs_17_.refs_16_
  20.9 0.0 copy-done.12
  20.9 0.6 fusion.14
  21.5 276.1 %forward.1 = (bf16[16,2,64,2048]{3,2,1,0:T(8,128)(2,1)}, bf16[16,2,64,2048]{3,2,1,0:T(8,128)(2,1)}, s32[16,1,8,128]{3,2,1,0:T(8,128)}, bf16[2,16,1,64,640]{4,3,2...) custom-call(bf16[2,64,2048]{2,1,0:T(8,128)(2,1)} %bitcast.96, ...), custom_call_target="tpu_custom_call" | custom-call | tf_op jit(solution)/shard_map/forward/pallas_call | solution.py:1015
  297.6 0.6 add_bitcast_fusion.me_ref
  298.2 83.5 %experts.1 = (bf16[2048,2048]{1,0:T(8,128)(2,1)}, bf16[2048,2048]{1,0:T(8,128)(2,1)}, bf16[1024,2048]{1,0:T(8,128)(2,1)}, bf16[1024,2048]{1,0:T(8,128)(2,1)}, bf...) custom-call(s32[1,2]{1,0:T(1,128)} %add_bitcast_fusion.me_ref, ...), custom_call_target="tpu_custom_call" | custom-call | tf_op jit(solution)/shard_map/experts/pallas_call | solution.py:663
  381.7 131.2 %sums.1 = (f32[4,32,2048]{2,1,0:T(8,128)}, f32[4,32,2048]{2,1,0:T(8,128)}, f32[16,8,128]{2,1,0:T(8,128)}, bf16[2,704,2048]{2,1,0:T(8,128)(2,1)}, f32[704,2048]{1...) custom-call(bf16[16,4,32,2048]{3,2,1,0:T(8,128)(2,1)} %bitcast.91, ...), custom_call_target="tpu_custom_call" | custom-call | tf_op jit(solution)/shard_map/sums/pallas_call | solution.py:1247
  513.0 7.4 fusion
  520.3 238.6 %backward.1 = (f32[128,2048]{1,0:T(8,128)}, f32[64,3072]{1,0:T(8,128)}, f32[16,4096]{1,0:T(8,128)}, f32[64,576]{1,0:T(8,128)}, f32[64,2048]{1,0:T(8,128)}, /*ind...) custom-call(f32[128,2048]{1,0:T(8,128)} %bitcast.98, ...), custom_call_target="tpu_custom_call" | custom-call | tf_op jit(solution)/shard_map/backward/pallas_call | solution.py:1709
  758.9 0.0 copy-start
  758.9 0.0 copy-start.3
  758.9 7.1 fusion.1
  766.0 0.0 copy-done
  766.0 1.8 copy-done.3
  767.8 3.0 fusion.2
  770.8 0.0 copy-done.9
  770.9 0.0 copy-done.6
  770.9 0.9 slice_add_fusion
  771.8 0.0 copy-done.2
  771.8 6.1 reshape.165
  777.9 5.7 reduce_sum.29
  783.6 0.9 slice_bitcast_fusion
  784.6 0.0 copy-start.11
  784.6 0.0 copy-start.1
  784.6 0.7 fusion.12
  785.3 0.6 copy.80
  785.9 1.4 squeeze.41
  787.4 0.6 copy.81
  788.0 0.0 copy-start.5
  788.0 1.4 squeeze.42
  789.4 0.7 dynamic-slice_bitcast_fusion.1
  790.1 0.6 dynamic-slice_bitcast_fusion.2
  790.7 0.6 fusion.11
  791.3 2.1 fusion.7
  793.4 2.3 copy.87
  795.7 0.9 copy.88
  796.6 0.0 copy-done.10
  796.6 0.7 copy.89
  797.3 0.7 copy.90
  798.0 0.8 copy.91
  (17 shorter events, 0.1 us)
Async XLA Ops:
  0.6 14.1 %copy-start.4 = (bf16[1024,576]{0,1:T(8,128)(2,1)S(1)}, bf16[1024,576]{0,1:T(8,128)(2,1)}, u32[]{:S(2)}) copy-start(bf16[1024,576]{0,1:T(8,128)(2,1)} %param.23) | copy-start | bytes 3538948
  15.6 5.2 copy-start.12
  758.9 7.1 copy-start
  758.9 8.9 %copy-start.3 = (bf16[2,1024,1408]{2,1,0:T(8,128)(2,1)S(1)}, bf16[2,1024,1408]{2,1,0:T(8,128)(2,1)}, u32[]{:S(2)}) copy-start(bf16[2,1024,1408]{2,1,0:T(8,128)(2,1)} %get-tuple-element.121) | copy-start | bytes 17301508
  767.8 3.0 copy-start.9
  767.8 3.0 copy-start.6
  767.8 4.0 copy-start.2
  784.6 4.9 copy-start.11
  784.6 6.7 copy-start.1
  788.0 7.7 copy-start.5
  788.0 10.0 %copy-start.7 = (f32[64,2048]{1,0:T(8,128)S(1)}, f32[64,2048]{1,0:T(8,128)}, u32[]{:S(2)}) copy-start(f32[64,2048]{1,0:T(8,128)} %get-tuple-element.168) | copy-start | bytes 1572868
  789.4 7.2 copy-start.10
  789.4 7.8 copy-start.8

commit v7 on v6

--- a/solution.py
+++ b/solution.py
@@ -152,9 +152,11 @@
     pl.semaphore_wait(barrier, sum(there.astype(jnp.int32) for there, _ in peers))
 
 
-def gather_steps(place, own_ref, out_ref, copy_sem, send_sem, recv_sem, sender):
+def gather_plan(place, own_ref, out_ref, copy_sem, send_sem, recv_sem):
     local = place.local
-    row, twin = local + place.row_step, local + place.twin_step
+    pieces = out_ref.shape[1]
+    row_at, twin_at = place.me + place.row_step, place.me + place.twin_step
+    segments, sends = [[]], []
 
     def push(kind, block, piece, target, source=None):
         spot = out_ref.at[block, piece]
@@ -166,45 +168,60 @@
             {"expert": target},
         )
 
+    def start(there, copy):
+        segments[-1].append((there, copy.start))
+        sends.append((there, copy))
+
     def arrive(there, block, piece):
-        @pl.when(there)
-        def _():
-            push(0, block, piece, place.me).wait_recv()
-
-    pieces = out_ref.shape[1]
+        segments[-1].append((there, push(0, block, piece, place.me).wait_recv))
+
     if own_ref is None:
         own_ref = out_ref.at[local]
     else:
         keep = pltpu.make_async_copy(own_ref, out_ref.at[local], copy_sem)
-        keep.start()
-    row_at, twin_at = place.me + place.row_step, place.me + place.twin_step
+        segments[-1].append((place.always, keep.start))
     for piece in range(pieces):
-        sender.start(place.upper, push(0, local, piece, place.me + INNER, own_ref))
-        sender.start(place.lower, push(1, local, piece, place.me - INNER, own_ref))
-        sender.start(place.always, push(2, local, piece, row_at, own_ref))
-        sender.start(place.always, push(3, local, piece, twin_at, own_ref))
-    yield
+        start(place.upper, push(0, local, piece, place.me + INNER, own_ref))
+        start(place.lower, push(1, local, piece, place.me - INNER, own_ref))
+        start(place.always, push(2, local, piece, row_at, own_ref))
+        start(place.always, push(3, local, piece, twin_at, own_ref))
     for step in range(1, place.outer + 1):
+        segments.append([])
         if step < place.outer:
             for piece in range(pieces):
                 for there, block, onward, target, kind in place.along(step):
                     arrive(there, block, piece)
-                    sender.start(there & onward, push(kind, block, piece, target))
-                    sender.start(there, push(2, block, piece, row_at))
-                    sender.start(there, push(3, block, piece, twin_at))
+                    start(there & onward, push(kind, block, piece, target))
+                    start(there, push(2, block, piece, row_at))
+                    start(there, push(3, block, piece, twin_at))
         for piece in range(pieces):
             for there, block, *_ in place.along(step - 1)[: 1 if step == 1 else 2]:
                 arrive(there, block + place.row_step, piece)
-                sender.start(there, push(3, block + place.row_step, piece, twin_at))
-        yield
+                start(there, push(3, block + place.row_step, piece, twin_at))
+    segments.append([])
     for step in range(place.outer):
         for piece in range(pieces):
             for there, block, *_ in place.along(step)[: 1 if step == 0 else 2]:
                 arrive(there, block + place.twin_step, piece)
                 arrive(there, block + place.twin_step + place.row_step, piece)
     if copy_sem is not None:
-        keep.wait()
-    yield
+        segments[-1].append((place.always, keep.wait))
+    return segments, sends
+
+
+def emit(actions):
+    for there, action in actions:
+        @pl.when(there)
+        def _():
+            action()
+
+
+def gather_steps(place, own_ref, out_ref, copy_sem, send_sem, recv_sem, sender):
+    segments, sends = gather_plan(place, own_ref, out_ref, copy_sem, send_sem, recv_sem)
+    sender.started += sends
+    for actions in segments:
+        emit(actions)
+        yield
 
 
 def add_into(target, first, *others):
@@ -516,132 +533,215 @@
     return [(at, min(most, size - at)) for at in range(0, size, most)]
 
 
-def expert_kernel(
-    me_ref, routes_ref, router_ref, rows_in, grads_in, *rest
-):
-    weights, rest = rest[:12], rest[12:]
-    (back_ref, out_ref, rows_ref, grad_ref, hidden_ref, gate_back_ref, up_back_ref, score_ref,
-     shared_hidden_ref, shared_gate_back_ref, shared_up_back_ref, slot_cotangent, pick_buf, gate_buf,
-     gate_w, up_w, down_w, shared_gate_w, shared_up_w, shared_down_w, weight_sem) = rest
-    targets = (shared_gate_w, shared_up_w, shared_down_w, gate_w, up_w, down_w)
-    shard_at = me_ref[0, 1]
-    loads = []
-    for index, target in enumerate(targets):
-        own, got = weights[2 * index], weights[2 * index + 1]
-        count = got.shape[0]
-        for step in range(count):
-            at = lax.rem(shard_at + step, count)
+def expert_kernel(shards, *refs):
+    (routes_ref, router_ref, rows_in, grads_in, shared_gate_own, shared_gate_got, shared_up_own, shared_up_got,
+     shared_down_own, shared_down_got, gate_own, gate_got, up_own, up_got, narrow_own, query_piece,
+     rows_ref, grad_ref, back_ref, out_ref, score_ref, hidden_ref, gate_back_ref, up_back_ref, shared_hidden_ref,
+     shared_gate_back_ref, shared_up_back_ref, narrow_got, full_query,
+     cotangent, hidden, gate_part, up_part, pick_all, gate_all, shared_hidden, shared_gate_back, shared_up_back,
+     gate_w, up_w, down_w, shared_gate_w, shared_up_w, shared_down_w,
+     weight_sem, save_sem, swap_send, swap_recv, piece_keep, piece_send, piece_recv) = refs
+    low = jnp.bfloat16
+    turn, step = pl.program_id(0), pl.program_id(1)
+    steps = pl.num_programs(1)
+    width, hidden_width = gate_w.shape
+    own_width = width // shards
+    senders, _, rows = routes_ref.shape
+    slots, tokens = pick_all.shape[1:]
+    capacity = slots // senders
+    experts = router_ref.shape[0]
+    plane = full_query.shape[1]
+    place = Place(plane)
+    me = place.me
+    sender = Sender()
+    others = [lax.rem(place.shard + other, shards) for other in range(1, shards)]
+
+    def at_step(number, turn_at=0):
+        return pl.when((turn == turn_at) & (step == number))
+
+    arrivals = []
+    for number, other in enumerate(others, 1):
+        push = remote(narrow_own, narrow_got.at[place.shard], swap_send.at[number], swap_recv.at[place.shard], {"shard": other})
+        arrivals.append(remote(narrow_own, narrow_got.at[other], swap_send.at[number], swap_recv.at[other], {"shard": other}))
+        sender.started.append((place.always, push))
+    pushes = [copy for _, copy in sender.started]
+    plans = [
+        gather_plan(
+            place, query_piece.at[other], full_query.at[other], piece_keep.at[number], piece_send.at[number],
+            piece_recv.at[number],
+        )
+        for number, other in enumerate(others)
+    ]
+    segments = [sum(parts, []) for parts in zip(*[plan[0] for plan in plans])]
+    for plan in plans:
+        sender.started += plan[1]
+
+    def loading(source, target, index, number):
+        return pltpu.make_async_copy(source, target, weight_sem.at[index, number])
+
+    def loads_of(index, own, got, target):
+        copies = []
+        for number in range(shards):
+            at = lax.rem(place.shard + number, shards)
             block = own.shape[0]
             spot = target.at[at] if len(target.shape) == 3 else target.at[pl.ds(pl.multiple_of(at * block, 16), block), :]
-            source = own if step == 0 else got.at[at]
-            loads.append(pltpu.make_async_copy(source, spot, weight_sem.at[index, step]))
-
-    def when_first(action):
-        @pl.when(pl.program_id(0) == 0)
+            copies.append(loading(own if number == 0 else got.at[at], spot, index, number))
+        return copies
+
+    early = (
+        loads_of(0, shared_gate_own, shared_gate_got, shared_gate_w)
+        + loads_of(1, shared_up_own, shared_up_got, shared_up_w)
+        + loads_of(2, shared_down_own, shared_down_got, shared_down_w)
+        + loads_of(3, gate_own, gate_got, gate_w)
+        + loads_of(4, up_own, up_got, up_w)
+    )
+    late = loads_of(5, narrow_own, narrow_got, down_w)
+
+    @at_step(0)
+    def _():
+        greet(place.neighbours() + [(place.always, {"shard": other}) for other in others])
+        for push in pushes:
+            push.start()
+        for load in early:
+            load.start()
+        emit(segments[0])
+
+    for number in range(1, len(segments)):
+
+        @at_step(number if number < 4 else min(number - 4, 2), number // 4 and 1)
         def _():
-            action()
-
-    def start_loads():
-        for load in loads:
+            emit(segments[number])
+
+    at_slots = pl.ds(pl.multiple_of(step * slots, slots), slots)
+    at_tokens = pl.ds(pl.multiple_of(step * tokens, tokens), tokens)
+
+    @pl.when(turn == 0)
+    def _():
+        logits = matmul_nt(router_ref[...], rows_in[...])
+        names = lax.broadcasted_iota(jnp.int32, (experts, rows), 0)
+        earlier = lax.broadcasted_iota(jnp.int32, (rows, rows), 0) <= lax.broadcasted_iota(jnp.int32, (rows, rows), 1)
+        earlier = jnp.where(earlier, 1.0, 0.0).astype(low)
+        slot_names = lax.broadcasted_iota(jnp.int32, (capacity, rows), 0).astype(jnp.float32)
+        pick_buf, gate_buf = pick_all.at[step], gate_all.at[at_slots, :]
+        pick_buf[...] = jnp.zeros(pick_buf.shape, low)
+        for number in range(senders):
+            routed = routes_ref[number]
+            chosen = jnp.zeros((experts, rows), jnp.float32)
+            for choice in range(TOP):
+                chosen = chosen + jnp.where(routed[choice : choice + 1] == names, 1.0, 0.0)
+            logit = jnp.where(chosen > 0.0, logits[:, number * rows : (number + 1) * rows], NEG)
+            expo = jnp.exp(logit - jnp.max(logit, axis=0, keepdims=True)) * chosen
+            dense = expo / jnp.sum(expo, axis=0, keepdims=True)
+            gate_row = jnp.sum(jnp.where(names == me, dense, 0.0), axis=0, keepdims=True)
+            mark = jnp.sum(jnp.where(routed == me, 1.0, 0.0), axis=0, keepdims=True)
+            rank = matmul(jnp.broadcast_to(mark, (8, rows)).astype(low), earlier)[:1] - 1.0
+            pick = jnp.where((slot_names == rank) & (mark > 0.0), 1.0, 0.0)
+            at = slice(number * capacity, (number + 1) * capacity)
+            pick_buf[at, number * rows : (number + 1) * rows] = pick.astype(low)
+            gate_buf[at, :] = jnp.sum(pick * gate_row, axis=1, keepdims=True)
+        gate = gate_buf[...]
+
+        def pick_step(index, _):
+            at = pl.ds(pl.multiple_of(index * 512, 512), 512)
+            rows_ref[:, at] = matmul(pick_buf[...], rows_in[:, at]).astype(low)
+            picked = matmul(pick_buf[...], grads_in[:, at])
+            cotangent[at_slots, at] = picked.astype(low)
+            grad_ref[:, at] = (gate * picked).astype(low)
+            return 0
+
+        lax.fori_loop(0, width // 512, pick_step, 0)
+
+        @pl.when(step == 0)
+        def _():
+            for load in early:
+                load.wait()
+
+        shared_pre, shared_up = 0.0, 0.0
+        for shard in range(shards):
+            part = rows_in[:, shard * own_width : (shard + 1) * own_width]
+            shared_pre = shared_pre + matmul(part, shared_gate_w[shard])
+            shared_up = shared_up + matmul(part, shared_up_w[shard])
+        swished, slope = swish_parts(shared_pre)
+        shared_hidden[at_tokens, :] = (swished * shared_up).astype(low)
+        shared_grad = matmul_nt(grads_in[...], shared_down_w[...])
+        shared_gate_back[at_tokens, :] = (shared_grad * shared_up * slope).astype(low)
+        shared_up_back[at_tokens, :] = (shared_grad * swished).astype(low)
+        for at, size in pieces_of(hidden_width, 512):
+            columns = slice(at, at + size)
+            gate_pre = matmul(rows_ref[...], gate_w[:, columns])
+            up_pre = matmul(rows_ref[...], up_w[:, columns])
+            swished, slope = swish_parts(gate_pre)
+            hidden[at_slots, columns] = (swished * up_pre).astype(low)
+            gate_part[at_slots, columns] = (up_pre * slope).astype(low)
+            up_part[at_slots, columns] = swished.astype(low)
+
+    @at_step(0, 1)
+    def _():
+        for arrival in arrivals:
+            arrival.wait_recv()
+        for load in late:
             load.start()
-
-    def wait_loads():
-        for load in loads:
+        for load in late:
             load.wait()
 
-    when_first(start_loads)
-    width = rows_in.shape[1]
-    hidden_width = gate_w.shape[1]
-    shards, own_width, _ = shared_gate_w.shape
-    senders, _, rows = routes_ref.shape
-    capacity = pick_buf.shape[0] // senders
-    experts = router_ref.shape[0]
-    low = jnp.bfloat16
-    me = me_ref[0, 0]
-
-    @pl.when(pl.program_id(0) == 0)
+    @pl.when(turn == 1)
     def _():
-        pick_buf[...] = jnp.zeros_like(pick_buf)
-
-    logits = matmul_nt(router_ref[...], rows_in[...])
-    names = lax.broadcasted_iota(jnp.int32, (experts, rows), 0)
-    earlier = lax.broadcasted_iota(jnp.int32, (rows, rows), 0) <= lax.broadcasted_iota(jnp.int32, (rows, rows), 1)
-    earlier = jnp.where(earlier, 1.0, 0.0).astype(low)
-    slot_names = lax.broadcasted_iota(jnp.int32, (capacity, rows), 0).astype(jnp.float32)
-    picks = []
-    for sender in range(senders):
-        routed = routes_ref[sender]
-        chosen = jnp.zeros((experts, rows), jnp.float32)
-        for choice in range(TOP):
-            chosen = chosen + jnp.where(routed[choice : choice + 1] == names, 1.0, 0.0)
-        logit = jnp.where(chosen > 0.0, logits[:, sender * rows : (sender + 1) * rows], NEG)
-        expo = jnp.exp(logit - jnp.max(logit, axis=0, keepdims=True)) * chosen
-        dense = expo / jnp.sum(expo, axis=0, keepdims=True)
-        gate_row = jnp.sum(jnp.where(names == me, dense, 0.0), axis=0, keepdims=True)
-        mark = jnp.sum(jnp.where(routed == me, 1.0, 0.0), axis=0, keepdims=True)
-        rank = matmul(jnp.broadcast_to(mark, (8, rows)).astype(low), earlier)[:1] - 1.0
-        pick = jnp.where((slot_names == rank) & (mark > 0.0), 1.0, 0.0)
-        picks.append(pick)
-        at = slice(sender * capacity, (sender + 1) * capacity)
-        pick_buf[at, sender * rows : (sender + 1) * rows] = pick.astype(low)
-        gate_buf[at, :] = jnp.sum(pick * gate_row, axis=1, keepdims=True)
-    gate = gate_buf[...]
-
-    def pick_step(index, _):
-        at = pl.ds(pl.multiple_of(index * 512, 512), 512)
-        rows_ref[:, at] = matmul(pick_buf[...], rows_in[:, at]).astype(low)
-        picked = matmul(pick_buf[...], grads_in[:, at])
-        slot_cotangent[:, at] = picked.astype(low)
-        grad_ref[:, at] = (gate * picked).astype(low)
-        return 0
-
-    lax.fori_loop(0, width // 512, pick_step, 0)
-    when_first(wait_loads)
-    shared_pre, shared_up = 0.0, 0.0
-    for shard in range(shards):
-        part = rows_in[:, shard * own_width : (shard + 1) * own_width]
-        shared_pre = shared_pre + matmul(part, shared_gate_w[shard])
-        shared_up = shared_up + matmul(part, shared_up_w[shard])
-    swished, slope = swish_parts(shared_pre)
-    shared_hidden_ref[...] = (swished * shared_up).astype(low)
-    shared_grad = matmul_nt(grads_in[...], shared_down_w[...])
-    shared_gate_back_ref[...] = (shared_grad * shared_up * slope).astype(low)
-    shared_up_back_ref[...] = (shared_grad * swished).astype(low)
-    for at, size in pieces_of(hidden_width, 512):
-        columns = slice(at, at + size)
-        gate_pre = matmul(rows_ref[...], gate_w[:, columns])
-        up_pre = matmul(rows_ref[...], up_w[:, columns])
-        swished, slope = swish_parts(gate_pre)
-        hidden_ref[:, columns] = (swished * up_pre).astype(low)
-        hidden_grad = matmul_nt(grad_ref[...], down_w[columns, :])
-        gate_back_ref[:, columns] = (hidden_grad * up_pre * slope).astype(low)
-        up_back_ref[:, columns] = (hidden_grad * swished).astype(low)
-
-    def out_step(index, score):
-        at = pl.ds(pl.multiple_of(index * 512, 512), 512)
-        shard = index * 512 // own_width
-        within = pl.ds(pl.multiple_of(index * 512 - shard * own_width, 512), 512)
-        expert_out = matmul(hidden_ref[...], down_w[:, at]).astype(low).astype(jnp.float32)
-        score = score + jnp.sum(expert_out * slot_cotangent[:, at].astype(jnp.float32), axis=1, keepdims=True)
-        out = matmul_tn(pick_buf[...], (gate * expert_out).astype(low))
-        out_ref[:, at] = (out + matmul(shared_hidden_ref[...], shared_down_w[:, at])).astype(low)
-        row_back = matmul_nt(gate_back_ref[...], gate_w[at, :]) + matmul_nt(up_back_ref[...], up_w[at, :])
-        back = (
-            matmul_tn(pick_buf[...], row_back.astype(low))
-            + matmul_nt(shared_gate_back_ref[...], shared_gate_w[shard, within, :])
-            + matmul_nt(shared_up_back_ref[...], shared_up_w[shard, within, :])
-        )
-        back_ref[:, at] = back.astype(low)
-        return score
-
-    score = lax.fori_loop(0, width // 512, out_step, jnp.zeros((gate.shape[0], 1), jnp.float32))
-    for sender in range(senders):
-        own = score[sender * capacity : (sender + 1) * capacity]
-        total = jnp.sum(picks[sender] * own, axis=0, keepdims=True)
-        score_ref[sender] = jnp.broadcast_to(total, score_ref.shape[1:])
-
-
-def expert_pass(me, routes, router, rows, grads, weights, capacity):
+        gate = gate_all[at_slots, :]
+        pick = pick_all[step]
+        slot_grad = (gate * cotangent[at_slots, :].astype(jnp.float32)).astype(low)
+        for at, size in pieces_of(hidden_width, 512):
+            columns = slice(at, at + size)
+            hidden_grad = matmul_nt(slot_grad, down_w[columns, :])
+            gate_part[at_slots, columns] = (hidden_grad * gate_part[at_slots, columns].astype(jnp.float32)).astype(low)
+            up_part[at_slots, columns] = (hidden_grad * up_part[at_slots, columns].astype(jnp.float32)).astype(low)
+
+        def out_step(index, score):
+            at = pl.ds(pl.multiple_of(index * 512, 512), 512)
+            shard = index * 512 // own_width
+            within = pl.ds(pl.multiple_of(index * 512 - shard * own_width, 512), 512)
+            expert_out = matmul(hidden[at_slots, :], down_w[:, at]).astype(low).astype(jnp.float32)
+            score = score + jnp.sum(expert_out * cotangent[at_slots, at].astype(jnp.float32), axis=1, keepdims=True)
+            out = matmul_tn(pick, (gate * expert_out).astype(low))
+            out_ref[:, at] = (out + matmul(shared_hidden[at_tokens, :], shared_down_w[:, at])).astype(low)
+            row_back = matmul_nt(gate_part[at_slots, :], gate_w[at, :]) + matmul_nt(up_part[at_slots, :], up_w[at, :])
+            back = (
+                matmul_tn(pick, row_back.astype(low))
+                + matmul_nt(shared_gate_back[at_tokens, :], shared_gate_w[shard, within, :])
+                + matmul_nt(shared_up_back[at_tokens, :], shared_up_w[shard, within, :])
+            )
+            back_ref[:, at] = back.astype(low)
+            return score
+
+        score = lax.fori_loop(0, width // 512, out_step, jnp.zeros((slots, 1), jnp.float32))
+        for number in range(senders):
+            at = slice(number * capacity, (number + 1) * capacity)
+            own_pick = pick[at, number * rows : (number + 1) * rows].astype(jnp.float32)
+            total = jnp.sum(own_pick * score[at], axis=0, keepdims=True)
+            score_ref[number] = jnp.broadcast_to(total, score_ref.shape[1:])
+
+    @pl.when((turn == 1) & (step == steps - 1))
+    def _():
+        saves = [
+            pltpu.make_async_copy(source, target, save_sem.at[index])
+            for index, (source, target) in enumerate(
+                (
+                    (hidden, hidden_ref),
+                    (gate_part, gate_back_ref),
+                    (up_part, up_back_ref),
+                    (shared_hidden, shared_hidden_ref),
+                    (shared_gate_back, shared_gate_back_ref),
+                    (shared_up_back, shared_up_back_ref),
+                )
+            )
+        ]
+        for save in saves:
+            save.start()
+        for save in saves:
+            save.wait()
+        sender.finish()
+
+
+def expert_pass(routes, router, rows, grads, weights, query_piece, capacity):
     plane, _, local = routes.shape
     senders = STEP_SENDERS
     tokens, slots = senders * local, senders * capacity
@@ -650,70 +750,81 @@
     width, hidden_width = rows.shape[1], weights[6].shape[1]
     units = weights[0].shape[1]
     low = jnp.bfloat16
-
-    def whole(array):
-        return pl.BlockSpec(array.shape, lambda i: (0,) * array.ndim, pipeline_mode=pl.Buffered(1))
-
-    def by_step(r, c):
-        return pl.BlockSpec((r, c), lambda i: (i, 0))
-
     total = steps * slots
-    shape = jax.ShapeDtypeStruct
-    route_block = pl.BlockSpec((senders, 8, local), lambda i: (i, 0, 0))
+    shape, scratch, dma = jax.ShapeDtypeStruct, pltpu.VMEM, pltpu.SemaphoreType.DMA
+    any_space = pl.BlockSpec(memory_space=pl.ANY)
+
+    def first(r, c):
+        return pl.BlockSpec((r, c), lambda turn, i: (i + turn * (steps - 1 - i), 0))
+
+    def second(r, c):
+        return pl.BlockSpec((r, c), lambda turn, i: (i * turn, 0))
+
     return pl.pallas_call(
-        expert_kernel,
-        grid=(steps,),
+        functools.partial(expert_kernel, shards),
+        grid=(2, steps),
         out_shape=[
+            shape((total, width), low),
+            shape((total, width), low),
             shape((steps * tokens, width), low),
             shape((steps * tokens, width), low),
-            shape((total, width), low),
-            shape((total, width), low),
+            shape((plane, 8, local), jnp.float32),
             shape((total, hidden_width), low),
             shape((total, hidden_width), low),
             shape((total, hidden_width), low),
-            shape((plane, 8, local), jnp.float32),
             shape((steps * tokens, units), low),
             shape((steps * tokens, units), low),
             shape((steps * tokens, units), low),
+            shape((shards,) + weights[10].shape, low),
+            shape((shards, plane) + query_piece.shape[1:], low),
         ],
         in_specs=[
-            pl.BlockSpec(memory_space=pltpu.SMEM),
-            route_block,
-            whole(router),
-            by_step(tokens, width),
-            by_step(tokens, width),
+            pl.BlockSpec((senders, 8, local), lambda turn, i: (i + turn * (steps - 1 - i), 0, 0)),
+            pl.BlockSpec(router.shape, lambda turn, i: (0, 0), pipeline_mode=pl.Buffered(1)),
+            first(tokens, width),
+            first(tokens, width),
         ]
-        + [pl.BlockSpec(memory_space=pl.ANY)] * len(weights),
+        + [any_space] * (len(weights) + 1),
         out_specs=[
-            by_step(tokens, width),
-            by_step(tokens, width),
-            by_step(slots, width),
-            by_step(slots, width),
-            by_step(slots, hidden_width),
-            by_step(slots, hidden_width),
-            by_step(slots, hidden_width),
-            route_block,
-            by_step(tokens, units),
-            by_step(tokens, units),
-            by_step(tokens, units),
-        ],
+            first(slots, width),
+            first(slots, width),
+            second(tokens, width),
+            second(tokens, width),
+            pl.BlockSpec((senders, 8, local), lambda turn, i: (i * turn, 0, 0)),
+        ]
+        + [any_space] * 8,
         scratch_shapes=[
-            pltpu.VMEM((slots, width), low),
-            pltpu.VMEM((slots, tokens), low),
-            pltpu.VMEM((slots, 1), jnp.float32),
-            pltpu.VMEM((width, hidden_width), low),
-            pltpu.VMEM((width, hidden_width), low),
-            pltpu.VMEM((hidden_width, width), low),
-            pltpu.VMEM((shards, width // shards, units), low),
-            pltpu.VMEM((shards, width // shards, units), low),
-            pltpu.VMEM((units, width), low),
-            pltpu.SemaphoreType.DMA((6, shards)),
+            scratch((total, width), low),
+            scratch((total, hidden_width), low),
+            scratch((total, hidden_width), low),
+            scratch((total, hidden_width), low),
+            scratch((steps, slots, tokens), low),
+            scratch((total, 1), jnp.float32),
+            scratch((steps * tokens, units), low),
+            scratch((steps * tokens, units), low),
+            scratch((steps * tokens, units), low),
+            scratch((width, hidden_width), low),
+            scratch((width, hidden_width), low),
+            scratch((hidden_width, width), low),
+            scratch((shards, width // shards, units), low),
+            scratch((shards, width // shards, units), low),
+            scratch((units, width), low),
+            dma((6, shards)),
+            dma((6,)),
+            dma((shards,)),
+            dma((shards,)),
+            dma((shards,)),
+            dma((shards, 4, plane, 1)),
+            dma((shards, plane, 1)),
         ],
         compiler_params=pltpu.CompilerParams(
-            vmem_limit_bytes=60 * 2**20, dimension_semantics=("arbitrary",)
+            vmem_limit_bytes=63 * 2**20,
+            dimension_semantics=("arbitrary", "arbitrary"),
+            collective_id=5,
+            has_side_effects=True,
         ),
         name="experts",
-    )(me, routes, router, rows, grads, *weights)
+    )(routes, router, rows, grads, *weights, query_piece)
 
 
 QUERIES = 256
@@ -772,9 +883,9 @@
 
 
 def forward_kernel(shards, plane, scale, last, *refs):
-    (tokens, cotangent, query_cols, down_half, up_half, out_half, query_half, gate_half, wide_half, narrow_half,
+    (tokens, cotangent, query_cols, down_half, up_half, out_half, query_half, gate_half, wide_half,
      shared_gate, shared_up, shared_down, routes, first_gain, latent_gain, second_gain, turn, sway, docs, row_docs,
-     all_normed, all_grads, all_routes, full_down, full_out, full_query, full_gate, full_up, full_narrow,
+     all_normed, all_grads, all_routes, full_down, full_out, query_piece, full_gate, full_up,
      full_shared_gate, full_shared_up, full_shared_down, normed_one,
      query, keys, value, key_latent, compressed, head_out, log_total, middle, up_buf,
      token_buf, normed_buf, query_buf, down_buf, out_buf, heads_buf, second_buf,
@@ -815,7 +926,7 @@
     )
     next(token_run)
     got_out = swap(at_piece(out_half), lambda shard: full_out.at[shard, wide.me])
-    got_wq = swap(at_piece(query_half), lambda shard: full_query.at[shard, wide.me])
+    waits = [swap(at_piece(query_half), lambda shard: query_piece.at[shard])]
     def piece_gathers(kind, full):
         return [
             gather_steps(
@@ -834,18 +945,16 @@
         next(run)
     got_query()
     got_up()
-    waits = [
+    waits += [
         swap(gate_half, lambda shard: full_gate.at[shard]),
         swap(wide_half, lambda shard: full_up.at[shard]),
     ]
     drain(token_run)
     got_out()
-    got_wq()
     waits += [
         swap(shared_gate, lambda shard: full_shared_gate.at[shard]),
         swap(shared_up, lambda shard: full_shared_up.at[shard]),
         swap(shared_down, lambda shard: full_shared_down.at[shard]),
-        swap(narrow_half, lambda shard: full_narrow.at[shard]),
     ]
     for run in down_runs:
         drain(run)
@@ -974,8 +1083,7 @@
     normed_run = gather_steps(
         wide, second_buf, all_normed, gather_keep.at[2], gather_send.at[2], gather_recv.at[2], sender
     )
-    wq_runs = piece_gathers(2, full_query)
-    runs = [normed_run, grad_run] + wq_runs
+    runs = [normed_run, grad_run]
     while runs:
         runs = [run for run in runs if next(run, "end") != "end"]
     save.wait()
@@ -997,7 +1105,8 @@
         shape((plane,) + pieces, low),
         shape((plane, 1) + routes.shape, jnp.int32),
     ]
-    out_shape += [shape((shards,) + block.shape, low) for block in (down_half, out_half, query_half) + blocks[5:]]
+    stacked = [down_half.shape, out_half.shape, query_half.shape[1:]] + [block.shape for block in blocks[5:]]
+    out_shape += [shape((shards,) + block, low) for block in stacked]
     out_shape += [
         shape((SEQ, width), low),
         shape((SEQ, head_dim + QK_ROPE), low),
@@ -1010,7 +1119,7 @@
         shape((local, width), jnp.float32),
         shape((shards,) + up_half.shape, low),
     ]
-    hbm_out = 13
+    hbm_out = 12
     dma = pltpu.SemaphoreType.DMA
     return pl.pallas_call(
         functools.partial(forward_kernel, shards, plane, scale, last),
@@ -1856,10 +1965,9 @@
         all_routes,
         full_down,
         full_out,
-        full_query,
+        query_piece,
         gate_single,
         up_single,
-        down_single,
         gate_shared,
         up_shared,
         down_shared,
@@ -1888,7 +1996,6 @@
             plane_pieces(query_weight),
             expert_gate[0],
             expert_up[0],
-            expert_down[0],
             gate_columns,
             up_columns,
             down_units,
@@ -1902,19 +2009,20 @@
     blocked = (SEQ_DEVICES, PIECES, local_rows // PIECES, width)
     shard_blocked = (shards, SEQ_DEVICES // shards) + blocked[1:]
     (
+        slot_rows,
+        slot_grad,
         normed_part,
         output_part,
-        slot_rows,
-        slot_grad,
+        token_scores,
         hidden,
         gate_pre_grad,
         up_pre_grad,
-        token_scores,
         shared_hidden,
         shared_gate_back,
         shared_up_back,
+        _,
+        full_query,
     ) = expert_pass(
-        jnp.stack([plane_at, shard_at]).astype(jnp.int32)[None],
         all_routes[:, 0],
         router_weight.T,
         all_normed,
@@ -1931,8 +2039,8 @@
             expert_up[0],
             up_single,
             expert_down[0],
-            down_single,
         ),
+        query_piece,
         capacity,
     )
     (

time: 804 us -> 782 us (0.973)
  Pallas kernels: 729 us -> 708 us
    pallas_call x1, Pallas kernels: 276 us -> 214 us  [forward_pass(): pl.pallas_call(functools.partial(forward_kernel, shards, plane, scale, la...]
    pallas_call x1, Pallas kernels: 83.5 us -> 125 us  [expert_pass(): pl.pallas_call(functools.partial(expert_kernel, shards), grid=(2, steps),...]
where the time goes in v7:
time: 782 us; the launch traced here: 777 us
  Pallas kernels  708 us (91%)
  local copies, waits for them, and re-layouts  35.2 us (5%)
  other arithmetic  32.6 us (4%)
    pallas_call x1, Pallas kernels, backward_pass(): pl.pallas_call(functools.partial(backward_kernel, shards, plane, scale, l...  239 us
    pallas_call x1, Pallas kernels, forward_pass(): pl.pallas_call(functools.partial(forward_kernel, shards, plane, scale, la...  214 us
    pallas_call x1, Pallas kernels, sums_pass(): pl.pallas_call(functools.partial(sums_kernel, shards, plane), out_shape=o...  130 us
    pallas_call x1, Pallas kernels, expert_pass(): pl.pallas_call(functools.partial(expert_kernel, shards), grid=(2, steps),...  125 us

profile of v7, /device:TPU:9, one launch (start us, length us, event | category | flops | bytes accessed | tf_op | source)
XLA Modules:
  0.0 776.9 jit_solution(12238879302975477923)
XLA Ops:
  0.6 0.0 copy-start.4
  0.7 1.3 constant_dynamic-slice_fusion.1
  2.0 1.4 constant_dynamic-slice_fusion.9
  3.4 1.1 pad_maximum_fusion.1.refs_2_
  4.4 1.6 constant_dynamic-slice_fusion.8.refs_4_
  6.0 0.8 reduce_window_sum.11
  6.9 0.1 select_reduce_fusion
  7.0 0.1 convert_reduce_fusion
  7.1 1.4 copy.76.refs_18_.refs_13_
  8.4 0.6 pad_bitcast_fusion.refs_19_.refs_14_
  9.0 1.9 constant_dynamic-slice_fusion.5
  11.0 1.0 fusion.8.refs_9_.refs_4_
  12.0 1.0 fusion.9.refs_10_.refs_6_
  13.0 1.0 constant_dynamic-slice_fusion.3
  14.0 0.8 pad.29.refs_11_.refs_8_
  14.8 0.0 copy-done.4
  14.8 0.7 copy.72
  15.5 0.1 fusion.13
  15.7 0.0 copy-start.12
  15.7 1.3 pad_maximum_fusion.refs_28_
  17.0 1.0 fusion.10
  18.1 0.1 tile.24
  18.2 1.3 copy.75.refs_17_
  19.5 0.1 tile.22
  19.6 1.3 copy.74.refs_16_
  20.9 0.0 copy-done.12
  20.9 0.6 fusion.14
  21.5 214.2 %forward.1 = (bf16[16,2,64,2048]{3,2,1,0:T(8,128)(2,1)}, bf16[16,2,64,2048]{3,2,1,0:T(8,128)(2,1)}, s32[16,1,8,128]{3,2,1,0:T(8,128)}, bf16[2,16,1,64,640]{4,3,2...) custom-call(bf16[2,64,2048]{2,1,0:T(8,128)(2,1)} %bitcast.91, ...), custom_call_target="tpu_custom_call" | custom-call | tf_op jit(solution)/shard_map/forward/pallas_call | solution.py:1124
  235.8 124.6 %experts.1 = (bf16[1024,2048]{1,0:T(8,128)(2,1)}, bf16[1024,2048]{1,0:T(8,128)(2,1)}, bf16[2048,2048]{1,0:T(8,128)(2,1)}, bf16[2048,2048]{1,0:T(8,128)(2,1)}, f3...) custom-call(s32[16,8,128]{2,1,0:T(8,128)} %bitcast.99, ...), custom_call_target="tpu_custom_call" | custom-call | tf_op jit(solution)/shard_map/experts/pallas_call | solution.py:763
  360.4 130.2 %sums.1 = (f32[4,32,2048]{2,1,0:T(8,128)}, f32[4,32,2048]{2,1,0:T(8,128)}, f32[16,8,128]{2,1,0:T(8,128)}, bf16[2,704,2048]{2,1,0:T(8,128)(2,1)}, f32[704,2048]{1...) custom-call(bf16[16,4,32,2048]{3,2,1,0:T(8,128)(2,1)} %bitcast.85, ...), custom_call_target="tpu_custom_call" | custom-call | tf_op jit(solution)/shard_map/sums/pallas_call | solution.py:1356
  490.6 7.4 fusion
  498.0 238.8 %backward.1 = (f32[128,2048]{1,0:T(8,128)}, f32[64,3072]{1,0:T(8,128)}, f32[16,4096]{1,0:T(8,128)}, f32[64,576]{1,0:T(8,128)}, f32[64,2048]{1,0:T(8,128)}, /*ind...) custom-call(f32[128,2048]{1,0:T(8,128)} %bitcast.93, ...), custom_call_target="tpu_custom_call" | custom-call | tf_op jit(solution)/shard_map/backward/pallas_call | solution.py:1818
  736.8 0.0 copy-start
  736.8 0.0 copy-start.3
  736.8 7.1 fusion.1
  743.9 0.0 copy-done
  743.9 1.8 copy-done.3
  745.7 3.0 fusion.2
  748.7 0.0 copy-done.9
  748.8 0.0 copy-done.6
  748.8 0.9 slice_add_fusion
  749.7 0.0 copy-done.2
  749.7 6.1 reshape.165
  755.9 5.7 reduce_sum.29
  761.5 0.9 slice_bitcast_fusion
  762.5 0.0 copy-start.11
  762.5 0.0 copy-start.1
  762.5 0.7 fusion.12
  763.2 0.6 copy.80
  763.8 1.4 squeeze.40
  765.3 0.6 copy.81
  765.9 0.0 copy-start.5
  765.9 0.0 copy-start.7
  765.9 1.4 squeeze.41
  767.4 0.7 dynamic-slice_bitcast_fusion.1
  768.0 0.6 dynamic-slice_bitcast_fusion.2
  768.6 0.6 fusion.11
  769.2 2.1 fusion.7
  771.3 2.3 copy.87
  773.6 0.9 copy.88
  774.5 0.0 copy-done.10
  774.5 0.7 copy.89
  775.2 0.7 copy.90
  775.9 0.8 copy.91
  (16 shorter events, 0.1 us)
Async XLA Ops:
  0.6 14.2 %copy-start.4 = (bf16[1024,576]{0,1:T(8,128)(2,1)S(1)}, bf16[1024,576]{0,1:T(8,128)(2,1)}, u32[]{:S(2)}) copy-start(bf16[1024,576]{0,1:T(8,128)(2,1)} %param.23) | copy-start | bytes 3538948
  15.7 5.2 copy-start.12
  736.8 7.1 copy-start
  736.8 8.9 %copy-start.3 = (bf16[2,1024,1408]{2,1,0:T(8,128)(2,1)S(1)}, bf16[2,1024,1408]{2,1,0:T(8,128)(2,1)}, u32[]{:S(2)}) copy-start(bf16[2,1024,1408]{2,1,0:T(8,128)(2,1)} %get-tuple-element.121) | copy-start | bytes 17301508
  745.7 3.0 copy-start.9
  745.7 3.0 copy-start.6
  745.7 4.0 copy-start.2
  762.5 4.9 copy-start.11
  762.5 6.7 copy-start.1
  765.9 7.7 copy-start.5
  765.9 10.0 %copy-start.7 = (f32[64,2048]{1,0:T(8,128)S(1)}, f32[64,2048]{1,0:T(8,128)}, u32[]{:S(2)}) copy-start(f32[64,2048]{1,0:T(8,128)} %get-tuple-element.168) | copy-start | bytes 1572868
  767.4 7.2 copy-start.10
  767.4 7.8 %copy-start.8 = (f32[16,4096]{1,0:T(8,128)S(1)}, f32[16,4096]{1,0:T(8,128)}, u32[]{:S(2)}) copy-start(f32[16,4096]{1,0:T(8,128)} %get-tuple-element.167) | copy-start | bytes 786436

commit v8 on v7

--- a/solution.py
+++ b/solution.py
@@ -3,6 +3,7 @@
 
 import jax
 import jax.numpy as jnp
+import numpy as np
 from jax import lax
 from jax.experimental import pallas as pl
 from jax.experimental.pallas import tpu as pltpu
@@ -535,12 +536,12 @@
 
 def expert_kernel(shards, *refs):
     (routes_ref, router_ref, rows_in, grads_in, shared_gate_own, shared_gate_got, shared_up_own, shared_up_got,
-     shared_down_own, shared_down_got, gate_own, gate_got, up_own, up_got, narrow_own, query_piece,
+     shared_down_own, shared_down_got, gate_own, gate_got, up_own, up_got, narrow_own, query_piece, all_rows,
      rows_ref, grad_ref, back_ref, out_ref, score_ref, hidden_ref, gate_back_ref, up_back_ref, shared_hidden_ref,
-     shared_gate_back_ref, shared_up_back_ref, narrow_got, full_query,
+     shared_got, narrow_got, full_query,
      cotangent, hidden, gate_part, up_part, pick_all, gate_all, shared_hidden, shared_gate_back, shared_up_back,
      gate_w, up_w, down_w, shared_gate_w, shared_up_w, shared_down_w,
-     weight_sem, save_sem, swap_send, swap_recv, piece_keep, piece_send, piece_recv) = refs
+     wide_buf, shared_term, weight_sem, save_sem, wide_sem, owner_send, owner_recv, owner_keep, swap_send, swap_recv, piece_keep, piece_send, piece_recv) = refs
     low = jnp.bfloat16
     turn, step = pl.program_id(0), pl.program_id(1)
     steps = pl.num_programs(1)
@@ -597,9 +598,13 @@
     )
     late = loads_of(5, narrow_own, narrow_got, down_w)
 
+    to_owners = Everyone(
+        place, plane, shards, lambda target: shared_term.at[target], shared_got, owner_send, owner_recv, owner_keep
+    )
+
     @at_step(0)
     def _():
-        greet(place.neighbours() + [(place.always, {"shard": other}) for other in others])
+        greet_everyone(place, plane, shards)
         for push in pushes:
             push.start()
         for load in early:
@@ -677,8 +682,26 @@
 
     @at_step(0, 1)
     def _():
+        tile = wide_buf.shape[2]
+        units = shared_hidden.shape[1]
+        per = tile // shared_term.shape[1]
+        copies = [
+            pltpu.make_async_copy(all_rows.at[:, at : at + tile], wide_buf.at[index % 2], wide_sem.at[index % 2])
+            for index, at in enumerate(range(0, width, tile))
+        ]
+        copies[0].start()
+        for index, copy in enumerate(copies):
+            if index + 1 < len(copies):
+                copies[index + 1].start()
+            copy.wait()
+            spot = slice(index * per, (index + 1) * per)
+            shape = (per, shared_term.shape[1], units)
+            for part, grads in enumerate((shared_gate_back, shared_up_back)):
+                term = matmul_tn(wide_buf[index % 2], grads[...]).astype(low)
+                shared_term[spot, :, part * units : (part + 1) * units] = term.reshape(shape)
         for arrival in arrivals:
             arrival.wait_recv()
+        to_owners.start()
         for load in late:
             load.start()
         for load in late:
@@ -729,8 +752,6 @@
                     (gate_part, gate_back_ref),
                     (up_part, up_back_ref),
                     (shared_hidden, shared_hidden_ref),
-                    (shared_gate_back, shared_gate_back_ref),
-                    (shared_up_back, shared_up_back_ref),
                 )
             )
         ]
@@ -738,6 +759,8 @@
             save.start()
         for save in saves:
             save.wait()
+        to_owners.wait()
+        to_owners.finish()
         sender.finish()
 
 
@@ -773,8 +796,7 @@
             shape((total, hidden_width), low),
             shape((total, hidden_width), low),
             shape((steps * tokens, units), low),
-            shape((steps * tokens, units), low),
-            shape((steps * tokens, units), low),
+            shape((shards * plane, width // (shards * plane), 2 * units), low),
             shape((shards,) + weights[10].shape, low),
             shape((shards, plane) + query_piece.shape[1:], low),
         ],
@@ -784,7 +806,7 @@
             first(tokens, width),
             first(tokens, width),
         ]
-        + [any_space] * (len(weights) + 1),
+        + [any_space] * (len(weights) + 2),
         out_specs=[
             first(slots, width),
             first(slots, width),
@@ -792,7 +814,7 @@
             second(tokens, width),
             pl.BlockSpec((senders, 8, local), lambda turn, i: (i * turn, 0, 0)),
         ]
-        + [any_space] * 8,
+        + [any_space] * 7,
         scratch_shapes=[
             scratch((total, width), low),
             scratch((total, hidden_width), low),
@@ -809,8 +831,14 @@
             scratch((shards, width // shards, units), low),
             scratch((shards, width // shards, units), low),
             scratch((units, width), low),
+            scratch((2, steps * tokens, 128), low),
+            scratch((shards * plane, width // (shards * plane), 2 * units), low),
             dma((6, shards)),
             dma((6,)),
+            dma((2,)),
+            dma((shards * plane,)),
+            dma((shards * plane,)),
+            dma(()),
             dma((shards,)),
             dma((shards,)),
             dma((shards,)),
@@ -824,15 +852,34 @@
             has_side_effects=True,
         ),
         name="experts",
-    )(routes, router, rows, grads, *weights, query_piece)
+    )(routes, router, rows, grads, *weights, query_piece, rows)
 
 
 QUERIES = 256
 KEYS = WINDOW + QUERIES
 
 
-def score_block(scale, query, keys, query_docs, key_docs):
+def document_ends(lengths, sequence):
+    ends, total = [], 0
+    for entry in range(lengths.shape[1]):
+        total = total + lengths[sequence, entry]
+        ends.append(total)
+    return ends
+
+
+def documents_at(positions, ends):
+    inside = sum(jnp.where(positions >= end, 1, 0) for end in ends)
+    return jnp.where(positions < 0, -1, inside)
+
+
+def query_documents(index, ends):
+    return documents_at(lax.broadcasted_iota(jnp.int32, (QUERIES, 1), 0) + index * QUERIES, ends)
+
+
+def score_block(scale, index, ends, query, keys):
     raw = matmul_nt(query, keys) * scale
+    query_docs = query_documents(index, ends)
+    key_docs = documents_at(lax.broadcasted_iota(jnp.int32, (1, KEYS), 1) + (index * QUERIES - WINDOW), ends)
     row = lax.broadcasted_iota(jnp.int32, raw.shape, 0) + WINDOW
     column = lax.broadcasted_iota(jnp.int32, raw.shape, 1)
     allowed = (query_docs == key_docs) & (column <= row) & (column > row - WINDOW)
@@ -884,7 +931,7 @@
 
 def forward_kernel(shards, plane, scale, last, *refs):
     (tokens, cotangent, query_cols, down_half, up_half, out_half, query_half, gate_half, wide_half,
-     shared_gate, shared_up, shared_down, routes, first_gain, latent_gain, second_gain, turn, sway, docs, row_docs,
+     shared_gate, shared_up, shared_down, routes, first_gain, latent_gain, second_gain, turn, sway, lengths,
      all_normed, all_grads, all_routes, full_down, full_out, query_piece, full_gate, full_up,
      full_shared_gate, full_shared_up, full_shared_down, normed_one,
      query, keys, value, key_latent, compressed, head_out, log_total, middle, up_buf,
@@ -895,7 +942,8 @@
     group = SEQ_DEVICES
     place, wide = Place(group), Place(plane)
     width = tokens.shape[-1]
-    rows = docs.shape[0] // group
+    rows = middle.shape[0]
+    ends = document_ends(lengths, (place.shard * plane + place.me) // group)
     sender = Sender()
     members = [lax.rem(place.local + step, group) for step in range(1, group)]
     peers = [(place.always, {"expert": place.base + member}) for member in members]
@@ -918,6 +966,12 @@
         )
 
     at_piece = lambda ref: ref.at[wide.me]
+    head_dim = QK_NOPE + QK_ROPE
+    start = place.local * head_dim // 128 * 128
+    odd = lax.rem(place.local * head_dim, 128) > 0
+    query_cols = query_cols.at[:, pl.ds(pl.multiple_of(start, 128), 2 * QK_NOPE)]
+    both = QK_NOPE + V_HEAD
+    up_half = up_half.at[:, pl.ds(pl.multiple_of(place.local * both, both), both)]
     got_query = swap(query_cols, lambda shard: query_buf.at[shard], True)
     got_down = swap(at_piece(down_half), lambda shard: full_down.at[shard, wide.me])
     got_up = swap(up_half, lambda shard: up_buf.at[shard], True)
@@ -986,15 +1040,23 @@
         normed_buf[at, :] = (values * root * first_gain[...]).astype(low)
         first = whole_dot(at, lambda shard: query_buf[shard])
         latent = whole_dot(at, lambda shard: down_buf[shard].reshape(own_width, -1))
-        turn_at, sway_at = turn[at, :QK_ROPE], sway[at, :QK_ROPE]
-        end = QK_NOPE + QK_ROPE
+        first = jnp.where(odd, pltpu.roll(first, first.shape[1] - QK_ROPE, 1), first)
+        turn_at, sway_at = turn[at, :], sway[at, :]
+        lane = lax.broadcasted_iota(jnp.int32, turn_at.shape, 1)
+
+        def rotated(values):
+            pair = jnp.where(lane < QK_ROPE, values, pltpu.roll(values, QK_ROPE, 1))
+            return pair * turn_at + swapped_halves(pair) * sway_at
+
         query[at, :QK_NOPE] = first[:, :QK_NOPE].astype(low)
-        query[at, QK_NOPE:end] = (first[:, QK_NOPE:end] * turn_at + first[:, end:] * sway_at).astype(low)
-        query[at, end:] = jnp.zeros((tile, QK_ROPE), low)
-        end = KV_RANK + QK_ROPE
-        key_rope = (latent[:, KV_RANK:end] * turn_at + latent[:, end:] * sway_at).astype(low)
+        query[at, QK_NOPE:] = jnp.where(lane < QK_ROPE, rotated(first[:, QK_NOPE:]), 0.0).astype(low)
+        key_rope = rotated(latent[:, KV_RANK:]).astype(low)
         latent = latent[:, :KV_RANK]
-        compressed[at, :] = latent
+
+        @pl.when(index == place.local // 2)
+        def _():
+            compressed[...] = jnp.where(lax.rem(place.local, 2) == 0, latent[:rows], latent[rows:])
+
         root = lax.rsqrt(jnp.mean(latent * latent, axis=1, keepdims=True) + EPS)
         normed_latent = (latent * root * latent_gain[...]).astype(low)
         key_latent[at, :] = normed_latent
@@ -1005,8 +1067,7 @@
         both = both.astype(low)
         later = pl.ds(pl.multiple_of(index * tile + WINDOW, tile), tile)
         keys[later, :QK_NOPE] = both[:, :QK_NOPE]
-        keys[later, QK_NOPE : QK_NOPE + QK_ROPE] = key_rope
-        keys[later, QK_NOPE + QK_ROPE :] = key_rope
+        keys[later, QK_NOPE:] = key_rope
         value[later, :] = both[:, QK_NOPE:]
         return 0
 
@@ -1027,17 +1088,17 @@
     def attend_tile(index, _):
         at = pl.ds(pl.multiple_of(index * QUERIES, QUERIES), QUERIES)
         window = pl.ds(pl.multiple_of(index * QUERIES, QUERIES), KEYS)
-        scores = score_block(scale, query[at, :], keys[window, :], docs[at, :], row_docs[:, window])
+        scores = score_block(scale, index, ends, query[at, :], keys[window, :])
         top = jnp.max(scores, axis=1, keepdims=True)
         expo = jnp.exp(scores - top)
         total = jnp.sum(expo, axis=1, keepdims=True)
         probs = (expo / total).astype(low)
-        real = jnp.where(docs[at, :] < last, 1.0, 0.0)
+        real = jnp.where(query_documents(index, ends) < last, 1.0, 0.0)
         head_out[at, :] = (matmul(probs, value[window, :]) * real).astype(low)
         log_total[at, :] = jnp.broadcast_to(top + jnp.log(total), (QUERIES, log_total.shape[1]))
         return 0
 
-    blocks = docs.shape[0] // QUERIES
+    blocks = query.shape[0] // QUERIES
     lax.fori_loop(0, blocks // 2, attend_tile, 0)
     for run in out_runs + [route_run]:
         drain(run)
@@ -1113,23 +1174,23 @@
         shape((SEQ + WINDOW, head_dim + QK_ROPE), low),
         shape((SEQ + WINDOW, V_HEAD), low),
         shape((SEQ, KV_RANK), low),
-        shape((SEQ, KV_RANK), jnp.float32),
+        shape((local, KV_RANK), jnp.float32),
         shape((SEQ, V_HEAD), low),
         shape((SEQ, 128), jnp.float32),
         shape((local, width), jnp.float32),
-        shape((shards,) + up_half.shape, low),
+        shape((shards, up_half.shape[0], QK_NOPE + V_HEAD), low),
     ]
     hbm_out = 12
     dma = pltpu.SemaphoreType.DMA
     return pl.pallas_call(
         functools.partial(forward_kernel, shards, plane, scale, last),
         out_shape=out_shape,
-        in_specs=[any_space] * (3 + len(blocks)) + [vmem] * (len(gains) + len(tables)),
+        in_specs=[any_space] * (3 + len(blocks)) + [vmem] * (len(gains) + len(tables) - 1) + [pl.BlockSpec(memory_space=pltpu.SMEM)],
         out_specs=[any_space] * hbm_out + [vmem] * (len(out_shape) - hbm_out),
         scratch_shapes=[
             pltpu.VMEM((SEQ_DEVICES,) + pieces, low),
             pltpu.VMEM((SEQ, width), low),
-            pltpu.VMEM((shards,) + query_cols.shape, low),
+            pltpu.VMEM((shards, query_cols.shape[0], 2 * QK_NOPE), low),
             pltpu.VMEM((shards,) + down_half.shape, low),
             pltpu.VMEM((shards,) + out_half.shape, low),
             pltpu.VMEM((local, HEADS * V_HEAD), low),
@@ -1155,10 +1216,9 @@
 
 
 def sums_kernel(shards, plane, *refs):
-    (normed_part, output_part, token_scores, slot_rows, slot_grad, hidden, gate_back, up_back, all_normed, all_grads,
-     shared_hidden, shared_gate_back, shared_up_back,
+    (normed_part, output_part, token_scores, slot_rows, slot_grad, hidden, gate_back, up_back, all_grads,
+     shared_hidden,
      back, output_sum, scores, down_got, down_own, gate_own, up_own, gate_send, up_send, narrow_own, narrow_send,
-     shared_term,
      down_send, pair_buf, stream_buf, wide_buf, own_stage, send_stage, down_stage,
      load_sem, stream_sem, stage_sem, score_send, score_recv, swap_send, swap_recv, *reduces) = refs
     low = jnp.bfloat16
@@ -1274,14 +1334,6 @@
 
     def shared_chunks():
         units = shared_hidden.shape[1]
-        per = tile // shared_term.shape[1]
-        for index, piece in streamed(all_normed, wide_buf, stream_sem.at[1]):
-            both = [matmul_tn(piece[...], grads[...]).astype(low) for grads in (shared_gate_back, shared_up_back)]
-            spot = slice(index * per, (index + 1) * per)
-            shape = (per, shared_term.shape[1], units)
-            shared_term[spot, :, :units] = both[0].reshape(shape)
-            shared_term[spot, :, units:] = both[1].reshape(shape)
-            yield
         own_units = units // shards
         for index, piece in streamed(all_grads, wide_buf, stream_sem.at[1]):
             term = matmul_tn(shared_hidden[...], piece[...])
@@ -1349,15 +1401,14 @@
         shape((shards, own_width, hidden_width), low),
         shape((units // shards, width), jnp.float32),
         shape((shards, units // shards, width), low),
-        shape((shards * plane, width // (shards * plane), 2 * units), low),
     ]
     dma, scratch = pltpu.SemaphoreType.DMA, pltpu.VMEM
     tile = 256
     outs = pl.pallas_call(
         functools.partial(sums_kernel, shards, plane),
         out_shape=out_shape,
-        in_specs=[any_space] * 10 + [vmem] * 3,
-        out_specs=[any_space] * 9 + [vmem] * 3,
+        in_specs=[any_space] * 9 + [vmem],
+        out_specs=[any_space] * 9 + [vmem] * 2,
         scratch_shapes=[
             scratch((shards, own_hidden, width), low),
             scratch((2, slots, hidden_width), low),
@@ -1477,27 +1528,29 @@
 
 def backward_kernel(shards, plane, scale, last, *refs):
     (back, scores, routes, middle, cotangent, tokens, first_gain, second_gain, latent_gain, router,
-     query, keys, value, docs, row_docs, log_total, turn, sway, key_latent, up_head, head_out,
-     compressed, full_out, full_query, full_down, normed_one, out_half, query_half, down_half, gate_send, up_send, narrow_send, shared_term,
-     input_grad, query_out, up_out, down_out, out_out, small_out,
-     gate_got, up_got, narrow_got, shared_got, mid_all,
+     lengths, query, keys, value, log_total, turn, sway, key_latent, up_head, head_out,
+     compressed, full_out, full_query, full_down, normed_one, out_half, query_half, down_half, gate_send, up_send, narrow_send, down_own, down_sum_got,
+     shared_moved, input_grad, query_out, up_out, down_out, out_out, small_out, shared_gate_out, shared_up_out,
+     gate_got, up_got, narrow_got, mid_all, down_total,
      stream_buf, wq_buf, wd_buf, own_columns, own_compressed, heads_sum, mid_buf, low_buf, heads_buf, grad_buf, key_sum, value_sum,
      part_buf, trade_buf, trade_got, pair_buf, query_term, query_got, up_term, up_got_buf, own_query, low_grad, low_all,
-     down_rows, down_got, out_rows, out_got, small_buf, small_got, key_got, *sems) = refs
-    (load_sem, whole_sem, stream_sem, swap_send, swap_recv, trade_send, trade_recv, gather_send, gather_recv, gather_keep,
+     down_rows, down_got, out_rows, out_got, small_buf, small_got, key_got, total_buf, part_in, *sems) = refs
+    (total_sem, part_sem, save_sem, load_sem, whole_sem, stream_sem, swap_send, swap_recv, trade_send, trade_recv, gather_send, gather_recv, gather_keep,
      all_send, all_recv, all_keep, rows_send, rows_recv, rows_keep, *reduce_scratch_refs) = sems
     low = jnp.bfloat16
     group = SEQ_DEVICES
     place = Place(group)
     local, width = middle.shape
     total = shards * plane
+    ends = document_ends(lengths, (place.shard * plane + place.me) // group)
     sender = Sender()
     greet_everyone(place, plane, shards)
     members = [lax.rem(place.local + step, group) for step in range(1, group)]
     others = [lax.rem(place.shard + step, shards) for step in range(1, shards)]
 
     shares = []
-    for number, (source, got) in enumerate(((gate_send, gate_got), (up_send, up_got), (narrow_send, narrow_got))):
+
+    def share(number, source, got):
         for step, other in enumerate(others, 1):
             sender.start(
                 place.always,
@@ -1508,6 +1561,8 @@
                 remote(source.at[other], got.at[other], swap_send.at[number, step], swap_recv.at[number, other],
                        {"shard": other})
             )
+
+    share(0, gate_send, gate_got)
     numbers = iter(range(16))
 
     def load(source, target):
@@ -1574,10 +1629,53 @@
         mine = place.shard == shard
         return [(mine, query_half.at[rows], target, 0), (~mine, full_query.at[shard, rows], target, 0)]
 
-    got_compressed = load(compressed.at[own_at, :], own_compressed)
+    got_compressed = load(compressed, own_compressed)
 
     def everyone(index, source, got):
         return Everyone(place, plane, shards, source, got, all_send.at[index], all_recv.at[index], all_keep.at[index])
+
+    def add_shards(own, got, result):
+        rows, columns = own.shape
+        size = 128 if rows % 128 == 0 else 176
+        lanes = pl.ds(0, columns)
+
+        def copies(index):
+            half, at = index % 2, pl.ds(index * size, size)
+            found = [pltpu.make_async_copy(own.at[at], total_buf.at[half, pl.ds(0, size), lanes], total_sem.at[half])]
+            for step, other in enumerate(others):
+                found.append(
+                    pltpu.make_async_copy(
+                        got.at[other, at], part_in.at[half, step, pl.ds(0, size), lanes], part_sem.at[half, step]
+                    )
+                )
+            return found, pltpu.make_async_copy(
+                total_buf.at[half, pl.ds(0, size), lanes], result.at[at], save_sem.at[half]
+            )
+
+        tiles_of = [copies(index) for index in range(rows // size)]
+        for copy in tiles_of[0][0]:
+            copy.start()
+        for index, (loads, save) in enumerate(tiles_of):
+            if index + 1 < len(tiles_of):
+                if index:
+                    tiles_of[index - 1][1].wait()
+                for copy in tiles_of[index + 1][0]:
+                    copy.start()
+            for copy in loads:
+                copy.wait()
+
+            def body(chunk, _):
+                at = pl.ds(pl.multiple_of(chunk * 16, 16), 16)
+                total = total_buf[index % 2, at, lanes]
+                for step in range(len(others)):
+                    total = total + part_in[index % 2, step, at, lanes].astype(jnp.float32)
+                total_buf[index % 2, at, lanes] = total
+                return 0
+
+            lax.fori_loop(0, size // 16, body, 0)
+            save.start()
+        for _, save in tiles_of[-2:]:
+            save.wait()
 
     experts = router.shape[0]
     values = middle[...]
@@ -1618,12 +1716,11 @@
     for step, member in enumerate(members):
         sender.start(place.always, head_trade(step, member, place.local))
     mid_run = gather_steps(place, low_buf, mid_all, gather_keep.at[0], gather_send.at[0], gather_recv.at[0], sender)
+    next(mid_run)
+    add_shards(down_own, down_sum_got, down_total)
     for step, member in enumerate(members):
         head_trade(step, member, member).wait_recv()
     keep_head.wait()
-    next(mid_run)
-    shared_trade = everyone(0, lambda target: shared_term.at[target], shared_got)
-    shared_trade.start()
 
     key_sum[...] = jnp.zeros_like(key_sum)
     value_sum[...] = jnp.zeros_like(value_sum)
@@ -1632,8 +1729,8 @@
         at = pl.ds(pl.multiple_of(index * QUERIES, QUERIES), QUERIES)
         window = pl.ds(pl.multiple_of(index * QUERIES, QUERIES), KEYS)
         tile, key_tile = query[at, :], keys[window, :]
-        head_grad = jnp.where(docs[at, :] < last, grad_buf[at, :], jnp.zeros((), low))
-        scores_at = score_block(scale, tile, key_tile, docs[at, :], row_docs[:, window])
+        head_grad = jnp.where(query_documents(index, ends) < last, grad_buf[at, :], jnp.zeros((), low))
+        scores_at = score_block(scale, index, ends, tile, key_tile)
         probs = jnp.exp(scores_at - log_total[at, :1])
         prob_grad = matmul_nt(head_grad, value[window, :])
         inner = jnp.sum(probs * prob_grad, axis=1, keepdims=True)
@@ -1646,13 +1743,16 @@
         value_sum[window, :] += matmul_tn(probs.astype(low), head_grad)
         return 0
 
-    blocks = docs.shape[0] // QUERIES
+    blocks = query.shape[0] // QUERIES
     for index in range(blocks // 2):
         attend_tile(jnp.int32(index), 0)
     next(mid_run)
     for index in range(blocks // 2, blocks):
         attend_tile(jnp.int32(index), 0)
     next(mid_run)
+
+    share(1, up_send, up_got)
+    share(2, narrow_send, narrow_got)
 
     lane = lax.broadcasted_iota(jnp.int32, (QUERIES, 2 * QK_ROPE), 1)
 
@@ -1693,7 +1793,18 @@
     query_trade.start()
     up_trade = everyone(2, lambda target: up_term.at[target], up_got_buf)
     up_trade.start()
+    units = shared_gate_out.shape[1] // total
+    padded = shared_moved.shape[2] // (2 * shards)
     next(reduce_run)
+    for member in range(plane):
+        block = 0.0
+        for shard in range(shards):
+            block = block + shared_moved[shard * plane + member].astype(jnp.float32)
+        for part, result in enumerate((shared_gate_out, shared_up_out)):
+            for shard in range(shards):
+                at = (part * shards + shard) * padded
+                spot = (shard * plane + member) * units
+                result[:, spot : spot + units] = block[:, at : at + units]
     drain(reduce_run)
     for step, member in enumerate(members):
         token_trade(step, member, member).wait_recv()
@@ -1774,15 +1885,14 @@
         out_sum = out_sum + out_got[sequence].astype(jnp.float32)
     down_out[...] = down_sum[:, : down_out.shape[1]]
     out_out[...] = out_sum
-    shared_trade.wait()
-    for share in shares:
-        share.wait_recv()
-    for trade in (shared_trade, query_trade, up_trade, small_trade):
+    for arrival in shares:
+        arrival.wait_recv()
+    for trade in (query_trade, up_trade, small_trade):
         trade.finish()
     sender.finish()
 
 
-def backward_pass(scale, last, small, tables, saved, weights, sends):
+def backward_pass(scale, last, small, tables, saved, weights, sends, owns, shared_moved, shared_width):
     shards, plane = lax.axis_size("shard"), lax.axis_size("expert")
     total = shards * plane
     low, shape = jnp.bfloat16, jax.ShapeDtypeStruct
@@ -1790,8 +1900,10 @@
     head_dim = QK_NOPE + QK_ROPE
     vmem, any_space = pl.BlockSpec(memory_space=pltpu.VMEM), pl.BlockSpec(memory_space=pl.ANY)
     inputs = list(small) + list(tables) + list(saved)
-    hbm = list(weights) + list(sends)
-    gate_send, up_send, narrow_send, shared_term = sends
+    spaces = [vmem] * len(inputs)
+    spaces[len(small)] = pl.BlockSpec(memory_space=pltpu.SMEM)
+    hbm = list(weights) + list(sends) + list(owns) + [shared_moved]
+    gate_send, up_send, narrow_send = sends
     experts = small[9].shape[0]
     small_rows = experts + 3 + -(experts + 3) % 8
     own_width = width // total
@@ -1802,11 +1914,13 @@
         shape((own_width, KV_RANK + QK_ROPE), jnp.float32),
         shape((own_width, width), jnp.float32),
         shape((small_rows, 128), jnp.float32),
+        shape((own_width, shared_width), jnp.float32),
+        shape((own_width, shared_width), jnp.float32),
         shape(gate_send.shape, low),
         shape(up_send.shape, low),
         shape(narrow_send.shape, low),
-        shape(shared_term.shape, low),
         shape((SEQ_DEVICES, PIECES, local // PIECES, width), low),
+        shape(owns[0].shape, jnp.float32),
     ]
     hbm_out = 5
     dma, scratch = pltpu.SemaphoreType.DMA, pltpu.VMEM
@@ -1818,7 +1932,7 @@
     return pl.pallas_call(
         functools.partial(backward_kernel, shards, plane, scale, last),
         out_shape=out_shape,
-        in_specs=[vmem] * len(inputs) + [any_space] * len(hbm),
+        in_specs=spaces + [any_space] * (len(hbm) - 1) + [vmem],
         out_specs=[vmem] * (len(out_shape) - hbm_out) + [any_space] * hbm_out,
         scratch_shapes=[
             scratch((2, shards, SEQ_DEVICES // shards) + pieces + (512,), low),
@@ -1851,6 +1965,11 @@
             scratch((width // 128, small_rows, 128), jnp.float32),
             scratch((total, small_rows, 128), jnp.float32),
             scratch(pieces + (KV_RANK,), jnp.float32),
+            scratch((2, 176, width), jnp.float32),
+            scratch((2, shards - 1, 176, width), low),
+            dma((2,)),
+            dma((2, shards)),
+            dma((2,)),
             dma((8,)),
             dma((shards,)),
             dma((2, shards)),
@@ -1914,15 +2033,7 @@
         return lax.dynamic_slice_in_dim(values, own_at, local_rows, 0)
 
     piece_rows = output_weight.shape[0] // plane
-    half = QK_ROPE // 2
-    query_columns = lax.dynamic_slice_in_dim(query_weight, head_at * head_dim, head_dim, 1)
-    query_turn, key_turn = query_columns[:, QK_NOPE:], latent_down[:, KV_RANK:]
-    query_cols = jnp.concatenate(
-        [query_columns, query_turn[:, half:], query_turn[:, :half]], axis=1
-    )
-    down_half = jnp.concatenate(
-        [latent_down, key_turn[:, half:], key_turn[:, :half]], axis=1
-    )
+    down_half = jnp.pad(latent_down, ((0, 0), (0, QK_ROPE)))
     units = shared_down.shape[0] // plane
     unit_pad = -units % 16
     padded_units = units + unit_pad
@@ -1947,17 +2058,10 @@
     def plane_pieces(weight):
         return weight.reshape(plane, 1, -1, weight.shape[1])
 
-    positions = jnp.arange(SEQ, dtype=jnp.int32)
-    cosine_part, sine_part = rotary_tables(positions, QK_ROPE)
-    sequence_count, entry_count = document_lengths.shape
-    ends = jnp.cumsum(document_lengths, axis=1)
-    picked = jnp.arange(sequence_count, dtype=jnp.int32)[:, None] == sequence_at
-    row_ends = jnp.sum(jnp.where(picked, ends, 0), axis=0)
-    documents = jnp.sum((positions[:, None] >= row_ends[None, :]).astype(jnp.int32), axis=1)
-    turn = jnp.tile(cosine_part, (1, 4))
-    sway = jnp.tile(jnp.concatenate([-sine_part, sine_part], axis=1), (1, 2))
-    docs = documents[:, None]
-    row_docs = jnp.pad(docs, ((WINDOW, 0), (0, 0)), constant_values=-1).T
+    angles = np.arange(SEQ)[:, None] * THETA ** (-np.arange(QK_ROPE // 2) / (QK_ROPE // 2))
+    turn = jnp.asarray(np.tile(np.cos(angles), (1, 4)), jnp.float32)
+    sway = jnp.asarray(np.tile(np.sin(angles), (1, 4)) * np.repeat([-1.0, 1.0, -1.0, 1.0], 32), jnp.float32)
+    entry_count = document_lengths.shape[1]
     route_rows = jnp.pad(routes.T, ((0, 8 - TOP), (0, 0)), constant_values=-1)
     (
         all_normed,
@@ -1987,11 +2091,9 @@
         tokens,
         cotangent,
         (
-            query_cols,
+            query_weight,
             plane_pieces(down_half),
-            lax.dynamic_slice_in_dim(
-                latent_up, head_at * (QK_NOPE + V_HEAD), QK_NOPE + V_HEAD, 1
-            ),
+            latent_up,
             plane_pieces(output_weight),
             plane_pieces(query_weight),
             expert_gate[0],
@@ -2002,7 +2104,7 @@
         ),
         route_rows,
         (first_gain[None], latent_gain[None], second_gain[None]),
-        (turn, sway, docs, row_docs),
+        (turn, sway, document_lengths),
     )
     all_normed = all_normed.reshape(-1, width)
     all_grads = all_grads.reshape(-1, width)
@@ -2018,8 +2120,7 @@
         gate_pre_grad,
         up_pre_grad,
         shared_hidden,
-        shared_gate_back,
-        shared_up_back,
+        shared_moved,
         _,
         full_query,
     ) = expert_pass(
@@ -2055,14 +2156,13 @@
         up_send,
         shared_down_own,
         shared_down_send,
-        shared_term,
     ) = sums_pass(
         normed_part.reshape(plane, local_rows, width),
         output_part.reshape(plane, local_rows, width),
         token_scores,
         (slot_rows, slot_grad, hidden, gate_pre_grad, up_pre_grad),
-        (all_normed, all_grads),
-        (shared_hidden, shared_gate_back, shared_up_back),
+        (all_grads,),
+        (shared_hidden,),
     )
     activations = (middle + output_sum).astype(jnp.bfloat16)
 
@@ -2080,11 +2180,13 @@
         latent_down_grad,
         output_weight_grad,
         small_sums,
+        shared_gate_grad,
+        shared_up_grad,
         gate_blocks,
         up_blocks,
         shared_blocks,
-        shared_moved,
         _,
+        expert_down_grad,
     ) = backward_pass(
         scale,
         entry_count - 1,
@@ -2100,7 +2202,7 @@
             latent_gain[None],
             router_weight.T,
         ),
-        (query, keys, value, docs, row_docs, log_total, turn, sway),
+        (document_lengths, query, keys, value, log_total, turn, sway),
         (key_latent, up_head.reshape(KV_RANK, -1), head_out),
         (
             compressed,
@@ -2112,17 +2214,14 @@
             query_weight,
             down_half,
         ),
-        (gate_send, up_send, shared_down_send, shared_term),
+        (gate_send, up_send, shared_down_send),
+        (down_own, down_blocks),
+        shared_moved,
+        shared_gate.shape[1],
     )
-    expert_gate_grad = sum_shards(gate_own, gate_blocks)[None]
-    expert_up_grad = sum_shards(up_own, up_blocks)[None]
-    expert_down_grad = sum_shards(down_own, down_blocks)[None]
+    expert_gate_grad = sum_shards(gate_own, gate_blocks)
+    expert_up_grad = sum_shards(up_own, up_blocks)
     shared_down_grad = sum_shards(shared_down_own, shared_blocks)[:units]
-    shared_moved = shared_moved.astype(jnp.float32).reshape(shards, plane, -1, 2, shards, padded_units)
-    shared_moved = jnp.sum(shared_moved, axis=0)[..., :units].transpose(2, 1, 3, 0, 4)
-    shared_moved = shared_moved.reshape(2, shared_moved.shape[1], -1)
-    shared_gate_grad = shared_moved[0]
-    shared_up_grad = shared_moved[1]
     own_width = width // all_devices
     number = shard_at * plane + plane_at
     own_small = lax.dynamic_slice_in_dim(small_sums, number * own_width % 128, own_width, 1)
@@ -2147,9 +2246,9 @@
         shared_gate_grad,
         shared_up_grad,
         shared_down_grad,
-        expert_gate_grad,
-        expert_up_grad,
-        expert_down_grad,
+        expert_gate_grad[None],
+        expert_up_grad[None],
+        expert_down_grad[None],
     )
 
 

time: 782 us -> 707 us (0.904)
  Pallas kernels: 708 us -> 667 us
  other arithmetic: 32.6 us -> 15.3 us
  local copies, waits for them, and re-layouts: 35.2 us -> 19.8 us
    pallas_call x1, Pallas kernels: 239 us -> 198 us  [backward_pass(): pl.pallas_call(functools.partial(backward_kernel, shards, plane, scale, l...]
    broadcast_in_dim x3 -> x2, other arithmetic: 17.4 us -> 10.1 us  [the longest x1 7.05 us: on_device(): expert_up_grad[None]]
where the time goes in v8:
time: 707 us; the launch traced here: 704 us
  Pallas kernels  667 us (94%)
  local copies, waits for them, and re-layouts  19.8 us (3%)
  other arithmetic  15.3 us (2%)
    pallas_call x1, Pallas kernels, forward_pass(): pl.pallas_call(functools.partial(forward_kernel, shards, plane, scale, la...  213 us
    pallas_call x1, Pallas kernels, backward_pass(): pl.pallas_call(functools.partial(backward_kernel, shards, plane, scale, l...  198 us
    pallas_call x1, Pallas kernels, sums_pass(): pl.pallas_call(functools.partial(sums_kernel, shards, plane), out_shape=o...  129 us
    pallas_call x1, Pallas kernels, expert_pass(): pl.pallas_call(functools.partial(expert_kernel, shards), grid=(2, steps),...  127 us

profile of v8, /device:TPU:9, one launch (start us, length us, event | category | flops | bytes accessed | tf_op | source)
XLA Modules:
  0.0 703.6 jit_solution(7671495663910846107)
XLA Ops:
  0.6 0.0 copy-start.3
  0.7 0.0 copy-start.13
  0.7 2.0 constant_dynamic-slice_fusion.3
  2.7 1.0 fusion.7.refs_9_.refs_4_
  3.7 1.0 fusion.8.refs_10_.refs_6_
  4.8 1.0 constant_dynamic-slice_fusion.1
  5.8 0.8 pad.30.refs_11_.refs_8_
  6.6 0.0 copy-done.3
  6.6 0.7 copy.36
  7.3 1.2 pad.25.refs_27_
  8.4 0.0 copy-done.13
  8.5 0.6 fusion.10
  9.1 212.9 %forward.1 = (bf16[16,2,64,2048]{3,2,1,0:T(8,128)(2,1)}, bf16[16,2,64,2048]{3,2,1,0:T(8,128)(2,1)}, s32[16,1,8,128]{3,2,1,0:T(8,128)}, bf16[2,16,1,64,640]{4,3,2...) custom-call(bf16[2,64,2048]{2,1,0:T(8,128)(2,1)} %bitcast.77, ...), custom_call_target="tpu_custom_call" | custom-call | tf_op jit(solution)/shard_map/forward/pallas_call | solution.py:1185
  221.9 127.2 %experts.1 = (bf16[1024,2048]{1,0:T(8,128)(2,1)}, bf16[1024,2048]{1,0:T(8,128)(2,1)}, bf16[2048,2048]{1,0:T(8,128)(2,1)}, bf16[2048,2048]{1,0:T(8,128)(2,1)}, f3...) custom-call(s32[16,8,128]{2,1,0:T(8,128)} %bitcast.83, ...), custom_call_target="tpu_custom_call" | custom-call | tf_op jit(solution)/shard_map/experts/pallas_call | solution.py:786
  349.1 129.1 %sums.1 = (f32[4,32,2048]{2,1,0:T(8,128)}, f32[4,32,2048]{2,1,0:T(8,128)}, f32[16,8,128]{2,1,0:T(8,128)}, bf16[2,704,2048]{2,1,0:T(8,128)(2,1)}, f32[704,2048]{1...) custom-call(bf16[16,4,32,2048]{3,2,1,0:T(8,128)(2,1)} %bitcast.68, ...), custom_call_target="tpu_custom_call" | custom-call | tf_op jit(solution)/shard_map/sums/pallas_call | solution.py:1407
  478.2 198.4 %backward.1 = (f32[128,2048]{1,0:T(8,128)}, f32[64,3072]{1,0:T(8,128)}, f32[16,4096]{1,0:T(8,128)}, f32[64,576]{1,0:T(8,128)}, f32[64,2048]{1,0:T(8,128)}, /*ind...) custom-call(f32[128,2048]{1,0:T(8,128)} %bitcast.79, ...), custom_call_target="tpu_custom_call" | custom-call | tf_op jit(solution)/shard_map/backward/pallas_call | solution.py:1932
  676.6 0.0 copy-start
  676.6 0.0 copy-start.2
  676.6 7.1 %fusion = f32[1,1024,1408]{2,1,0:T(8,128)} fusion(f32[1024,1408]{1,0:T(8,128)} %get-tuple-element.123, bf16[2,1024,1408]{2,1,0:T(8,128)(2,1)} %get-tuple-element.124, s32[]{:T(128)S(6)} %select_n.51), kind=kLoop, calls=%fused_computation.1 | loop fusion | flops 2883584 | bytes 14417924 | tf_op jit(solution)/shard_map/broadcast_in_dim | solution.py:2250
  683.7 0.0 copy-done
  683.7 1.8 copy-done.2
  685.5 0.0 copy-start.10
  685.5 0.0 copy-start.7
  685.5 0.0 copy-start.12
  685.5 0.0 copy-start.1
  685.5 3.0 fusion.1
  688.5 0.0 copy-start.4
  688.5 0.0 copy-done.10
  688.6 0.0 copy-done.7
  688.6 0.0 slice-start
  688.6 0.9 slice_add_fusion
  689.5 0.0 copy-done.12
  689.5 0.7 dynamic-slice_bitcast_fusion.1
  690.2 0.6 dynamic-slice_bitcast_fusion.2
  690.8 0.0 copy-start.11
  690.8 0.0 copy-start.9
  690.8 0.0 copy-start.8
  690.8 0.0 copy-start.6
  690.8 0.0 copy-start.5
  690.8 0.6 fusion.9
  691.4 0.0 copy-done.1
  691.4 2.2 fusion.6
  693.7 0.0 slice-start.1
  693.7 2.4 copy.46
  696.1 0.0 copy-done.4
  696.1 0.9 copy.47
  697.0 0.0 copy-done.11
  697.0 0.7 copy.48
  697.7 0.0 copy-done.9
  697.7 0.7 copy.49
  698.4 0.0 copy-done.8
  698.4 0.8 copy.50
  699.2 0.0 copy-done.6
  699.2 0.9 copy.51
  700.0 0.0 copy-done.5
  700.0 0.9 copy.52
  700.9 0.0 slice-done
  700.9 0.0 slice-done.1
  700.9 2.5 copy.53
  (3 shorter events, 0.0 us)
Async XLA Ops:
  0.6 5.9 copy-start.3
  0.7 7.8 %copy-start.13 = (s32[128,6]{0,1:T(8,128)S(1)}, s32[128,6]{0,1:T(8,128)}, u32[]{:S(2)}) copy-start(s32[128,6]{0,1:T(8,128)} %param.22) | copy-start | bytes 9220
  676.6 7.1 %copy-start = (f32[1024,1408]{1,0:T(8,128)S(1)}, f32[1024,1408]{1,0:T(8,128)}, u32[]{:S(2)}) copy-start(f32[1024,1408]{1,0:T(8,128)} %get-tuple-element.121) | copy-start | bytes 17301508
  676.6 8.9 %copy-start.2 = (bf16[2,1024,1408]{2,1,0:T(8,128)(2,1)S(1)}, bf16[2,1024,1408]{2,1,0:T(8,128)(2,1)}, u32[]{:S(2)}) copy-start(bf16[2,1024,1408]{2,1,0:T(8,128)(2,1)} %get-tuple-element.122) | copy-start | bytes 17301508
  685.5 3.0 copy-start.10
  685.5 3.0 copy-start.7
  685.5 4.0 copy-start.12
  685.5 5.9 copy-start.1
  688.5 7.6 %copy-start.4 = (f32[64,3072]{1,0:T(8,128)S(1)}, f32[64,3072]{1,0:T(8,128)}, u32[]{:S(2)}) copy-start(f32[64,3072]{1,0:T(8,128)} %get-tuple-element.155) | copy-start | bytes 2359300
  688.6 12.3 %slice-start = ((s8[5767168]{0:T(1024)(128)(4,1)}), s8[1572864]{0:T(1024)(128)(4,1)S(1)}, s32[]{:S(2)}) async-start(s8[5767168]{0:T(1024)(128)(4,1)} %bitcast.72), calls=%async_computation | async-start | bytes 3145728
  690.8 6.2 copy-start.11
  690.8 6.9 copy-start.9
  690.8 7.6 %copy-start.8 = (f32[64,2048]{1,0:T(8,128)S(1)}, f32[64,2048]{1,0:T(8,128)}, u32[]{:S(2)}) copy-start(f32[64,2048]{1,0:T(8,128)} %get-tuple-element.159) | copy-start | bytes 1572868
  690.8 8.4 %copy-start.6 = (f32[64,2816]{1,0:T(8,128)S(1)}, f32[64,2816]{1,0:T(8,128)}, u32[]{:S(2)}) copy-start(f32[64,2816]{1,0:T(8,128)} %get-tuple-element.162) | copy-start | bytes 2162692
  690.8 9.2 %copy-start.5 = (f32[64,2816]{1,0:T(8,128)S(1)}, f32[64,2816]{1,0:T(8,128)}, u32[]{:S(2)}) copy-start(f32[64,2816]{1,0:T(8,128)} %get-tuple-element.163) | copy-start | bytes 2162692
  693.7 7.2 %slice-start.1 = ((s8[5767168]{0:T(1024)(128)(4,1)}), s8[4194304]{0:T(1024)(128)(4,1)S(1)}, s32[]{:S(2)}) async-start(s8[5767168]{0:T(1024)(128)(4,1)} %bitcast.72), calls=%async_computation.1 | async-start | bytes 8388608

commit v9 on v8

--- a/solution.py
+++ b/solution.py
@@ -1363,6 +1363,9 @@
     for index in range(units):
         next(work, None)
         next(back_run)
+        if index >= units // 2:
+            next(output_run, None)
+            next(output_run, None)
     for index in range(units):
         next(work, None)
         next(output_run, None)

time: 707 us -> 695 us (0.983)
  Pallas kernels: 667 us -> 655 us
    pallas_call x1, Pallas kernels: 129 us -> 116 us  [sums_pass(): pl.pallas_call(functools.partial(sums_kernel, shards, plane), out_shape=o...]
where the time goes in v9:
time: 695 us; the launch traced here: 691 us
  Pallas kernels  655 us (94%)
  local copies, waits for them, and re-layouts  19.8 us (3%)
  other arithmetic  15.3 us (2%)
    pallas_call x1, Pallas kernels, forward_pass(): pl.pallas_call(functools.partial(forward_kernel, shards, plane, scale, la...  213 us
    pallas_call x1, Pallas kernels, backward_pass(): pl.pallas_call(functools.partial(backward_kernel, shards, plane, scale, l...  199 us
    pallas_call x1, Pallas kernels, expert_pass(): pl.pallas_call(functools.partial(expert_kernel, shards), grid=(2, steps),...  127 us
    pallas_call x1, Pallas kernels, sums_pass(): pl.pallas_call(functools.partial(sums_kernel, shards, plane), out_shape=o...  116 us

profile of v9, /device:TPU:9, one launch (start us, length us, event | category | flops | bytes accessed | tf_op | source)
XLA Modules:
  0.0 691.2 jit_solution(8611466675273700475)
XLA Ops:
  0.6 0.0 copy-start.3
  0.7 0.0 copy-start.13
  0.7 2.0 constant_dynamic-slice_fusion.3
  2.7 1.0 fusion.7.refs_9_.refs_4_
  3.7 1.0 fusion.8.refs_10_.refs_6_
  4.8 1.0 constant_dynamic-slice_fusion.1
  5.8 0.8 pad.30.refs_11_.refs_8_
  6.6 0.0 copy-done.3
  6.6 0.7 copy.36
  7.3 1.2 pad.25.refs_27_
  8.4 0.0 copy-done.13
  8.5 0.6 fusion.10
  9.1 212.9 %forward.1 = (bf16[16,2,64,2048]{3,2,1,0:T(8,128)(2,1)}, bf16[16,2,64,2048]{3,2,1,0:T(8,128)(2,1)}, s32[16,1,8,128]{3,2,1,0:T(8,128)}, bf16[2,16,1,64,640]{4,3,2...) custom-call(bf16[2,64,2048]{2,1,0:T(8,128)(2,1)} %bitcast.77, ...), custom_call_target="tpu_custom_call" | custom-call | tf_op jit(solution)/shard_map/forward/pallas_call | solution.py:1185
  221.9 127.2 %experts.1 = (bf16[1024,2048]{1,0:T(8,128)(2,1)}, bf16[1024,2048]{1,0:T(8,128)(2,1)}, bf16[2048,2048]{1,0:T(8,128)(2,1)}, bf16[2048,2048]{1,0:T(8,128)(2,1)}, f3...) custom-call(s32[16,8,128]{2,1,0:T(8,128)} %bitcast.83, ...), custom_call_target="tpu_custom_call" | custom-call | tf_op jit(solution)/shard_map/experts/pallas_call | solution.py:786
  349.1 116.3 %sums.1 = (f32[4,32,2048]{2,1,0:T(8,128)}, f32[4,32,2048]{2,1,0:T(8,128)}, f32[16,8,128]{2,1,0:T(8,128)}, bf16[2,704,2048]{2,1,0:T(8,128)(2,1)}, f32[704,2048]{1...) custom-call(bf16[16,4,32,2048]{3,2,1,0:T(8,128)(2,1)} %bitcast.68, ...), custom_call_target="tpu_custom_call" | custom-call | tf_op jit(solution)/shard_map/sums/pallas_call | solution.py:1410
  465.5 198.7 %backward.1 = (f32[128,2048]{1,0:T(8,128)}, f32[64,3072]{1,0:T(8,128)}, f32[16,4096]{1,0:T(8,128)}, f32[64,576]{1,0:T(8,128)}, f32[64,2048]{1,0:T(8,128)}, /*ind...) custom-call(f32[128,2048]{1,0:T(8,128)} %bitcast.79, ...), custom_call_target="tpu_custom_call" | custom-call | tf_op jit(solution)/shard_map/backward/pallas_call | solution.py:1935
  664.2 0.0 copy-start
  664.2 0.0 copy-start.2
  664.2 7.1 %fusion = f32[1,1024,1408]{2,1,0:T(8,128)} fusion(f32[1024,1408]{1,0:T(8,128)} %get-tuple-element.123, bf16[2,1024,1408]{2,1,0:T(8,128)(2,1)} %get-tuple-element.124, s32[]{:T(128)S(6)} %select_n.51), kind=kLoop, calls=%fused_computation.1 | loop fusion | flops 2883584 | bytes 14417924 | tf_op jit(solution)/shard_map/broadcast_in_dim | solution.py:2253
  671.3 0.0 copy-done
  671.3 1.8 copy-done.2
  673.1 0.0 copy-start.10
  673.1 0.0 copy-start.7
  673.1 0.0 copy-start.12
  673.1 0.0 copy-start.1
  673.1 3.0 fusion.1
  676.1 0.0 copy-start.4
  676.1 0.0 copy-done.10
  676.2 0.0 copy-done.7
  676.2 0.0 slice-start
  676.2 0.9 slice_add_fusion
  677.1 0.0 copy-done.12
  677.1 0.7 dynamic-slice_bitcast_fusion.1
  677.8 0.6 dynamic-slice_bitcast_fusion.2
  678.4 0.0 copy-start.11
  678.4 0.0 copy-start.9
  678.4 0.0 copy-start.8
  678.4 0.0 copy-start.6
  678.4 0.0 copy-start.5
  678.4 0.6 fusion.9
  679.0 0.0 copy-done.1
  679.0 2.2 fusion.6
  681.3 0.0 slice-start.1
  681.3 2.4 copy.46
  683.7 0.0 copy-done.4
  683.7 0.9 copy.47
  684.6 0.0 copy-done.11
  684.6 0.7 copy.48
  685.3 0.0 copy-done.9
  685.3 0.7 copy.49
  686.0 0.0 copy-done.8
  686.0 0.8 copy.50
  686.8 0.0 copy-done.6
  686.8 0.9 copy.51
  687.6 0.0 copy-done.5
  687.6 0.9 copy.52
  688.5 0.0 slice-done
  688.5 0.0 slice-done.1
  688.5 2.5 copy.53
  (3 shorter events, 0.0 us)
Async XLA Ops:
  0.6 5.9 copy-start.3
  0.7 7.8 %copy-start.13 = (s32[128,6]{0,1:T(8,128)S(1)}, s32[128,6]{0,1:T(8,128)}, u32[]{:S(2)}) copy-start(s32[128,6]{0,1:T(8,128)} %param.22) | copy-start | bytes 9220
  664.2 7.1 %copy-start = (f32[1024,1408]{1,0:T(8,128)S(1)}, f32[1024,1408]{1,0:T(8,128)}, u32[]{:S(2)}) copy-start(f32[1024,1408]{1,0:T(8,128)} %get-tuple-element.121) | copy-start | bytes 17301508
  664.2 8.9 %copy-start.2 = (bf16[2,1024,1408]{2,1,0:T(8,128)(2,1)S(1)}, bf16[2,1024,1408]{2,1,0:T(8,128)(2,1)}, u32[]{:S(2)}) copy-start(bf16[2,1024,1408]{2,1,0:T(8,128)(2,1)} %get-tuple-element.122) | copy-start | bytes 17301508
  673.1 3.0 copy-start.10
  673.1 3.0 copy-start.7
  673.1 4.0 copy-start.12
  673.1 5.9 copy-start.1
  676.1 7.6 %copy-start.4 = (f32[64,3072]{1,0:T(8,128)S(1)}, f32[64,3072]{1,0:T(8,128)}, u32[]{:S(2)}) copy-start(f32[64,3072]{1,0:T(8,128)} %get-tuple-element.155) | copy-start | bytes 2359300
  676.2 12.3 %slice-start = ((s8[5767168]{0:T(1024)(128)(4,1)}), s8[1572864]{0:T(1024)(128)(4,1)S(1)}, s32[]{:S(2)}) async-start(s8[5767168]{0:T(1024)(128)(4,1)} %bitcast.72), calls=%async_computation | async-start | bytes 3145728
  678.4 6.2 copy-start.11
  678.4 6.9 copy-start.9
  678.4 7.6 %copy-start.8 = (f32[64,2048]{1,0:T(8,128)S(1)}, f32[64,2048]{1,0:T(8,128)}, u32[]{:S(2)}) copy-start(f32[64,2048]{1,0:T(8,128)} %get-tuple-element.159) | copy-start | bytes 1572868
  678.4 8.4 %copy-start.6 = (f32[64,2816]{1,0:T(8,128)S(1)}, f32[64,2816]{1,0:T(8,128)}, u32[]{:S(2)}) copy-start(f32[64,2816]{1,0:T(8,128)} %get-tuple-element.162) | copy-start | bytes 2162692
  678.4 9.2 %copy-start.5 = (f32[64,2816]{1,0:T(8,128)S(1)}, f32[64,2816]{1,0:T(8,128)}, u32[]{:S(2)}) copy-start(f32[64,2816]{1,0:T(8,128)} %get-tuple-element.163) | copy-start | bytes 2162692
  681.3 7.2 %slice-start.1 = ((s8[5767168]{0:T(1024)(128)(4,1)}), s8[4194304]{0:T(1024)(128)(4,1)S(1)}, s32[]{:S(2)}) async-start(s8[5767168]{0:T(1024)(128)(4,1)} %bitcast.72), calls=%async_computation.1 | async-start | bytes 8388608
